TPU v7x, 32 devices: a whole 2x2x4 slice. The times are simulated.
32 devices in a mesh: row: 4 (over z), col: 8 (over y, x, core).
Axes of the slice: x: 2, y: 2, z: 4, core: 2. Of those that a mesh axis runs over, the one named last changes fastest.
Arguments:
- tokens: bfloat16 [32768, 1024], P(('row', 'col')), may hold values from -6 to 6
- condition: bfloat16 [32, 1024], P('row', 'col'), may hold values from -6 to 6
- mod_weight: bfloat16 [1024, 6, 1024], P('row', None, 'col'), may hold values from -0.1875 to 0.1875
- mod_bias: bfloat16 [6, 1024], P(None, 'col'), may hold values from -4 to 4
- qkv_weight: bfloat16 [1024, 16, 192], P('row', 'col'), may hold values from -0.1875 to 0.1875
- qv_bias: bfloat16 [16, 128], P('col'), may hold values from -4 to 4
- out_weight: bfloat16 [16, 64, 1024], P('col', None, 'row'), may hold values from -0.75 to 0.75
- out_bias: bfloat16 [1024], P('col'), may hold values from -4 to 4
- fc1_weight: bfloat16 [1024, 4096], P('row', 'col'), may hold values from -0.1875 to 0.1875
- fc1_bias: bfloat16 [4096], P('col'), may hold values from -4 to 4
- fc2_weight: bfloat16 [4096, 1024], P('col', 'row'), may hold values from -0.09375 to 0.09375
- fc2_bias: bfloat16 [1024], P('col'), may hold values from -4 to 4
- cotangent: bfloat16 [32768, 1024], P(('row', 'col')), may hold values from -6 to 6
Outputs:
- layer_out: bfloat16 [32768, 1024], P(('row', 'col'))
- tokens_grad: float32 [32768, 1024], P(('row', 'col'))
- condition_grad: float32 [32, 1024], P('row', 'col')
- mod_weight_grad: float32 [1024, 6, 1024], P('row', None, 'col')
- mod_bias_grad: float32 [6, 1024], P(None, 'col')
- qkv_weight_grad: float32 [1024, 16, 192], P('row', 'col')
- qv_bias_grad: float32 [16, 128], P('col')
- out_weight_grad: float32 [16, 64, 1024], P('col', None, 'row')
- out_bias_grad: float32 [1024], P('col')
- fc1_weight_grad: float32 [1024, 4096], P('row', 'col')
- fc1_bias_grad: float32 [4096], P('col')
- fc2_weight_grad: float32 [4096, 1024], P('col', 'row')
- fc2_bias_grad: float32 [1024], P('col')
All inputs are finite; a program needn't handle non-finite values.
Results may differ from a plain program's by a relative error of at most 0.02.
Values may be sent and summed in bfloat16 or wider, within the bound.
No kernel may reach another device: no remote copies, remote signals or barrier semaphores. Data moves between devices by JAX's collectives and lax.ppermute only.
A program may use at most 320 MiB of HBM per device.

v0:
```python
import math

import jax
import jax.numpy as jnp
from jax import lax
from jax.sharding import PartitionSpec as P

D = 1024
HD = 64
LEN = 1024


EPSILON = 1e-06
PRECISE = lax.Precision.HIGHEST
CONTRACT_ROWS = (((0,), (0,)), ((), ()))
CONTRACT_COLS = (((1,), (1,)), ((), ()))


def silu_fn(values):
    return values * jax.nn.sigmoid(values)


def gelu_tanh(values):
    return (
        0.5
        * values
        * (
            1.0
            + jnp.tanh(math.sqrt(2.0 / math.pi) * (values + 0.044715 * values * values * values))
        )
    )


def to_items(array, seq_rows):
    heads_here = array.shape[1]
    return (
        array.reshape(seq_rows, LEN, heads_here, HD)
        .transpose(0, 2, 1, 3)
        .reshape(seq_rows * heads_here, LEN, HD)
    )


def from_items(array, seq_rows):
    heads_here = array.shape[0] // seq_rows
    return (
        array.reshape(seq_rows, heads_here, LEN, HD)
        .transpose(0, 2, 1, 3)
        .reshape(seq_rows * LEN, heads_here * HD)
    )


def normalize(resid):
    average = jnp.mean(resid, 1, keepdims=True)
    spread = jnp.mean(resid * resid, 1, keepdims=True) - average * average
    inv_std = lax.rsqrt(spread + EPSILON)
    return ((resid - average) * inv_std, inv_std)


def normalize_back(grad_norm, normed, inv_std):
    average = jnp.mean(grad_norm, 1, keepdims=True)
    crossed = jnp.mean(grad_norm * normed, 1, keepdims=True)
    return inv_std * (grad_norm - average - normed * crossed)


def first_product(hidden, weight_rows):
    return (
        jnp.dot(
            lax.all_gather(hidden, "col", axis=0, tiled=True),
            weight_rows,
            preferred_element_type=jnp.float32,
        ),
        hidden,
    )


def first_weight_grad(hidden, grad_low):
    return lax.dot_general(
        lax.all_gather(hidden, "col", axis=0, tiled=True),
        grad_low,
        CONTRACT_ROWS,
        preferred_element_type=jnp.float32,
    )


def branch_total(partial_rows):
    return lax.psum_scatter(
        partial_rows.astype(jnp.bfloat16), "col", scatter_dimension=0, tiled=True
    ).astype(jnp.float32)


def input_total(partial_rows):
    return lax.psum_scatter(
        partial_rows.astype(jnp.bfloat16), "col", scatter_dimension=0, tiled=True
    ).astype(jnp.float32)


def to_tokens(head_rows):
    return lax.all_to_all(head_rows, "col", split_axis=0, concat_axis=1, tiled=True)


def group_sum(left, right, groups, form):
    parts = jnp.einsum(
        form, left.reshape(left.shape[0], groups, -1), right, preferred_element_type=jnp.float32
    )
    return jnp.sum(parts.astype(jnp.bfloat16).astype(jnp.float32), 0)


def second_back(grad_low, acts_low, weight_rows):
    incoming = lax.all_gather(grad_low, "col", axis=0, tiled=True)
    block_grad = lax.dot_general(
        incoming, weight_rows, CONTRACT_COLS, preferred_element_type=jnp.float32
    )
    grad_weight = lax.dot_general(
        acts_low, incoming, CONTRACT_ROWS, preferred_element_type=jnp.float32
    )
    return (block_grad, grad_weight)


def attend(queries, key_rows, value_rows):
    scores = lax.dot_general(
        queries, key_rows, CONTRACT_COLS, preferred_element_type=jnp.float32
    ) * HD ** (-0.5)
    row_max = jnp.max(scores, 1, keepdims=True)
    expon = jnp.exp(scores - row_max)
    row_total = jnp.sum(expon, 1, keepdims=True)
    prob_low = (expon / row_total).astype(jnp.bfloat16)
    mixed_rows = jnp.dot(prob_low, value_rows, preferred_element_type=jnp.float32)
    return (mixed_rows.astype(jnp.bfloat16), (row_max + jnp.log(row_total))[:, 0])


def attend_back(queries, key_rows, value_rows, log_total, grad_rows):
    scores = lax.dot_general(
        queries, key_rows, CONTRACT_COLS, preferred_element_type=jnp.float32
    ) * HD ** (-0.5)
    prob_rows = jnp.exp(scores - log_total[:, None])
    grad_value = lax.dot_general(
        prob_rows.astype(jnp.bfloat16), grad_rows, CONTRACT_ROWS, preferred_element_type=jnp.float32
    )
    grad_probs = lax.dot_general(
        grad_rows, value_rows, CONTRACT_COLS, preferred_element_type=jnp.float32
    )
    row_inner = jnp.sum(prob_rows * grad_probs, 1, keepdims=True)
    grad_scores = (prob_rows * (grad_probs - row_inner)).astype(jnp.bfloat16)
    grad_query = jnp.dot(grad_scores, key_rows, preferred_element_type=jnp.float32) * HD ** (-0.5)
    grad_key = lax.dot_general(
        grad_scores, queries, CONTRACT_ROWS, preferred_element_type=jnp.float32
    ) * HD ** (-0.5)
    return (
        grad_query.astype(jnp.bfloat16),
        grad_key.astype(jnp.bfloat16),
        grad_value.astype(jnp.bfloat16),
    )


def per_device(
    tokens,
    condition,
    mod_weight,
    mod_bias,
    qkv_weight,
    qv_bias,
    out_weight,
    out_bias,
    fc1_weight,
    fc1_bias,
    fc2_weight,
    fc2_bias,
    cotangent,
):
    local_rows = tokens.shape[0]
    col_count = lax.axis_size("col")
    row_tokens = local_rows * col_count
    seq_rows = row_tokens // LEN
    local_heads = qkv_weight.shape[1]
    local_width = mod_bias.shape[1]
    mod_w, qkv_w, out_w, fc1_w, fc2_w = (
        lax.all_gather(mod_weight, "row", axis=0, tiled=True),
        lax.all_gather(qkv_weight, "row", axis=0, tiled=True),
        lax.all_gather(out_weight, "row", axis=2, tiled=True),
        lax.all_gather(fc1_weight, "row", axis=0, tiled=True),
        lax.all_gather(fc2_weight, "row", axis=1, tiled=True),
    )
    qkv_flat = qkv_w.reshape(D, local_heads * 3 * HD)
    out_flat = out_w.reshape(local_heads * HD, D)
    mod_flat = mod_w.reshape(D, 6 * local_width)
    cond_whole, out_bias_all, fc2_bias_all, qkv_whole, out_whole = (
        lax.all_gather(condition, "col", axis=1, tiled=True),
        lax.all_gather(out_bias, "col", axis=0, tiled=True),
        lax.all_gather(fc2_bias, "col", axis=0, tiled=True),
        lax.all_gather(qkv_w, "col", axis=1, tiled=True),
        lax.all_gather(out_w, "col", axis=0, tiled=True),
    )
    cond_act = silu_fn(cond_whole.astype(jnp.float32)).astype(jnp.bfloat16)
    modulation = jnp.dot(cond_act, mod_flat, preferred_element_type=jnp.float32).reshape(
        seq_rows, 6, local_width
    ) + mod_bias.astype(jnp.float32)
    mod_whole = lax.all_gather(modulation, "col", axis=2, tiled=True)
    owner = (lax.axis_index("col") * local_rows + lax.iota(jnp.int32, local_rows)) // LEN
    choose = (owner[:, None] == lax.iota(jnp.int32, seq_rows)[None, :]).astype(jnp.float32)
    per_token = jnp.dot(
        choose,
        mod_whole.reshape(seq_rows, 6 * D),
        precision=PRECISE,
        preferred_element_type=jnp.float32,
    ).reshape(local_rows, 6, D)
    shift_attn = per_token[:, 0]
    scale_attn = per_token[:, 1]
    gate_attn = per_token[:, 2]
    shift_feed = per_token[:, 3]
    scale_feed = per_token[:, 4]
    gate_feed = per_token[:, 5]
    resid = tokens.astype(jnp.float32)
    normed_attn, inv_attn = normalize(resid)
    hidden_attn = (normed_attn * (1.0 + scale_attn) + shift_attn).astype(jnp.bfloat16)
    projected, features_attn = first_product(hidden_attn, qkv_flat)
    projected = projected.reshape(row_tokens, local_heads, 3 * HD)
    q_rows = (projected[..., :HD] + qv_bias[:, :HD]).astype(jnp.bfloat16)
    k_rows = projected[..., HD : 2 * HD].astype(jnp.bfloat16)
    v_rows = (projected[..., 2 * HD :] + qv_bias[:, HD:]).astype(jnp.bfloat16)
    q_items = to_items(q_rows, seq_rows)
    k_items = to_items(k_rows, seq_rows)
    v_items = to_items(v_rows, seq_rows)
    mixed_items, log_totals = lax.map(
        lambda bundle: attend(bundle[0], bundle[1], bundle[2]), (q_items, k_items, v_items)
    )
    mixed_flat = from_items(mixed_items, seq_rows)
    mixed_tokens = to_tokens(mixed_flat)
    attention_out = group_sum(
        mixed_tokens, out_whole.reshape(col_count, -1, D), col_count, "tcm,cmd->ctd"
    ) + out_bias_all.astype(jnp.float32)
    resid_mid = resid + gate_attn * attention_out
    normed_feed, inv_feed = normalize(resid_mid)
    hidden_feed = (normed_feed * (1.0 + scale_feed) + shift_feed).astype(jnp.bfloat16)
    pre_act, features_feed = first_product(hidden_feed, fc1_w)
    pre_act = pre_act + fc1_bias
    gelu_out, gelu_pull = jax.vjp(gelu_tanh, pre_act)
    activation = gelu_out.astype(jnp.bfloat16)
    feed_out = branch_total(
        jnp.dot(activation, fc2_w, preferred_element_type=jnp.float32)
    ) + fc2_bias_all.astype(jnp.float32)
    layer_out = (resid_mid + gate_feed * feed_out).astype(jnp.bfloat16)
    upstream = cotangent.astype(jnp.float32)
    grad_feed = upstream * gate_feed
    bias_fc2 = jnp.sum(grad_feed, 0)
    grad_activation, grad_fc2 = second_back(grad_feed.astype(jnp.bfloat16), activation, fc2_w)
    grad_pre = gelu_pull(grad_activation)[0].astype(jnp.bfloat16)
    bias_fc1 = jnp.sum(grad_pre.astype(jnp.float32), 0)
    grad_fc1 = first_weight_grad(hidden_feed, grad_pre)
    grad_hidden_feed = input_total(
        lax.dot_general(grad_pre, fc1_w, CONTRACT_COLS, preferred_element_type=jnp.float32)
    )
    grad_resid_mid = upstream + normalize_back(
        grad_hidden_feed * (1.0 + scale_feed), normed_feed, inv_feed
    )
    grad_attention = grad_resid_mid * gate_attn
    bias_out = jnp.sum(grad_attention, 0)
    grad_mixed, grad_out = second_back(grad_attention.astype(jnp.bfloat16), mixed_flat, out_flat)
    grad_items = to_items(
        grad_mixed.astype(jnp.bfloat16).reshape(row_tokens, local_heads, HD), seq_rows
    )
    grad_q_items, grad_k_items, grad_v_items = lax.map(
        lambda bundle: attend_back(bundle[0], bundle[1], bundle[2], bundle[3], bundle[4]),
        (q_items, k_items, v_items, log_totals, grad_items),
    )
    grad_q = from_items(grad_q_items, seq_rows).reshape(row_tokens, local_heads, HD)
    grad_k = from_items(grad_k_items, seq_rows).reshape(row_tokens, local_heads, HD)
    grad_v = from_items(grad_v_items, seq_rows).reshape(row_tokens, local_heads, HD)
    bias_qv = jnp.concatenate(
        [jnp.sum(grad_q.astype(jnp.float32), 0), jnp.sum(grad_v.astype(jnp.float32), 0)], -1
    )
    grad_projected = jnp.concatenate([grad_q, grad_k, grad_v], -1).reshape(
        row_tokens, local_heads * 3 * HD
    )
    grad_qkv = first_weight_grad(hidden_attn, grad_projected).reshape(D, local_heads, 3 * HD)
    grad_tokens = to_tokens(grad_projected)
    grad_hidden_attn = group_sum(
        grad_tokens, qkv_whole.reshape(D, col_count, -1), col_count, "tcj,dcj->ctd"
    )
    tokens_grad = grad_resid_mid + normalize_back(
        grad_hidden_attn * (1.0 + scale_attn), normed_attn, inv_attn
    )
    token_terms = jnp.stack(
        [
            grad_hidden_attn,
            grad_hidden_attn * normed_attn,
            grad_resid_mid * attention_out,
            grad_hidden_feed,
            grad_hidden_feed * normed_feed,
            upstream * feed_out,
        ],
        1,
    ).reshape(local_rows, 6 * D)
    latent_part = lax.dot_general(
        choose, token_terms, CONTRACT_ROWS, precision=PRECISE, preferred_element_type=jnp.float32
    ).reshape(seq_rows, 6, D)
    bias_pair = jnp.stack([bias_out, bias_fc2], 0)
    grad_modulation, bias_pair_col = (
        lax.psum_scatter(
            latent_part.astype(jnp.bfloat16), "col", scatter_dimension=2, tiled=True
        ).astype(jnp.float32),
        lax.psum_scatter(
            bias_pair.astype(jnp.bfloat16), "col", scatter_dimension=1, tiled=True
        ).astype(jnp.float32),
    )
    bias_mod = jnp.sum(grad_modulation, 0)
    grad_mod_flat = grad_modulation.reshape(seq_rows, 6 * local_width)
    grad_mod_weight = lax.dot_general(
        cond_act.astype(jnp.float32),
        grad_mod_flat,
        CONTRACT_ROWS,
        precision=PRECISE,
        preferred_element_type=jnp.float32,
    ).reshape(D, 6, local_width)
    grad_cond_part = lax.dot_general(
        grad_mod_flat,
        mod_flat.astype(jnp.float32),
        CONTRACT_COLS,
        precision=PRECISE,
        preferred_element_type=jnp.float32,
    )
    grad_cond_act = lax.psum_scatter(
        grad_cond_part.astype(jnp.bfloat16), "col", scatter_dimension=1, tiled=True
    ).astype(jnp.float32)
    silu_vals, silu_pull = jax.vjp(silu_fn, condition.astype(jnp.float32))
    condition_grad = silu_pull(grad_cond_act)[0]
    grad_out_blocks = grad_out.reshape(local_heads, HD, D)
    mod_part, qkv_part, out_part, fc1_part, fc2_part = (
        lax.psum_scatter(
            grad_mod_weight.astype(jnp.bfloat16), "row", scatter_dimension=0, tiled=True
        ).astype(jnp.float32),
        lax.psum_scatter(
            grad_qkv.astype(jnp.bfloat16), "row", scatter_dimension=0, tiled=True
        ).astype(jnp.float32),
        lax.psum_scatter(
            grad_out_blocks.astype(jnp.bfloat16), "row", scatter_dimension=2, tiled=True
        ).astype(jnp.float32),
        lax.psum_scatter(
            grad_fc1.astype(jnp.bfloat16), "row", scatter_dimension=0, tiled=True
        ).astype(jnp.float32),
        lax.psum_scatter(
            grad_fc2.astype(jnp.bfloat16), "row", scatter_dimension=1, tiled=True
        ).astype(jnp.float32),
    )
    mod_bias_grad, qv_bias_grad, out_bias_grad, fc1_bias_grad, fc2_bias_grad = lax.psum(
        (bias_mod, bias_qv, bias_pair_col[0], bias_fc1, bias_pair_col[1]), "row"
    )
    return (
        layer_out,
        tokens_grad,
        condition_grad,
        mod_part,
        mod_bias_grad,
        qkv_part,
        qv_bias_grad,
        out_part,
        out_bias_grad,
        fc1_part,
        fc1_bias_grad,
        fc2_part,
        fc2_bias_grad,
    )


def solution(mesh):
    return jax.shard_map(
        per_device,
        mesh=mesh,
        in_specs=(
            P(("row", "col"), None),
            P("row", "col"),
            P("row", None, "col"),
            P(None, "col"),
            P("row", "col", None),
            P("col", None),
            P("col", None, "row"),
            P("col"),
            P("row", "col"),
            P("col"),
            P("col", "row"),
            P("col"),
            P(("row", "col"), None),
        ),
        out_specs=(
            P(("row", "col"), None),
            P(("row", "col"), None),
            P("row", "col"),
            P("row", None, "col"),
            P(None, "col"),
            P("row", "col", None),
            P("col", None),
            P("col", None, "row"),
            P("col"),
            P("row", "col"),
            P("col"),
            P("col", "row"),
            P("col"),
        ),
        check_vma=False,
    )
```

profile of v0, /device:TPU:0, one launch (start us, length us, event | category | flops | bytes accessed | tf_op | source)
XLA Modules:
  0.0 1637.6 jit_solution(4250089723080989469)
XLA Ops:
  11.5 10.4 all_gather.47
  22.6 26.9 %all-gather.12.cloned.1.call-done = bf16[1024,6,128]{2,0,1:T(8,128)(2,1)} async-done(((bf16[256,6,128]{2,0,1:T(8,128)(2,1)}), bf16[1024,6,128]{2,0,1:T(8,128)(2,1)}) %all-gather.12.cloned.1.call-update) | async-done | bytes 1572880 | tf_op jit(solution)/shard_map/all_gather | solution.py:177
  53.9 9.5 all_gather.49
  63.4 10.0 fusion.122
  73.5 8.3 copy-done
  84.4 14.7 all_gather.52
  99.2 17.9 %all_gather.51 = bf16[1024,2,192]{0,2,1:T(8,128)(2,1)S(1)} all-gather(bf16[256,2,192]{0,2,1:T(8,128)(2,1)} %param.21), channel_id=1, replica_groups=mesh['row'=4,'col'=8] {'row'}, dimensions={0}, use_global_device_ids=true | all-gather | bytes 983040 | tf_op jit(solution)/shard_map/all_gather | solution.py:178
  117.1 55.2 %all-gather.14.cloned.1.call-done = bf16[8192,1024]{0,1:T(8,128)(2,1)} async-done(((bf16[1024,1024]{0,1:T(8,128)(2,1)}), bf16[8192,1024]{0,1:T(8,128)(2,1)}) %all-gather.14.cloned.1.call-update) | async-done | bytes 16777232 | tf_op jit(solution)/shard_map/all_gather | solution.py:68
  172.3 10.9 fusion.67
  209.6 113.9 %while.26 = (s32[]{:T(128)}, bf16[16,1024,64]{1,2,0:T(8,128)(2,1)}, f32[16,1024]{1,0:T(8,128)}, bf16[16,1024,64]{2,1,0:T(8,128)(2,1)}, bf16[16,1024,64]{2,1,0:T(...) while((s32[]{:T(128)}, bf16[16,1024,64]{1,2,0:T(8,128)(2,1)}, f32[16,1024]{1,0:T(8,128)}, ...), condition=%wide.region_5.6_spmd, body=%wide.region_2.5_spmd.sunk | while | flops 277937152 | bytes 13543521 | solution.py:223
  332.4 28.9 %all-gather = bf16[8,1,128]{2,1,0:T(2,128)(2,1)S(1)} all-gather(bf16[1,1,128]{2,1,0:T(2,128)(2,1)S(1)} %bitcast.406), channel_id=1, replica_groups=mesh['row'=4,'col'=8] {'col'}, dimensions={0}, use_global_device_ids=true | all-gather | bytes 2304 | tf_op jit(solution)/shard_map/all_gather | solution.py:188
  365.3 9.0 convert_reduce_fusion.1
  374.2 5.4 copy.96
  383.9 8.8 fusion.99
  394.2 87.9 %all-gather.18.cloned.1.call-done = bf16[8192,1024]{0,1:T(8,128)(2,1)} async-done(((bf16[1024,1024]{0,1:T(8,128)(2,1)}), bf16[8192,1024]{0,1:T(8,128)(2,1)}) %all-gather.18.cloned.1.call-update) | async-done | bytes 16777232 | tf_op jit(solution)/shard_map/all_gather | solution.py:68
  482.1 16.0 fusion.150
  498.1 15.6 all-gather.22.cloned.1.call-done
  513.8 90.1 %all-gather.24.cloned.1.call-done = bf16[8192,1024]{0,1:T(8,128)(2,1)} async-done(((bf16[1024,1024]{0,1:T(8,128)(2,1)}), bf16[8192,1024]{0,1:T(8,128)(2,1)}) %all-gather.24.cloned.1.call-update) | async-done | bytes 16777232 | tf_op jit(solution)/shard_map/all_gather | solution.py:109
  603.9 32.3 %convert_reduce_fusion.2 = (f32[512]{0:T(512)}, bf16[8192,512]{1,0:T(8,128)(2,1)}) fusion(f32[8192,512]{1,0:T(8,128)} %fusion.150, f32[512]{0:T(512)S(1)} %convert_element_type.182, bf16[8192,1024]{0,1:T(8,128)(2,1)} %all-gather.24.cloned.1.call-done, bf16[512,1024]{1,0:T(8,128)(2,1)} %all-gather.22.cloned.1.call-done), kind=kOutput, calls=%fused_computation.78 | convolution fusion | flops 8703180800 | bytes 42995712 | tf_op jit(solution)/shard_map/dot_general | solution.py:110
  636.1 15.3 convolution_convert_fusion
  652.7 17.5 %convolution_convert_fusion.1 = bf16[8192,1024]{0,1:T(8,128)(2,1)} fusion(bf16[512,1024]{1,0:T(8,128)(2,1)S(1)} %copy-done.37, f32[8192,512]{1,0:T(8,128)} %fusion.150, f32[512]{0:T(512)S(1)} %convert_element_type.182), kind=kOutput, calls=%fused_computation.81 | convolution fusion | flops 8640266240 | bytes 34605056 | tf_op jit(solution)/shard_map/dot_general | solution.py:239
  670.8 8.7 all-gather.1
  679.6 88.0 %reduce-scatter.19.cloned.1.call-done = bf16[1024,1024]{0,1:T(8,128)(2,1)} async-done(((bf16[8192,1024]{0,1:T(8,128)(2,1)}), bf16[1024,1024]{0,1:T(8,128)(2,1)}) %reduce-scatter.19.cloned.1.call-update) | async-done | bytes 2097168 | tf_op jit(solution)/shard_map/reduce_scatter | solution.py:92
  772.9 114.3 %reduce-scatter.17.cloned.1.call-done = bf16[1024,1024]{0,1:T(8,128)(2,1)} async-done(((bf16[8192,1024]{0,1:T(8,128)(2,1)}), bf16[1024,1024]{0,1:T(8,128)(2,1)}) %reduce-scatter.17.cloned.1.call-update) | async-done | bytes 2097168 | tf_op jit(solution)/shard_map/reduce_scatter | solution.py:86
  887.1 11.9 fusion.102
  899.8 89.3 %all-gather.26.cloned.1.call-done = bf16[8192,1024]{0,1:T(8,128)(2,1)} async-done(((bf16[1024,1024]{0,1:T(8,128)(2,1)}), bf16[8192,1024]{0,1:T(8,128)(2,1)}) %all-gather.26.cloned.1.call-update) | async-done | bytes 16777232 | tf_op jit(solution)/shard_map/all_gather | solution.py:109
  989.0 9.8 convolution_convert_fusion.2
  1009.2 189.9 %while.27 = (s32[]{:T(128)}, bf16[16,1024,64]{1,2,0:T(8,128)(2,1)}, bf16[16,1024,64]{1,2,0:T(8,128)(2,1)}, bf16[16,1024,64]{1,2,0:T(8,128)(2,1)S(1)}, bf16[16,10...) while((s32[]{:T(128)}, bf16[16,1024,64]{1,2,0:T(8,128)(2,1)}, ...), condition=%wide.region_15.16_spmd, body=%wide.region_13.15_spmd.sunk | while | flops 683998208 | bytes 33457264 | solution.py:261
  1224.8 10.2 copy.136
  1235.0 9.1 copy.106
  1249.1 71.3 %all-to-all-done.1 = bf16[8,1024,384]{2,1,0:T(8,128)(2,1)} async-done(((bf16[8,1024,384]{2,1,0:T(8,128)(2,1)}), bf16[8,1024,384]{2,1,0:T(8,128)(2,1)}, u32[]{:S(2)}, u32[]{:S(2)}) %all-to-all-start.1) | async-done | bytes 6291488 | tf_op jit(solution)/shard_map/all_to_all | solution.py:98
  1320.5 15.0 convert_reduce_fusion
  1335.5 5.3 copy.108
  1362.7 14.4 fusion.113
  1383.0 18.6 %convolution_convert_fusion.4 = bf16[512,1024]{1,0:T(8,128)(2,1)} fusion(bf16[8192,1024]{0,1:T(8,128)(2,1)} %all-gather.24.cloned.1.call-done, f32[8192,512]{1,0:T(8,128)} %fusion.150, f32[512]{0:T(512)S(1)} %convert_element_type.182), kind=kOutput, calls=%fused_computation.151 | convolution fusion | flops 8632401920 | bytes 34605056 | tf_op jit(solution)/shard_map/dot_general | solution.py:113
  1401.7 15.6 convolution_convert_fusion.5
  1423.1 13.0 fusion.110
  1436.1 12.9 fusion.105
  1449.1 9.0 fusion.101
  1466.9 6.7 reduce-scatter.27.cloned.1.call-done
  1485.8 8.3 reduce-scatter.25.cloned.1.call-done
  1495.6 22.8 %reduce-scatter.23.cloned.1.call-done = bf16[256,2,192]{0,2,1:T(8,128)(2,1)} async-done(((bf16[1024,2,192]{0,2,1:T(8,128)(2,1)}), bf16[256,2,192]{0,2,1:T(8,128)(2,1)}) %reduce-scatter.23.cloned.1.call-update) | async-done | bytes 196624 | tf_op jit(solution)/shard_map/reduce_scatter | solution.py:331
  1520.1 8.9 fusion.86
  1529.0 5.4 copy.115
  1534.4 19.8 %reduce-scatter.35.cloned.1.call-done = bf16[128,2]{1,0:T(8,128)(2,1)} async-done(((bf16[1024,2]{1,0:T(8,128)(2,1)}), bf16[128,2]{1,0:T(8,128)(2,1)}) %reduce-scatter.35.cloned.1.call-update) | async-done | bytes 528
  1555.1 12.4 all-reduce
  1567.5 23.5 %reduce-scatter.33.cloned.1.call-done = bf16[128,8]{1,0:T(8,128)(2,1)} async-done(((bf16[1024,8]{1,0:T(8,128)(2,1)}), bf16[128,8]{1,0:T(8,128)(2,1)}) %reduce-scatter.33.cloned.1.call-update) | async-done | bytes 2064
  1592.5 36.2 %reduce-scatter.21.cloned.1.call-done = bf16[256,6,128]{2,0,1:T(8,128)(2,1)} async-done(((bf16[1024,6,128]{2,0,1:T(8,128)(2,1)}), bf16[256,6,128]{2,0,1:T(8,128)(2,1)}) %reduce-scatter.21.cloned.1.call-update) | async-done | bytes 393232 | tf_op jit(solution)/shard_map/reduce_scatter | solution.py:328
  (392 shorter events, 461.2 us)
Async XLA Ops:
  7.2 4.4 copy-start.29
  7.2 42.2 %all-gather.12.cloned.1.call-start = ((), (), s32[]{:S(2)}) async-start(), calls=%async_computation.12 | async-start | bytes 1966080 | tf_op jit(solution)/shard_map/all_gather | solution.py:177
  7.9 164.4 %all-gather.14.cloned.1.call-start = ((), (), s32[]{:S(2)}) async-start(), calls=%async_computation.13 | async-start | bytes 18874368 | tf_op jit(solution)/shard_map/all_gather | solution.py:68
  11.5 368.1 %copy-start.4 = (bf16[1024,1024]{0,1:T(8,128)(2,1)}, bf16[1024,1024]{0,1:T(8,128)(2,1)S(1)}, u32[]{:S(2)}) copy-start(bf16[1024,1024]{0,1:T(8,128)(2,1)S(1)} %copy.89) | copy-start | bytes 6291460
  21.9 32.0 %copy-start.18 = (bf16[8,1024]{1,0:T(8,128)(2,1)}, bf16[8,1024]{1,0:T(8,128)(2,1)S(1)}, u32[]{:S(2)}) copy-start(bf16[8,1024]{1,0:T(8,128)(2,1)S(1)} %all_gather.47) | copy-start | bytes 49156
  21.9 51.5 %copy-start.25 = (s32[1024]{0:T(1024)}, s32[1024]{0:T(1024)S(1)}, u32[]{:S(2)}) copy-start(s32[1024]{0:T(1024)S(1)} %add_select_fusion) | copy-start | bytes 12292
  22.5 50.9 %copy-start.20 = (f32[1024]{0:T(1024)}, f32[1024]{0:T(1024)S(1)}, u32[]{:S(2)}) copy-start(f32[1024]{0:T(1024)S(1)} %get-tuple-element.233) | copy-start | bytes 12292
  22.6 50.9 %copy-start.22 = (f32[1024]{0:T(1024)}, f32[1024]{0:T(1024)S(1)}, u32[]{:S(2)}) copy-start(f32[1024]{0:T(1024)S(1)} %get-tuple-element.234) | copy-start | bytes 12292
  73.4 8.3 copy-start
  81.7 17.4 %copy-start.31 = (bf16[2,128]{1,0:T(2,128)(2,1)S(1)}, bf16[2,128]{1,0:T(2,128)(2,1)}, u32[]{:S(2)}) copy-start(bf16[2,128]{1,0:T(2,128)(2,1)} %param.22) | copy-start | bytes 1540
  84.3 280.9 %all-gather.16.cloned.1.call-start = ((), (), s32[]{:S(2)}) async-start(), calls=%async_computation.14 | async-start | bytes 2359296 | tf_op jit(solution)/shard_map/all_gather | solution.py:191
  117.1 66.1 %copy-start.16 = (bf16[1024,2,192]{0,2,1:T(8,128)(2,1)}, bf16[1024,2,192]{0,2,1:T(8,128)(2,1)S(1)}, u32[]{:S(2)}) copy-start(bf16[1024,2,192]{0,2,1:T(8,128)(2,1)S(1)} %all_gather.51) | copy-start | bytes 2359300
  323.5 8.9 copy-start.34
  327.4 37.9 %all-to-all-start = ((bf16[8,1024,128]{2,1,0:T(8,128)(2,1)}), bf16[8,1024,128]{2,1,0:T(8,128)(2,1)}, u32[]{:S(2)}, u32[]{:S(2)}) async-start(bf16[8,1024,128]{2,1,0:T(8,128)(2,1)} %copy.95), calls=%async_computation | async-start | bytes 4194304 | tf_op jit(solution)/shard_map/all_to_all | solution.py:98
  331.8 62.4 %all-gather.20.cloned.1.call-start = ((), (), s32[]{:S(2)}) async-start(), calls=%async_computation.16 | async-start | bytes 1310720 | tf_op jit(solution)/shard_map/all_gather | solution.py:180
  332.4 149.8 %all-gather.18.cloned.1.call-start = ((), (), s32[]{:S(2)}) async-start(), calls=%async_computation.15 | async-start | bytes 18874368 | tf_op jit(solution)/shard_map/all_gather | solution.py:68
  361.3 18.3 %copy-start.27 = (f32[8,1,128]{2,1,0:T(1,128)}, f32[8,1,128]{2,1,0:T(1,128)S(1)}, u32[]{:S(2)}) copy-start(f32[8,1,128]{2,1,0:T(1,128)S(1)} %convert_element_type.216) | copy-start | bytes 12292
  379.6 4.3 copy-start.7
  383.9 8.8 copy-start.1
  392.7 121.0 %all-gather.22.cloned.1.call-start = ((), (), s32[]{:S(2)}) async-start(), calls=%async_computation.17 | async-start | bytes 1310720 | tf_op jit(solution)/shard_map/all_gather | solution.py:181
  393.3 210.5 %all-gather.24.cloned.1.call-start = ((), (), s32[]{:S(2)}) async-start(), calls=%async_computation.19 | async-start | bytes 18874368 | tf_op jit(solution)/shard_map/all_gather | solution.py:109
  394.1 373.5 %reduce-scatter.19.cloned.1.call-start = ((), (), s32[]{:S(2)}) async-start(), calls=%async_computation.20 | async-start | bytes 18874368 | tf_op jit(solution)/shard_map/reduce_scatter | solution.py:92
  498.1 138.0 %copy-start.36 = (bf16[1024,512]{1,0:T(8,128)(2,1)S(1)}, bf16[1024,512]{1,0:T(8,128)(2,1)}, u32[]{:S(2)}) copy-start(bf16[1024,512]{1,0:T(8,128)(2,1)} %all-gather.20.cloned.1.call-done) | copy-start | bytes 3145732
  651.5 235.7 %reduce-scatter.17.cloned.1.call-start = ((), (), s32[]{:S(2)}) async-start(), calls=%async_computation.18 | async-start | bytes 18874368 | tf_op jit(solution)/shard_map/reduce_scatter | solution.py:86
  670.2 318.8 %all-gather.26.cloned.1.call-start = ((), (), s32[]{:S(2)}) async-start(), calls=%async_computation.21 | async-start | bytes 18874368 | tf_op jit(solution)/shard_map/all_gather | solution.py:109
  679.6 207.6 %copy-start.8 = (bf16[1024,1024]{0,1:T(8,128)(2,1)S(1)}, bf16[1024,1024]{0,1:T(8,128)(2,1)}, u32[]{:S(2)}) copy-start(bf16[1024,1024]{0,1:T(8,128)(2,1)} %copy.98) | copy-start | bytes 6291460
  887.1 101.9 %copy-start.17 = (bf16[2,64,1024]{2,1,0:T(8,128)(2,1)S(1)}, bf16[2,64,1024]{2,1,0:T(8,128)(2,1)}, u32[]{:S(2)}) copy-start(bf16[2,64,1024]{2,1,0:T(8,128)(2,1)} %all_gather.52) | copy-start | bytes 786436
  899.0 350.1 %all-gather.28.cloned.1.call-start = ((), (), s32[]{:S(2)}) async-start(), calls=%async_computation.22 | async-start | bytes 7077888 | tf_op jit(solution)/shard_map/all_gather | solution.py:190
  1199.1 9.5 copy-start.12
  1224.8 10.2 copy-start.13
  1244.1 76.4 %all-to-all-start.1 = ((bf16[8,1024,384]{2,1,0:T(8,128)(2,1)}), bf16[8,1024,384]{2,1,0:T(8,128)(2,1)}, u32[]{:S(2)}, u32[]{:S(2)}) async-start(bf16[8,1024,384]{2,1,0:T(8,128)(2,1)} %copy.106), calls=%async_computation.3 | async-start | bytes 12582912 | tf_op jit(solution)/shard_map/all_to_all | solution.py:98
  1248.9 210.2 %reduce-scatter.31.cloned.1.call-start = ((), (), s32[]{:S(2)}) async-start(), calls=%async_computation.28 | async-start | bytes 294912
  1340.8 4.9 copy-start.3
  1340.8 4.9 copy-start.5
  1340.8 4.9 copy-start.21
  1340.8 4.9 copy-start.23
  1345.8 5.0 copy-start.10
  1345.8 5.0 copy-start.28
  1383.0 82.1 %reduce-scatter.29.cloned.1.call-start = ((), (), s32[]{:S(2)}) async-start(), calls=%async_computation.27 | async-start | bytes 1310720 | tf_op jit(solution)/shard_map/reduce_scatter | solution.py:340
  1401.6 71.9 %reduce-scatter.27.cloned.1.call-start = ((), (), s32[]{:S(2)}) async-start(), calls=%async_computation.26 | async-start | bytes 1310720 | tf_op jit(solution)/shard_map/reduce_scatter | solution.py:337
  1417.3 76.8 %reduce-scatter.25.cloned.1.call-start = ((), (), s32[]{:S(2)}) async-start(), calls=%async_computation.25 | async-start | bytes 327680 | tf_op jit(solution)/shard_map/reduce_scatter | solution.py:334
  1436.1 82.4 %reduce-scatter.23.cloned.1.call-start = ((), (), s32[]{:S(2)}) async-start(), calls=%async_computation.24 | async-start | bytes 983040 | tf_op jit(solution)/shard_map/reduce_scatter | solution.py:331
  1449.0 14.2 copy-start.19
  1449.0 105.2 %reduce-scatter.35.cloned.1.call-start = ((), (), s32[]{:S(2)}) async-start(), calls=%async_computation.30 | async-start | bytes 294912
  1459.0 132.1 %reduce-scatter.33.cloned.1.call-start = ((), (), s32[]{:S(2)}) async-start(), calls=%async_computation.29 | async-start | bytes 294912
  1462.9 165.7 %reduce-scatter.21.cloned.1.call-start = ((), (), s32[]{:S(2)}) async-start(), calls=%async_computation.23 | async-start | bytes 1966080 | tf_op jit(solution)/shard_map/reduce_scatter | solution.py:328
  1529.0 26.1 %copy-start.32 = (f32[512]{0:T(512)S(1)}, f32[512]{0:T(512)}, u32[]{:S(2)}) copy-start(f32[512]{0:T(512)} %get-tuple-element.217) | copy-start | bytes 6148
  1529.0 62.9 %copy-start.30 = (bf16[8,128]{1,0:T(8,128)(2,1)S(1)}, bf16[8,128]{1,0:T(8,128)(2,1)}, u32[]{:S(2)}) copy-start(bf16[8,128]{1,0:T(8,128)(2,1)} %param.18) | copy-start | bytes 6148
  (11 other events, 26.1 us)
Sparse Core Ops, SparseCore 0:
  9.6 39.7 all-gather.11
  84.5 87.8 all-gather.13
  174.2 27.8 all-gather.15
  333.9 29.4 all-gather.19
  392.9 89.2 all-gather.17
  483.5 30.1 all-gather.21
  515.7 88.1 all-gather.23
  651.6 115.9 reduce-scatter.18
  771.2 115.9 reduce-scatter.16
  899.2 89.8 all-gather.25
  991.5 45.5 all-gather.27
  1383.1 32.9 reduce-scatter.30
  1418.4 27.1 reduce-scatter.28
  1447.8 25.7 reduce-scatter.26
  1475.8 18.3 reduce-scatter.24
  1496.9 21.5 reduce-scatter.22
  1521.3 32.8 reduce-scatter.34
  1557.4 33.6 reduce-scatter.32
  1593.4 35.2 reduce-scatter.20
where the time goes:
time: 1650 us; the launch traced here: 1640 us
  waiting for transfers between devices  759 us (46%)
  matrix products  444 us (27%)
  local copies, waits for them, and re-layouts  183 us (11%)
  other arithmetic  113 us (7%)
  blocking collectives  103 us (6%)
    all_gather x2, waiting for transfers between devices, second_back(): incoming = lax.all_gather(grad_low, 'col', axis=0, tiled=True)  179 us
    all_gather x2, waiting for transfers between devices, first_product(): lax.all_gather(hidden, 'col', axis=0, tiled=True)  143 us
    reduce_scatter x1, waiting for transfers between devices, branch_total(): lax.psum_scatter(partial_rows.astype(jnp.bfloat16), 'col', scatter_dimens...  114 us
    reduce_scatter x1, waiting for transfers between devices, input_total(): lax.psum_scatter(partial_rows.astype(jnp.bfloat16), 'col', scatter_dimens...  88 us
    all_to_all x2, waiting for transfers between devices, to_tokens(): lax.all_to_all(head_rows, 'col', split_axis=0, concat_axis=1, tiled=True)  71.4 us
    unnamed x97, local copies, waits for them, and re-layouts  69.7 us
    unnamed x22, waiting for transfers between devices  46.7 us
    dot_general x2, matrix products, second_back(): lax.dot_general(incoming, weight_rows, CONTRACT_COLS, preferred_element_t...  42.1 us
  transfers between devices with their start and end apart: 21, of which 15 were waited for; matrix products, arithmetic and copies ran while one was open for 36% of the time, Pallas kernels for 0%

commit v1 on v0

v1 whole, which is shorter than its diff:
```python
import functools
import math

import jax
import jax.numpy as jnp
from jax import lax
from jax.experimental import pallas as pl
from jax.experimental.pallas import tpu as pltpu
from jax.sharding import PartitionSpec as P

D = 1024
HD = 64
LEN = 1024
PAIR = 2 * HD

EPSILON = 1e-06
PRECISE = lax.Precision.HIGHEST
NN = (((1,), (0,)), ((), ()))
NT = (((1,), (1,)), ((), ()))
TN = (((0,), (0,)), ((), ()))
F32 = jnp.float32
BF16 = jnp.bfloat16
QUERY_ROWS = 512
VMEM_BYTES = 56 * 1024 * 1024


def dot(left, right, dims=NN):
    return lax.dot_general(left, right, dims, preferred_element_type=F32)


def silu_fn(values):
    return values * jax.nn.sigmoid(values)


def gelu_both(values):
    c = math.sqrt(2.0 / math.pi)
    square = values * values
    t = jnp.tanh(c * values * (1.0 + 0.044715 * square))
    half = 0.5 * (1.0 + t)
    slope = half + 0.5 * values * (1.0 - t * t) * (c * (1.0 + 3.0 * 0.044715 * square))
    return values * half, slope


def normalize(resid):
    average = jnp.mean(resid, 1, keepdims=True)
    spread = jnp.mean(resid * resid, 1, keepdims=True) - average * average
    inv_std = lax.rsqrt(spread + EPSILON)
    return ((resid - average) * inv_std, inv_std)


def normalize_back(grad_norm, normed, inv_std):
    average = jnp.mean(grad_norm, 1, keepdims=True)
    crossed = jnp.mean(grad_norm * normed, 1, keepdims=True)
    return inv_std * (grad_norm - average - normed * crossed)


def after(array, *earlier):
    return lax.optimization_barrier((array, *earlier))[0]


def head_lanes(shape, head):
    lane = lax.broadcasted_iota(jnp.int32, shape, 1)
    return lane < HD if head == 0 else lane >= HD


def attend_kernel(q_ref, k_ref, v_ref, mixed_ref, log_ref):
    queries = q_ref[...] * jnp.asarray(HD**-0.5, BF16)
    key_rows = k_ref[...]
    value_rows = v_ref[...]
    mask = head_lanes(key_rows.shape, 0)
    zero = jnp.zeros_like(key_rows)
    keys = (jnp.where(mask, key_rows, zero), jnp.where(mask, zero, key_rows))
    length = queries.shape[0]
    for start in range(0, length, QUERY_ROWS):
        stop = start + QUERY_ROWS
        q_part = queries[start:stop]
        outs = []
        for head in range(2):
            scores = dot(keys[head], q_part, NT)
            top = jnp.max(scores, 0, keepdims=True)
            expon = jnp.exp(scores - top)
            total = jnp.sum(expon, 0, keepdims=True)
            out = dot(value_rows, expon.astype(BF16), TN) / total
            outs.append(out[head * HD : (head + 1) * HD])
            log_ref[0, 0, head : head + 1, start:stop] = top + jnp.log(total)
        mixed_ref[start:stop, :] = jnp.concatenate(outs, 0).T.astype(BF16)


def attend_back_kernel(q_ref, k_ref, v_ref, mixed_ref, grad_ref, log_ref, out_ref):
    scale = jnp.asarray(HD**-0.5, BF16)
    queries = q_ref[...] * scale
    key_rows = k_ref[...]
    value_rows = v_ref[...]
    grad_rows = grad_ref[...]
    mask = head_lanes(key_rows.shape, 0)
    zero = jnp.zeros_like(key_rows)
    keys = (jnp.where(mask, key_rows, zero), jnp.where(mask, zero, key_rows))
    values = (jnp.where(mask, value_rows, zero), jnp.where(mask, zero, value_rows))
    keys_scaled = key_rows * scale
    product = grad_rows.astype(F32) * mixed_ref[...].astype(F32)
    picks = (
        lax.broadcasted_iota(jnp.int32, (8, PAIR), 0)
        == lax.broadcasted_iota(jnp.int32, (8, PAIR), 1) // HD
    ).astype(F32)
    inner = lax.dot_general(picks, product, NT, precision=PRECISE, preferred_element_type=F32)
    length = queries.shape[0]
    grad_k = [None, None]
    grad_v = [None, None]
    for start in range(0, length, QUERY_ROWS):
        stop = start + QUERY_ROWS
        q_part = queries[start:stop]
        g_part = grad_rows[start:stop]
        outs = []
        for head in range(2):
            scores = dot(keys[head], q_part, NT)
            probs = jnp.exp(scores - log_ref[0, 0, head : head + 1, start:stop])
            grad_probs = dot(values[head], g_part, NT)
            grad_scores = (probs * (grad_probs - inner[head : head + 1, start:stop])).astype(BF16)
            part_v = dot(probs.astype(BF16), g_part)
            part_k = dot(grad_scores, q_part)
            grad_v[head] = part_v if grad_v[head] is None else grad_v[head] + part_v
            grad_k[head] = part_k if grad_k[head] is None else grad_k[head] + part_k
            out = dot(keys_scaled, grad_scores, TN)
            outs.append(out[head * HD : (head + 1) * HD])
        out_ref[start:stop, 0:PAIR] = jnp.concatenate(outs, 0).T.astype(BF16)
    out_ref[:, PAIR : 2 * PAIR] = jnp.where(mask, grad_k[0], grad_k[1]).astype(BF16)
    out_ref[:, 2 * PAIR :] = jnp.where(mask, grad_v[0], grad_v[1]).astype(BF16)


def attention_specs(latents, pairs):
    part = lambda offset: pl.BlockSpec((LEN, PAIR), lambda s, p: (s, 3 * p + offset))
    plain = pl.BlockSpec((LEN, PAIR), lambda s, p: (s, p))
    logs = pl.BlockSpec((1, 1, 2, LEN), lambda s, p: (s, p, 0, 0))
    return [part(0), part(1), part(2)], plain, logs


def attend(projected, latents, pairs):
    parts, plain, logs = attention_specs(latents, pairs)
    rows = projected.shape[0]
    return pl.pallas_call(
        attend_kernel,
        grid=(latents, pairs),
        in_specs=parts,
        out_specs=[plain, logs],
        out_shape=[
            jax.ShapeDtypeStruct((rows, pairs * PAIR), BF16),
            jax.ShapeDtypeStruct((latents, pairs, 2, LEN), F32),
        ],
        compiler_params=pltpu.CompilerParams(vmem_limit_bytes=VMEM_BYTES),
        cost_estimate=pl.CostEstimate(
            flops=latents * pairs * 2 * 2 * 2 * LEN * LEN * PAIR,
            bytes_accessed=rows * pairs * PAIR * 8,
            transcendentals=latents * pairs * 2 * LEN * LEN,
        ),
        name="attend",
    )(projected, projected, projected)


def attend_back(projected, mixed, grad_mixed, log_totals, latents, pairs):
    parts, plain, logs = attention_specs(latents, pairs)
    rows = projected.shape[0]
    return pl.pallas_call(
        attend_back_kernel,
        grid=(latents, pairs),
        in_specs=[*parts, plain, plain, logs],
        out_specs=pl.BlockSpec((LEN, 3 * PAIR), lambda s, p: (s, p)),
        out_shape=jax.ShapeDtypeStruct((rows, pairs * 3 * PAIR), BF16),
        compiler_params=pltpu.CompilerParams(vmem_limit_bytes=VMEM_BYTES),
        cost_estimate=pl.CostEstimate(
            flops=latents * pairs * 2 * 5 * 2 * LEN * LEN * PAIR,
            bytes_accessed=rows * pairs * PAIR * 16,
            transcendentals=latents * pairs * 2 * LEN * LEN,
        ),
        name="attend_back",
    )(projected, projected, projected, mixed, grad_mixed, log_totals)


class Grid:
    def __init__(self):
        self.rows = lax.axis_size("row")
        self.cols = lax.axis_size("col")
        self.chips = self.cols // 2
        self.bits = [1 << b for b in range(self.chips.bit_length() - 1)]
        self.orders = (self.bits, self.bits[::-1])
        self.row = lax.axis_index("row")
        self.col = lax.axis_index("col")
        self.core = self.col % 2
        source = lax.iota(jnp.int32, self.chips) ^ (self.col // 2)
        self.choose = (
            (2 * source + self.core)[:, None] == lax.iota(jnp.int32, self.cols)[None, :]
        ).astype(F32)

    def swap(self, array, flip):
        pairs = [(i, i ^ flip) for i in range(self.cols)]
        return lax.ppermute(array, "col", pairs)

    def swap_core(self, array):
        return self.swap(array, 1)

    def swap_chip(self, array, bit):
        return self.swap(array, 2 * bit)

    def to_relative(self, blocks):
        flat = blocks.reshape(self.cols, -1).astype(F32)
        picked = lax.dot_general(
            self.choose, flat, NN, precision=PRECISE, preferred_element_type=F32
        )
        return picked.reshape((self.chips,) + blocks.shape[1:])

    def to_absolute(self, blocks):
        flat = blocks.reshape(self.chips, -1)
        placed = lax.dot_general(
            self.choose, flat, TN, precision=PRECISE, preferred_element_type=F32
        )
        return placed.reshape((self.cols,) + blocks.shape[1:])

    def gather_rows(self, block):
        count = self.rows
        got = [block]
        for step in range(1, count):
            got.append(
                lax.ppermute(block, "row", [(i, (i + step) % count) for i in range(count)])
            )
        stacked = jnp.stack(got)
        ordered = [
            lax.dynamic_index_in_dim(stacked, (self.row - i) % count, 0, keepdims=False)
            for i in range(count)
        ]
        return jnp.concatenate(ordered, 0), got[-1]

    def scatter_rows(self, whole):
        count = self.rows
        blocks = whole.reshape(count, whole.shape[0] // count, whole.shape[1])
        total = lax.dynamic_index_in_dim(blocks, self.row, 0, keepdims=False).astype(F32)
        for step in range(1, count):
            sent = lax.dynamic_index_in_dim(blocks, (self.row + step) % count, 0, keepdims=False)
            total = total + lax.ppermute(
                sent, "row", [(i, (i + step) % count) for i in range(count)]
            ).astype(F32)
        return total

    def gather_chips(self, block, order):
        held, ids = block, [0]
        for number, bit in enumerate(order):
            got = self.swap_chip(held, bit)
            new_ids = [bit ^ i for i in ids]
            if number == len(order) - 1:
                return held, ids, got, new_ids
            held, ids = jnp.concatenate([held, got], 1), ids + new_ids

    def scatter_chips(self, keep, send, order):
        for number, bit in enumerate(order[::-1]):
            total = keep + self.swap_chip(send, bit).astype(F32)
            if number == len(order) - 1:
                return total
            half = total.shape[1] // 2
            keep, send = total[:, :half], total[:, half:].astype(BF16)


def split_columns(array, ids):
    width = array.shape[1] // len(ids)
    return {i: array[:, n * width : (n + 1) * width] for n, i in enumerate(ids)}


def all_exchange(pieces):
    return lax.all_to_all(pieces, ("row", "col"), 0, 0, tiled=True)


def per_device(
    tokens,
    condition,
    mod_weight,
    mod_bias,
    qkv_weight,
    qv_bias,
    out_weight,
    out_bias,
    fc1_weight,
    fc1_bias,
    fc2_weight,
    fc2_bias,
    cotangent,
):
    grid = Grid()
    rows, cols, chips = grid.rows, grid.cols, grid.chips
    devices = rows * cols
    local_rows = tokens.shape[0]
    both_rows = 2 * local_rows
    latents = both_rows // LEN
    span = LEN // local_rows
    seq_rows = condition.shape[0]
    seqs = seq_rows * rows
    row_width = D // rows
    col_width = D // cols
    local_heads = qkv_weight.shape[1]
    local_units = fc1_weight.shape[1]
    plane_heads = local_heads * chips
    pairs = plane_heads // 2
    qkv_width = local_heads * 3 * HD
    out_width = local_heads * HD

    if local_heads % 2 == 0:
        qkv_local = (
            qkv_weight.reshape(row_width, local_heads // 2, 2, 3, HD)
            .transpose(0, 1, 3, 2, 4)
            .reshape(row_width, qkv_width)
        )
    else:
        qkv_local = qkv_weight.reshape(row_width, qkv_width)
    attn_local = jnp.concatenate(
        [qkv_local, out_weight.reshape(out_width, row_width).T], 1
    )
    attn_width = qkv_width + out_width
    fc1_local = fc1_weight
    fc2_local = fc2_weight.T

    small = jnp.concatenate(
        [
            condition.reshape(-1),
            fc1_bias,
            qv_bias.reshape(-1),
            out_bias,
            fc2_bias,
        ]
    )
    small_all = all_exchange(
        jnp.broadcast_to(small.reshape(1, -1, 128), (devices, small.size // 128, 128))
    ).reshape(rows, cols, -1)
    cut = seq_rows * col_width
    cond_all = (
        small_all[:, :, :cut]
        .reshape(rows, cols, seq_rows, col_width)
        .transpose(0, 2, 1, 3)
        .reshape(seqs, D)
    )
    biases = small_all[0, :, cut:]
    fc1_bias_all = biases[:, :local_units]
    qv_bias_all = biases[:, local_units : local_units + local_heads * PAIR]
    out_bias_all = biases[:, -2 * col_width : -col_width].reshape(1, D).astype(F32)
    fc2_bias_all = biases[:, -col_width:].reshape(1, D).astype(F32)

    cond_act = silu_fn(cond_all.astype(F32)).astype(BF16)
    cond_act = lax.dynamic_slice_in_dim(cond_act, grid.row * row_width, row_width, 1)
    mod_flat = mod_weight.reshape(row_width, 6 * col_width)
    own_bias = jnp.where(grid.row == 0, mod_bias.astype(F32), 0.0)
    mod_part = dot(cond_act, mod_flat).reshape(seqs, 6, col_width) + own_bias
    mod_part = jnp.broadcast_to(
        mod_part[:, None], (seqs, span, 6, col_width)
    ).reshape(devices, 6, col_width)
    modulation = (
        all_exchange(mod_part)
        .reshape(rows, cols, 6, col_width)
        .sum(0)
        .transpose(1, 0, 2)
        .reshape(6, 1, D)
    )
    shift_attn, scale_attn, gate_attn, shift_feed, scale_feed, gate_feed = modulation

    attn_rows, mark = grid.gather_rows(attn_local)
    fc1_rows, mark = grid.gather_rows(after(fc1_local, mark))
    fc2_rows, mark = grid.gather_rows(after(fc2_local, mark))
    half = D // 2
    top = grid.gather_chips(attn_rows[:half], grid.orders[0])
    low = grid.gather_chips(attn_rows[half:], grid.orders[1])
    attn_top = {**split_columns(top[0], top[1]), **split_columns(top[2], top[3])}
    attn_low = {**split_columns(low[0], low[1]), **split_columns(low[2], low[3])}
    attn_blocks = [jnp.concatenate([attn_top[i], attn_low[i]], 0) for i in range(chips)]
    if local_heads % 2 == 0:
        qkv_w = jnp.concatenate([b[:, :qkv_width] for b in attn_blocks], 1)
    else:
        qkv_w = (
            jnp.stack([b[:, :qkv_width] for b in attn_blocks], 1)
            .reshape(D, pairs, 2, 3, HD)
            .transpose(0, 1, 3, 2, 4)
            .reshape(D, pairs * 3 * PAIR)
        )
    out_w = jnp.concatenate([b[:, qkv_width:] for b in attn_blocks], 1)

    def gather_units(rows_held, earlier):
        rows_held = after(rows_held, *earlier)
        middle = local_units // 2
        first = grid.gather_chips(rows_held[:, :middle], grid.orders[0])
        second = grid.gather_chips(rows_held[:, middle:], grid.orders[1])
        groups = [first[0], first[2], second[0], second[2]]
        ids = [(0, first[1]), (0, first[3]), (1, second[1]), (1, second[3])]
        return groups, ids

    fc1_groups, unit_ids = gather_units(fc1_rows, (top[2], low[2]))
    fc2_groups, unit_ids = gather_units(fc2_rows, (fc1_groups[1], fc1_groups[3]))

    fc1_bias_rel = grid.to_relative(fc1_bias_all).reshape(chips, 2, local_units // 2)
    fc1_bias_groups = [
        jnp.concatenate([fc1_bias_rel[i, part] for i in ids]) for part, ids in unit_ids
    ]
    qv_rel = grid.to_relative(qv_bias_all).reshape(pairs, 2, 2, HD).transpose(0, 2, 1, 3)
    qkv_bias_rel = jnp.concatenate(
        [qv_rel[:, :1], jnp.zeros_like(qv_rel[:, :1]), qv_rel[:, 1:]], 1
    ).reshape(1, pairs * 3 * PAIR)

    def both(mine):
        return jnp.concatenate([mine, grid.swap_core(mine)], 0)

    def own_total(partial):
        theirs = partial[local_rows:].astype(BF16)
        return partial[:local_rows] + grid.swap_core(theirs).astype(F32)

    resid = tokens.astype(F32)
    normed_attn, inv_attn = normalize(resid)
    hidden_attn = both((normed_attn * (1.0 + scale_attn) + shift_attn).astype(BF16))
    upstream = cotangent.astype(F32)
    grad_feed = upstream * gate_feed
    bias_fc2 = jnp.sum(grad_feed, 0)
    grad_feed_low = both(grad_feed.astype(BF16))

    projected = (dot(hidden_attn, qkv_w) + qkv_bias_rel).astype(BF16)
    mixed, log_totals = attend(projected, latents, pairs)
    attention_out = own_total(dot(mixed, out_w, NT)) + out_bias_all
    resid_mid = resid + gate_attn * attention_out
    normed_feed, inv_feed = normalize(resid_mid)
    hidden_feed = both((normed_feed * (1.0 + scale_feed) + shift_feed).astype(BF16))
    acts, slopes = [], []
    for weight, bias in zip(fc1_groups, fc1_bias_groups):
        act, slope = gelu_both(dot(hidden_feed, weight) + bias)
        acts.append(act.astype(BF16))
        slopes.append(slope.astype(BF16))

    def scatter_units(left, rights):
        sums = []
        for number, order in enumerate(grid.orders):
            send = dot(left, rights[2 * number + 1], TN).astype(BF16)
            keep = dot(left, rights[2 * number], TN)
            sums.append(grid.scatter_chips(keep, send, order))
        return grid.scatter_rows(jnp.concatenate(sums, 1).astype(BF16))

    fc2_part = scatter_units(grad_feed_low, acts).T
    grad_pres = [
        (dot(grad_feed_low, weight) * slope.astype(F32)).astype(BF16)
        for weight, slope in zip(fc2_groups, slopes)
    ]
    bias_fc1 = [jnp.sum(g.astype(F32), 0) for g in grad_pres]
    fc1_part = scatter_units(hidden_feed, grad_pres)
    grad_hidden_feed = own_total(
        sum(dot(g, weight, NT) for g, weight in zip(grad_pres, fc1_groups))
    )
    feed_out = (
        own_total(sum(dot(a, weight, NT) for a, weight in zip(acts, fc2_groups))) + fc2_bias_all
    )
    layer_out = (resid_mid + gate_feed * feed_out).astype(BF16)

    grad_resid_mid = upstream + normalize_back(
        grad_hidden_feed * (1.0 + scale_feed), normed_feed, inv_feed
    )
    grad_attention = grad_resid_mid * gate_attn
    bias_out = jnp.sum(grad_attention, 0)
    grad_attention_low = both(grad_attention.astype(BF16))

    grad_mixed = dot(grad_attention_low, out_w).astype(BF16)
    grad_out = dot(grad_attention_low, mixed, TN)
    grad_projected = attend_back(projected, mixed, grad_mixed, log_totals, latents, pairs)
    bias_qkv = jnp.sum(grad_projected.astype(F32), 0)
    grad_qkv = dot(hidden_attn, grad_projected, TN)
    if local_heads % 2 == 0:
        grad_qkv = grad_qkv.reshape(D, chips, qkv_width)
    else:
        grad_qkv = (
            grad_qkv.reshape(D, pairs, 3, 2, HD).transpose(0, 1, 3, 2, 4).reshape(D, chips, qkv_width)
        )
    grad_out = grad_out.reshape(D, chips, out_width)

    def pick(part, ids):
        lines = slice(0, half) if part == 0 else slice(half, D)
        return jnp.concatenate(
            [jnp.concatenate([grad_qkv[lines, i], grad_out[lines, i]], 1) for i in ids], 1
        )

    attn_sums = []
    for number, gathered in enumerate((top, low)):
        attn_sums.append(
            grid.scatter_chips(
                pick(number, gathered[1]),
                pick(number, gathered[3]).astype(BF16),
                grid.orders[number],
            )
        )
    attn_part = grid.scatter_rows(jnp.concatenate(attn_sums, 0).astype(BF16))
    qkv_part = attn_part[:, :qkv_width]
    if local_heads % 2 == 0:
        qkv_part = qkv_part.reshape(row_width, local_heads // 2, 3, 2, HD).transpose(0, 1, 3, 2, 4)
    qkv_part = qkv_part.reshape(row_width, local_heads, 3 * HD)
    out_part = attn_part[:, qkv_width:].T.reshape(local_heads, HD, row_width)

    grad_hidden_attn = own_total(dot(grad_projected, qkv_w, NT))
    tokens_grad = grad_resid_mid + normalize_back(
        grad_hidden_attn * (1.0 + scale_attn), normed_attn, inv_attn
    )

    mod_rows = jnp.stack(
        [
            jnp.sum(grad_hidden_attn, 0),
            jnp.sum(grad_hidden_attn * normed_attn, 0),
            jnp.sum(grad_resid_mid * attention_out, 0),
            jnp.sum(grad_hidden_feed, 0),
            jnp.sum(grad_hidden_feed * normed_feed, 0),
            jnp.sum(upstream * feed_out, 0),
            bias_out,
            bias_fc2,
        ]
    )
    mod_rows = mod_rows.reshape(8, cols, col_width).transpose(1, 0, 2)
    fc1_split = [split_columns(b[None], ids) for b, (_, ids) in zip(bias_fc1, unit_ids)]
    first_half = {**fc1_split[0], **fc1_split[1]}
    second_half = {**fc1_split[2], **fc1_split[3]}
    fc1_rel = jnp.concatenate(
        [jnp.concatenate([first_half[i], second_half[i]], 1) for i in range(chips)], 0
    )
    qkv_rel = bias_qkv.reshape(pairs, 3, 2, HD)
    qv_rel = jnp.stack([qkv_rel[:, 0], qkv_rel[:, 2]], 2).reshape(chips, local_heads * PAIR)
    hidden_rows = grid.to_absolute(jnp.concatenate([fc1_rel, qv_rel], 1)).reshape(
        cols, -1, col_width
    )
    pieces = jnp.concatenate([mod_rows, hidden_rows], 1)
    pieces = jnp.broadcast_to(pieces[None], (rows,) + pieces.shape).reshape(
        devices, -1, col_width
    )
    arrived = all_exchange(pieces)
    grad_modulation = arrived[:, :6].reshape(seqs, span, 6, col_width).sum(1)
    sums = arrived[:, 6:].sum(0)
    out_bias_grad = sums[0]
    fc2_bias_grad = sums[1]
    hidden_sums = sums[2:].reshape(-1)
    fc1_bias_grad = hidden_sums[:local_units]
    qv_bias_grad = hidden_sums[local_units:].reshape(local_heads, PAIR)
    mod_bias_grad = jnp.sum(grad_modulation, 0)
    grad_mod_flat = grad_modulation.reshape(seqs, 6 * col_width)
    mod_part_grad = lax.dot_general(
        cond_act.astype(F32), grad_mod_flat, TN, precision=PRECISE, preferred_element_type=F32
    ).reshape(row_width, 6, col_width)
    cond_part = lax.dot_general(
        grad_mod_flat,
        mod_flat.astype(F32),
        NT,
        precision=PRECISE,
        preferred_element_type=F32,
    )
    cond_pieces = lax.dynamic_update_slice_in_dim(
        jnp.zeros((seqs, D), F32), cond_part, grid.row * row_width, 1
    )
    cond_pieces = (
        cond_pieces.reshape(rows, seq_rows, cols, col_width)
        .transpose(0, 2, 1, 3)
        .reshape(devices, seq_rows, col_width)
    )
    grad_cond_act = all_exchange(cond_pieces).sum(0)
    _, silu_pull = jax.vjp(silu_fn, condition.astype(F32))
    condition_grad = silu_pull(grad_cond_act)[0]
    return (
        layer_out,
        tokens_grad,
        condition_grad,
        mod_part_grad,
        mod_bias_grad,
        qkv_part,
        qv_bias_grad,
        out_part,
        out_bias_grad,
        fc1_part,
        fc1_bias_grad,
        fc2_part,
        fc2_bias_grad,
    )


def solution(mesh):
    return jax.shard_map(
        per_device,
        mesh=mesh,
        in_specs=(
            P(("row", "col"), None),
            P("row", "col"),
            P("row", None, "col"),
            P(None, "col"),
            P("row", "col", None),
            P("col", None),
            P("col", None, "row"),
            P("col"),
            P("row", "col"),
            P("col"),
            P("col", "row"),
            P("col"),
            P(("row", "col"), None),
        ),
        out_specs=(
            P(("row", "col"), None),
            P(("row", "col"), None),
            P("row", "col"),
            P("row", None, "col"),
            P(None, "col"),
            P("row", "col", None),
            P("col", None),
            P("col", None, "row"),
            P("col"),
            P("row", "col"),
            P("col"),
            P("col", "row"),
            P("col"),
        ),
        check_vma=False,
    )
```

time: 1650 us -> 692 us (0.42)
  waiting for transfers between devices: 759 us -> 199 us
  matrix products: 444 us -> 207 us
  local copies, waits for them, and re-layouts: 183 us -> 60.9 us
  blocking collectives: 103 us -> 0 us
  Pallas kernels: 0 us -> 77.5 us
  starting transfers between devices: 10.5 us -> 73.3 us
  other arithmetic: 113 us -> 67.1 us
    all_gather x9 -> x0, waiting for transfers between devices: 365 us -> none  [the longest x2 179 us: second_back(): incoming = lax.all_gather(grad_low, 'col', axis=0, tiled=True)]
    reduce_scatter x7 -> x0, waiting for transfers between devices: 276 us -> none  [the longest x1 114 us: branch_total(): lax.psum_scatter(partial_rows.astype(jnp.bfloat16), 'col', scatter_dimens...]
    dot_general x129 -> x36, matrix products: 444 us -> 207 us  [the longest x31 202 us: dot(): return lax.dot_general(left, right, dims, preferred_element_type=F32)]
    ppermute x0 -> x50, waiting for transfers between devices: none -> 187 us  [the longest x32 94.1 us: swap(): return lax.ppermute(array, 'col', pairs)]
    all_gather x6 -> x0, blocking collectives: 90.1 us -> none  [the longest x1 28.9 us: per_device(): lax.all_gather(out_bias, 'col', axis=0, tiled=True)]
    pallas_call x0 -> x2, Pallas kernels: none -> 77.5 us  [the longest x1 47.9 us: attend_back(): pl.pallas_call(attend_back_kernel, grid=(latents, pairs), in_specs=[*part...]
    all_to_all x2 -> x4, waiting for transfers between devices: 71.4 us -> 12.4 us  [all_exchange(): return lax.all_to_all(pieces, ('row', 'col'), 0, 0, tiled=True)]
    ppermute x0 -> x50, starting transfers between devices: none -> 53.5 us  [the longest x32 21 us: swap(): return lax.ppermute(array, 'col', pairs)]
  transfers between devices with their start and end apart: 21 -> 54, of which waited for: 15 -> 25; matrix products, arithmetic and copies ran while one was open for 36% -> 39% of each run, Pallas kernels for 0% -> 0%
where the time goes in v1:
time: 692 us; the launch traced here: 687 us
  matrix products  207 us (30%)
  waiting for transfers between devices  199 us (29%)
  Pallas kernels  77.5 us (11%)
  starting transfers between devices  73.3 us (11%)
  other arithmetic  67.1 us (10%)
  local copies, waits for them, and re-layouts  60.9 us (9%)
    dot_general x31, matrix products, dot(): return lax.dot_general(left, right, dims, preferred_element_type=F32)  202 us
    ppermute x32, waiting for transfers between devices, swap(): return lax.ppermute(array, 'col', pairs)  94.1 us
    ppermute x9, waiting for transfers between devices, scatter_rows(): lax.ppermute(sent, 'row', [(i, (i + step) % count) for i in range(count)])  48.2 us
    pallas_call x1, Pallas kernels, attend_back(): pl.pallas_call(attend_back_kernel, grid=(latents, pairs), in_specs=[*part...  47.9 us
    ppermute x9, waiting for transfers between devices, gather_rows(): lax.ppermute(block, 'row', [(i, (i + step) % count) for i in range(count)])  44.5 us
    pallas_call x1, Pallas kernels, attend(): pl.pallas_call(attend_kernel, grid=(latents, pairs), in_specs=parts, out_...  29.6 us
    ppermute x32, starting transfers between devices, swap(): return lax.ppermute(array, 'col', pairs)  21 us
    ppermute x9, starting transfers between devices, gather_rows(): lax.ppermute(block, 'row', [(i, (i + step) % count) for i in range(count)])  20.4 us
  transfers between devices with their start and end apart: 54, of which 25 were waited for; matrix products, arithmetic and copies ran while one was open for 39% of the time, Pallas kernels for 0%

profile of v1, /device:TPU:0, one launch (start us, length us, event | category | flops | bytes accessed | tf_op | source)
XLA Modules:
  0.0 687.5 jit_solution(14365138304087883184)
XLA Ops:
  21.0 5.5 collective-permute-done.3
  38.0 5.5 collective-permute-start.16
  50.3 17.5 %collective-permute-done.15 = bf16[256,512]{0,1:T(8,128)(2,1)S(1)} collective-permute-done((bf16[256,512]{0,1:T(8,128)(2,1)S(1)}, bf16[256,512]{0,1:T(8,128)(2,1)S(1)}, u32[]{:S(2)}, u32[]{:S(2)}) %collective-permute-start.15) | collective-permute-done | bytes 262176 | tf_op jit(solution)/shard_map/ppermute | solution.py:222
  76.2 7.9 %collective-permute-done.5 = bf16[512,512]{0,1:T(8,128)(2,1)S(1)} collective-permute-done((bf16[512,512]{0,1:T(8,128)(2,1)}, bf16[512,512]{0,1:T(8,128)(2,1)S(1)}, u32[]{:S(2)}, u32[]{:S(2)}) %collective-permute-start.5) | collective-permute-done | bytes 524320 | tf_op jit(solution)/shard_map/ppermute | solution.py:195
  92.0 18.0 %collective-permute-done.6 = bf16[512,1024]{0,1:T(8,128)(2,1)} collective-permute-done((bf16[512,1024]{0,1:T(8,128)(2,1)}, bf16[512,1024]{0,1:T(8,128)(2,1)}, u32[]{:S(2)}, u32[]{:S(2)}) %collective-permute-start.6) | collective-permute-done | bytes 1048608 | tf_op jit(solution)/shard_map/ppermute | solution.py:195
  115.0 13.2 %add_convert_fusion.q_ref.k_ref.v_ref = bf16[2048,1536]{1,0:T(8,128)(2,1)} fusion(f32[1536]{0:T(1024)S(1)} %add.419, bf16[1024,1024]{1,0:T(8,128)(2,1)} %collective-permute-done, bf16[1024,1024]{1,0:T(8,128)(2,1)} %fusion.9, bf16[1024,384]{0,1:T(8,128)(2,1)S(1)} %fusion.43, bf16[1024,384]{0,1:T(8,128)(2,1)S(1)} %fusion.41, ...), kind=kOutput, calls=%fused_computation.1 | convolution fusion | flops 6469713920 | bytes 13637632 | tf_op jit(solution)/shard_map/dot_general | solution.py:28
  128.2 29.6 %attend.1 = (bf16[2048,512]{1,0:T(8,128)(2,1)}, f32[2,4,2,1024]{3,2,1,0:T(2,128)}) custom-call(bf16[2048,1536]{1,0:T(8,128)(2,1)} %add_convert_fusion.q_ref.k_ref.v_ref, bf16[2048,1536]{1,0:T(8,128)(2,1)} %add_convert_fusion.q_ref.k_ref.v_ref, bf16[2048,1536]{1,0:T(8,128)(2,1)} %add_convert_fusion.q_ref.k_ref.v_ref), custom_call_target="tpu_custom_call" | custom-call | flops 8589934592 | bytes 8388608 | tf_op jit(solution)/shard_map/attend/pallas_call | solution.py:140
  166.6 17.1 %collective-permute-done.11 = bf16[256,512]{1,0:T(8,128)(2,1)S(1)} collective-permute-done((bf16[256,512]{1,0:T(8,128)(2,1)S(1)}, bf16[256,512]{1,0:T(8,128)(2,1)S(1)}, u32[]{:S(2)}, u32[]{:S(2)}) %collective-permute-start.11) | collective-permute-done | bytes 262176 | tf_op jit(solution)/shard_map/ppermute | solution.py:222
  186.8 11.1 %collective-permute-done.18 = bf16[1024,256]{1,0:T(8,128)(2,1)S(1)} collective-permute-done((bf16[1024,256]{1,0:T(8,128)(2,1)S(1)}, bf16[1024,256]{1,0:T(8,128)(2,1)S(1)}, u32[]{:S(2)}, u32[]{:S(2)}) %collective-permute-start.18) | collective-permute-done | bytes 524320 | tf_op jit(solution)/shard_map/ppermute | solution.py:195
  210.3 13.1 %collective-permute-done.19 = bf16[1024,512]{1,0:T(8,128)(2,1)} collective-permute-done((bf16[1024,512]{1,0:T(8,128)(2,1)}, bf16[1024,512]{1,0:T(8,128)(2,1)}, u32[]{:S(2)}, u32[]{:S(2)}) %collective-permute-start.19) | collective-permute-done | bytes 1048608 | tf_op jit(solution)/shard_map/ppermute | solution.py:195
  226.9 11.1 %collective-permute-done.20 = bf16[1024,256]{0,1:T(8,128)(2,1)S(1)} collective-permute-done((bf16[1024,256]{0,1:T(8,128)(2,1)S(1)}, bf16[1024,256]{0,1:T(8,128)(2,1)S(1)}, u32[]{:S(2)}, u32[]{:S(2)}) %collective-permute-start.20) | collective-permute-done | bytes 524320 | tf_op jit(solution)/shard_map/ppermute | solution.py:195
  245.5 5.8 convolution_convert_fusion.2
  251.6 12.5 %collective-permute-done.21 = bf16[1024,512]{0,1:T(8,128)(2,1)S(1)} collective-permute-done((bf16[1024,512]{0,1:T(8,128)(2,1)S(1)}, bf16[1024,512]{0,1:T(8,128)(2,1)S(1)}, u32[]{:S(2)}, u32[]{:S(2)}) %collective-permute-start.21) | collective-permute-done | bytes 1048608 | tf_op jit(solution)/shard_map/ppermute | solution.py:195
  264.2 7.3 %convert_reduce_fusion.2 = (f32[512]{0:T(512)S(1)}, bf16[2048,512]{1,0:T(8,128)(2,1)S(1)}) fusion(f32[2048,512]{1,0:T(8,128)S(1)} %fusion.127, f32[512]{0:T(512)S(1)} %pad_maximum_fusion.36, bf16[1024,512]{0,1:T(8,128)(2,1)S(1)} %collective-permute-done.21, bf16[1024,1024]{1,0:T(8,128)(2,1)} %collective-permute-done.25, bf16[1024,1024]{1,0:T(8,128)(2,1)} %fusion.1), kind=kOutput, calls=%fused_computation.42 | convolution fusion | flops 2179988992 | bytes 11538432 | tf_op jit(solution)/shard_map/dot_general | solution.py:28
  272.1 5.0 convolution_convert_fusion.4
  281.5 5.8 convolution_convert_fusion.1
  291.8 10.2 %convert_reduce_fusion.4 = (f32[512]{0:T(512)S(1)}, bf16[2048,512]{1,0:T(8,128)(2,1)}) fusion(f32[2048,512]{1,0:T(8,128)S(1)} %fusion.119, f32[512]{0:T(512)S(1)} %pad_maximum_fusion.37, bf16[1024,256]{0,1:T(8,128)(2,1)S(1)} %collective-permute-done.22, bf16[1024,256]{0,1:T(8,128)(2,1)S(1)} %get-tuple-element.73, ...), kind=kOutput, calls=%fused_computation.44 | convolution fusion | flops 2182086144 | bytes 11538432 | tf_op jit(solution)/shard_map/dot_general | solution.py:28
  302.5 7.5 %convert_reduce_fusion.3 = (f32[512]{0:T(512)S(1)}, bf16[2048,512]{1,0:T(8,128)(2,1)S(1)}) fusion(f32[2048,512]{1,0:T(8,128)S(1)} %fusion.126, f32[512]{0:T(512)S(1)} %pad_maximum_fusion.38, bf16[1024,512]{0,1:T(8,128)(2,1)S(1)} %collective-permute-done.23, bf16[1024,1024]{1,0:T(8,128)(2,1)} %collective-permute-done.25, bf16[1024,1024]{1,0:T(8,128)(2,1)} %fusion.1), kind=kOutput, calls=%fused_computation.43 | convolution fusion | flops 2179988992 | bytes 11538432 | tf_op jit(solution)/shard_map/dot_general | solution.py:28
  310.6 5.1 convolution_convert_fusion.3
  317.4 6.7 fusion.122
  324.0 6.2 fusion.116
  336.2 6.1 fusion.117
  342.3 10.2 %add_add_fusion.1 = f32[2048,1024]{1,0:T(8,128)S(1)} fusion(f32[2048,1024]{1,0:T(8,128)} %fusion.116, f32[2048,1024]{1,0:T(8,128)} %fusion.117, f32[2048,1024]{1,0:T(8,128)} %fusion.122, bf16[1024,512]{0,1:T(8,128)(2,1)S(1)} %copy-done.33, f32[2048,512]{1,0:T(8,128)S(1)} %fusion.126, f32[512]{0:T(512)S(1)} %pad_maximum_fusion.38), kind=kOutput, calls=%fused_computation.3 | convolution fusion | flops 2164260864 | bytes 38799360 | tf_op jit(solution)/shard_map/dot_general | solution.py:28
  354.2 9.0 %convert_reduce_fusion.5 = (f32[512]{0:T(512)}, bf16[2048,512]{1,0:T(8,128)(2,1)S(1)}) fusion(f32[2048,512]{1,0:T(8,128)} %copy-done.101, f32[512]{0:T(512)S(1)} %pad_maximum_fusion.35, bf16[1024,256]{0,1:T(8,128)(2,1)S(1)} %copy-done.51, bf16[1024,256]{0,1:T(8,128)(2,1)S(1)} %copy-done.22, bf16[1024,1024]{1,0:T(8,128)(2,1)} %collective-permute-done.25, ...), kind=kOutput, calls=%fused_computation.45 | convolution fusion | flops 2182086144 | bytes 11538432 | tf_op jit(solution)/shard_map/dot_general | solution.py:28
  363.2 7.7 %fusion.140 = f32[2048,1024]{1,0:T(8,128)} fusion(bf16[2048,512]{1,0:T(8,128)(2,1)S(1)} %copy-done.100, bf16[1024,512]{1,0:T(8,128)(2,1)} %collective-permute-done.17), kind=kOutput, calls=%fused_computation.353 | convolution fusion | flops 2147483648 | bytes 11534336 | tf_op jit(solution)/shard_map/dot_general | solution.py:28
  370.9 5.8 fusion.118
  376.8 5.6 fusion.120
  382.4 12.3 %add_add_fusion = f32[2048,1024]{1,0:T(8,128)S(1)} fusion(f32[2048,1024]{1,0:T(8,128)} %fusion.118, f32[2048,1024]{1,0:T(8,128)} %fusion.120, f32[2048,1024]{1,0:T(8,128)} %fusion.140, bf16[2048,512]{1,0:T(8,128)(2,1)} %copy-done.20, bf16[1024,512]{1,0:T(8,128)(2,1)} %collective-permute-done.19), kind=kOutput, calls=%fused_computation.2 | convolution fusion | flops 2153775104 | bytes 36700160 | tf_op jit(solution)/shard_map/dot_general | solution.py:28
  396.9 5.3 convert_add_fusion.2
  409.6 5.0 convert_add_fusion.5
  416.2 5.2 convert_add_fusion.3
  426.7 8.7 %fusion = (f32[1024]{0:T(1024)S(1)}, f32[1024]{0:T(1024)}, bf16[1024,1024]{1,0:T(8,128)(2,1)}, f32[1024]{0:T(1024)}, f32[1024]{0:T(1024)}, /*index=5*/f32[1024,1024]{1,0:T(8,128)S(1)}) fusion(bf16[1024,1024]{1,0:T(8,128)(2,1)S(1)} %copy-done.8, f32[1024]{0:T(1024)S(1)} %copy-done.73, f32[1024]{0:T(1024)S(1)} %copy-done.77, ...), kind=kLoop, calls=%fused_computation.12 | loop fusion | flops 29356032 | bytes 31510528 | tf_op jit(solution)/shard_map/reduce_sum | solution.py:412
  440.5 6.2 collective-permute-done.37
  460.1 18.7 %collective-permute-done.41 = bf16[256,512]{1,0:T(8,128)(2,1)S(1)} collective-permute-done((bf16[256,512]{1,0:T(8,128)(2,1)}, bf16[256,512]{1,0:T(8,128)(2,1)S(1)}, u32[]{:S(2)}, u32[]{:S(2)}) %collective-permute-start.41) | collective-permute-done | bytes 262176 | tf_op jit(solution)/shard_map/ppermute | solution.py:237
  479.7 12.2 %collective-permute-done.48 = bf16[256,512]{0,1:T(8,128)(2,1)S(1)} collective-permute-done((bf16[256,512]{0,1:T(8,128)(2,1)S(1)}, bf16[256,512]{0,1:T(8,128)(2,1)S(1)}, u32[]{:S(2)}, u32[]{:S(2)}) %collective-permute-start.48) | collective-permute-done | bytes 262176 | tf_op jit(solution)/shard_map/ppermute | solution.py:237
  492.8 5.9 fusion.18
  501.1 5.9 convolution_convert_fusion.grad_ref
  507.0 47.9 %attend_back.1 = bf16[2048,1536]{1,0:T(8,128)(2,1)} custom-call(bf16[2048,1536]{1,0:T(8,128)(2,1)} %add_convert_fusion.q_ref.k_ref.v_ref, bf16[2048,1536]{1,0:T(8,128)(2,1)} %add_convert_fusion.q_ref.k_ref.v_ref, bf16[2048,1536]{1,0:T(8,128)(2,1)} %add_convert_fusion.q_ref.k_ref.v_ref, bf16[2048,512]{1,0:T(8,128)(2,1)} %get-tuple-element.19.mixed_ref, ...), custom_call_target="tpu_custom_call" | custom-call | flops 21474836480 | bytes 16777216 | tf_op jit(solution)/shard_map/attend_back/pallas_call | solution.py:162
  554.9 10.6 %fusion.19 = f32[1024,1536]{1,0:T(8,128)S(1)} fusion(bf16[2048,1536]{1,0:T(8,128)(2,1)} %attend_back.1, bf16[1024,1024]{1,0:T(8,128)(2,1)} %collective-permute-done, bf16[1024,1024]{1,0:T(8,128)(2,1)} %fusion.9), kind=kOutput, calls=%fused_computation.84 | convolution fusion | flops 6450839552 | bytes 16777216 | tf_op jit(solution)/shard_map/dot_general | solution.py:28
  572.2 9.6 %fusion.44 = f32[2048,1024]{1,0:T(8,128)} fusion(bf16[2048,1536]{1,0:T(8,128)(2,1)S(1)} %bitcast.274, bf16[1024,384]{0,1:T(8,128)(2,1)S(1)} %copy-done.38, bf16[1024,384]{0,1:T(8,128)(2,1)S(1)} %copy-done.42, bf16[1024,384]{0,1:T(8,128)(2,1)S(1)} %copy-done.40, bf16[1024,384]{0,1:T(8,128)(2,1)S(1)} %copy-done.44), kind=kOutput, calls=%fused_computation.179 | convolution fusion | flops 6455033856 | bytes 17825792 | tf_op jit(solution)/shard_map/dot_general | solution.py:28
  584.9 7.7 %reshape.288 = f32[1024,4,384]{2,1,0:T(4,128)} reshape(f32[1024,1536]{1,0:T(8,128)} %copy-done.2) | data formatting | bytes 12582912 | tf_op jit(solution)/shard_map/reshape | solution.py:463
  607.9 10.5 %collective-permute-done.30 = bf16[512,512]{1,0:T(8,128)(2,1)} collective-permute-done((bf16[512,512]{1,0:T(8,128)(2,1)}, bf16[512,512]{1,0:T(8,128)(2,1)}, u32[]{:S(2)}, u32[]{:S(2)}) %collective-permute-start.30) | collective-permute-done | bytes 524320 | tf_op jit(solution)/shard_map/ppermute | solution.py:195
  621.9 5.2 collective-permute-start.33
  633.8 9.8 %collective-permute-done.34 = bf16[256,512]{0,1:T(8,128)(2,1)} collective-permute-done((bf16[256,512]{0,1:T(8,128)(2,1)S(1)}, bf16[256,512]{0,1:T(8,128)(2,1)}, u32[]{:S(2)}, u32[]{:S(2)}) %collective-permute-start.34) | collective-permute-done | bytes 262176 | tf_op jit(solution)/shard_map/ppermute | solution.py:237
  646.4 4.3 fusion.14
  651.6 10.6 %all-to-all-start.2 = ((f32[32,14,128]{2,1,0:T(8,128)}), f32[32,14,128]{2,1,0:T(8,128)S(1)}, u32[]{:S(2)}, u32[]{:S(2)}) async-start(f32[32,14,128]{2,1,0:T(8,128)} %bitcast.76), calls=%async_computation.2 | async-start | bytes 524288 | tf_op jit(solution)/shard_map/all_to_all | solution.py:266
  662.2 6.3 fusion.13
  681.6 5.0 all-to-all-done.3
  (459 shorter events, 205.8 us)
Async XLA Ops:
  2.5 46.7 %collective-permute-start.2 = (bf16[256,512]{0,1:T(8,128)(2,1)S(1)}, bf16[256,512]{0,1:T(8,128)(2,1)S(1)}, u32[]{:S(2)}, u32[]{:S(2)}) collective-permute-start(bf16[256,512]{0,1:T(8,128)(2,1)S(1)} %get-tuple-element.97), channel_id=1, source_target_pairs={{0,16},{8,24},{16,0},{24,8},{1,17},{9,25},{17,1},{25,9},{2,18},{10... | collective-permute-start | bytes 786440 | tf_op jit(solution)/shard_map/ppermute | solution.py:222
  6.6 42.6 %collective-permute-start.1 = (bf16[256,512]{0,1:T(8,128)(2,1)S(1)}, bf16[256,512]{0,1:T(8,128)(2,1)S(1)}, u32[]{:S(2)}, u32[]{:S(2)}) collective-permute-start(bf16[256,512]{0,1:T(8,128)(2,1)S(1)} %get-tuple-element.97), channel_id=1, source_target_pairs={{0,8},{8,16},{16,24},{24,0},{1,9},{9,17},{17,25},{25,1},{2,10},{10... | collective-permute-start | bytes 786440 | tf_op jit(solution)/shard_map/ppermute | solution.py:222
  8.2 18.3 %collective-permute-start.3 = (bf16[256,512]{0,1:T(8,128)(2,1)S(1)}, bf16[256,512]{0,1:T(8,128)(2,1)S(1)}, u32[]{:S(2)}, u32[]{:S(2)}) collective-permute-start(bf16[256,512]{0,1:T(8,128)(2,1)S(1)} %get-tuple-element.97), channel_id=1, source_target_pairs={{0,24},{8,0},{16,8},{24,16},{1,25},{9,1},{17,9},{25,17},{2,26},{10... | collective-permute-start | bytes 786440 | tf_op jit(solution)/shard_map/ppermute | solution.py:222
  15.1 19.2 %all-to-all-start = ((bf16[32,16,128]{2,1,0:T(8,128)(2,1)}), bf16[32,16,128]{2,1,0:T(8,128)(2,1)S(1)}, u32[]{:S(2)}, u32[]{:S(2)}) async-start(bf16[32,16,128]{2,1,0:T(8,128)(2,1)} %broadcast_in_dim.23), calls=%async_computation | async-start | bytes 262144 | tf_op jit(solution)/shard_map/all_to_all | solution.py:266
  38.0 12.2 %collective-permute-start.16 = (bf16[256,512]{0,1:T(8,128)(2,1)S(1)}, bf16[256,512]{0,1:T(8,128)(2,1)S(1)}, u32[]{:S(2)}, u32[]{:S(2)}) collective-permute-start(bf16[256,512]{0,1:T(8,128)(2,1)S(1)} %bitcast.296), channel_id=1, source_target_pairs={{0,24},{8,0},{16,8},{24,16},{1,25},{9,1},{17,9},{25,17},{2,26},{10... | collective-permute-start | bytes 786440 | tf_op jit(solution)/shard_map/ppermute | solution.py:222
  43.5 24.3 %collective-permute-start.15 = (bf16[256,512]{0,1:T(8,128)(2,1)S(1)}, bf16[256,512]{0,1:T(8,128)(2,1)S(1)}, u32[]{:S(2)}, u32[]{:S(2)}) collective-permute-start(bf16[256,512]{0,1:T(8,128)(2,1)S(1)} %bitcast.297), channel_id=1, source_target_pairs={{0,16},{8,24},{16,0},{24,8},{1,17},{9,25},{17,1},{25,9},{2,18},{10... | collective-permute-start | bytes 786440 | tf_op jit(solution)/shard_map/ppermute | solution.py:222
  43.5 24.3 %collective-permute-start.14 = (bf16[256,512]{0,1:T(8,128)(2,1)S(1)}, bf16[256,512]{0,1:T(8,128)(2,1)S(1)}, u32[]{:S(2)}, u32[]{:S(2)}) collective-permute-start(bf16[256,512]{0,1:T(8,128)(2,1)S(1)} %bitcast.298), channel_id=1, source_target_pairs={{0,8},{8,16},{16,24},{24,0},{1,9},{9,17},{17,25},{25,1},{2,10},{10... | collective-permute-start | bytes 786440 | tf_op jit(solution)/shard_map/ppermute | solution.py:222
  45.4 28.7 %all-to-all-start.1 = ((f32[32,6,128]{2,1,0:T(8,128)}), f32[32,6,128]{2,1,0:T(8,128)S(1)}, u32[]{:S(2)}, u32[]{:S(2)}) async-start(f32[32,6,128]{2,1,0:T(8,128)} %copy.89), calls=%async_computation.1 | async-start | bytes 262144 | tf_op jit(solution)/shard_map/all_to_all | solution.py:266
  70.5 13.5 %collective-permute-start.5 = (bf16[512,512]{0,1:T(8,128)(2,1)}, bf16[512,512]{0,1:T(8,128)(2,1)S(1)}, u32[]{:S(2)}, u32[]{:S(2)}) collective-permute-start(bf16[512,512]{0,1:T(8,128)(2,1)} %pad_maximum_fusion.30), channel_id=1, source_target_pairs={{0,4},{1,5},{2,6},{3,7},{4,0},{5,1},{6,2},{7,3},{8,12},{9,13},{10,... | collective-permute-start | bytes 1572872 | tf_op jit(solution)/shard_map/ppermute | solution.py:195
  72.0 14.4 %collective-permute-start.4 = (bf16[512,512]{0,1:T(8,128)(2,1)}, bf16[512,512]{0,1:T(8,128)(2,1)S(1)}, u32[]{:S(2)}, u32[]{:S(2)}) collective-permute-start(bf16[512,512]{0,1:T(8,128)(2,1)} %pad_maximum_fusion.29), channel_id=1, source_target_pairs={{0,2},{1,3},{2,0},{3,1},{4,6},{5,7},{6,4},{7,5},{8,10},{9,11},{10,... | collective-permute-start | bytes 1572872 | tf_op jit(solution)/shard_map/ppermute | solution.py:195
  86.1 24.0 %collective-permute-start.6 = (bf16[512,1024]{0,1:T(8,128)(2,1)}, bf16[512,1024]{0,1:T(8,128)(2,1)}, u32[]{:S(2)}, u32[]{:S(2)}) collective-permute-start(bf16[512,1024]{0,1:T(8,128)(2,1)} %pad_maximum_fusion.14), channel_id=1, source_target_pairs={{0,2},{1,3},{2,0},{3,1},{4,6},{5,7},{6,4},{7,5},{8,10},{9,11},{10,... | collective-permute-start | bytes 3145736 | tf_op jit(solution)/shard_map/ppermute | solution.py:195
  88.5 23.6 %collective-permute-start.7 = (bf16[512,1024]{0,1:T(8,128)(2,1)}, bf16[512,1024]{0,1:T(8,128)(2,1)}, u32[]{:S(2)}, u32[]{:S(2)}) collective-permute-start(bf16[512,1024]{0,1:T(8,128)(2,1)} %pad_maximum_fusion.15), channel_id=1, source_target_pairs={{0,4},{1,5},{2,6},{3,7},{4,0},{5,1},{6,2},{7,3},{8,12},{9,13},{10,... | collective-permute-start | bytes 3145736 | tf_op jit(solution)/shard_map/ppermute | solution.py:195
  90.9 24.1 %collective-permute-start = (bf16[1024,1024]{1,0:T(8,128)(2,1)}, bf16[1024,1024]{1,0:T(8,128)(2,1)}, u32[]{:S(2)}, u32[]{:S(2)}) collective-permute-start(bf16[1024,1024]{1,0:T(8,128)(2,1)} %fusion.9), channel_id=1, source_target_pairs={{0,1},{1,0},{2,3},{3,2},{4,5},{5,4},{6,7},{7,6},{8,9},{9,8},{10,11... | collective-permute-start | bytes 6291464 | tf_op jit(solution)/shard_map/ppermute | solution.py:195
  162.2 40.0 %collective-permute-start.8 = (bf16[1024,1024]{1,0:T(8,128)(2,1)S(1)}, bf16[1024,1024]{1,0:T(8,128)(2,1)S(1)}, u32[]{:S(2)}, u32[]{:S(2)}) collective-permute-start(bf16[1024,1024]{1,0:T(8,128)(2,1)S(1)} %slice.576), channel_id=1, source_target_pairs={{0,1},{1,0},{2,3},{3,2},{4,5},{5,4},{6,7},{7,6},{8,9},{9,8},{10,11... | collective-permute-start | bytes 6291464 | tf_op jit(solution)/shard_map/ppermute | solution.py:195
  163.0 20.8 %collective-permute-start.11 = (bf16[256,512]{1,0:T(8,128)(2,1)S(1)}, bf16[256,512]{1,0:T(8,128)(2,1)S(1)}, u32[]{:S(2)}, u32[]{:S(2)}) collective-permute-start(bf16[256,512]{1,0:T(8,128)(2,1)S(1)} %copy-done.55), channel_id=1, source_target_pairs={{0,16},{8,24},{16,0},{24,8},{1,17},{9,25},{17,1},{25,9},{2,18},{10... | collective-permute-start | bytes 786440 | tf_op jit(solution)/shard_map/ppermute | solution.py:222
  166.3 17.5 %collective-permute-start.10 = (bf16[256,512]{1,0:T(8,128)(2,1)S(1)}, bf16[256,512]{1,0:T(8,128)(2,1)S(1)}, u32[]{:S(2)}, u32[]{:S(2)}) collective-permute-start(bf16[256,512]{1,0:T(8,128)(2,1)S(1)} %copy-done.55), channel_id=1, source_target_pairs={{0,8},{8,16},{16,24},{24,0},{1,9},{9,17},{17,25},{25,1},{2,10},{10... | collective-permute-start | bytes 786440 | tf_op jit(solution)/shard_map/ppermute | solution.py:222
  184.1 13.8 %collective-permute-start.18 = (bf16[1024,256]{1,0:T(8,128)(2,1)S(1)}, bf16[1024,256]{1,0:T(8,128)(2,1)S(1)}, u32[]{:S(2)}, u32[]{:S(2)}) collective-permute-start(bf16[1024,256]{1,0:T(8,128)(2,1)S(1)} %get-tuple-element.74), channel_id=1, source_target_pairs={{0,4},{1,5},{2,6},{3,7},{4,0},{5,1},{6,2},{7,3},{8,12},{9,13},{10,... | collective-permute-start | bytes 1572872 | tf_op jit(solution)/shard_map/ppermute | solution.py:195
  184.5 16.3 %collective-permute-start.13 = (bf16[1024,256]{1,0:T(8,128)(2,1)S(1)}, bf16[1024,256]{1,0:T(8,128)(2,1)S(1)}, u32[]{:S(2)}, u32[]{:S(2)}) collective-permute-start(bf16[1024,256]{1,0:T(8,128)(2,1)S(1)} %get-tuple-element.75), channel_id=1, source_target_pairs={{0,2},{1,3},{2,0},{3,1},{4,6},{5,7},{6,4},{7,5},{8,10},{9,11},{10,... | collective-permute-start | bytes 1572872 | tf_op jit(solution)/shard_map/ppermute | solution.py:195
  199.1 24.4 %collective-permute-start.19 = (bf16[1024,512]{1,0:T(8,128)(2,1)}, bf16[1024,512]{1,0:T(8,128)(2,1)}, u32[]{:S(2)}, u32[]{:S(2)}) collective-permute-start(bf16[1024,512]{1,0:T(8,128)(2,1)} %pad_maximum_fusion.21), channel_id=1, source_target_pairs={{0,2},{1,3},{2,0},{3,1},{4,6},{5,7},{6,4},{7,5},{8,10},{9,11},{10,... | collective-permute-start | bytes 3145736 | tf_op jit(solution)/shard_map/ppermute | solution.py:195
  201.9 24.1 %collective-permute-start.17 = (bf16[1024,512]{1,0:T(8,128)(2,1)}, bf16[1024,512]{1,0:T(8,128)(2,1)}, u32[]{:S(2)}, u32[]{:S(2)}) collective-permute-start(bf16[1024,512]{1,0:T(8,128)(2,1)} %pad_maximum_fusion.18), channel_id=1, source_target_pairs={{0,4},{1,5},{2,6},{3,7},{4,0},{5,1},{6,2},{7,3},{8,12},{9,13},{10,... | collective-permute-start | bytes 3145736 | tf_op jit(solution)/shard_map/ppermute | solution.py:195
  204.5 36.8 %collective-permute-start.9 = (bf16[1024,1024]{1,0:T(8,128)(2,1)S(1)}, bf16[1024,1024]{1,0:T(8,128)(2,1)}, u32[]{:S(2)}, u32[]{:S(2)}) collective-permute-start(bf16[1024,1024]{1,0:T(8,128)(2,1)S(1)} %add_convert_fusion.6), channel_id=1, source_target_pairs={{0,1},{1,0},{2,3},{3,2},{4,5},{5,4},{6,7},{7,6},{8,9},{9,8},{10,11... | collective-permute-start | bytes 6291464 | tf_op jit(solution)/shard_map/ppermute | solution.py:195
  208.8 36.8 %collective-permute-start.25 = (bf16[1024,1024]{1,0:T(8,128)(2,1)}, bf16[1024,1024]{1,0:T(8,128)(2,1)}, u32[]{:S(2)}, u32[]{:S(2)}) collective-permute-start(bf16[1024,1024]{1,0:T(8,128)(2,1)} %fusion.1), channel_id=1, source_target_pairs={{0,1},{1,0},{2,3},{3,2},{4,5},{5,4},{6,7},{7,6},{8,9},{9,8},{10,11... | collective-permute-start | bytes 6291464 | tf_op jit(solution)/shard_map/ppermute | solution.py:195
  238.0 26.2 %collective-permute-start.21 = (bf16[1024,512]{0,1:T(8,128)(2,1)S(1)}, bf16[1024,512]{0,1:T(8,128)(2,1)S(1)}, u32[]{:S(2)}, u32[]{:S(2)}) collective-permute-start(bf16[1024,512]{0,1:T(8,128)(2,1)S(1)} %pad_maximum_fusion.22), channel_id=1, source_target_pairs={{0,4},{1,5},{2,6},{3,7},{4,0},{5,1},{6,2},{7,3},{8,12},{9,13},{10,... | collective-permute-start | bytes 3145736 | tf_op jit(solution)/shard_map/ppermute | solution.py:195
  238.5 64.0 %collective-permute-start.23 = (bf16[1024,512]{0,1:T(8,128)(2,1)S(1)}, bf16[1024,512]{0,1:T(8,128)(2,1)S(1)}, u32[]{:S(2)}, u32[]{:S(2)}) collective-permute-start(bf16[1024,512]{0,1:T(8,128)(2,1)S(1)} %pad_maximum_fusion.23), channel_id=1, source_target_pairs={{0,2},{1,3},{2,0},{3,1},{4,6},{5,7},{6,4},{7,5},{8,10},{9,11},{10,... | collective-permute-start | bytes 3145736 | tf_op jit(solution)/shard_map/ppermute | solution.py:195
  251.3 164.8 %collective-permute-start.43 = (bf16[1024,512]{1,0:T(8,128)(2,1)}, bf16[1024,512]{1,0:T(8,128)(2,1)}, u32[]{:S(2)}, u32[]{:S(2)}) collective-permute-start(bf16[1024,512]{1,0:T(8,128)(2,1)} %convolution_convert_fusion.2), channel_id=1, source_target_pairs={{0,4},{1,5},{2,6},{3,7},{4,0},{5,1},{6,2},{7,3},{8,12},{9,13},{10,... | collective-permute-start | bytes 3145736 | tf_op jit(solution)/shard_map/ppermute | solution.py:195
  277.1 131.5 %collective-permute-start.36 = (bf16[1024,512]{1,0:T(8,128)(2,1)}, bf16[1024,512]{1,0:T(8,128)(2,1)}, u32[]{:S(2)}, u32[]{:S(2)}) collective-permute-start(bf16[1024,512]{1,0:T(8,128)(2,1)} %convolution_convert_fusion.4), channel_id=1, source_target_pairs={{0,4},{1,5},{2,6},{3,7},{4,0},{5,1},{6,2},{7,3},{8,12},{9,13},{10,... | collective-permute-start | bytes 3145736 | tf_op jit(solution)/shard_map/ppermute | solution.py:195
  287.4 107.7 %collective-permute-start.45 = (bf16[1024,512]{1,0:T(8,128)(2,1)}, bf16[1024,512]{1,0:T(8,128)(2,1)}, u32[]{:S(2)}, u32[]{:S(2)}) collective-permute-start(bf16[1024,512]{1,0:T(8,128)(2,1)} %convolution_convert_fusion.1), channel_id=1, source_target_pairs={{0,2},{1,3},{2,0},{3,1},{4,6},{5,7},{6,4},{7,5},{8,10},{9,11},{10,... | collective-permute-start | bytes 3145736 | tf_op jit(solution)/shard_map/ppermute | solution.py:195
  315.7 86.6 %collective-permute-start.38 = (bf16[1024,512]{1,0:T(8,128)(2,1)}, bf16[1024,512]{1,0:T(8,128)(2,1)}, u32[]{:S(2)}, u32[]{:S(2)}) collective-permute-start(bf16[1024,512]{1,0:T(8,128)(2,1)} %convolution_convert_fusion.3), channel_id=1, source_target_pairs={{0,2},{1,3},{2,0},{3,1},{4,6},{5,7},{6,4},{7,5},{8,10},{9,11},{10,... | collective-permute-start | bytes 3145736 | tf_op jit(solution)/shard_map/ppermute | solution.py:195
  354.1 72.5 %collective-permute-start.24 = (bf16[1024,1024]{1,0:T(8,128)(2,1)}, bf16[1024,1024]{1,0:T(8,128)(2,1)}, u32[]{:S(2)}, u32[]{:S(2)}) collective-permute-start(bf16[1024,1024]{1,0:T(8,128)(2,1)} %slice.575), channel_id=1, source_target_pairs={{0,1},{1,0},{2,3},{3,2},{4,5},{5,4},{6,7},{7,6},{8,9},{9,8},{10,11... | collective-permute-start | bytes 6291464 | tf_op jit(solution)/shard_map/ppermute | solution.py:195
  395.0 26.8 %collective-permute-start.26 = (bf16[1024,1024]{1,0:T(8,128)(2,1)S(1)}, bf16[1024,1024]{1,0:T(8,128)(2,1)S(1)}, u32[]{:S(2)}, u32[]{:S(2)}) collective-permute-start(bf16[1024,1024]{1,0:T(8,128)(2,1)S(1)} %slice.574), channel_id=1, source_target_pairs={{0,1},{1,0},{2,3},{3,2},{4,5},{5,4},{6,7},{7,6},{8,9},{9,8},{10,11... | collective-permute-start | bytes 6291464 | tf_op jit(solution)/shard_map/ppermute | solution.py:195
  402.3 46.5 %collective-permute-start.46 = (bf16[1024,256]{1,0:T(8,128)(2,1)S(1)}, bf16[1024,256]{1,0:T(8,128)(2,1)}, u32[]{:S(2)}, u32[]{:S(2)}) collective-permute-start(bf16[1024,256]{1,0:T(8,128)(2,1)S(1)} %slice.577), channel_id=1, source_target_pairs={{0,4},{1,5},{2,6},{3,7},{4,0},{5,1},{6,2},{7,3},{8,12},{9,13},{10,... | collective-permute-start | bytes 1572872 | tf_op jit(solution)/shard_map/ppermute | solution.py:195
  408.6 28.7 %collective-permute-start.39 = (bf16[1024,256]{1,0:T(8,128)(2,1)S(1)}, bf16[1024,256]{1,0:T(8,128)(2,1)}, u32[]{:S(2)}, u32[]{:S(2)}) collective-permute-start(bf16[1024,256]{1,0:T(8,128)(2,1)S(1)} %slice.579), channel_id=1, source_target_pairs={{0,4},{1,5},{2,6},{3,7},{4,0},{5,1},{6,2},{7,3},{8,12},{9,13},{10,... | collective-permute-start | bytes 1572872 | tf_op jit(solution)/shard_map/ppermute | solution.py:195
  421.5 28.5 %collective-permute-start.44 = (bf16[1024,256]{1,0:T(8,128)(2,1)S(1)}, bf16[1024,256]{1,0:T(8,128)(2,1)}, u32[]{:S(2)}, u32[]{:S(2)}) collective-permute-start(bf16[1024,256]{1,0:T(8,128)(2,1)S(1)} %slice.578), channel_id=1, source_target_pairs={{0,2},{1,3},{2,0},{3,1},{4,6},{5,7},{6,4},{7,5},{8,10},{9,11},{10,... | collective-permute-start | bytes 1572872 | tf_op jit(solution)/shard_map/ppermute | solution.py:195
  421.9 24.8 %collective-permute-start.37 = (bf16[1024,256]{1,0:T(8,128)(2,1)S(1)}, bf16[1024,256]{1,0:T(8,128)(2,1)}, u32[]{:S(2)}, u32[]{:S(2)}) collective-permute-start(bf16[1024,256]{1,0:T(8,128)(2,1)S(1)} %slice.580), channel_id=1, source_target_pairs={{0,2},{1,3},{2,0},{3,1},{4,6},{5,7},{6,4},{7,5},{8,10},{9,11},{10,... | collective-permute-start | bytes 1572872 | tf_op jit(solution)/shard_map/ppermute | solution.py:195
  437.3 55.5 %collective-permute-start.27 = (bf16[1024,1024]{1,0:T(8,128)(2,1)}, bf16[1024,1024]{1,0:T(8,128)(2,1)}, u32[]{:S(2)}, u32[]{:S(2)}) collective-permute-start(bf16[1024,1024]{1,0:T(8,128)(2,1)} %multiply_convert_fusion.8), channel_id=1, source_target_pairs={{0,1},{1,0},{2,3},{3,2},{4,5},{5,4},{6,7},{7,6},{8,9},{9,8},{10,11... | collective-permute-start | bytes 6291464 | tf_op jit(solution)/shard_map/ppermute | solution.py:195
  448.8 30.0 %collective-permute-start.41 = (bf16[256,512]{1,0:T(8,128)(2,1)}, bf16[256,512]{1,0:T(8,128)(2,1)S(1)}, u32[]{:S(2)}, u32[]{:S(2)}) collective-permute-start(bf16[256,512]{1,0:T(8,128)(2,1)} %get-tuple-element.62), channel_id=1, source_target_pairs={{0,16},{8,24},{16,0},{24,8},{1,17},{9,25},{17,1},{25,9},{2,18},{10... | collective-permute-start | bytes 786440 | tf_op jit(solution)/shard_map/ppermute | solution.py:237
  451.7 27.1 %collective-permute-start.42 = (bf16[256,512]{1,0:T(8,128)(2,1)S(1)}, bf16[256,512]{1,0:T(8,128)(2,1)S(1)}, u32[]{:S(2)}, u32[]{:S(2)}) collective-permute-start(bf16[256,512]{1,0:T(8,128)(2,1)S(1)} %get-tuple-element.63), channel_id=1, source_target_pairs={{0,24},{8,0},{16,8},{24,16},{1,25},{9,1},{17,9},{25,17},{2,26},{10... | collective-permute-start | bytes 786440 | tf_op jit(solution)/shard_map/ppermute | solution.py:237
  455.6 24.1 %collective-permute-start.47 = (bf16[256,512]{0,1:T(8,128)(2,1)S(1)}, bf16[256,512]{0,1:T(8,128)(2,1)S(1)}, u32[]{:S(2)}, u32[]{:S(2)}) collective-permute-start(bf16[256,512]{0,1:T(8,128)(2,1)S(1)} %get-tuple-element.58), channel_id=1, source_target_pairs={{0,8},{8,16},{16,24},{24,0},{1,9},{9,17},{17,25},{25,1},{2,10},{10... | collective-permute-start | bytes 786440 | tf_op jit(solution)/shard_map/ppermute | solution.py:237
  460.1 31.8 %collective-permute-start.48 = (bf16[256,512]{0,1:T(8,128)(2,1)S(1)}, bf16[256,512]{0,1:T(8,128)(2,1)S(1)}, u32[]{:S(2)}, u32[]{:S(2)}) collective-permute-start(bf16[256,512]{0,1:T(8,128)(2,1)S(1)} %get-tuple-element.59), channel_id=1, source_target_pairs={{0,16},{8,24},{16,0},{24,8},{1,17},{9,25},{17,1},{25,9},{2,18},{10... | collective-permute-start | bytes 786440 | tf_op jit(solution)/shard_map/ppermute | solution.py:237
  478.8 13.1 %collective-permute-start.49 = (bf16[256,512]{0,1:T(8,128)(2,1)S(1)}, bf16[256,512]{0,1:T(8,128)(2,1)S(1)}, u32[]{:S(2)}, u32[]{:S(2)}) collective-permute-start(bf16[256,512]{0,1:T(8,128)(2,1)S(1)} %get-tuple-element.60), channel_id=1, source_target_pairs={{0,24},{8,0},{16,8},{24,16},{1,25},{9,1},{17,9},{25,17},{2,26},{10... | collective-permute-start | bytes 786440 | tf_op jit(solution)/shard_map/ppermute | solution.py:237
  567.3 36.8 %collective-permute-start.31 = (bf16[512,1024]{1,0:T(8,128)(2,1)}, bf16[512,1024]{1,0:T(8,128)(2,1)S(1)}, u32[]{:S(2)}, u32[]{:S(2)}) collective-permute-start(bf16[512,1024]{1,0:T(8,128)(2,1)} %pad_maximum_fusion.25), channel_id=1, source_target_pairs={{0,2},{1,3},{2,0},{3,1},{4,6},{5,7},{6,4},{7,5},{8,10},{9,11},{10,... | collective-permute-start | bytes 3145736 | tf_op jit(solution)/shard_map/ppermute | solution.py:195
  568.8 32.4 %collective-permute-start.29 = (bf16[512,1024]{1,0:T(8,128)(2,1)}, bf16[512,1024]{1,0:T(8,128)(2,1)}, u32[]{:S(2)}, u32[]{:S(2)}) collective-permute-start(bf16[512,1024]{1,0:T(8,128)(2,1)} %pad_maximum_fusion.24), channel_id=1, source_target_pairs={{0,4},{1,5},{2,6},{3,7},{4,0},{5,1},{6,2},{7,3},{8,12},{9,13},{10,... | collective-permute-start | bytes 3145736 | tf_op jit(solution)/shard_map/ppermute | solution.py:195
  596.4 50.0 %collective-permute-start.28 = (bf16[1024,1024]{1,0:T(8,128)(2,1)}, bf16[1024,1024]{1,0:T(8,128)(2,1)}, u32[]{:S(2)}, u32[]{:S(2)}) collective-permute-start(bf16[1024,1024]{1,0:T(8,128)(2,1)} %slice.573), channel_id=1, source_target_pairs={{0,1},{1,0},{2,3},{3,2},{4,5},{5,4},{6,7},{7,6},{8,9},{9,8},{10,11... | collective-permute-start | bytes 6291464 | tf_op jit(solution)/shard_map/ppermute | solution.py:195
  603.7 14.7 %collective-permute-start.30 = (bf16[512,512]{1,0:T(8,128)(2,1)}, bf16[512,512]{1,0:T(8,128)(2,1)}, u32[]{:S(2)}, u32[]{:S(2)}) collective-permute-start(bf16[512,512]{1,0:T(8,128)(2,1)} %slice.582), channel_id=1, source_target_pairs={{0,2},{1,3},{2,0},{3,1},{4,6},{5,7},{6,4},{7,5},{8,10},{9,11},{10,... | collective-permute-start | bytes 1572872 | tf_op jit(solution)/shard_map/ppermute | solution.py:195
  605.8 14.1 %collective-permute-start.32 = (bf16[512,512]{1,0:T(8,128)(2,1)S(1)}, bf16[512,512]{1,0:T(8,128)(2,1)S(1)}, u32[]{:S(2)}, u32[]{:S(2)}) collective-permute-start(bf16[512,512]{1,0:T(8,128)(2,1)S(1)} %slice.581), channel_id=1, source_target_pairs={{0,4},{1,5},{2,6},{3,7},{4,0},{5,1},{6,2},{7,3},{8,12},{9,13},{10,... | collective-permute-start | bytes 1572872 | tf_op jit(solution)/shard_map/ppermute | solution.py:195
  627.1 16.5 %collective-permute-start.34 = (bf16[256,512]{0,1:T(8,128)(2,1)S(1)}, bf16[256,512]{0,1:T(8,128)(2,1)}, u32[]{:S(2)}, u32[]{:S(2)}) collective-permute-start(bf16[256,512]{0,1:T(8,128)(2,1)S(1)} %bitcast.294), channel_id=1, source_target_pairs={{0,16},{8,24},{16,0},{24,8},{1,17},{9,25},{17,1},{25,9},{2,18},{10... | collective-permute-start | bytes 786440 | tf_op jit(solution)/shard_map/ppermute | solution.py:237
  627.1 16.5 %collective-permute-start.35 = (bf16[256,512]{0,1:T(8,128)(2,1)S(1)}, bf16[256,512]{0,1:T(8,128)(2,1)}, u32[]{:S(2)}, u32[]{:S(2)}) collective-permute-start(bf16[256,512]{0,1:T(8,128)(2,1)S(1)} %bitcast.293), channel_id=1, source_target_pairs={{0,24},{8,0},{16,8},{24,16},{1,25},{9,1},{17,9},{25,17},{2,26},{10... | collective-permute-start | bytes 786440 | tf_op jit(solution)/shard_map/ppermute | solution.py:237
  651.6 21.3 %all-to-all-start.2 = ((f32[32,14,128]{2,1,0:T(8,128)}), f32[32,14,128]{2,1,0:T(8,128)S(1)}, u32[]{:S(2)}, u32[]{:S(2)}) async-start(f32[32,14,128]{2,1,0:T(8,128)} %bitcast.76), calls=%async_computation.2 | async-start | bytes 524288 | tf_op jit(solution)/shard_map/all_to_all | solution.py:266
  (115 other events, 1914.7 us)

commit v2 on v1

--- a/solution.py
+++ b/solution.py
@@ -22,6 +22,7 @@
 BF16 = jnp.bfloat16
 QUERY_ROWS = 512
 VMEM_BYTES = 56 * 1024 * 1024
+SMALL_COST = pl.CostEstimate(flops=1000, bytes_accessed=1000, transcendentals=0)
 
 
 def dot(left, right, dims=NN):
@@ -35,10 +36,10 @@
 def gelu_both(values):
     c = math.sqrt(2.0 / math.pi)
     square = values * values
-    t = jnp.tanh(c * values * (1.0 + 0.044715 * square))
-    half = 0.5 * (1.0 + t)
-    slope = half + 0.5 * values * (1.0 - t * t) * (c * (1.0 + 3.0 * 0.044715 * square))
-    return values * half, slope
+    half = 0.5 + 0.5 * jnp.tanh(values * (c + (c * 0.044715) * square))
+    gelu = values * half
+    slope = half + gelu * (1.0 - half) * (2.0 * c + (6.0 * c * 0.044715) * square)
+    return gelu, slope
 
 
 def normalize(resid):
@@ -63,10 +64,11 @@
     return lane < HD if head == 0 else lane >= HD
 
 
-def attend_kernel(q_ref, k_ref, v_ref, mixed_ref, log_ref):
+def attend_kernel(q_ref, k_ref, v_ref, *refs):
+    mixed_ref, log_ref = refs[-2:]
     queries = q_ref[...] * jnp.asarray(HD**-0.5, BF16)
     key_rows = k_ref[...]
-    value_rows = v_ref[...]
+    values_across = v_ref[...].T
     mask = head_lanes(key_rows.shape, 0)
     zero = jnp.zeros_like(key_rows)
     keys = (jnp.where(mask, key_rows, zero), jnp.where(mask, zero, key_rows))
@@ -80,23 +82,23 @@
             top = jnp.max(scores, 0, keepdims=True)
             expon = jnp.exp(scores - top)
             total = jnp.sum(expon, 0, keepdims=True)
-            out = dot(value_rows, expon.astype(BF16), TN) / total
-            outs.append(out[head * HD : (head + 1) * HD])
+            out = dot(values_across[head * HD : (head + 1) * HD], expon.astype(BF16))
+            outs.append(out / total)
             log_ref[0, 0, head : head + 1, start:stop] = top + jnp.log(total)
         mixed_ref[start:stop, :] = jnp.concatenate(outs, 0).T.astype(BF16)
 
 
-def attend_back_kernel(q_ref, k_ref, v_ref, mixed_ref, grad_ref, log_ref, out_ref):
+def attend_back_kernel(q_ref, k_ref, v_ref, mixed_ref, grad_ref, log_ref, out_ref, sums_ref):
     scale = jnp.asarray(HD**-0.5, BF16)
     queries = q_ref[...] * scale
     key_rows = k_ref[...]
     value_rows = v_ref[...]
     grad_rows = grad_ref[...]
-    mask = head_lanes(key_rows.shape, 0)
-    zero = jnp.zeros_like(key_rows)
+    mask = head_lanes(value_rows.shape, 0)
+    zero = jnp.zeros_like(value_rows)
     keys = (jnp.where(mask, key_rows, zero), jnp.where(mask, zero, key_rows))
     values = (jnp.where(mask, value_rows, zero), jnp.where(mask, zero, value_rows))
-    keys_scaled = key_rows * scale
+    keys_across = (key_rows * scale).T
     product = grad_rows.astype(F32) * mixed_ref[...].astype(F32)
     picks = (
         lax.broadcasted_iota(jnp.int32, (8, PAIR), 0)
@@ -120,59 +122,344 @@
             part_k = dot(grad_scores, q_part)
             grad_v[head] = part_v if grad_v[head] is None else grad_v[head] + part_v
             grad_k[head] = part_k if grad_k[head] is None else grad_k[head] + part_k
-            out = dot(keys_scaled, grad_scores, TN)
-            outs.append(out[head * HD : (head + 1) * HD])
+            outs.append(dot(keys_across[head * HD : (head + 1) * HD], grad_scores))
         out_ref[start:stop, 0:PAIR] = jnp.concatenate(outs, 0).T.astype(BF16)
     out_ref[:, PAIR : 2 * PAIR] = jnp.where(mask, grad_k[0], grad_k[1]).astype(BF16)
     out_ref[:, 2 * PAIR :] = jnp.where(mask, grad_v[0], grad_v[1]).astype(BF16)
-
-
-def attention_specs(latents, pairs):
-    part = lambda offset: pl.BlockSpec((LEN, PAIR), lambda s, p: (s, 3 * p + offset))
-    plain = pl.BlockSpec((LEN, PAIR), lambda s, p: (s, p))
-    logs = pl.BlockSpec((1, 1, 2, LEN), lambda s, p: (s, p, 0, 0))
+    sums_ref[0, 0] = jnp.sum(out_ref[...].astype(F32).reshape(length // 8, 8, 3 * PAIR), 0)
+
+
+def attention_specs(first):
+    part = lambda offset: pl.BlockSpec((LEN, PAIR), lambda s, p: (s, 3 * (p + first) + offset))
+    plain = pl.BlockSpec((LEN, PAIR), lambda s, p: (s, p + first))
+    logs = pl.BlockSpec((1, 1, 2, LEN), lambda s, p: (s, p + first, 0, 0))
     return [part(0), part(1), part(2)], plain, logs
 
 
-def attend(projected, latents, pairs):
-    parts, plain, logs = attention_specs(latents, pairs)
+def attend(projected, latents, pairs, first, count, earlier=()):
+    parts, plain, logs = attention_specs(first)
     rows = projected.shape[0]
     return pl.pallas_call(
         attend_kernel,
-        grid=(latents, pairs),
-        in_specs=parts,
+        grid=(latents, count),
+        in_specs=parts + [pl.BlockSpec(memory_space=pl.ANY)] * len(earlier),
         out_specs=[plain, logs],
         out_shape=[
             jax.ShapeDtypeStruct((rows, pairs * PAIR), BF16),
             jax.ShapeDtypeStruct((latents, pairs, 2, LEN), F32),
         ],
+        input_output_aliases={3 + i: i for i in range(len(earlier))},
         compiler_params=pltpu.CompilerParams(vmem_limit_bytes=VMEM_BYTES),
-        cost_estimate=pl.CostEstimate(
-            flops=latents * pairs * 2 * 2 * 2 * LEN * LEN * PAIR,
-            bytes_accessed=rows * pairs * PAIR * 8,
-            transcendentals=latents * pairs * 2 * LEN * LEN,
-        ),
+        cost_estimate=SMALL_COST,
         name="attend",
-    )(projected, projected, projected)
-
-
-def attend_back(projected, mixed, grad_mixed, log_totals, latents, pairs):
-    parts, plain, logs = attention_specs(latents, pairs)
+    )(projected, projected, projected, *earlier)
+
+
+def attend_back(projected, mixed, grad_mixed, log_totals, latents, first, count):
+    parts, plain, logs = attention_specs(first)
     rows = projected.shape[0]
     return pl.pallas_call(
         attend_back_kernel,
-        grid=(latents, pairs),
+        grid=(latents, count),
         in_specs=[*parts, plain, plain, logs],
-        out_specs=pl.BlockSpec((LEN, 3 * PAIR), lambda s, p: (s, p)),
-        out_shape=jax.ShapeDtypeStruct((rows, pairs * 3 * PAIR), BF16),
+        out_specs=[
+            pl.BlockSpec((LEN, 3 * PAIR), lambda s, p: (s, p)),
+            pl.BlockSpec((1, 1, 8, 3 * PAIR), lambda s, p: (s, p, 0, 0)),
+        ],
+        out_shape=[
+            jax.ShapeDtypeStruct((rows, count * 3 * PAIR), BF16),
+            jax.ShapeDtypeStruct((latents, count, 8, 3 * PAIR), F32),
+        ],
         compiler_params=pltpu.CompilerParams(vmem_limit_bytes=VMEM_BYTES),
-        cost_estimate=pl.CostEstimate(
-            flops=latents * pairs * 2 * 5 * 2 * LEN * LEN * PAIR,
-            bytes_accessed=rows * pairs * PAIR * 16,
-            transcendentals=latents * pairs * 2 * LEN * LEN,
-        ),
+        cost_estimate=SMALL_COST,
         name="attend_back",
     )(projected, projected, projected, mixed, grad_mixed, log_totals)
+
+
+def kernel_call(body, grid, in_specs, out_specs, out_shape, name):
+    return pl.pallas_call(
+        body,
+        grid=grid,
+        in_specs=in_specs,
+        out_specs=out_specs,
+        out_shape=out_shape,
+        compiler_params=pltpu.CompilerParams(vmem_limit_bytes=VMEM_BYTES),
+        cost_estimate=SMALL_COST,
+        name=name,
+    )
+
+
+def whole(array):
+    return pl.BlockSpec(array.shape, lambda *step: (0,) * array.ndim)
+
+
+def row_specs(local_rows, tile, width):
+    count = local_rows // tile
+    mine = pl.BlockSpec((tile, width), lambda i: (jnp.minimum(i, count - 1), 0))
+    theirs = pl.BlockSpec((tile, width), lambda i: (jnp.maximum(i - count, 0), 0))
+    return count, mine, theirs
+
+
+def rows_product(pair, weights, extra, kind):
+    local_rows, depth = pair[0].shape
+    tile = min(512, local_rows)
+    count, mine, theirs = row_specs(local_rows, tile, depth)
+    widths = [w.shape[1] for w in weights]
+    width = sum(widths)
+    total = 2 * local_rows
+
+    def body(*refs):
+        mine_ref, theirs_ref = refs[:2]
+        weight_refs = refs[2 : 2 + len(weights)]
+        extra_ref = refs[2 + len(weights)]
+        out_refs = refs[3 + len(weights) :]
+        step = pl.program_id(0)
+        left = jnp.where(step < count, mine_ref[...], theirs_ref[...])
+        if kind == "slope":
+
+            @pl.when(step == 0)
+            def _():
+                out_refs[1][...] = jnp.zeros(out_refs[1].shape, F32)
+
+        start = 0
+        for ref, span in zip(weight_refs, widths):
+            for low in range(0, span, 256):
+                cols = slice(start + low, start + low + 256)
+                product = dot(left, ref[:, low : low + 256])
+                if kind == "bias":
+                    out_refs[0][:, cols] = (product + extra_ref[:, cols]).astype(BF16)
+                elif kind == "gelu":
+                    act, slope = gelu_both(product + extra_ref[:, cols])
+                    out_refs[0][:, cols] = act.astype(BF16)
+                    out_refs[1][:, cols] = slope.astype(BF16)
+                else:
+                    grad = (product * extra_ref[:, cols].astype(F32)).astype(BF16)
+                    out_refs[0][:, cols] = grad
+                    out_refs[1][:, cols] += jnp.sum(
+                        grad.astype(F32).reshape(tile // 8, 8, 256), 0
+                    )
+            start += span
+
+    rows_out = pl.BlockSpec((tile, width), lambda i: (i, 0))
+    low_shape = jax.ShapeDtypeStruct((total, width), BF16)
+    if kind == "bias":
+        out_specs, out_shape = [rows_out], [low_shape]
+    elif kind == "gelu":
+        out_specs, out_shape = [rows_out, rows_out], [low_shape, low_shape]
+    else:
+        out_specs = [rows_out, pl.BlockSpec((8, width), lambda i: (0, 0))]
+        out_shape = [low_shape, jax.ShapeDtypeStruct((8, width), F32)]
+    extra_spec = rows_out if kind == "slope" else whole(extra)
+    return kernel_call(
+        body,
+        (2 * count,),
+        [mine, theirs, *[whole(w) for w in weights], extra_spec],
+        out_specs,
+        out_shape,
+        "rows_" + kind,
+    )(*pair, *weights, extra)
+
+
+def columns_of(refs, start, stop):
+    for ref in refs:
+        if start < ref.shape[1]:
+            return ref[:, start:stop]
+        start, stop = start - ref.shape[1], stop - ref.shape[1]
+
+
+def rows_total(lefts, weights):
+    local_rows = lefts[0].shape[0] // 2
+    tile = min(512, local_rows)
+    count = local_rows // tile
+    width = weights[0].shape[0]
+    ends = set()
+    for arrays in (lefts, weights):
+        end = 0
+        for array in arrays:
+            end += array.shape[1]
+            ends.add(end)
+    ends = sorted(ends)
+
+    def body(*refs):
+        left_refs = refs[: len(lefts)]
+        weight_refs = refs[len(lefts) : -2]
+        mine_ref, theirs_ref = refs[-2:]
+        total = None
+        for start, stop in zip([0] + ends, ends):
+            part = dot(columns_of(left_refs, start, stop), columns_of(weight_refs, start, stop), NT)
+            total = part if total is None else total + part
+        step = pl.program_id(0)
+
+        @pl.when(step < count)
+        def _():
+            mine_ref[...] = total
+
+        @pl.when(step >= count)
+        def _():
+            theirs_ref[...] = total.astype(BF16)
+
+    return kernel_call(
+        body,
+        (2 * count,),
+        [pl.BlockSpec((tile, a.shape[1]), lambda i: (i, 0)) for a in lefts]
+        + [whole(w) for w in weights],
+        [
+            pl.BlockSpec((tile, width), lambda i: (jnp.minimum(i, count - 1), 0)),
+            pl.BlockSpec((tile, width), lambda i: (jnp.maximum(i - count, 0), 0)),
+        ],
+        [
+            jax.ShapeDtypeStruct((local_rows, width), F32),
+            jax.ShapeDtypeStruct((local_rows, width), BF16),
+        ],
+        "rows_total",
+    )(*lefts, *weights)
+
+
+def token_kernel(body, arrays, rows_of, out_types, sums, name):
+    tokens = arrays[0].shape[0]
+    tile = min(256, tokens)
+    outs = len(out_types)
+
+    def kernel(*refs):
+        values = [ref[...].astype(F32) for ref in refs[: len(arrays)]]
+        rows_ref = refs[len(arrays)]
+        rows = [rows_ref[i : i + 1, :] for i in range(8)]
+        results, columns = body(values, rows)
+        out_refs = refs[len(arrays) + 1 :]
+        for ref, result in zip(out_refs, results):
+            ref[...] = result.astype(ref.dtype)
+        if sums:
+            sum_ref = out_refs[outs]
+
+            @pl.when(pl.program_id(0) == 0)
+            def _():
+                sum_ref[...] = jnp.zeros(sum_ref.shape, F32)
+
+            for i, column in enumerate(columns):
+                sum_ref[i] += jnp.sum(column.reshape(tile // 8, 8, D), 0)
+
+    tokens_spec = pl.BlockSpec((tile, D), lambda i: (i, 0))
+    out_specs = [tokens_spec] * outs
+    out_shape = [jax.ShapeDtypeStruct((tokens, D), t) for t in out_types]
+    if sums:
+        out_specs = out_specs + [pl.BlockSpec((sums, 8, D), lambda i: (0, 0, 0))]
+        out_shape = out_shape + [jax.ShapeDtypeStruct((sums, 8, D), F32)]
+    return kernel_call(
+        kernel,
+        (tokens // tile,),
+        [tokens_spec] * len(arrays) + [whole(rows_of)],
+        out_specs,
+        out_shape,
+        name,
+    )(*arrays, rows_of)
+
+
+def middle_body(values, rows):
+    mine, theirs, tokens = values
+    gate, shift, scale, bias = rows[2], rows[3], rows[4], rows[6]
+    attention_out = mine + theirs + bias
+    normed, _ = normalize(tokens + gate * attention_out)
+    return [attention_out, normed * (1.0 + scale) + shift], []
+
+
+def middle_back_body(values, rows):
+    mine, theirs, upstream, tokens, attention_out = values
+    gate, scale = rows[2], rows[4]
+    grad_hidden = mine + theirs
+    normed, inv_std = normalize(tokens + gate * attention_out)
+    grad = upstream + normalize_back(grad_hidden * (1.0 + scale), normed, inv_std)
+    grad_attention = grad * gate
+    return [grad, grad_attention], [
+        grad_hidden,
+        grad_hidden * normed,
+        grad * attention_out,
+        grad_attention,
+    ]
+
+
+def first_back_body(values, rows):
+    mine, theirs, tokens, grad_resid = values
+    scale = rows[1]
+    grad_hidden = mine + theirs
+    normed, inv_std = normalize(tokens)
+    grad = grad_resid + normalize_back(grad_hidden * (1.0 + scale), normed, inv_std)
+    return [grad], [grad_hidden, grad_hidden * normed]
+
+
+def last_body(values, rows):
+    mine, theirs, tokens, attention_out, upstream = values
+    gate_attn, gate_feed, bias = rows[2], rows[5], rows[7]
+    feed_out = mine + theirs + bias
+    resid_mid = tokens + gate_attn * attention_out
+    return [resid_mid + gate_feed * feed_out], [upstream * feed_out, upstream * gate_feed]
+
+
+def columns_product(pair, right, added, cuts):
+    local_rows, depth = pair[0].shape
+    width = right.shape[1]
+    tile = 256
+    starts = [sum(cuts[:i]) for i in range(len(cuts))]
+    add_width = width // max(1, len(added))
+
+    def body(mine_ref, theirs_ref, right_ref, *refs):
+        add_refs = refs[: len(added)]
+        out_refs = refs[len(added) :]
+        mine, theirs = mine_ref[...].T, theirs_ref[...].T
+        for ref, start, span in zip(out_refs, starts, cuts):
+            total = dot(mine, right_ref[:local_rows, start : start + span])
+            total = total + dot(theirs, right_ref[local_rows:, start : start + span])
+            if added:
+                place = start % add_width
+                total = total + add_refs[start // add_width][:, place : place + span].astype(F32)
+            ref[...] = total.astype(BF16)
+
+    token_spec = pl.BlockSpec((local_rows, tile), lambda i: (0, i))
+    outs = kernel_call(
+        body,
+        (depth // tile,),
+        [token_spec, token_spec, whole(right)]
+        + [pl.BlockSpec((tile, add_width), lambda i: (i, 0)) for _ in added],
+        [pl.BlockSpec((tile, span), lambda i: (i, 0)) for span in cuts],
+        [jax.ShapeDtypeStruct((depth, span), BF16) for span in cuts],
+        "columns_product",
+    )(*pair, right, *added)
+    return outs
+
+
+def assemble(top, low, qkv_width, out_width):
+    parts = [top[0], top[2], low[0], low[2]]
+    ids = [top[1], top[3], low[1], low[3]]
+    half, width = parts[0].shape
+    block = qkv_width + out_width
+    blocks = 2 * width // block
+    tile = 128
+
+    def body(a_ref, b_ref, c_ref, d_ref, qkv_ref, out_ref):
+        for number, ref in enumerate((a_ref, b_ref, c_ref, d_ref)):
+            for place, i in enumerate(ids[number]):
+                start = place * block
+                qkv_ref[number // 2, :, i * qkv_width : (i + 1) * qkv_width] = ref[
+                    :, start : start + qkv_width
+                ]
+                out_ref[number // 2, :, i * out_width : (i + 1) * out_width] = ref[
+                    :, start + qkv_width : start + block
+                ]
+
+    qkv, out = kernel_call(
+        body,
+        (half // tile,),
+        [pl.BlockSpec((tile, width), lambda i: (i, 0))] * 4,
+        [
+            pl.BlockSpec((2, tile, blocks * qkv_width), lambda i: (0, i, 0)),
+            pl.BlockSpec((2, tile, blocks * out_width), lambda i: (0, i, 0)),
+        ],
+        [
+            jax.ShapeDtypeStruct((2, half, blocks * qkv_width), BF16),
+            jax.ShapeDtypeStruct((2, half, blocks * out_width), BF16),
+        ],
+        "assemble",
+    )(*parts)
+    return qkv.reshape(2 * half, -1), out.reshape(2 * half, -1)
 
 
 class Grid:
@@ -239,19 +526,32 @@
             ).astype(F32)
         return total
 
-    def gather_chips(self, block, order):
+    def gather_early(self, block, order, late=()):
         held, ids = block, [0]
-        for number, bit in enumerate(order):
+        for bit in order[:-1]:
             got = self.swap_chip(held, bit)
-            new_ids = [bit ^ i for i in ids]
-            if number == len(order) - 1:
-                return held, ids, got, new_ids
-            held, ids = jnp.concatenate([held, got], 1), ids + new_ids
-
-    def scatter_chips(self, keep, send, order):
-        for number, bit in enumerate(order[::-1]):
-            total = keep + self.swap_chip(send, bit).astype(F32)
-            if number == len(order) - 1:
+            if bit == order[-2]:
+                got = after(got, *late)
+            held = jnp.concatenate([held, got], 1)
+            ids = ids + [bit ^ i for i in ids]
+        return held, ids
+
+    def early_ids(self, order):
+        ids = [0]
+        for bit in order[:-1]:
+            ids = ids + [bit ^ i for i in ids]
+        return ids
+
+    def gather_last(self, held, ids, order):
+        return self.swap_chip(held, order[-1]), [order[-1] ^ i for i in ids]
+
+    def scatter_chips(self, keep, send, order, late=()):
+        for bit in order[-2::-1]:
+            got = self.swap_chip(send, bit)
+            if bit == order[-2]:
+                got = after(got, *late)
+            total = keep.astype(F32) + got.astype(F32)
+            if bit == order[0]:
                 return total
             half = total.shape[1] // 2
             keep, send = total[:, :half], total[:, half:].astype(BF16)
@@ -355,42 +655,52 @@
         .reshape(6, 1, D)
     )
     shift_attn, scale_attn, gate_attn, shift_feed, scale_feed, gate_feed = modulation
+    token_rows = jnp.concatenate([modulation.reshape(6, D), out_bias_all, fc2_bias_all], 0)
 
     attn_rows, mark = grid.gather_rows(attn_local)
-    fc1_rows, mark = grid.gather_rows(after(fc1_local, mark))
-    fc2_rows, mark = grid.gather_rows(after(fc2_local, mark))
+    fc1_rows = lax.all_gather(after(fc1_local, mark), "row", axis=0, tiled=True)
+    fc2_rows = lax.all_gather(after(fc2_local, fc1_rows), "row", axis=0, tiled=True)
     half = D // 2
-    top = grid.gather_chips(attn_rows[:half], grid.orders[0])
-    low = grid.gather_chips(attn_rows[half:], grid.orders[1])
-    attn_top = {**split_columns(top[0], top[1]), **split_columns(top[2], top[3])}
-    attn_low = {**split_columns(low[0], low[1]), **split_columns(low[2], low[3])}
-    attn_blocks = [jnp.concatenate([attn_top[i], attn_low[i]], 0) for i in range(chips)]
+    top = grid.gather_early(attn_rows[:half], grid.orders[0])
+    low = grid.gather_early(attn_rows[half:], grid.orders[1])
+    top = top + grid.gather_last(*top, grid.orders[0])
+    low = low + grid.gather_last(*low, grid.orders[1])
     if local_heads % 2 == 0:
-        qkv_w = jnp.concatenate([b[:, :qkv_width] for b in attn_blocks], 1)
+        qkv_w, out_w = assemble(top, low, qkv_width, out_width)
     else:
+        attn_top = {**split_columns(top[0], top[1]), **split_columns(top[2], top[3])}
+        attn_low = {**split_columns(low[0], low[1]), **split_columns(low[2], low[3])}
+        attn_blocks = [jnp.concatenate([attn_top[i], attn_low[i]], 0) for i in range(chips)]
         qkv_w = (
             jnp.stack([b[:, :qkv_width] for b in attn_blocks], 1)
             .reshape(D, pairs, 2, 3, HD)
             .transpose(0, 1, 3, 2, 4)
             .reshape(D, pairs * 3 * PAIR)
         )
-    out_w = jnp.concatenate([b[:, qkv_width:] for b in attn_blocks], 1)
-
-    def gather_units(rows_held, earlier):
+        out_w = jnp.concatenate([b[:, qkv_width:] for b in attn_blocks], 1)
+
+    middle = local_units // 2
+
+    def units_early(rows_held, earlier, late):
         rows_held = after(rows_held, *earlier)
-        middle = local_units // 2
-        first = grid.gather_chips(rows_held[:, :middle], grid.orders[0])
-        second = grid.gather_chips(rows_held[:, middle:], grid.orders[1])
-        groups = [first[0], first[2], second[0], second[2]]
-        ids = [(0, first[1]), (0, first[3]), (1, second[1]), (1, second[3])]
-        return groups, ids
-
-    fc1_groups, unit_ids = gather_units(fc1_rows, (top[2], low[2]))
-    fc2_groups, unit_ids = gather_units(fc2_rows, (fc1_groups[1], fc1_groups[3]))
-
+        parts = (rows_held[:, :middle], rows_held[:, middle:])
+        held = [grid.gather_early(p, order, late) for p, order in zip(parts, grid.orders)]
+        return [h[0] for h in held], [h[1] for h in held]
+
+    def units_last(held, ids, *earlier):
+        got = [
+            grid.gather_last(after(h, *earlier), i, order)
+            for h, i, order in zip(held, ids, grid.orders)
+        ]
+        return [g[0] for g in got], [g[1] for g in got]
+
+    ids_a = [grid.early_ids(order) for order in grid.orders]
     fc1_bias_rel = grid.to_relative(fc1_bias_all).reshape(chips, 2, local_units // 2)
+    ids_b = [[order[-1] ^ i for i in ids] for ids, order in zip(ids_a, grid.orders)]
+    unit_ids = (ids_a, ids_b)
     fc1_bias_groups = [
-        jnp.concatenate([fc1_bias_rel[i, part] for i in ids]) for part, ids in unit_ids
+        jnp.concatenate([fc1_bias_rel[i, part] for part in range(2) for i in ids[part]])[None]
+        for ids in unit_ids
     ]
     qv_rel = grid.to_relative(qv_bias_all).reshape(pairs, 2, 2, HD).transpose(0, 2, 1, 3)
     qkv_bias_rel = jnp.concatenate(
@@ -398,89 +708,147 @@
     ).reshape(1, pairs * 3 * PAIR)
 
     def both(mine):
-        return jnp.concatenate([mine, grid.swap_core(mine)], 0)
-
-    def own_total(partial):
-        theirs = partial[local_rows:].astype(BF16)
-        return partial[:local_rows] + grid.swap_core(theirs).astype(F32)
+        return (mine, grid.swap_core(mine))
+
+    def own_total(lefts, weights):
+        mine, theirs = rows_total(lefts, weights)
+        return mine, grid.swap_core(theirs)
+
+    def send_units(left, right):
+        width = right.shape[1]
+        sent = columns_product(left, right, [], [width // 2] * 2)
+        got = [grid.swap_chip(a, order[-1]) for a, order in zip(sent, grid.orders)]
+        return got, sent[0]
+
+    def sum_chips(kept, late):
+        sums = [
+            grid.scatter_chips(kept[2 * n], kept[2 * n + 1], order, late)
+            for n, order in enumerate(grid.orders)
+        ]
+        return jnp.concatenate(sums, 1).astype(BF16)
+
+    def sum_rows(parts):
+        return lax.psum_scatter(parts, "row", scatter_dimension=0, tiled=True)
 
     resid = tokens.astype(F32)
-    normed_attn, inv_attn = normalize(resid)
+    normed_attn, _ = normalize(resid)
     hidden_attn = both((normed_attn * (1.0 + scale_attn) + shift_attn).astype(BF16))
-    upstream = cotangent.astype(F32)
-    grad_feed = upstream * gate_feed
-    bias_fc2 = jnp.sum(grad_feed, 0)
-    grad_feed_low = both(grad_feed.astype(BF16))
-
-    projected = (dot(hidden_attn, qkv_w) + qkv_bias_rel).astype(BF16)
-    mixed, log_totals = attend(projected, latents, pairs)
-    attention_out = own_total(dot(mixed, out_w, NT)) + out_bias_all
-    resid_mid = resid + gate_attn * attention_out
-    normed_feed, inv_feed = normalize(resid_mid)
-    hidden_feed = both((normed_feed * (1.0 + scale_feed) + shift_feed).astype(BF16))
-    acts, slopes = [], []
-    for weight, bias in zip(fc1_groups, fc1_bias_groups):
-        act, slope = gelu_both(dot(hidden_feed, weight) + bias)
-        acts.append(act.astype(BF16))
-        slopes.append(slope.astype(BF16))
-
-    def scatter_units(left, rights):
-        sums = []
-        for number, order in enumerate(grid.orders):
-            send = dot(left, rights[2 * number + 1], TN).astype(BF16)
-            keep = dot(left, rights[2 * number], TN)
-            sums.append(grid.scatter_chips(keep, send, order))
-        return grid.scatter_rows(jnp.concatenate(sums, 1).astype(BF16))
-
-    fc2_part = scatter_units(grad_feed_low, acts).T
-    grad_pres = [
-        (dot(grad_feed_low, weight) * slope.astype(F32)).astype(BF16)
-        for weight, slope in zip(fc2_groups, slopes)
-    ]
-    bias_fc1 = [jnp.sum(g.astype(F32), 0) for g in grad_pres]
-    fc1_part = scatter_units(hidden_feed, grad_pres)
-    grad_hidden_feed = own_total(
-        sum(dot(g, weight, NT) for g, weight in zip(grad_pres, fc1_groups))
-    )
-    feed_out = (
-        own_total(sum(dot(a, weight, NT) for a, weight in zip(acts, fc2_groups))) + fc2_bias_all
-    )
-    layer_out = (resid_mid + gate_feed * feed_out).astype(BF16)
-
-    grad_resid_mid = upstream + normalize_back(
-        grad_hidden_feed * (1.0 + scale_feed), normed_feed, inv_feed
-    )
-    grad_attention = grad_resid_mid * gate_attn
-    bias_out = jnp.sum(grad_attention, 0)
-    grad_attention_low = both(grad_attention.astype(BF16))
-
-    grad_mixed = dot(grad_attention_low, out_w).astype(BF16)
-    grad_out = dot(grad_attention_low, mixed, TN)
-    grad_projected = attend_back(projected, mixed, grad_mixed, log_totals, latents, pairs)
-    bias_qkv = jnp.sum(grad_projected.astype(F32), 0)
-    grad_qkv = dot(hidden_attn, grad_projected, TN)
+    grad_feed_low = both((cotangent.astype(F32) * gate_feed).astype(BF16))
+
+    (projected,) = rows_product(hidden_attn, [qkv_w], qkv_bias_rel, "bias")
+    fc1_a, _ = units_early(fc1_rows, (top[2], low[2]), (projected,))
+    fc1_b, _ = units_last(fc1_a, ids_a)
+    projected = after(projected, *fc1_a)
+    middle_pair = pairs // 2
+    first_half = attend(projected, latents, pairs, 0, middle_pair)
+    fc2_a, _ = units_early(fc2_rows, (first_half[0], *fc1_b), ())
+    mixed, log_totals = attend(
+        after(projected, first_half[0], *fc1_b),
+        latents,
+        pairs,
+        middle_pair,
+        pairs - middle_pair,
+        first_half,
+    )
+    fc2_b, _ = units_last(fc2_a, ids_a, mixed)
+    mixed = after(mixed, *fc2_a)
+    totals = own_total([mixed], [out_w])
+    attention_out, hidden_feed = token_kernel(
+        middle_body, [*totals, tokens], token_rows, [F32, BF16], 0, "middle"
+    )
+    hidden_feed = both(hidden_feed)
+    act_a, slope_a = rows_product(hidden_feed, fc1_a, fc1_bias_groups[0], "gelu")
+    act_b, slope_b = rows_product(
+        (after(hidden_feed[0], act_a), hidden_feed[1]), fc1_b, fc1_bias_groups[1], "gelu"
+    )
+    act_b = after(act_b, *fc2_b)
+
+    fc2_got, _ = send_units(grad_feed_low, act_b)
+    grad_a, bias_a = rows_product(
+        (after(grad_feed_low[0], act_b), grad_feed_low[1]), fc2_a, slope_a, "slope"
+    )
+    grad_b, bias_b = rows_product(
+        (after(grad_feed_low[0], grad_a), grad_feed_low[1]), fc2_b, slope_b, "slope"
+    )
+    bias_fc1 = [bias_a, bias_b]
+    grad_b = after(grad_b, *fc2_got)
+    totals = own_total([grad_a, grad_b], fc1_a + fc1_b)
+    fc1_got, sent = send_units(hidden_feed, after(grad_b, totals[0]))
+    grad_resid_mid, grad_attention_low, middle_sums = token_kernel(
+        middle_back_body,
+        [after(totals[0], sent), totals[1], cotangent, tokens, attention_out],
+        token_rows,
+        [F32, BF16],
+        4,
+        "middle_back",
+    )
+    grad_attention_low = both(grad_attention_low)
+    fc2_kept = columns_product(
+        grad_feed_low, after(act_a, grad_attention_low[0]), fc2_got, [act_a.shape[1] // 4] * 4
+    )
+
+    (grad_mixed,) = rows_product(
+        grad_attention_low, [out_w], jnp.zeros((1, out_w.shape[1]), F32), "bias"
+    )
+    fc1_kept = columns_product(
+        hidden_feed, after(grad_a, grad_mixed), fc1_got, [grad_a.shape[1] // 4] * 4
+    )
+    (grad_out,) = columns_product(
+        grad_attention_low, after(mixed, grad_mixed), [], [mixed.shape[1]]
+    )
+    grad_mixed = after(grad_mixed, grad_out, fc1_kept[0])
+    grad_late, bias_late = attend_back(
+        projected, mixed, grad_mixed, log_totals, latents, 1, pairs - 1
+    )
+    fc2_sums = sum_chips(fc2_kept, (grad_late,))
+    fc1_sums = sum_chips(fc1_kept, (grad_late,))
+    late_chips = chips * (pairs - 1) // pairs
+    qkv_late = columns_product(hidden_attn, grad_late, [], [qkv_width] * late_chips) if (
+        local_heads % 2 == 0
+    ) else None
+    early_input = after(grad_mixed, grad_late, fc2_sums, fc1_sums)
+    grad_early, bias_early = attend_back(
+        projected, mixed, early_input, log_totals, latents, 0, 1
+    )
+    fc2_part = sum_rows(fc2_sums)
+    fc1_part = sum_rows(fc1_sums)
+    bias_qkv = jnp.concatenate([bias_early, bias_late], 1).sum((0, 2))
     if local_heads % 2 == 0:
-        grad_qkv = grad_qkv.reshape(D, chips, qkv_width)
+        qkv_early = columns_product(hidden_attn, grad_early, [], [qkv_width])
+        grad_qkv = [*qkv_early, *qkv_late]
     else:
+        grad_projected = jnp.concatenate([grad_early, grad_late], 1)
+        (grad_qkv,) = columns_product(hidden_attn, grad_projected, [], [3 * PAIR * pairs])
         grad_qkv = (
             grad_qkv.reshape(D, pairs, 3, 2, HD).transpose(0, 1, 3, 2, 4).reshape(D, chips, qkv_width)
         )
-    grad_out = grad_out.reshape(D, chips, out_width)
+        grad_qkv = [grad_qkv[:, i] for i in range(chips)]
 
     def pick(part, ids):
         lines = slice(0, half) if part == 0 else slice(half, D)
         return jnp.concatenate(
-            [jnp.concatenate([grad_qkv[lines, i], grad_out[lines, i]], 1) for i in ids], 1
+            [
+                array
+                for i in ids
+                for array in (
+                    grad_qkv[i][lines],
+                    grad_out[lines, i * out_width : (i + 1) * out_width],
+                )
+            ],
+            1,
         )
 
+    attn_got = [
+        grid.swap_chip(pick(number, gathered[3]), grid.orders[number][-1])
+        for number, gathered in enumerate((top, low))
+    ]
     attn_sums = []
     for number, gathered in enumerate((top, low)):
+        order = grid.orders[number]
+        kept = pick(number, gathered[1]).astype(F32) + attn_got[number].astype(F32)
+        middle = kept.shape[1] // 2
         attn_sums.append(
-            grid.scatter_chips(
-                pick(number, gathered[1]),
-                pick(number, gathered[3]).astype(BF16),
-                grid.orders[number],
-            )
+            grid.scatter_chips(kept[:, :middle], kept[:, middle:].astype(BF16), order)
         )
     attn_part = grid.scatter_rows(jnp.concatenate(attn_sums, 0).astype(BF16))
     qkv_part = attn_part[:, :qkv_width]
@@ -489,27 +857,28 @@
     qkv_part = qkv_part.reshape(row_width, local_heads, 3 * HD)
     out_part = attn_part[:, qkv_width:].T.reshape(local_heads, HD, row_width)
 
-    grad_hidden_attn = own_total(dot(grad_projected, qkv_w, NT))
-    tokens_grad = grad_resid_mid + normalize_back(
-        grad_hidden_attn * (1.0 + scale_attn), normed_attn, inv_attn
-    )
-
-    mod_rows = jnp.stack(
-        [
-            jnp.sum(grad_hidden_attn, 0),
-            jnp.sum(grad_hidden_attn * normed_attn, 0),
-            jnp.sum(grad_resid_mid * attention_out, 0),
-            jnp.sum(grad_hidden_feed, 0),
-            jnp.sum(grad_hidden_feed * normed_feed, 0),
-            jnp.sum(upstream * feed_out, 0),
-            bias_out,
-            bias_fc2,
-        ]
+    totals = own_total([after(grad_early, *attn_got), grad_late], [qkv_w])
+    tokens_grad, first_sums = token_kernel(
+        first_back_body, [*totals, tokens, grad_resid_mid], token_rows, [F32], 2, "first_back"
+    )
+    totals = own_total([after(act_a, totals[0], fc2_part, *attn_sums), act_b], fc2_a + fc2_b)
+    layer_out, last_sums = token_kernel(
+        last_body, [after(totals[0], fc1_part), totals[1], tokens, attention_out, cotangent], token_rows, [BF16], 2, "last"
+    )
+
+    first_sums, middle_sums, last_sums = (
+        sums.sum(1) for sums in (first_sums, middle_sums, last_sums)
+    )
+    mod_rows = jnp.concatenate(
+        [first_sums, middle_sums[2:3], middle_sums[:2], last_sums[:1], middle_sums[3:], last_sums[1:]]
     )
     mod_rows = mod_rows.reshape(8, cols, col_width).transpose(1, 0, 2)
-    fc1_split = [split_columns(b[None], ids) for b, (_, ids) in zip(bias_fc1, unit_ids)]
-    first_half = {**fc1_split[0], **fc1_split[1]}
-    second_half = {**fc1_split[2], **fc1_split[3]}
+    bias_fc1 = [b.sum(0, keepdims=True) for b in bias_fc1]
+    first_half, second_half = {}, {}
+    for sums, ids in zip(bias_fc1, unit_ids):
+        middle = sums.shape[1] // 2
+        first_half.update(split_columns(sums[:, :middle], ids[0]))
+        second_half.update(split_columns(sums[:, middle:], ids[1]))
     fc1_rel = jnp.concatenate(
         [jnp.concatenate([first_half[i], second_half[i]], 1) for i in range(chips)], 0
     )
@@ -563,9 +932,9 @@
         qv_bias_grad,
         out_part,
         out_bias_grad,
-        fc1_part,
+        fc1_part.astype(F32),
         fc1_bias_grad,
-        fc2_part,
+        fc2_part.astype(F32).T,
         fc2_bias_grad,
     )
 

time: 692 us -> 510 us (0.74)
  Pallas kernels: 77.5 us -> 291 us
  matrix products: 207 us -> 4.14 us
  waiting for transfers between devices: 199 us -> 66.3 us
  other arithmetic: 67.1 us -> 35 us
  local copies, waits for them, and re-layouts: 60.9 us -> 37.8 us
  starting transfers between devices: 73.3 us -> 53.9 us
  between operations: 2.79 us -> 15.2 us
    pallas_call x2 -> x26, Pallas kernels: 77.5 us -> 291 us  [the longest x6 60.8 us: rows_product(): kernel_call(body, (2 * count,), [mine, theirs, *[whole(w) for w in weight...]
    dot_general x31 -> x1, matrix products: 202 us -> 0.24 us  [dot(): return lax.dot_general(left, right, dims, preferred_element_type=F32)]
    ppermute x32, waiting for transfers between devices: 94.1 us -> 40.7 us  [swap(): return lax.ppermute(array, 'col', pairs)]
    ppermute x9 -> x3, waiting for transfers between devices: 48.2 us -> 0.01 us  [scatter_rows(): lax.ppermute(sent, 'row', [(i, (i + step) % count) for i in range(count)])]
    ppermute x9 -> x3, waiting for transfers between devices: 44.5 us -> 0.01 us  [gather_rows(): lax.ppermute(block, 'row', [(i, (i + step) % count) for i in range(count)])]
    reduce_sum x4 -> x6, other arithmetic: 16.9 us -> 1.84 us  [the longest x3 1.78 us: per_device(): sums.sum(1)]
    ppermute x9 -> x3, starting transfers between devices: 20.4 us -> 6.11 us  [gather_rows(): lax.ppermute(block, 'row', [(i, (i + step) % count) for i in range(count)])]
    reshape x5 -> x1, local copies, waits for them, and re-layouts: 14 us -> 0.68 us  [per_device(): qkv_bias_rel = jnp.concatenate([qv_rel[:, :1], jnp.zeros_like(qv_rel[:, :...]
  transfers between devices with their start and end apart: 54 -> 46, of which waited for: 25 -> 12; matrix products, arithmetic and copies ran while one was open for 39% -> 12% of each run, Pallas kernels for 0% -> 48%
where the time goes in v2:
time: 510 us; the launch traced here: 503 us
  Pallas kernels  291 us (57%)
  waiting for transfers between devices  66.3 us (13%)
  starting transfers between devices  53.9 us (11%)
  local copies, waits for them, and re-layouts  37.8 us (7%)
  other arithmetic  35 us (7%)
  between operations  15.2 us (3%)
    pallas_call x6, Pallas kernels, rows_product(): kernel_call(body, (2 * count,), [mine, theirs, *[whole(w) for w in weight...  60.8 us
    pallas_call x7, Pallas kernels, columns_product(): kernel_call(body, (depth // tile,), [token_spec, token_spec, whole(right)...  58.7 us
    pallas_call x2, Pallas kernels, attend_back(): pl.pallas_call(attend_back_kernel, grid=(latents, count), in_specs=[*part...  52.3 us
    pallas_call x4, Pallas kernels, rows_total(): kernel_call(body, (2 * count,), [pl.BlockSpec((tile, a.shape[1]), lambda...  49.6 us
    ppermute x32, waiting for transfers between devices, swap(): return lax.ppermute(array, 'col', pairs)  40.7 us
    pallas_call x4, Pallas kernels, token_kernel(): kernel_call(kernel, (tokens // tile,), [tokens_spec] * len(arrays) + [who...  32.6 us
    pallas_call x2, Pallas kernels, attend(): pl.pallas_call(attend_kernel, grid=(latents, count), in_specs=parts + [pl...  32.4 us
    ppermute x32, starting transfers between devices, swap(): return lax.ppermute(array, 'col', pairs)  27.5 us
  transfers between devices with their start and end apart: 46, of which 12 were waited for; matrix products, arithmetic and copies ran while one was open for 12% of the time, Pallas kernels for 48%

profile of v2, /device:TPU:0, one launch (start us, length us, event | category | flops | bytes accessed | tf_op | source)
XLA Modules:
  0.0 503.4 jit_solution(14069907276999824725)
XLA Ops:
  9.1 5.1 %collective-permute-start.3 = (bf16[256,512]{0,1:T(8,128)(2,1)S(1)}, bf16[256,512]{0,1:T(8,128)(2,1)S(1)}, u32[]{:S(2)}, u32[]{:S(2)}) collective-permute-start(bf16[256,512]{0,1:T(8,128)(2,1)S(1)} %get-tuple-element.271), channel_id=1, source_target_pairs={{0,24},{8,0},{16,8},{24,16},{1,25},{9,1},{17,9},{25,17},{2,26},{10... | collective-permute-start | bytes 786440 | tf_op jit(solution)/shard_map/ppermute | solution.py:509
  19.9 5.6 %all-to-all-start = ((bf16[32,16,128]{2,1,0:T(8,128)(2,1)}), bf16[32,16,128]{2,1,0:T(8,128)(2,1)S(1)}, u32[]{:S(2)}, u32[]{:S(2)}) async-start(bf16[32,16,128]{2,1,0:T(8,128)(2,1)} %broadcast_in_dim.44), calls=%async_computation | async-start | bytes 262144 | tf_op jit(solution)/shard_map/all_to_all | solution.py:566
  25.5 2.3 convert_reduce_fusion
  28.1 12.8 %all-to-all-done = bf16[32,16,128]{2,1,0:T(8,128)(2,1)S(1)} async-done(((bf16[32,16,128]{2,1,0:T(8,128)(2,1)}), bf16[32,16,128]{2,1,0:T(8,128)(2,1)S(1)}, u32[]{:S(2)}, u32[]{:S(2)}) %all-to-all-start) | async-done | bytes 131104 | tf_op jit(solution)/shard_map/all_to_all | solution.py:566
  42.1 3.2 all-to-all-start.1
  51.3 2.4 all-to-all-done.1
  53.7 2.1 fusion.3.refs_0_.mine_ref
  56.1 6.1 %collective-permute-done.6 = bf16[512,512]{1,0:T(8,128)(2,1)} collective-permute-done((bf16[512,512]{1,0:T(8,128)(2,1)}, bf16[512,512]{1,0:T(8,128)(2,1)}, u32[]{:S(2)}, u32[]{:S(2)}) %collective-permute-start.6) | collective-permute-done | bytes 524320 | tf_op jit(solution)/shard_map/ppermute | solution.py:482
  64.8 2.1 pad_maximum_fusion.1.a_ref
  70.8 17.4 %collective-permute-done.7.d_ref = bf16[512,1024]{1,0:T(8,128)(2,1)} collective-permute-done((bf16[512,1024]{1,0:T(8,128)(2,1)S(1)}, bf16[512,1024]{1,0:T(8,128)(2,1)}, u32[]{:S(2)}, u32[]{:S(2)}) %collective-permute-start.7) | collective-permute-done | bytes 1048608 | tf_op jit(solution)/shard_map/ppermute | solution.py:482
  88.3 3.3 collective-permute-done.5.b_ref
  91.6 2.2 fusion.49
  97.5 4.8 assemble.1
  103.6 11.0 %rows_bias.2.q_ref.k_ref.v_ref = bf16[2048,1536]{1,0:T(8,128)(2,1)} custom-call(bf16[1024,1024]{1,0:T(8,128)(2,1)} %fusion.3.refs_0_.mine_ref, bf16[1024,1024]{1,0:T(8,128)(2,1)} %copy-done.3, bf16[1024,1536]{1,0:T(8,128)(2,1)} %bitcast.129, f32[1,1536]{1,0:T(1,128)} %reshape.209.refs_3_), custom_call_target="tpu_custom_call" | custom-call | flops 1000 | bytes 1000 | tf_op jit(solution)/shard_map/rows_bias/pallas_call | solution.py:253
  119.5 16.2 %attend.2 = (bf16[2048,512]{1,0:T(8,128)(2,1)}, f32[2,4,2,1024]{3,2,1,0:T(2,128)}) custom-call(bf16[2048,1536]{1,0:T(8,128)(2,1)} %rows_bias.2.q_ref.k_ref.v_ref, bf16[2048,1536]{1,0:T(8,128)(2,1)} %rows_bias.2.q_ref.k_ref.v_ref, bf16[2048,1536]{1,0:T(8,128)(2,1)} %rows_bias.2.q_ref.k_ref.v_ref), custom_call_target="tpu_custom_call" | custom-call | flops 1000 | bytes 1000 | tf_op jit(solution)/shard_map/attend/pallas_call | solution.py:142
  135.7 3.3 collective-permute-done.11.refs_3_.refs_5_
  139.0 2.4 collective-permute-done.10.refs_2_.refs_4_
  144.3 16.2 %attend.3 = (bf16[2048,512]{1,0:T(8,128)(2,1)}, f32[2,4,2,1024]{3,2,1,0:T(2,128)}) custom-call(bf16[2048,1536]{1,0:T(8,128)(2,1)} %rows_bias.2.q_ref.k_ref.v_ref, bf16[2048,1536]{1,0:T(8,128)(2,1)} %rows_bias.2.q_ref.k_ref.v_ref, bf16[2048,1536]{1,0:T(8,128)(2,1)} %rows_bias.2.q_ref.k_ref.v_ref, ...), custom_call_target="tpu_custom_call", output_to_operand_aliasing={{0}: (3, {}), {1}: (4, {})} | custom-call | flops 1000 | bytes 1000 | tf_op jit(solution)/shard_map/attend/pallas_call | solution.py:142
  161.7 7.1 %rows_total.4 = (f32[1024,1024]{1,0:T(8,128)}, bf16[1024,1024]{1,0:T(8,128)(2,1)}) custom-call(bf16[2048,512]{1,0:T(8,128)(2,1)} %get-tuple-element.132.refs_0_.right_ref.mixed_ref, bf16[1024,512]{1,0:T(8,128)(2,1)} %bitcast.132), custom_call_target="tpu_custom_call" | custom-call | flops 1000 | bytes 1000 | tf_op jit(solution)/shard_map/rows_total/pallas_call | solution.py:301
  169.5 3.7 collective-permute-done.14.refs_1_
  174.6 6.6 %middle.1 = (f32[1024,1024]{1,0:T(8,128)}, bf16[1024,1024]{1,0:T(8,128)(2,1)}) custom-call(f32[1024,1024]{1,0:T(8,128)} %get-tuple-element.107.refs_0_, bf16[1024,1024]{1,0:T(8,128)(2,1)} %copy-done.20, bf16[1024,1024]{1,0:T(8,128)(2,1)} %refs_2_.7, f32[8,1024]{1,0:T(8,128)} %pad_maximum_fusion.16.refs_3_.refs_5_.refs_4_), custom_call_target="tpu_custom_call" | custom-call | flops 1000 | bytes 1000 | tf_op jit(solution)/shard_map/middle/pallas_call | solution.py:347
  186.3 12.1 %rows_gelu.2 = (bf16[2048,1024]{1,0:T(8,128)(2,1)}, bf16[2048,1024]{1,0:T(8,128)(2,1)}) custom-call(bf16[1024,1024]{1,0:T(8,128)(2,1)} %get-tuple-element.111.refs_0_.mine_ref, bf16[1024,1024]{1,0:T(8,128)(2,1)} %collective-permute-done.15.refs_1_.theirs_ref, bf16[1024,512]{1,0:T(8,128)(2,1)} %copy-done.6, bf16[1024,512]{1,0:T(8,128)(2,1)} %copy-done.5, ...), custom_call_target="tpu_custom_call" | custom-call | flops 1000 | bytes 1000 | tf_op jit(solution)/shard_map/rows_gelu/pallas_call | solution.py:253
  198.4 11.9 %rows_gelu.3 = (bf16[2048,1024]{1,0:T(8,128)(2,1)}, bf16[2048,1024]{1,0:T(8,128)(2,1)}) custom-call(bf16[1024,1024]{1,0:T(8,128)(2,1)} %get-tuple-element.111.refs_0_.mine_ref, bf16[1024,1024]{1,0:T(8,128)(2,1)} %collective-permute-done.15.refs_1_.theirs_ref, bf16[1024,512]{1,0:T(8,128)(2,1)} %collective-permute-done.10.refs_2_.refs_4_, ...), custom_call_target="tpu_custom_call" | custom-call | flops 1000 | bytes 1000 | tf_op jit(solution)/shard_map/rows_gelu/pallas_call | solution.py:253
  210.3 8.5 %columns_product.7 = (bf16[1024,512]{1,0:T(8,128)(2,1)}, bf16[1024,512]{1,0:T(8,128)(2,1)}) custom-call(bf16[1024,1024]{1,0:T(8,128)(2,1)} %copy-done.1, bf16[1024,1024]{1,0:T(8,128)(2,1)} %collective-permute-done.18.refs_1_.theirs_ref, bf16[2048,1024]{1,0:T(8,128)(2,1)} %get-tuple-element.115.right_ref.refs_1_), custom_call_target="tpu_custom_call" | custom-call | flops 1000 | bytes 1000 | tf_op jit(solution)/shard_map/columns_product/pallas_call | solution.py:417
  220.7 9.7 %rows_slope.2 = (bf16[2048,1024]{1,0:T(8,128)(2,1)}, f32[8,1024]{1,0:T(8,128)}) custom-call(bf16[1024,1024]{1,0:T(8,128)(2,1)} %copy-done.1, bf16[1024,1024]{1,0:T(8,128)(2,1)} %collective-permute-done.18.refs_1_.theirs_ref, bf16[1024,512]{1,0:T(8,128)(2,1)} %pad_maximum_fusion.5.refs_2_, bf16[1024,512]{1,0:T(8,128)(2,1)} %copy-done.4, ...), custom_call_target="tpu_custom_call" | custom-call | flops 1000 | bytes 1000 | tf_op jit(solution)/shard_map/rows_slope/pallas_call | solution.py:253
  230.4 9.8 %rows_slope.3 = (bf16[2048,1024]{1,0:T(8,128)(2,1)}, f32[8,1024]{1,0:T(8,128)}) custom-call(bf16[1024,1024]{1,0:T(8,128)(2,1)} %copy-done.1, bf16[1024,1024]{1,0:T(8,128)(2,1)} %collective-permute-done.18.refs_1_.theirs_ref, bf16[1024,512]{1,0:T(8,128)(2,1)} %collective-permute-done.16.refs_2_.refs_4_, ...), custom_call_target="tpu_custom_call" | custom-call | flops 1000 | bytes 1000 | tf_op jit(solution)/shard_map/rows_slope/pallas_call | solution.py:253
  240.2 3.4 collective-permute-done.19.refs_0_
  244.6 14.9 %rows_total.5 = (f32[1024,1024]{1,0:T(8,128)}, bf16[1024,1024]{1,0:T(8,128)(2,1)}) custom-call(bf16[2048,1024]{1,0:T(8,128)(2,1)} %get-tuple-element.133.refs_0_.right_ref, bf16[2048,1024]{1,0:T(8,128)(2,1)} %get-tuple-element.126.refs_1_.right_ref, bf16[1024,512]{1,0:T(8,128)(2,1)} %copy-done.6, bf16[1024,512]{1,0:T(8,128)(2,1)} %copy-done.5, ...), custom_call_target="tpu_custom_call" | custom-call | flops 1000 | bytes 1000 | tf_op jit(solution)/shard_map/rows_total/pallas_call | solution.py:301
  259.6 8.5 %columns_product.8 = (bf16[1024,512]{1,0:T(8,128)(2,1)}, bf16[1024,512]{1,0:T(8,128)(2,1)}) custom-call(bf16[1024,1024]{1,0:T(8,128)(2,1)} %get-tuple-element.111.refs_0_.mine_ref, bf16[1024,1024]{1,0:T(8,128)(2,1)} %collective-permute-done.15.refs_1_.theirs_ref, bf16[2048,1024]{1,0:T(8,128)(2,1)} %get-tuple-element.126.refs_1_.right_ref), custom_call_target="tpu_custom_call" | custom-call | flops 1000 | bytes 1000 | tf_op jit(solution)/shard_map/columns_product/pallas_call | solution.py:417
  269.4 9.9 %middle_back.1 = (f32[1024,1024]{1,0:T(8,128)}, bf16[1024,1024]{1,0:T(8,128)(2,1)}, f32[4,8,1024]{2,1,0:T(8,128)}) custom-call(f32[1024,1024]{1,0:T(8,128)} %get-tuple-element.128.refs_0_, bf16[1024,1024]{1,0:T(8,128)(2,1)} %copy-done.19, bf16[1024,1024]{1,0:T(8,128)(2,1)} %refs_4_.1, bf16[1024,1024]{1,0:T(8,128)(2,1)} %refs_2_.7, ...), custom_call_target="tpu_custom_call" | custom-call | flops 1000 | bytes 1000 | tf_op jit(solution)/shard_map/middle_back/pallas_call | solution.py:347
  281.6 9.3 %columns_product.11 = (bf16[1024,256]{1,0:T(8,128)(2,1)}, bf16[1024,256]{1,0:T(8,128)(2,1)}, bf16[1024,256]{1,0:T(8,128)(2,1)}, bf16[1024,256]{1,0:T(8,128)(2,1)}) custom-call(bf16[1024,1024]{1,0:T(8,128)(2,1)} %copy-done.1, bf16[1024,1024]{1,0:T(8,128)(2,1)} %collective-permute-done.18.refs_1_.theirs_ref, ...), custom_call_target="tpu_custom_call" | custom-call | flops 1000 | bytes 1000 | tf_op jit(solution)/shard_map/columns_product/pallas_call | solution.py:417
  294.5 6.3 %rows_bias.3.grad_ref = bf16[2048,512]{1,0:T(8,128)(2,1)} custom-call(bf16[1024,1024]{1,0:T(8,128)(2,1)} %get-tuple-element.131.refs_0_.mine_ref, bf16[1024,1024]{1,0:T(8,128)(2,1)} %copy-done.7, bf16[1024,512]{1,0:T(8,128)(2,1)} %bitcast.133, f32[1,512]{1,0:T(1,128)} %broadcast_in_dim.49.refs_3_), custom_call_target="tpu_custom_call" | custom-call | flops 1000 | bytes 1000 | tf_op jit(solution)/shard_map/rows_bias/pallas_call | solution.py:253
  300.8 6.3 %columns_product.9 = bf16[1024,512]{1,0:T(8,128)(2,1)} custom-call(bf16[1024,1024]{1,0:T(8,128)(2,1)} %get-tuple-element.131.refs_0_.mine_ref, bf16[1024,1024]{1,0:T(8,128)(2,1)} %copy-done.7, bf16[2048,512]{1,0:T(8,128)(2,1)} %get-tuple-element.132.refs_0_.right_ref.mixed_ref), custom_call_target="tpu_custom_call" | custom-call | flops 1000 | bytes 1000 | tf_op jit(solution)/shard_map/columns_product/pallas_call | solution.py:417
  309.1 9.1 %columns_product.10 = (bf16[1024,256]{1,0:T(8,128)(2,1)}, bf16[1024,256]{1,0:T(8,128)(2,1)}, bf16[1024,256]{1,0:T(8,128)(2,1)}, bf16[1024,256]{1,0:T(8,128)(2,1)}) custom-call(bf16[1024,1024]{1,0:T(8,128)(2,1)} %get-tuple-element.111.refs_0_.mine_ref, bf16[1024,1024]{1,0:T(8,128)(2,1)} %collective-permute-done.15.refs_1_.theirs_ref, ...), custom_call_target="tpu_custom_call" | custom-call | flops 1000 | bytes 1000 | tf_op jit(solution)/shard_map/columns_product/pallas_call | solution.py:417
  320.0 37.9 %attend_back.2 = (bf16[2048,1152]{1,0:T(8,128)(2,1)}, f32[2,3,8,384]{3,2,1,0:T(8,128)}) custom-call(bf16[2048,1536]{1,0:T(8,128)(2,1)} %rows_bias.2.q_ref.k_ref.v_ref, bf16[2048,1536]{1,0:T(8,128)(2,1)} %rows_bias.2.q_ref.k_ref.v_ref, bf16[2048,1536]{1,0:T(8,128)(2,1)} %rows_bias.2.q_ref.k_ref.v_ref, ...), custom_call_target="tpu_custom_call" | custom-call | flops 1000 | bytes 1000 | tf_op jit(solution)/shard_map/attend_back/pallas_call | solution.py:161
  358.9 10.9 %columns_product.12 = (bf16[1024,384]{1,0:T(8,128)(2,1)}, bf16[1024,384]{1,0:T(8,128)(2,1)}, bf16[1024,384]{1,0:T(8,128)(2,1)}) custom-call(bf16[1024,1024]{1,0:T(8,128)(2,1)} %fusion.3.refs_0_.mine_ref, bf16[1024,1024]{1,0:T(8,128)(2,1)} %copy-done.3, bf16[2048,1152]{1,0:T(8,128)(2,1)} %get-tuple-element.138.right_ref.refs_1_), custom_call_target="tpu_custom_call" | custom-call | flops 1000 | bytes 1000 | tf_op jit(solution)/shard_map/columns_product/pallas_call | solution.py:417
  382.0 14.3 %attend_back.3 = (bf16[2048,384]{1,0:T(8,128)(2,1)}, f32[2,1,8,384]{3,2,1,0:T(8,128)}) custom-call(bf16[2048,1536]{1,0:T(8,128)(2,1)} %rows_bias.2.q_ref.k_ref.v_ref, bf16[2048,1536]{1,0:T(8,128)(2,1)} %rows_bias.2.q_ref.k_ref.v_ref, bf16[2048,1536]{1,0:T(8,128)(2,1)} %rows_bias.2.q_ref.k_ref.v_ref, ...), custom_call_target="tpu_custom_call" | custom-call | flops 1000 | bytes 1000 | tf_op jit(solution)/shard_map/attend_back/pallas_call | solution.py:161
  396.4 6.1 %columns_product.13 = bf16[1024,384]{1,0:T(8,128)(2,1)} custom-call(bf16[1024,1024]{1,0:T(8,128)(2,1)} %fusion.3.refs_0_.mine_ref, bf16[1024,1024]{1,0:T(8,128)(2,1)} %copy-done.3, bf16[2048,384]{1,0:T(8,128)(2,1)} %get-tuple-element.156.refs_0_.right_ref), custom_call_target="tpu_custom_call" | custom-call | flops 1000 | bytes 1000 | tf_op jit(solution)/shard_map/columns_product/pallas_call | solution.py:417
  411.9 12.9 %rows_total.6 = (f32[1024,1024]{1,0:T(8,128)}, bf16[1024,1024]{1,0:T(8,128)(2,1)}) custom-call(bf16[2048,384]{1,0:T(8,128)(2,1)} %get-tuple-element.156.refs_0_.right_ref, bf16[2048,1152]{1,0:T(8,128)(2,1)} %get-tuple-element.138.right_ref.refs_1_, bf16[1024,1536]{1,0:T(8,128)(2,1)} %bitcast.130), custom_call_target="tpu_custom_call" | custom-call | flops 1000 | bytes 1000 | tf_op jit(solution)/shard_map/rows_total/pallas_call | solution.py:301
  427.9 14.7 %rows_total.7 = (f32[1024,1024]{1,0:T(8,128)}, bf16[1024,1024]{1,0:T(8,128)(2,1)}) custom-call(bf16[2048,1024]{1,0:T(8,128)(2,1)} %get-tuple-element.158.right_ref.refs_0_, bf16[2048,1024]{1,0:T(8,128)(2,1)} %get-tuple-element.115.right_ref.refs_1_, bf16[1024,512]{1,0:T(8,128)(2,1)} %pad_maximum_fusion.5.refs_2_, bf16[1024,512]{1,0:T(8,128)(2,1)} %copy-done.4, ...), custom_call_target="tpu_custom_call" | custom-call | flops 1000 | bytes 1000 | tf_op jit(solution)/shard_map/rows_total/pallas_call | solution.py:301
  445.2 2.2 collective-permute-start.36
  449.7 8.3 %first_back.1 = (f32[1024,1024]{1,0:T(8,128)}, f32[2,8,1024]{2,1,0:T(8,128)}) custom-call(f32[1024,1024]{1,0:T(8,128)} %get-tuple-element.157.refs_0_, bf16[1024,1024]{1,0:T(8,128)(2,1)} %collective-permute-done.34.refs_1_, bf16[1024,1024]{1,0:T(8,128)(2,1)} %refs_2_.7, f32[1024,1024]{1,0:T(8,128)} %get-tuple-element.164.refs_3_, ...), custom_call_target="tpu_custom_call" | custom-call | flops 1000 | bytes 1000 | tf_op jit(solution)/shard_map/first_back/pallas_call | solution.py:347
  460.2 7.8 %last.1 = (bf16[1024,1024]{1,0:T(8,128)(2,1)}, f32[2,8,1024]{2,1,0:T(8,128)}) custom-call(f32[1024,1024]{1,0:T(8,128)} %get-tuple-element.160.refs_0_, bf16[1024,1024]{1,0:T(8,128)(2,1)} %copy-done.18, bf16[1024,1024]{1,0:T(8,128)(2,1)} %refs_2_.7, f32[1024,1024]{1,0:T(8,128)} %get-tuple-element.130.refs_4_.refs_3_, bf16[1024,1024]{1,0:T(8,128)(2,1)} %refs_4_.1, ...), custom_call_target="tpu_custom_call" | custom-call | flops 1000 | bytes 1000 | tf_op jit(solution)/shard_map/last/pallas_call | solution.py:347
  469.6 2.6 all-to-all-start.2
  476.9 5.9 %all-to-all-done.2 = f32[32,14,128]{2,1,0:T(8,128)S(1)} async-done(((f32[32,14,128]{2,1,0:T(8,128)}), f32[32,14,128]{2,1,0:T(8,128)S(1)}, u32[]{:S(2)}, u32[]{:S(2)}) %all-to-all-start.2) | async-done | bytes 229408 | tf_op jit(solution)/shard_map/all_to_all | solution.py:566
  485.2 2.6 all-to-all-start.3
  489.5 2.2 fusion.9
  491.6 4.4 all-to-all-done.3
  (296 shorter events, 99.8 us)
Async XLA Ops:
  9.1 36.3 %collective-permute-start.3 = (bf16[256,512]{0,1:T(8,128)(2,1)S(1)}, bf16[256,512]{0,1:T(8,128)(2,1)S(1)}, u32[]{:S(2)}, u32[]{:S(2)}) collective-permute-start(bf16[256,512]{0,1:T(8,128)(2,1)S(1)} %get-tuple-element.271), channel_id=1, source_target_pairs={{0,24},{8,0},{16,8},{24,16},{1,25},{9,1},{17,9},{25,17},{2,26},{10... | collective-permute-start | bytes 786440 | tf_op jit(solution)/shard_map/ppermute | solution.py:509
  14.2 31.2 %collective-permute-start.1 = (bf16[256,512]{0,1:T(8,128)(2,1)S(1)}, bf16[256,512]{0,1:T(8,128)(2,1)S(1)}, u32[]{:S(2)}, u32[]{:S(2)}) collective-permute-start(bf16[256,512]{0,1:T(8,128)(2,1)S(1)} %get-tuple-element.271), channel_id=1, source_target_pairs={{0,8},{8,16},{16,24},{24,0},{1,9},{9,17},{17,25},{25,1},{2,10},{10... | collective-permute-start | bytes 786440 | tf_op jit(solution)/shard_map/ppermute | solution.py:509
  14.2 31.2 %collective-permute-start.2 = (bf16[256,512]{0,1:T(8,128)(2,1)S(1)}, bf16[256,512]{0,1:T(8,128)(2,1)S(1)}, u32[]{:S(2)}, u32[]{:S(2)}) collective-permute-start(bf16[256,512]{0,1:T(8,128)(2,1)S(1)} %get-tuple-element.271), channel_id=1, source_target_pairs={{0,16},{8,24},{16,0},{24,8},{1,17},{9,25},{17,1},{25,9},{2,18},{10... | collective-permute-start | bytes 786440 | tf_op jit(solution)/shard_map/ppermute | solution.py:509
  19.9 21.1 %all-to-all-start = ((bf16[32,16,128]{2,1,0:T(8,128)(2,1)}), bf16[32,16,128]{2,1,0:T(8,128)(2,1)S(1)}, u32[]{:S(2)}, u32[]{:S(2)}) async-start(bf16[32,16,128]{2,1,0:T(8,128)(2,1)} %broadcast_in_dim.44), calls=%async_computation | async-start | bytes 262144 | tf_op jit(solution)/shard_map/all_to_all | solution.py:566
  42.1 11.6 %all-to-all-start.1 = ((f32[32,6,128]{2,1,0:T(8,128)}), f32[32,6,128]{2,1,0:T(8,128)S(1)}, u32[]{:S(2)}, u32[]{:S(2)}) async-start(f32[32,6,128]{2,1,0:T(8,128)} %copy.96), calls=%async_computation.1 | async-start | bytes 262144 | tf_op jit(solution)/shard_map/all_to_all | solution.py:566
  45.3 46.2 %all-gather.3.cloned.1.call-start = ((), (), s32[]{:S(2)}) async-start(), calls=%async_computation.6 | async-start | bytes 1310720 | tf_op jit(solution)/shard_map/all_gather | solution.py:661
  46.8 15.3 %collective-permute-start.6 = (bf16[512,512]{1,0:T(8,128)(2,1)}, bf16[512,512]{1,0:T(8,128)(2,1)}, u32[]{:S(2)}, u32[]{:S(2)}) collective-permute-start(bf16[512,512]{1,0:T(8,128)(2,1)} %pad_maximum_fusion.13), channel_id=1, source_target_pairs={{0,4},{1,5},{2,6},{3,7},{4,0},{5,1},{6,2},{7,3},{8,12},{9,13},{10,... | collective-permute-start | bytes 1572872 | tf_op jit(solution)/shard_map/ppermute | solution.py:482
  49.8 15.1 %collective-permute-start.4 = (bf16[512,512]{1,0:T(8,128)(2,1)}, bf16[512,512]{1,0:T(8,128)(2,1)}, u32[]{:S(2)}, u32[]{:S(2)}) collective-permute-start(bf16[512,512]{1,0:T(8,128)(2,1)} %pad_maximum_fusion.12), channel_id=1, source_target_pairs={{0,2},{1,3},{2,0},{3,1},{4,6},{5,7},{6,4},{7,5},{8,10},{9,11},{10,... | collective-permute-start | bytes 1572872 | tf_op jit(solution)/shard_map/ppermute | solution.py:482
  51.2 84.4 %all-gather.5.cloned.1.call-start = ((), (), s32[]{:S(2)}) async-start(), calls=%async_computation.7 | async-start | bytes 1310720 | tf_op jit(solution)/shard_map/all_gather | solution.py:662
  55.9 46.4 %collective-permute-start = (bf16[1024,1024]{1,0:T(8,128)(2,1)}, bf16[1024,1024]{1,0:T(8,128)(2,1)S(1)}, u32[]{:S(2)}, u32[]{:S(2)}) collective-permute-start(bf16[1024,1024]{1,0:T(8,128)(2,1)} %fusion.3.refs_0_.mine_ref), channel_id=1, source_target_pairs={{0,1},{1,0},{2,3},{3,2},{4,5},{5,4},{6,7},{7,6},{8,9},{9,8},{10,11... | collective-permute-start | bytes 6291464 | tf_op jit(solution)/shard_map/ppermute | solution.py:482
  63.4 30.4 %copy-start.12 = (bf16[512,1024]{1,0:T(8,128)(2,1)}, bf16[512,1024]{1,0:T(8,128)(2,1)S(1)}, u32[]{:S(2)}) copy-start(bf16[512,1024]{1,0:T(8,128)(2,1)S(1)} %pad_maximum_fusion.2.c_ref) | copy-start | bytes 3145732
  63.4 24.9 %collective-permute-start.7 = (bf16[512,1024]{1,0:T(8,128)(2,1)S(1)}, bf16[512,1024]{1,0:T(8,128)(2,1)}, u32[]{:S(2)}, u32[]{:S(2)}) collective-permute-start(bf16[512,1024]{1,0:T(8,128)(2,1)S(1)} %pad_maximum_fusion.2.c_ref), channel_id=1, source_target_pairs={{0,2},{1,3},{2,0},{3,1},{4,6},{5,7},{6,4},{7,5},{8,10},{9,11},{10,... | collective-permute-start | bytes 3145736 | tf_op jit(solution)/shard_map/ppermute | solution.py:482
  67.0 24.6 %collective-permute-start.5 = (bf16[512,1024]{1,0:T(8,128)(2,1)}, bf16[512,1024]{1,0:T(8,128)(2,1)}, u32[]{:S(2)}, u32[]{:S(2)}) collective-permute-start(bf16[512,1024]{1,0:T(8,128)(2,1)} %pad_maximum_fusion.1.a_ref), channel_id=1, source_target_pairs={{0,4},{1,5},{2,6},{3,7},{4,0},{5,1},{6,2},{7,3},{8,12},{9,13},{10,... | collective-permute-start | bytes 3145736 | tf_op jit(solution)/shard_map/ppermute | solution.py:482
  93.8 20.8 %collective-permute-start.9 = (bf16[1024,256]{1,0:T(8,128)(2,1)}, bf16[1024,256]{1,0:T(8,128)(2,1)S(1)}, u32[]{:S(2)}, u32[]{:S(2)}) collective-permute-start(bf16[1024,256]{1,0:T(8,128)(2,1)} %get-tuple-element.254), channel_id=1, source_target_pairs={{0,4},{1,5},{2,6},{3,7},{4,0},{5,1},{6,2},{7,3},{8,12},{9,13},{10,... | collective-permute-start | bytes 1572872 | tf_op jit(solution)/shard_map/ppermute | solution.py:482
  95.1 19.5 %collective-permute-start.8 = (bf16[1024,256]{1,0:T(8,128)(2,1)}, bf16[1024,256]{1,0:T(8,128)(2,1)S(1)}, u32[]{:S(2)}, u32[]{:S(2)}) collective-permute-start(bf16[1024,256]{1,0:T(8,128)(2,1)} %get-tuple-element.255), channel_id=1, source_target_pairs={{0,2},{1,3},{2,0},{3,1},{4,6},{5,7},{6,4},{7,5},{8,10},{9,11},{10,... | collective-permute-start | bytes 1572872 | tf_op jit(solution)/shard_map/ppermute | solution.py:482
  96.2 331.7 %reduce-scatter.3.cloned.1.call-start = ((), (), s32[]{:S(2)}) async-start(), calls=%async_computation.8 | async-start | bytes 1310720 | tf_op jit(solution)/shard_map/reduce_scatter | solution.py:731
  115.9 23.1 %collective-permute-start.11 = (bf16[1024,512]{1,0:T(8,128)(2,1)S(1)}, bf16[1024,512]{1,0:T(8,128)(2,1)S(1)}, u32[]{:S(2)}, u32[]{:S(2)}) collective-permute-start(bf16[1024,512]{1,0:T(8,128)(2,1)S(1)} %pad_maximum_fusion.4.refs_3_), channel_id=1, source_target_pairs={{0,2},{1,3},{2,0},{3,1},{4,6},{5,7},{6,4},{7,5},{8,10},{9,11},{10,... | collective-permute-start | bytes 3145736 | tf_op jit(solution)/shard_map/ppermute | solution.py:482
  118.6 22.7 %collective-permute-start.10 = (bf16[1024,512]{1,0:T(8,128)(2,1)S(1)}, bf16[1024,512]{1,0:T(8,128)(2,1)}, u32[]{:S(2)}, u32[]{:S(2)}) collective-permute-start(bf16[1024,512]{1,0:T(8,128)(2,1)S(1)} %pad_maximum_fusion.3.refs_2_), channel_id=1, source_target_pairs={{0,4},{1,5},{2,6},{3,7},{4,0},{5,1},{6,2},{7,3},{8,12},{9,13},{10,... | collective-permute-start | bytes 3145736 | tf_op jit(solution)/shard_map/ppermute | solution.py:482
  142.6 17.8 %collective-permute-start.13 = (bf16[1024,256]{1,0:T(8,128)(2,1)S(1)}, bf16[1024,256]{1,0:T(8,128)(2,1)S(1)}, u32[]{:S(2)}, u32[]{:S(2)}) collective-permute-start(bf16[1024,256]{1,0:T(8,128)(2,1)S(1)} %get-tuple-element.252), channel_id=1, source_target_pairs={{0,4},{1,5},{2,6},{3,7},{4,0},{5,1},{6,2},{7,3},{8,12},{9,13},{10,... | collective-permute-start | bytes 1572872 | tf_op jit(solution)/shard_map/ppermute | solution.py:482
  143.3 17.3 %collective-permute-start.12 = (bf16[1024,256]{1,0:T(8,128)(2,1)S(1)}, bf16[1024,256]{1,0:T(8,128)(2,1)S(1)}, u32[]{:S(2)}, u32[]{:S(2)}) collective-permute-start(bf16[1024,256]{1,0:T(8,128)(2,1)S(1)} %get-tuple-element.253), channel_id=1, source_target_pairs={{0,2},{1,3},{2,0},{3,1},{4,6},{5,7},{6,4},{7,5},{8,10},{9,11},{10,... | collective-permute-start | bytes 1572872 | tf_op jit(solution)/shard_map/ppermute | solution.py:482
  168.8 4.4 collective-permute-start.14
  181.2 5.1 %collective-permute-start.15 = (bf16[1024,1024]{1,0:T(8,128)(2,1)}, bf16[1024,1024]{1,0:T(8,128)(2,1)}, u32[]{:S(2)}, u32[]{:S(2)}) collective-permute-start(bf16[1024,1024]{1,0:T(8,128)(2,1)} %get-tuple-element.111.refs_0_.mine_ref), channel_id=1, source_target_pairs={{0,1},{1,0},{2,3},{3,2},{4,5},{5,4},{6,7},{7,6},{8,9},{9,8},{10,11... | collective-permute-start | bytes 6291464 | tf_op jit(solution)/shard_map/ppermute | solution.py:482
  181.9 28.4 %collective-permute-start.18 = (bf16[1024,1024]{1,0:T(8,128)(2,1)S(1)}, bf16[1024,1024]{1,0:T(8,128)(2,1)}, u32[]{:S(2)}, u32[]{:S(2)}) collective-permute-start(bf16[1024,1024]{1,0:T(8,128)(2,1)S(1)} %multiply_convert_fusion.refs_0_.mine_ref), channel_id=1, source_target_pairs={{0,1},{1,0},{2,3},{3,2},{4,5},{5,4},{6,7},{7,6},{8,9},{9,8},{10,11... | collective-permute-start | bytes 6291464 | tf_op jit(solution)/shard_map/ppermute | solution.py:482
  182.4 27.9 %collective-permute-start.17 = (bf16[1024,512]{1,0:T(8,128)(2,1)S(1)}, bf16[1024,512]{1,0:T(8,128)(2,1)}, u32[]{:S(2)}, u32[]{:S(2)}) collective-permute-start(bf16[1024,512]{1,0:T(8,128)(2,1)S(1)} %pad_maximum_fusion.6.refs_3_), channel_id=1, source_target_pairs={{0,2},{1,3},{2,0},{3,1},{4,6},{5,7},{6,4},{7,5},{8,10},{9,11},{10,... | collective-permute-start | bytes 3145736 | tf_op jit(solution)/shard_map/ppermute | solution.py:482
  183.4 26.9 %collective-permute-start.16 = (bf16[1024,512]{1,0:T(8,128)(2,1)}, bf16[1024,512]{1,0:T(8,128)(2,1)}, u32[]{:S(2)}, u32[]{:S(2)}) collective-permute-start(bf16[1024,512]{1,0:T(8,128)(2,1)} %pad_maximum_fusion.5.refs_2_), channel_id=1, source_target_pairs={{0,4},{1,5},{2,6},{3,7},{4,0},{5,1},{6,2},{7,3},{8,12},{9,13},{10,... | collective-permute-start | bytes 3145736 | tf_op jit(solution)/shard_map/ppermute | solution.py:482
  218.8 24.9 %collective-permute-start.19 = (bf16[1024,512]{1,0:T(8,128)(2,1)}, bf16[1024,512]{1,0:T(8,128)(2,1)S(1)}, u32[]{:S(2)}, u32[]{:S(2)}) collective-permute-start(bf16[1024,512]{1,0:T(8,128)(2,1)} %get-tuple-element.122), channel_id=1, source_target_pairs={{0,4},{1,5},{2,6},{3,7},{4,0},{5,1},{6,2},{7,3},{8,12},{9,13},{10,... | collective-permute-start | bytes 3145736 | tf_op jit(solution)/shard_map/ppermute | solution.py:482
  219.5 25.1 %collective-permute-start.20 = (bf16[1024,512]{1,0:T(8,128)(2,1)}, bf16[1024,512]{1,0:T(8,128)(2,1)S(1)}, u32[]{:S(2)}, u32[]{:S(2)}) collective-permute-start(bf16[1024,512]{1,0:T(8,128)(2,1)} %get-tuple-element.123), channel_id=1, source_target_pairs={{0,2},{1,3},{2,0},{3,1},{4,6},{5,7},{6,4},{7,5},{8,10},{9,11},{10,... | collective-permute-start | bytes 3145736 | tf_op jit(solution)/shard_map/ppermute | solution.py:482
  259.6 8.5 %collective-permute-start.21 = (bf16[1024,1024]{1,0:T(8,128)(2,1)}, bf16[1024,1024]{1,0:T(8,128)(2,1)S(1)}, u32[]{:S(2)}, u32[]{:S(2)}) collective-permute-start(bf16[1024,1024]{1,0:T(8,128)(2,1)} %get-tuple-element.129), channel_id=1, source_target_pairs={{0,1},{1,0},{2,3},{3,2},{4,5},{5,4},{6,7},{7,6},{8,9},{9,8},{10,11... | collective-permute-start | bytes 6291464 | tf_op jit(solution)/shard_map/ppermute | solution.py:482
  279.3 13.9 %collective-permute-start.22 = (bf16[1024,1024]{1,0:T(8,128)(2,1)}, bf16[1024,1024]{1,0:T(8,128)(2,1)S(1)}, u32[]{:S(2)}, u32[]{:S(2)}) collective-permute-start(bf16[1024,1024]{1,0:T(8,128)(2,1)} %get-tuple-element.131.refs_0_.mine_ref), channel_id=1, source_target_pairs={{0,1},{1,0},{2,3},{3,2},{4,5},{5,4},{6,7},{7,6},{8,9},{9,8},{10,11... | collective-permute-start | bytes 6291464 | tf_op jit(solution)/shard_map/ppermute | solution.py:482
  279.8 27.3 %collective-permute-start.23 = (bf16[1024,512]{1,0:T(8,128)(2,1)S(1)}, bf16[1024,512]{1,0:T(8,128)(2,1)S(1)}, u32[]{:S(2)}, u32[]{:S(2)}) collective-permute-start(bf16[1024,512]{1,0:T(8,128)(2,1)S(1)} %copy-done.52), channel_id=1, source_target_pairs={{0,4},{1,5},{2,6},{3,7},{4,0},{5,1},{6,2},{7,3},{8,12},{9,13},{10,... | collective-permute-start | bytes 3145736 | tf_op jit(solution)/shard_map/ppermute | solution.py:482
  280.6 26.5 %collective-permute-start.24 = (bf16[1024,512]{1,0:T(8,128)(2,1)S(1)}, bf16[1024,512]{1,0:T(8,128)(2,1)S(1)}, u32[]{:S(2)}, u32[]{:S(2)}) collective-permute-start(bf16[1024,512]{1,0:T(8,128)(2,1)S(1)} %copy-done.51), channel_id=1, source_target_pairs={{0,2},{1,3},{2,0},{3,1},{4,6},{5,7},{6,4},{7,5},{8,10},{9,11},{10,... | collective-permute-start | bytes 3145736 | tf_op jit(solution)/shard_map/ppermute | solution.py:482
  290.9 67.0 %collective-permute-start.25 = (bf16[1024,256]{1,0:T(8,128)(2,1)}, bf16[1024,256]{1,0:T(8,128)(2,1)S(1)}, u32[]{:S(2)}, u32[]{:S(2)}) collective-permute-start(bf16[1024,256]{1,0:T(8,128)(2,1)} %get-tuple-element.141), channel_id=1, source_target_pairs={{0,2},{1,3},{2,0},{3,1},{4,6},{5,7},{6,4},{7,5},{8,10},{9,11},{10,... | collective-permute-start | bytes 1572872 | tf_op jit(solution)/shard_map/ppermute | solution.py:482
  291.9 66.9 %collective-permute-start.26 = (bf16[1024,256]{1,0:T(8,128)(2,1)}, bf16[1024,256]{1,0:T(8,128)(2,1)S(1)}, u32[]{:S(2)}, u32[]{:S(2)}) collective-permute-start(bf16[1024,256]{1,0:T(8,128)(2,1)} %get-tuple-element.144), channel_id=1, source_target_pairs={{0,4},{1,5},{2,6},{3,7},{4,0},{5,1},{6,2},{7,3},{8,12},{9,13},{10,... | collective-permute-start | bytes 1572872 | tf_op jit(solution)/shard_map/ppermute | solution.py:482
  318.2 60.3 %collective-permute-start.27 = (bf16[1024,256]{1,0:T(8,128)(2,1)}, bf16[1024,256]{1,0:T(8,128)(2,1)}, u32[]{:S(2)}, u32[]{:S(2)}) collective-permute-start(bf16[1024,256]{1,0:T(8,128)(2,1)} %get-tuple-element.146), channel_id=1, source_target_pairs={{0,2},{1,3},{2,0},{3,1},{4,6},{5,7},{6,4},{7,5},{8,10},{9,11},{10,... | collective-permute-start | bytes 1572872 | tf_op jit(solution)/shard_map/ppermute | solution.py:482
  319.3 60.3 %collective-permute-start.28 = (bf16[1024,256]{1,0:T(8,128)(2,1)}, bf16[1024,256]{1,0:T(8,128)(2,1)}, u32[]{:S(2)}, u32[]{:S(2)}) collective-permute-start(bf16[1024,256]{1,0:T(8,128)(2,1)} %get-tuple-element.149), channel_id=1, source_target_pairs={{0,4},{1,5},{2,6},{3,7},{4,0},{5,1},{6,2},{7,3},{8,12},{9,13},{10,... | collective-permute-start | bytes 1572872 | tf_op jit(solution)/shard_map/ppermute | solution.py:482
  320.0 37.9 %copy-start.10 = (bf16[1024,512]{1,0:T(8,128)(2,1)S(1)}, bf16[1024,512]{1,0:T(8,128)(2,1)}, u32[]{:S(2)}) copy-start(bf16[1024,512]{1,0:T(8,128)(2,1)} %columns_product.9) | copy-start | bytes 3145732
  372.3 31.4 %collective-permute-start.30 = (bf16[512,1024]{1,0:T(8,128)(2,1)}, bf16[512,1024]{1,0:T(8,128)(2,1)S(1)}, u32[]{:S(2)}, u32[]{:S(2)}) collective-permute-start(bf16[512,1024]{1,0:T(8,128)(2,1)} %pad_maximum_fusion.10), channel_id=1, source_target_pairs={{0,2},{1,3},{2,0},{3,1},{4,6},{5,7},{6,4},{7,5},{8,10},{9,11},{10,... | collective-permute-start | bytes 3145736 | tf_op jit(solution)/shard_map/ppermute | solution.py:482
  374.7 74.9 %reduce-scatter.5.cloned.1.call-start = ((), (), s32[]{:S(2)}) async-start(), calls=%async_computation.9 | async-start | bytes 1310720 | tf_op jit(solution)/shard_map/reduce_scatter | solution.py:731
  377.2 30.6 %collective-permute-start.29 = (bf16[512,1024]{1,0:T(8,128)(2,1)}, bf16[512,1024]{1,0:T(8,128)(2,1)}, u32[]{:S(2)}, u32[]{:S(2)}) collective-permute-start(bf16[512,1024]{1,0:T(8,128)(2,1)} %pad_maximum_fusion.9), channel_id=1, source_target_pairs={{0,4},{1,5},{2,6},{3,7},{4,0},{5,1},{6,2},{7,3},{8,12},{9,13},{10,... | collective-permute-start | bytes 3145736 | tf_op jit(solution)/shard_map/ppermute | solution.py:482
  407.2 17.7 %collective-permute-start.32 = (bf16[512,512]{1,0:T(8,128)(2,1)}, bf16[512,512]{1,0:T(8,128)(2,1)}, u32[]{:S(2)}, u32[]{:S(2)}) collective-permute-start(bf16[512,512]{1,0:T(8,128)(2,1)} %slice.351), channel_id=1, source_target_pairs={{0,4},{1,5},{2,6},{3,7},{4,0},{5,1},{6,2},{7,3},{8,12},{9,13},{10,... | collective-permute-start | bytes 1572872 | tf_op jit(solution)/shard_map/ppermute | solution.py:482
  410.8 15.4 %collective-permute-start.31 = (bf16[512,512]{1,0:T(8,128)(2,1)S(1)}, bf16[512,512]{1,0:T(8,128)(2,1)}, u32[]{:S(2)}, u32[]{:S(2)}) collective-permute-start(bf16[512,512]{1,0:T(8,128)(2,1)S(1)} %slice.352), channel_id=1, source_target_pairs={{0,2},{1,3},{2,0},{3,1},{4,6},{5,7},{6,4},{7,5},{8,10},{9,11},{10,... | collective-permute-start | bytes 1572872 | tf_op jit(solution)/shard_map/ppermute | solution.py:482
  424.9 24.8 %collective-permute-start.34 = (bf16[1024,1024]{1,0:T(8,128)(2,1)}, bf16[1024,1024]{1,0:T(8,128)(2,1)}, u32[]{:S(2)}, u32[]{:S(2)}) collective-permute-start(bf16[1024,1024]{1,0:T(8,128)(2,1)} %get-tuple-element.163), channel_id=1, source_target_pairs={{0,1},{1,0},{2,3},{3,2},{4,5},{5,4},{6,7},{7,6},{8,9},{9,8},{10,11... | collective-permute-start | bytes 6291464 | tf_op jit(solution)/shard_map/ppermute | solution.py:482
  442.6 16.2 %collective-permute-start.33 = (bf16[1024,1024]{1,0:T(8,128)(2,1)}, bf16[1024,1024]{1,0:T(8,128)(2,1)S(1)}, u32[]{:S(2)}, u32[]{:S(2)}) collective-permute-start(bf16[1024,1024]{1,0:T(8,128)(2,1)} %get-tuple-element.161), channel_id=1, source_target_pairs={{0,1},{1,0},{2,3},{3,2},{4,5},{5,4},{6,7},{7,6},{8,9},{9,8},{10,11... | collective-permute-start | bytes 6291464 | tf_op jit(solution)/shard_map/ppermute | solution.py:482
  443.7 28.6 %collective-permute-start.35 = (bf16[256,512]{0,1:T(8,128)(2,1)S(1)}, bf16[256,512]{0,1:T(8,128)(2,1)}, u32[]{:S(2)}, u32[]{:S(2)}) collective-permute-start(bf16[256,512]{0,1:T(8,128)(2,1)S(1)} %bitcast.150), channel_id=1, source_target_pairs={{0,8},{8,16},{16,24},{24,0},{1,9},{9,17},{17,25},{25,1},{2,10},{10... | collective-permute-start | bytes 786440 | tf_op jit(solution)/shard_map/ppermute | solution.py:524
  445.2 27.0 %collective-permute-start.36 = (bf16[256,512]{0,1:T(8,128)(2,1)S(1)}, bf16[256,512]{0,1:T(8,128)(2,1)}, u32[]{:S(2)}, u32[]{:S(2)}) collective-permute-start(bf16[256,512]{0,1:T(8,128)(2,1)S(1)} %bitcast.151), channel_id=1, source_target_pairs={{0,16},{8,24},{16,0},{24,8},{1,17},{9,25},{17,1},{25,9},{2,18},{10... | collective-permute-start | bytes 786440 | tf_op jit(solution)/shard_map/ppermute | solution.py:524
  447.6 24.7 %collective-permute-start.37 = (bf16[256,512]{0,1:T(8,128)(2,1)S(1)}, bf16[256,512]{0,1:T(8,128)(2,1)}, u32[]{:S(2)}, u32[]{:S(2)}) collective-permute-start(bf16[256,512]{0,1:T(8,128)(2,1)S(1)} %bitcast.152), channel_id=1, source_target_pairs={{0,24},{8,0},{16,8},{24,16},{1,25},{9,1},{17,9},{25,17},{2,26},{10... | collective-permute-start | bytes 786440 | tf_op jit(solution)/shard_map/ppermute | solution.py:524
  469.6 13.2 %all-to-all-start.2 = ((f32[32,14,128]{2,1,0:T(8,128)}), f32[32,14,128]{2,1,0:T(8,128)S(1)}, u32[]{:S(2)}, u32[]{:S(2)}) async-start(f32[32,14,128]{2,1,0:T(8,128)} %bitcast.54), calls=%async_computation.4 | async-start | bytes 524288 | tf_op jit(solution)/shard_map/all_to_all | solution.py:566
  485.2 10.8 %all-to-all-start.3 = ((f32[32,8,128]{2,1,0:T(8,128)}), f32[32,8,128]{2,1,0:T(8,128)S(1)}, u32[]{:S(2)}, u32[]{:S(2)}) async-start(f32[32,8,128]{2,1,0:T(8,128)} %bitcast.58), calls=%async_computation.5 | async-start | bytes 262144 | tf_op jit(solution)/shard_map/all_to_all | solution.py:566
  (51 other events, 424.5 us)
Sparse Core Ops, SparseCore 0:
  51.4 27.0 all-gather.2
  96.3 27.4 all-gather.4
  374.9 26.5 reduce-scatter.2
  412.1 26.3 reduce-scatter.4

commit v3 on v2

--- a/solution.py
+++ b/solution.py
@@ -21,7 +21,8 @@
 F32 = jnp.float32
 BF16 = jnp.bfloat16
 QUERY_ROWS = 512
-VMEM_BYTES = 56 * 1024 * 1024
+TOKEN_ROWS = 32
+VMEM_BYTES = 40 * 1024 * 1024
 SMALL_COST = pl.CostEstimate(flops=1000, bytes_accessed=1000, transcendentals=0)
 
 
@@ -193,6 +194,15 @@
     return pl.BlockSpec(array.shape, lambda *step: (0,) * array.ndim)
 
 
+def pieces_of(array, ids, width):
+    return {i: (array, place, width) for place, i in enumerate(ids)}
+
+
+def piece_spec(piece):
+    array, block, width = piece
+    return pl.BlockSpec((array.shape[0], width), lambda *step: (0, block))
+
+
 def row_specs(local_rows, tile, width):
     count = local_rows // tile
     mine = pl.BlockSpec((tile, width), lambda i: (jnp.minimum(i, count - 1), 0))
@@ -204,7 +214,7 @@
     local_rows, depth = pair[0].shape
     tile = min(512, local_rows)
     count, mine, theirs = row_specs(local_rows, tile, depth)
-    widths = [w.shape[1] for w in weights]
+    widths = [piece[2] for piece in weights]
     width = sum(widths)
     total = 2 * local_rows
 
@@ -253,11 +263,11 @@
     return kernel_call(
         body,
         (2 * count,),
-        [mine, theirs, *[whole(w) for w in weights], extra_spec],
+        [mine, theirs, *[piece_spec(w) for w in weights], extra_spec],
         out_specs,
         out_shape,
         "rows_" + kind,
-    )(*pair, *weights, extra)
+    )(*pair, *[w[0] for w in weights], extra)
 
 
 def columns_of(refs, start, stop):
@@ -271,12 +281,12 @@
     local_rows = lefts[0].shape[0] // 2
     tile = min(512, local_rows)
     count = local_rows // tile
-    width = weights[0].shape[0]
+    width = weights[0][0].shape[0]
     ends = set()
-    for arrays in (lefts, weights):
+    for spans in ([a.shape[1] for a in lefts], [w[2] for w in weights]):
         end = 0
-        for array in arrays:
-            end += array.shape[1]
+        for span in spans:
+            end += span
             ends.add(end)
     ends = sorted(ends)
 
@@ -302,7 +312,7 @@
         body,
         (2 * count,),
         [pl.BlockSpec((tile, a.shape[1]), lambda i: (i, 0)) for a in lefts]
-        + [whole(w) for w in weights],
+        + [piece_spec(w) for w in weights],
         [
             pl.BlockSpec((tile, width), lambda i: (jnp.minimum(i, count - 1), 0)),
             pl.BlockSpec((tile, width), lambda i: (jnp.maximum(i - count, 0), 0)),
@@ -312,7 +322,7 @@
             jax.ShapeDtypeStruct((local_rows, width), BF16),
         ],
         "rows_total",
-    )(*lefts, *weights)
+    )(*lefts, *[w[0] for w in weights])
 
 
 def token_kernel(body, arrays, rows_of, out_types, sums, name):
@@ -321,13 +331,9 @@
     outs = len(out_types)
 
     def kernel(*refs):
-        values = [ref[...].astype(F32) for ref in refs[: len(arrays)]]
         rows_ref = refs[len(arrays)]
+        out_refs = refs[len(arrays) + 1 :]
         rows = [rows_ref[i : i + 1, :] for i in range(8)]
-        results, columns = body(values, rows)
-        out_refs = refs[len(arrays) + 1 :]
-        for ref, result in zip(out_refs, results):
-            ref[...] = result.astype(ref.dtype)
         if sums:
             sum_ref = out_refs[outs]
 
@@ -335,8 +341,14 @@
             def _():
                 sum_ref[...] = jnp.zeros(sum_ref.shape, F32)
 
+        for start in range(0, tile, TOKEN_ROWS):
+            lines = slice(start, start + TOKEN_ROWS)
+            values = [ref[lines, :].astype(F32) for ref in refs[: len(arrays)]]
+            results, columns = body(values, rows)
+            for ref, result in zip(out_refs, results):
+                ref[lines, :] = result.astype(ref.dtype)
             for i, column in enumerate(columns):
-                sum_ref[i] += jnp.sum(column.reshape(tile // 8, 8, D), 0)
+                sum_ref[i] += jnp.sum(column.reshape(TOKEN_ROWS // 8, 8, D), 0)
 
     tokens_spec = pl.BlockSpec((tile, D), lambda i: (i, 0))
     out_specs = [tokens_spec] * outs
@@ -394,36 +406,46 @@
     return [resid_mid + gate_feed * feed_out], [upstream * feed_out, upstream * gate_feed]
 
 
-def columns_product(pair, right, added, cuts):
+def columns_product(pair, right, added, outs, width):
     local_rows, depth = pair[0].shape
-    width = right.shape[1]
+    rows = right.shape[0]
     tile = 256
-    starts = [sum(cuts[:i]) for i in range(len(cuts))]
-    add_width = width // max(1, len(added))
-
-    def body(mine_ref, theirs_ref, right_ref, *refs):
-        add_refs = refs[: len(added)]
-        out_refs = refs[len(added) :]
+    blocks = [i for ids in outs for i in ids]
+    extra = list(added)
+    per_extra = len(blocks) // max(1, len(extra))
+
+    def body(mine_ref, theirs_ref, *refs):
+        right_refs = refs[: len(blocks)]
+        add_refs = refs[len(blocks) : len(blocks) + len(extra)]
+        out_refs = refs[len(blocks) + len(extra) :]
         mine, theirs = mine_ref[...].T, theirs_ref[...].T
-        for ref, start, span in zip(out_refs, starts, cuts):
-            total = dot(mine, right_ref[:local_rows, start : start + span])
-            total = total + dot(theirs, right_ref[local_rows:, start : start + span])
-            if added:
-                place = start % add_width
-                total = total + add_refs[start // add_width][:, place : place + span].astype(F32)
-            ref[...] = total.astype(BF16)
+        number = 0
+        for ref, ids in zip(out_refs, outs):
+            for place in range(len(ids)):
+                total = dot(mine, right_refs[number][:local_rows])
+                total = total + dot(theirs, right_refs[number][local_rows:])
+                if extra:
+                    start = number % per_extra * width
+                    part = add_refs[number // per_extra][:, start : start + width]
+                    total = total + part.astype(F32)
+                ref[:, place * width : (place + 1) * width] = total.astype(BF16)
+                number += 1
 
     token_spec = pl.BlockSpec((local_rows, tile), lambda i: (0, i))
-    outs = kernel_call(
+
+    def out_spec(count):
+        return pl.BlockSpec((tile, count * width), lambda i: (i, 0))
+
+    return kernel_call(
         body,
         (depth // tile,),
-        [token_spec, token_spec, whole(right)]
-        + [pl.BlockSpec((tile, add_width), lambda i: (i, 0)) for _ in added],
-        [pl.BlockSpec((tile, span), lambda i: (i, 0)) for span in cuts],
-        [jax.ShapeDtypeStruct((depth, span), BF16) for span in cuts],
+        [token_spec, token_spec]
+        + [pl.BlockSpec((rows, width), lambda i, b=b: (0, b)) for b in blocks]
+        + [out_spec(per_extra) for _ in extra],
+        [out_spec(len(ids)) for ids in outs],
+        [jax.ShapeDtypeStruct((depth, len(ids) * width), BF16) for ids in outs],
         "columns_product",
-    )(*pair, right, *added)
-    return outs
+    )(*pair, *[right] * len(blocks), *extra)
 
 
 def assemble(top, low, qkv_width, out_width):
@@ -625,7 +647,15 @@
     )
     small_all = all_exchange(
         jnp.broadcast_to(small.reshape(1, -1, 128), (devices, small.size // 128, 128))
-    ).reshape(rows, cols, -1)
+    )
+
+    attn_rows, mark = grid.gather_rows(after(attn_local, small_all))
+    fc1_rows = lax.all_gather(fc1_local, "row", axis=0, tiled=True)
+    fc2_rows = lax.all_gather(after(fc2_local, mark), "row", axis=0, tiled=True)
+    half = D // 2
+    top = grid.gather_early(attn_rows[:half], grid.orders[0])
+    low = grid.gather_early(attn_rows[half:], grid.orders[1])
+    small_all = small_all.reshape(rows, cols, -1)
     cut = seq_rows * col_width
     cond_all = (
         small_all[:, :, :cut]
@@ -657,12 +687,6 @@
     shift_attn, scale_attn, gate_attn, shift_feed, scale_feed, gate_feed = modulation
     token_rows = jnp.concatenate([modulation.reshape(6, D), out_bias_all, fc2_bias_all], 0)
 
-    attn_rows, mark = grid.gather_rows(attn_local)
-    fc1_rows = lax.all_gather(after(fc1_local, mark), "row", axis=0, tiled=True)
-    fc2_rows = lax.all_gather(after(fc2_local, fc1_rows), "row", axis=0, tiled=True)
-    half = D // 2
-    top = grid.gather_early(attn_rows[:half], grid.orders[0])
-    low = grid.gather_early(attn_rows[half:], grid.orders[1])
     top = top + grid.gather_last(*top, grid.orders[0])
     low = low + grid.gather_last(*low, grid.orders[1])
     if local_heads % 2 == 0:
@@ -679,29 +703,7 @@
         )
         out_w = jnp.concatenate([b[:, qkv_width:] for b in attn_blocks], 1)
 
-    middle = local_units // 2
-
-    def units_early(rows_held, earlier, late):
-        rows_held = after(rows_held, *earlier)
-        parts = (rows_held[:, :middle], rows_held[:, middle:])
-        held = [grid.gather_early(p, order, late) for p, order in zip(parts, grid.orders)]
-        return [h[0] for h in held], [h[1] for h in held]
-
-    def units_last(held, ids, *earlier):
-        got = [
-            grid.gather_last(after(h, *earlier), i, order)
-            for h, i, order in zip(held, ids, grid.orders)
-        ]
-        return [g[0] for g in got], [g[1] for g in got]
-
-    ids_a = [grid.early_ids(order) for order in grid.orders]
-    fc1_bias_rel = grid.to_relative(fc1_bias_all).reshape(chips, 2, local_units // 2)
-    ids_b = [[order[-1] ^ i for i in ids] for ids, order in zip(ids_a, grid.orders)]
-    unit_ids = (ids_a, ids_b)
-    fc1_bias_groups = [
-        jnp.concatenate([fc1_bias_rel[i, part] for part in range(2) for i in ids[part]])[None]
-        for ids in unit_ids
-    ]
+    fc1_bias_rel = grid.to_relative(fc1_bias_all).reshape(1, chips * local_units)
     qv_rel = grid.to_relative(qv_bias_all).reshape(pairs, 2, 2, HD).transpose(0, 2, 1, 3)
     qkv_bias_rel = jnp.concatenate(
         [qv_rel[:, :1], jnp.zeros_like(qv_rel[:, :1]), qv_rel[:, 1:]], 1
@@ -714,19 +716,6 @@
         mine, theirs = rows_total(lefts, weights)
         return mine, grid.swap_core(theirs)
 
-    def send_units(left, right):
-        width = right.shape[1]
-        sent = columns_product(left, right, [], [width // 2] * 2)
-        got = [grid.swap_chip(a, order[-1]) for a, order in zip(sent, grid.orders)]
-        return got, sent[0]
-
-    def sum_chips(kept, late):
-        sums = [
-            grid.scatter_chips(kept[2 * n], kept[2 * n + 1], order, late)
-            for n, order in enumerate(grid.orders)
-        ]
-        return jnp.concatenate(sums, 1).astype(BF16)
-
     def sum_rows(parts):
         return lax.psum_scatter(parts, "row", scatter_dimension=0, tiled=True)
 
@@ -735,90 +724,111 @@
     hidden_attn = both((normed_attn * (1.0 + scale_attn) + shift_attn).astype(BF16))
     grad_feed_low = both((cotangent.astype(F32) * gate_feed).astype(BF16))
 
-    (projected,) = rows_product(hidden_attn, [qkv_w], qkv_bias_rel, "bias")
-    fc1_a, _ = units_early(fc1_rows, (top[2], low[2]), (projected,))
-    fc1_b, _ = units_last(fc1_a, ids_a)
-    projected = after(projected, *fc1_a)
-    middle_pair = pairs // 2
-    first_half = attend(projected, latents, pairs, 0, middle_pair)
-    fc2_a, _ = units_early(fc2_rows, (first_half[0], *fc1_b), ())
-    mixed, log_totals = attend(
-        after(projected, first_half[0], *fc1_b),
-        latents,
-        pairs,
-        middle_pair,
-        pairs - middle_pair,
-        first_half,
-    )
-    fc2_b, _ = units_last(fc2_a, ids_a, mixed)
-    mixed = after(mixed, *fc2_a)
-    totals = own_total([mixed], [out_w])
+    (projected,) = rows_product(hidden_attn, [(qkv_w, 0, qkv_w.shape[1])], qkv_bias_rel, "bias")
+    order1, order2 = grid.orders
+    fc1_a, ids1_a = grid.gather_early(after(fc1_rows, top[2], low[2]), order1, (projected,))
+    fc1_b, ids1_b = grid.gather_last(fc1_a, ids1_a, order1)
+    unit_ids = range(chips)
+    fc1_pieces = {
+        **pieces_of(fc1_a, ids1_a, local_units), **pieces_of(fc1_b, ids1_b, local_units)
+    }
+    fc1_all = [fc1_pieces[i] for i in unit_ids]
+    mixed, log_totals = attend(after(projected, fc1_a), latents, pairs, 0, pairs)
+    fc2_a, ids2_a = grid.gather_early(after(fc2_rows, projected), order2, (mixed,))
+    fc2_b, ids2_b = grid.gather_last(fc2_a, ids2_a, order2)
+    fc2_pieces = {
+        **pieces_of(fc2_a, ids2_a, local_units), **pieces_of(fc2_b, ids2_b, local_units)
+    }
+    fc2_all = [fc2_pieces[i] for i in unit_ids]
+    mixed = after(mixed, fc2_a)
+    out_all = [(out_w, 0, out_w.shape[1])]
+    totals = own_total([mixed], out_all)
     attention_out, hidden_feed = token_kernel(
-        middle_body, [*totals, tokens], token_rows, [F32, BF16], 0, "middle"
+        middle_body,
+        [after(totals[0], fc1_b), totals[1], tokens],
+        token_rows,
+        [F32, BF16],
+        0,
+        "middle",
     )
     hidden_feed = both(hidden_feed)
-    act_a, slope_a = rows_product(hidden_feed, fc1_a, fc1_bias_groups[0], "gelu")
-    act_b, slope_b = rows_product(
-        (after(hidden_feed[0], act_a), hidden_feed[1]), fc1_b, fc1_bias_groups[1], "gelu"
-    )
-    act_b = after(act_b, *fc2_b)
-
-    fc2_got, _ = send_units(grad_feed_low, act_b)
-    grad_a, bias_a = rows_product(
-        (after(grad_feed_low[0], act_b), grad_feed_low[1]), fc2_a, slope_a, "slope"
-    )
-    grad_b, bias_b = rows_product(
-        (after(grad_feed_low[0], grad_a), grad_feed_low[1]), fc2_b, slope_b, "slope"
-    )
-    bias_fc1 = [bias_a, bias_b]
-    grad_b = after(grad_b, *fc2_got)
-    totals = own_total([grad_a, grad_b], fc1_a + fc1_b)
-    fc1_got, sent = send_units(hidden_feed, after(grad_b, totals[0]))
+    acts, slopes = rows_product(hidden_feed, fc1_all, fc1_bias_rel, "gelu")
+
+    def send_units(left, right, orders):
+        count = len(orders)
+        outs = [
+            [count * (order[-1] ^ i) + part for i in grid.early_ids(order)]
+            for part, order in enumerate(orders)
+        ]
+        sent = columns_product(left, right, [], outs, local_units // count)
+        return [grid.swap_chip(a, order[-1]) for a, order in zip(sent, orders)], sent[0]
+
+    def keep_units(left, right, got, orders):
+        count = len(orders)
+        outs = []
+        for part, order in enumerate(orders):
+            places = [count * i + part for i in grid.early_ids(order)]
+            outs += [places[: len(places) // 2], places[len(places) // 2 :]]
+        return columns_product(left, right, got, outs, local_units // count)
+
+    def sum_chips(kept, orders, late):
+        sums = [
+            grid.scatter_chips(kept[2 * part], kept[2 * part + 1], order, late)
+            for part, order in enumerate(orders)
+        ]
+        return jnp.concatenate(sums, 1).astype(BF16)
+
+    fc2_got, fc2_sent = send_units(grad_feed_low, acts, grid.orders)
+    grad_pre, bias_fc1 = rows_product(
+        (after(grad_feed_low[0], fc2_sent), grad_feed_low[1]), fc2_all, slopes, "slope"
+    )
+    fc1_got, sent = send_units(hidden_feed, grad_pre, [order1])
+    totals = own_total([after(grad_pre, sent, *fc2_got)], fc1_all)
+    fc2_kept = keep_units(grad_feed_low, after(acts, totals[0]), fc2_got, grid.orders)
     grad_resid_mid, grad_attention_low, middle_sums = token_kernel(
         middle_back_body,
-        [after(totals[0], sent), totals[1], cotangent, tokens, attention_out],
+        [after(totals[0], fc2_kept[0]), totals[1], cotangent, tokens, attention_out],
         token_rows,
         [F32, BF16],
         4,
         "middle_back",
     )
     grad_attention_low = both(grad_attention_low)
-    fc2_kept = columns_product(
-        grad_feed_low, after(act_a, grad_attention_low[0]), fc2_got, [act_a.shape[1] // 4] * 4
-    )
 
     (grad_mixed,) = rows_product(
-        grad_attention_low, [out_w], jnp.zeros((1, out_w.shape[1]), F32), "bias"
-    )
-    fc1_kept = columns_product(
-        hidden_feed, after(grad_a, grad_mixed), fc1_got, [grad_a.shape[1] // 4] * 4
+        grad_attention_low, out_all, jnp.zeros((1, out_w.shape[1]), F32), "bias"
     )
     (grad_out,) = columns_product(
-        grad_attention_low, after(mixed, grad_mixed), [], [mixed.shape[1]]
-    )
-    grad_mixed = after(grad_mixed, grad_out, fc1_kept[0])
+        grad_attention_low, after(mixed, grad_mixed), [], [[0]], mixed.shape[1]
+    )
+    grad_mixed = after(grad_mixed, grad_out)
     grad_late, bias_late = attend_back(
         projected, mixed, grad_mixed, log_totals, latents, 1, pairs - 1
     )
-    fc2_sums = sum_chips(fc2_kept, (grad_late,))
-    fc1_sums = sum_chips(fc1_kept, (grad_late,))
+    fc2_sums = sum_chips(fc2_kept, grid.orders, (grad_late,))
+    fc1_kept = keep_units(hidden_feed, after(grad_pre, grad_late), fc1_got, [order1])
     late_chips = chips * (pairs - 1) // pairs
-    qkv_late = columns_product(hidden_attn, grad_late, [], [qkv_width] * late_chips) if (
+    qkv_late = columns_product(
+        hidden_attn, grad_late, [], [[i] for i in range(late_chips)], qkv_width
+    ) if (
         local_heads % 2 == 0
     ) else None
-    early_input = after(grad_mixed, grad_late, fc2_sums, fc1_sums)
+    early_input = after(grad_mixed, grad_late, fc2_sums, fc1_kept[0])
     grad_early, bias_early = attend_back(
         projected, mixed, early_input, log_totals, latents, 0, 1
     )
+    fc1_sums = sum_chips(fc1_kept, [order1], (grad_early,))
     fc2_part = sum_rows(fc2_sums)
     fc1_part = sum_rows(fc1_sums)
     bias_qkv = jnp.concatenate([bias_early, bias_late], 1).sum((0, 2))
     if local_heads % 2 == 0:
-        qkv_early = columns_product(hidden_attn, grad_early, [], [qkv_width])
+        qkv_early = columns_product(hidden_attn, grad_early, [], [[0]], qkv_width)
         grad_qkv = [*qkv_early, *qkv_late]
     else:
         grad_projected = jnp.concatenate([grad_early, grad_late], 1)
-        (grad_qkv,) = columns_product(hidden_attn, grad_projected, [], [3 * PAIR * pairs])
+        (grad_qkv,) = columns_product(
+            hidden_attn, grad_projected, [], [[0]], 3 * PAIR * pairs
+        )
         grad_qkv = (
             grad_qkv.reshape(D, pairs, 3, 2, HD).transpose(0, 1, 3, 2, 4).reshape(D, chips, qkv_width)
         )
@@ -857,11 +867,11 @@
     qkv_part = qkv_part.reshape(row_width, local_heads, 3 * HD)
     out_part = attn_part[:, qkv_width:].T.reshape(local_heads, HD, row_width)
 
-    totals = own_total([after(grad_early, *attn_got), grad_late], [qkv_w])
+    totals = own_total([after(grad_early, *attn_got), grad_late], [(qkv_w, 0, qkv_w.shape[1])])
     tokens_grad, first_sums = token_kernel(
         first_back_body, [*totals, tokens, grad_resid_mid], token_rows, [F32], 2, "first_back"
     )
-    totals = own_total([after(act_a, totals[0], fc2_part, *attn_sums), act_b], fc2_a + fc2_b)
+    totals = own_total([after(acts, totals[0], fc2_part, *attn_sums)], fc2_all)
     layer_out, last_sums = token_kernel(
         last_body, [after(totals[0], fc1_part), totals[1], tokens, attention_out, cotangent], token_rows, [BF16], 2, "last"
     )
@@ -873,15 +883,7 @@
         [first_sums, middle_sums[2:3], middle_sums[:2], last_sums[:1], middle_sums[3:], last_sums[1:]]
     )
     mod_rows = mod_rows.reshape(8, cols, col_width).transpose(1, 0, 2)
-    bias_fc1 = [b.sum(0, keepdims=True) for b in bias_fc1]
-    first_half, second_half = {}, {}
-    for sums, ids in zip(bias_fc1, unit_ids):
-        middle = sums.shape[1] // 2
-        first_half.update(split_columns(sums[:, :middle], ids[0]))
-        second_half.update(split_columns(sums[:, middle:], ids[1]))
-    fc1_rel = jnp.concatenate(
-        [jnp.concatenate([first_half[i], second_half[i]], 1) for i in range(chips)], 0
-    )
+    fc1_rel = bias_fc1.sum(0).reshape(chips, local_units)
     qkv_rel = bias_qkv.reshape(pairs, 3, 2, HD)
     qv_rel = jnp.stack([qkv_rel[:, 0], qkv_rel[:, 2]], 2).reshape(chips, local_heads * PAIR)
     hidden_rows = grid.to_absolute(jnp.concatenate([fc1_rel, qv_rel], 1)).reshape(

time: 510 us -> 532 us (1.043)
  waiting for transfers between devices: 66.3 us -> 122 us
  Pallas kernels: 291 us -> 248 us
  local copies, waits for them, and re-layouts: 37.8 us -> 61.6 us
  other arithmetic: 35 us -> 25.6 us
    unnamed x114 -> x143, local copies, waits for them, and re-layouts: 17.2 us -> 49.7 us
    ppermute x3, waiting for transfers between devices: 0.01 us -> 31.6 us  [gather_rows(): lax.ppermute(block, 'row', [(i, (i + step) % count) for i in range(count)])]
    ppermute x32 -> x26, waiting for transfers between devices: 40.7 us -> 71.6 us  [swap(): return lax.ppermute(array, 'col', pairs)]
    pallas_call x13 -> x11, Pallas kernels: 119 us -> 98.4 us  [the longest x7 52.9 us: columns_product(): kernel_call(body, (depth // tile,), [token_spec, token_spec] + [pl.BlockS...]
    pallas_call x4, Pallas kernels: 49.6 us -> 38.8 us  [rows_total(): kernel_call(body, (2 * count,), [pl.BlockSpec((tile, a.shape[1]), lambda...]
    pallas_call x4, Pallas kernels: 32.6 us -> 24.3 us  [token_kernel(): kernel_call(kernel, (tokens // tile,), [tokens_spec] * len(arrays) + [who...]
    all_to_all x4, waiting for transfers between devices: 25.5 us -> 18.1 us  [all_exchange(): return lax.all_to_all(pieces, ('row', 'col'), 0, 0, tiled=True)]
    ppermute x32 -> x26, starting transfers between devices: 27.5 us -> 24.2 us  [swap(): return lax.ppermute(array, 'col', pairs)]
  transfers between devices with their start and end apart: 46 -> 40, of which waited for: 12 -> 16; matrix products, arithmetic and copies ran while one was open for 12% -> 8% of each run, Pallas kernels for 48% -> 43%
where the time goes in v3:
time: 532 us; the launch traced here: 526 us
  Pallas kernels  248 us (47%)
  waiting for transfers between devices  122 us (23%)
  local copies, waits for them, and re-layouts  61.6 us (12%)
  starting transfers between devices  49.7 us (9%)
  other arithmetic  25.6 us (5%)
  between operations  15.2 us (3%)
    ppermute x26, waiting for transfers between devices, swap(): return lax.ppermute(array, 'col', pairs)  71.6 us
    pallas_call x7, Pallas kernels, columns_product(): kernel_call(body, (depth // tile,), [token_spec, token_spec] + [pl.BlockS...  52.9 us
    pallas_call x2, Pallas kernels, attend_back(): pl.pallas_call(attend_back_kernel, grid=(latents, count), in_specs=[*part...  49.8 us
    unnamed x143, local copies, waits for them, and re-layouts  49.7 us
    pallas_call x4, Pallas kernels, rows_product(): kernel_call(body, (2 * count,), [mine, theirs, *[piece_spec(w) for w in w...  45.4 us
    pallas_call x4, Pallas kernels, rows_total(): kernel_call(body, (2 * count,), [pl.BlockSpec((tile, a.shape[1]), lambda...  38.8 us
    pallas_call x1, Pallas kernels, attend(): pl.pallas_call(attend_kernel, grid=(latents, count), in_specs=parts + [pl...  33.7 us
    ppermute x3, waiting for transfers between devices, gather_rows(): lax.ppermute(block, 'row', [(i, (i + step) % count) for i in range(count)])  31.6 us
  transfers between devices with their start and end apart: 40, of which 16 were waited for; matrix products, arithmetic and copies ran while one was open for 8% of the time, Pallas kernels for 43%

profile of v3, /device:TPU:0, one launch (start us, length us, event | category | flops | bytes accessed | tf_op | source)
XLA Modules:
  0.0 526.2 jit_solution(17982541232880459398)
XLA Ops:
  11.9 7.3 %all-to-all-start = ((bf16[32,16,128]{2,1,0:T(8,128)(2,1)}), bf16[32,16,128]{2,1,0:T(8,128)(2,1)S(1)}, u32[]{:S(2)}, u32[]{:S(2)}) async-start(bf16[32,16,128]{2,1,0:T(8,128)(2,1)} %broadcast_in_dim.32), calls=%async_computation | async-start | bytes 262144 | tf_op jit(solution)/shard_map/all_to_all | solution.py:588
  21.8 2.4 convert_reduce_fusion
  24.2 3.2 all-to-all-done
  28.5 2.7 all-to-all-start.1
  31.4 3.7 collective-permute-start.3
  36.2 4.7 all-to-all-done.1
  44.7 13.3 %collective-permute-done.3 = bf16[256,512]{0,1:T(8,128)(2,1)S(1)} collective-permute-done((bf16[256,512]{0,1:T(8,128)(2,1)S(1)}, bf16[256,512]{0,1:T(8,128)(2,1)S(1)}, u32[]{:S(2)}, u32[]{:S(2)}) %collective-permute-start.3) | collective-permute-done | bytes 262176 | tf_op jit(solution)/shard_map/ppermute | solution.py:531
  58.0 4.9 collective-permute-done.1
  62.9 13.4 %collective-permute-done.2 = bf16[256,512]{0,1:T(8,128)(2,1)} collective-permute-done((bf16[256,512]{0,1:T(8,128)(2,1)S(1)}, bf16[256,512]{0,1:T(8,128)(2,1)}, u32[]{:S(2)}, u32[]{:S(2)}) %collective-permute-start.2) | collective-permute-done | bytes 262176 | tf_op jit(solution)/shard_map/ppermute | solution.py:531
  84.9 8.0 %collective-permute-done.6 = bf16[512,512]{1,0:T(8,128)(2,1)} collective-permute-done((bf16[512,512]{1,0:T(8,128)(2,1)}, bf16[512,512]{1,0:T(8,128)(2,1)}, u32[]{:S(2)}, u32[]{:S(2)}) %collective-permute-start.6) | collective-permute-done | bytes 524320 | tf_op jit(solution)/shard_map/ppermute | solution.py:504
  100.4 18.4 %collective-permute-done.7.d_ref = bf16[512,1024]{1,0:T(8,128)(2,1)} collective-permute-done((bf16[512,1024]{1,0:T(8,128)(2,1)S(1)}, bf16[512,1024]{1,0:T(8,128)(2,1)}, u32[]{:S(2)}, u32[]{:S(2)}) %collective-permute-start.7) | collective-permute-done | bytes 1048608 | tf_op jit(solution)/shard_map/ppermute | solution.py:504
  118.8 3.5 collective-permute-done.5.b_ref
  124.7 2.9 assemble.1
  127.6 8.8 %rows_bias.2.q_ref.k_ref.v_ref = bf16[2048,1536]{1,0:T(8,128)(2,1)S(1)} custom-call(bf16[1024,1024]{1,0:T(8,128)(2,1)} %fusion.3.refs_0_.mine_ref, bf16[1024,1024]{1,0:T(8,128)(2,1)} %collective-permute-done.refs_1_.theirs_ref, bf16[1024,1536]{1,0:T(8,128)(2,1)S(1)} %bitcast.122, f32[1,1536]{1,0:T(1,128)S(1)} %reshape.212.refs_3_), custom_call_target="tpu_custom_call" | custom-call | flops 1000 | bytes 1000 | tf_op jit(solution)/shard_map/rows_bias/pallas_call | solution.py:263
  136.4 2.6 copy-done
  143.4 2.4 collective-permute-done.8
  148.7 2.8 copy-done.1
  151.5 33.7 %attend.1 = (bf16[2048,512]{1,0:T(8,128)(2,1)S(1)}, f32[2,4,2,1024]{3,2,1,0:T(2,128)S(1)}) custom-call(bf16[2048,1536]{1,0:T(8,128)(2,1)S(1)} %copy-done.1, bf16[2048,1536]{1,0:T(8,128)(2,1)S(1)} %copy-done.1, bf16[2048,1536]{1,0:T(8,128)(2,1)S(1)} %copy-done.1), custom_call_target="tpu_custom_call" | custom-call | flops 1000 | bytes 1000 | tf_op jit(solution)/shard_map/attend/pallas_call | solution.py:143
  185.4 3.3 rows_total.4
  190.7 17.9 %collective-permute-done.10.refs_4_.refs_5_.refs_3_ = bf16[1024,1024]{1,0:T(8,128)(2,1)S(1)} collective-permute-done((bf16[1024,1024]{1,0:T(8,128)(2,1)S(1)}, bf16[1024,1024]{1,0:T(8,128)(2,1)S(1)}, u32[]{:S(2)}, u32[]{:S(2)}) %collective-permute-start.10) | collective-permute-done | bytes 2097184 | tf_op jit(solution)/shard_map/ppermute | solution.py:504
  208.7 6.0 %middle.1 = (f32[1024,1024]{1,0:T(8,128)S(1)}, bf16[1024,1024]{1,0:T(8,128)(2,1)}) custom-call(f32[1024,1024]{1,0:T(8,128)} %copy-done.36, bf16[1024,1024]{1,0:T(8,128)(2,1)S(1)} %collective-permute-done.11.refs_1_, bf16[1024,1024]{1,0:T(8,128)(2,1)S(1)} %copy-done.4, f32[8,1024]{1,0:T(8,128)S(1)} %pad_maximum_fusion.11.refs_3_.refs_5_.refs_4_), custom_call_target="tpu_custom_call" | custom-call | flops 1000 | bytes 1000 | tf_op jit(solution)/shard_map/middle/pallas_call | solution.py:359
  221.0 19.8 %rows_gelu.1 = (bf16[2048,2048]{1,0:T(8,128)(2,1)}, bf16[2048,2048]{1,0:T(8,128)(2,1)}) custom-call(bf16[1024,1024]{1,0:T(8,128)(2,1)} %get-tuple-element.90.refs_0_.mine_ref, bf16[1024,1024]{1,0:T(8,128)(2,1)S(1)} %collective-permute-done.12.refs_1_.theirs_ref, bf16[1024,1024]{1,0:T(8,128)(2,1)S(1)} %constant_dynamic-update-slice_fusion.1.refs_2_.refs_3_.refs_1_, ...), custom_call_target="tpu_custom_call" | custom-call | flops 1000 | bytes 1000 | tf_op jit(solution)/shard_map/rows_gelu/pallas_call | solution.py:263
  240.8 9.1 %columns_product.7 = (bf16[1024,512]{1,0:T(8,128)(2,1)}, bf16[1024,512]{1,0:T(8,128)(2,1)}) custom-call(bf16[1024,1024]{1,0:T(8,128)(2,1)S(1)} %multiply_convert_fusion.mine_ref.refs_0_, bf16[1024,1024]{1,0:T(8,128)(2,1)S(1)} %collective-permute-done.13.theirs_ref.refs_1_, bf16[2048,2048]{1,0:T(8,128)(2,1)} %get-tuple-element.123.refs_0_.refs_1_.refs_2_.refs_3_, ...), custom_call_target="tpu_custom_call" | custom-call | flops 1000 | bytes 1000 | tf_op jit(solution)/shard_map/columns_product/pallas_call | solution.py:439
  252.6 13.8 %collective-permute-done.14.refs_3_.refs_5_.refs_2_.refs_4_ = bf16[1024,1024]{1,0:T(8,128)(2,1)S(1)} collective-permute-done((bf16[1024,1024]{1,0:T(8,128)(2,1)S(1)}, bf16[1024,1024]{1,0:T(8,128)(2,1)S(1)}, u32[]{:S(2)}, u32[]{:S(2)}) %collective-permute-start.14) | collective-permute-done | bytes 2097184 | tf_op jit(solution)/shard_map/ppermute | solution.py:504
  266.3 14.0 %rows_slope.1 = (bf16[2048,2048]{1,0:T(8,128)(2,1)}, f32[8,2048]{1,0:T(8,128)S(1)}) custom-call(bf16[1024,1024]{1,0:T(8,128)(2,1)S(1)} %multiply_convert_fusion.mine_ref.refs_0_, bf16[1024,1024]{1,0:T(8,128)(2,1)S(1)} %collective-permute-done.13.theirs_ref.refs_1_, bf16[1024,1024]{1,0:T(8,128)(2,1)S(1)} %constant_dynamic-update-slice_fusion.3.refs_2_.refs_4_.refs_1_.refs_3_, ...), custom_call_target="tpu_custom_call" | custom-call | flops 1000 | bytes 1000 | tf_op jit(solution)/shard_map/rows_slope/pallas_call | solution.py:263
  280.3 8.7 %columns_product.8 = bf16[1024,1024]{1,0:T(8,128)(2,1)} custom-call(bf16[1024,1024]{1,0:T(8,128)(2,1)} %get-tuple-element.90.refs_0_.mine_ref, bf16[1024,1024]{1,0:T(8,128)(2,1)S(1)} %copy-done.20, bf16[2048,2048]{1,0:T(8,128)(2,1)} %get-tuple-element.114.refs_0_.refs_1_, bf16[2048,2048]{1,0:T(8,128)(2,1)} %get-tuple-element.114.refs_0_.refs_1_), custom_call_target="tpu_custom_call" | custom-call | flops 1000 | bytes 1000 | tf_op jit(solution)/shard_map/columns_product/pallas_call | solution.py:439
  290.1 11.6 %rows_total.5 = (f32[1024,1024]{1,0:T(8,128)S(1)}, bf16[1024,1024]{1,0:T(8,128)(2,1)S(1)}) custom-call(bf16[2048,2048]{1,0:T(8,128)(2,1)} %get-tuple-element.114.refs_0_.refs_1_, bf16[1024,1024]{1,0:T(8,128)(2,1)S(1)} %constant_dynamic-update-slice_fusion.1.refs_2_.refs_3_.refs_1_, ...), custom_call_target="tpu_custom_call" | custom-call | flops 1000 | bytes 1000 | tf_op jit(solution)/shard_map/rows_total/pallas_call | solution.py:311
  305.0 8.0 %columns_product.9 = (bf16[1024,256]{1,0:T(8,128)(2,1)S(1)}, bf16[1024,256]{1,0:T(8,128)(2,1)S(1)}, bf16[1024,256]{1,0:T(8,128)(2,1)S(1)}, bf16[1024,256]{1,0:T(8,128)(2,1)S(1)}) custom-call(bf16[1024,1024]{1,0:T(8,128)(2,1)S(1)} %multiply_convert_fusion.mine_ref.refs_0_, bf16[1024,1024]{1,0:T(8,128)(2,1)S(1)} %copy-done.18, ...), custom_call_target="tpu_custom_call" | custom-call | flops 1000 | bytes 1000 | tf_op jit(solution)/shard_map/columns_product/pallas_call | solution.py:439
  313.0 6.5 %middle_back.1 = (f32[1024,1024]{1,0:T(8,128)S(1)}, bf16[1024,1024]{1,0:T(8,128)(2,1)S(1)}, f32[4,8,1024]{2,1,0:T(8,128)S(1)}) custom-call(f32[1024,1024]{1,0:T(8,128)} %copy-done.35, bf16[1024,1024]{1,0:T(8,128)(2,1)S(1)} %collective-permute-done.17.refs_1_, bf16[1024,1024]{1,0:T(8,128)(2,1)S(1)} %copy-done.15, bf16[1024,1024]{1,0:T(8,128)(2,1)S(1)} %copy-done.4, ...), custom_call_target="tpu_custom_call" | custom-call | flops 1000 | bytes 1000 | tf_op jit(solution)/shard_map/middle_back/pallas_call | solution.py:359
  325.8 2.9 rows_bias.3.grad_ref
  328.7 3.6 columns_product.10
  332.3 37.5 %attend_back.2 = (bf16[2048,1152]{1,0:T(8,128)(2,1)S(1)}, f32[2,3,8,384]{3,2,1,0:T(8,128)S(1)}) custom-call(bf16[2048,1536]{1,0:T(8,128)(2,1)} %copy-done, bf16[2048,1536]{1,0:T(8,128)(2,1)} %copy-done, bf16[2048,1536]{1,0:T(8,128)(2,1)} %copy-done, bf16[2048,512]{1,0:T(8,128)(2,1)S(1)} %get-tuple-element.105.refs_0_.mixed_ref, ...), custom_call_target="tpu_custom_call" | custom-call | flops 1000 | bytes 1000 | tf_op jit(solution)/shard_map/attend_back/pallas_call | solution.py:162
  369.8 2.2 copy-done.2
  373.5 2.3 copy-done.3
  375.8 8.8 %columns_product.12 = (bf16[1024,384]{1,0:T(8,128)(2,1)S(1)}, bf16[1024,384]{1,0:T(8,128)(2,1)S(1)}, bf16[1024,384]{1,0:T(8,128)(2,1)S(1)}) custom-call(bf16[1024,1024]{1,0:T(8,128)(2,1)} %fusion.3.refs_0_.mine_ref, bf16[1024,1024]{1,0:T(8,128)(2,1)} %collective-permute-done.refs_1_.theirs_ref, bf16[2048,1152]{1,0:T(8,128)(2,1)S(1)} %copy-done.3, ...), custom_call_target="tpu_custom_call" | custom-call | flops 1000 | bytes 1000 | tf_op jit(solution)/shard_map/columns_product/pallas_call | solution.py:439
  388.3 9.4 %columns_product.11 = (bf16[1024,512]{1,0:T(8,128)(2,1)S(1)}, bf16[1024,512]{1,0:T(8,128)(2,1)}) custom-call(bf16[1024,1024]{1,0:T(8,128)(2,1)} %get-tuple-element.90.refs_0_.mine_ref, bf16[1024,1024]{1,0:T(8,128)(2,1)S(1)} %copy-done.21, bf16[2048,2048]{1,0:T(8,128)(2,1)} %get-tuple-element.114.refs_0_.refs_1_, ...), custom_call_target="tpu_custom_call" | custom-call | flops 1000 | bytes 1000 | tf_op jit(solution)/shard_map/columns_product/pallas_call | solution.py:439
  398.2 12.3 %attend_back.3 = (bf16[2048,384]{1,0:T(8,128)(2,1)S(1)}, f32[2,1,8,384]{3,2,1,0:T(8,128)S(1)}) custom-call(bf16[2048,1536]{1,0:T(8,128)(2,1)S(1)} %bitcast.121, bf16[2048,1536]{1,0:T(8,128)(2,1)S(1)} %bitcast.121, bf16[2048,1536]{1,0:T(8,128)(2,1)S(1)} %bitcast.121, bf16[2048,512]{1,0:T(8,128)(2,1)S(1)} %copy-done.10, bf16[2048,512]{1,0:T(8,128)(2,1)S(1)} %copy-done.23, ...), custom_call_target="tpu_custom_call" | custom-call | flops 1000 | bytes 1000 | tf_op jit(solution)/shard_map/attend_back/pallas_call | solution.py:162
  410.5 5.3 %columns_product.13 = bf16[1024,384]{1,0:T(8,128)(2,1)S(1)} custom-call(bf16[1024,1024]{1,0:T(8,128)(2,1)} %fusion.3.refs_0_.mine_ref, bf16[1024,1024]{1,0:T(8,128)(2,1)} %collective-permute-done.refs_1_.theirs_ref, bf16[2048,384]{1,0:T(8,128)(2,1)S(1)} %get-tuple-element.121.refs_0_), custom_call_target="tpu_custom_call" | custom-call | flops 1000 | bytes 1000 | tf_op jit(solution)/shard_map/columns_product/pallas_call | solution.py:439
  423.4 11.2 %rows_total.6 = (f32[1024,1024]{1,0:T(8,128)S(1)}, bf16[1024,1024]{1,0:T(8,128)(2,1)}) custom-call(bf16[2048,384]{1,0:T(8,128)(2,1)S(1)} %copy-done.28, bf16[2048,1152]{1,0:T(8,128)(2,1)} %copy-done.2, bf16[1024,1536]{1,0:T(8,128)(2,1)S(1)} %bitcast.123), custom_call_target="tpu_custom_call" | custom-call | flops 1000 | bytes 1000 | tf_op jit(solution)/shard_map/rows_total/pallas_call | solution.py:311
  439.6 5.0 collective-permute-done.24
  449.0 12.6 %rows_total.7 = (f32[1024,1024]{1,0:T(8,128)S(1)}, bf16[1024,1024]{1,0:T(8,128)(2,1)}) custom-call(bf16[2048,2048]{1,0:T(8,128)(2,1)} %get-tuple-element.123.refs_0_.refs_1_.refs_2_.refs_3_, bf16[1024,1024]{1,0:T(8,128)(2,1)S(1)} %copy-done.6, bf16[1024,1024]{1,0:T(8,128)(2,1)S(1)} %copy-done.8, bf16[1024,1024]{1,0:T(8,128)(2,1)S(1)} %copy-done.6, ...), custom_call_target="tpu_custom_call" | custom-call | flops 1000 | bytes 1000 | tf_op jit(solution)/shard_map/rows_total/pallas_call | solution.py:311
  467.7 2.4 collective-permute-start.31
  474.6 6.0 %first_back.1 = (f32[1024,1024]{1,0:T(8,128)}, f32[2,8,1024]{2,1,0:T(8,128)S(1)}) custom-call(f32[1024,1024]{1,0:T(8,128)S(1)} %copy-done.32, bf16[1024,1024]{1,0:T(8,128)(2,1)} %collective-permute-done.28.refs_1_, bf16[1024,1024]{1,0:T(8,128)(2,1)S(1)} %copy-done.4, f32[1024,1024]{1,0:T(8,128)S(1)} %copy-done.30, ...), custom_call_target="tpu_custom_call" | custom-call | flops 1000 | bytes 1000 | tf_op jit(solution)/shard_map/first_back/pallas_call | solution.py:359
  484.4 5.9 %last.1 = (bf16[1024,1024]{1,0:T(8,128)(2,1)}, f32[2,8,1024]{2,1,0:T(8,128)S(1)}) custom-call(f32[1024,1024]{1,0:T(8,128)S(1)} %copy-done.34, bf16[1024,1024]{1,0:T(8,128)(2,1)} %collective-permute-done.27.refs_1_, bf16[1024,1024]{1,0:T(8,128)(2,1)S(1)} %copy-done.4, f32[1024,1024]{1,0:T(8,128)} %copy-done.24, bf16[1024,1024]{1,0:T(8,128)(2,1)S(1)} %copy-done.16, ...), custom_call_target="tpu_custom_call" | custom-call | flops 1000 | bytes 1000 | tf_op jit(solution)/shard_map/last/pallas_call | solution.py:359
  491.1 3.9 all-to-all-start.2
  499.7 5.9 %all-to-all-done.2 = f32[32,14,128]{2,1,0:T(8,128)S(1)} async-done(((f32[32,14,128]{2,1,0:T(8,128)}), f32[32,14,128]{2,1,0:T(8,128)S(1)}, u32[]{:S(2)}, u32[]{:S(2)}) %all-to-all-start.2) | async-done | bytes 229408 | tf_op jit(solution)/shard_map/all_to_all | solution.py:588
  508.0 2.6 all-to-all-start.3
  514.5 4.4 all-to-all-done.3
  (300 shorter events, 109.7 us)
Async XLA Ops:
  11.9 15.5 %all-to-all-start = ((bf16[32,16,128]{2,1,0:T(8,128)(2,1)}), bf16[32,16,128]{2,1,0:T(8,128)(2,1)S(1)}, u32[]{:S(2)}, u32[]{:S(2)}) async-start(bf16[32,16,128]{2,1,0:T(8,128)(2,1)} %broadcast_in_dim.32), calls=%async_computation | async-start | bytes 262144 | tf_op jit(solution)/shard_map/all_to_all | solution.py:588
  19.2 81.2 %all-gather.3.cloned.1.call-start = ((), (), s32[]{:S(2)}) async-start(), calls=%async_computation.6 | async-start | bytes 1310720 | tf_op jit(solution)/shard_map/all_gather | solution.py:653
  21.8 19.7 %copy-start.4 = (bf16[1024,1024]{1,0:T(8,128)(2,1)S(1)}, bf16[1024,1024]{1,0:T(8,128)(2,1)}, u32[]{:S(2)}) copy-start(bf16[1024,1024]{1,0:T(8,128)(2,1)} %refs_2_.7) | copy-start | bytes 6291460
  28.5 12.4 %all-to-all-start.1 = ((f32[32,6,128]{2,1,0:T(8,128)}), f32[32,6,128]{2,1,0:T(8,128)S(1)}, u32[]{:S(2)}, u32[]{:S(2)}) async-start(f32[32,6,128]{2,1,0:T(8,128)} %copy.94), calls=%async_computation.1 | async-start | bytes 262144 | tf_op jit(solution)/shard_map/all_to_all | solution.py:588
  31.2 109.5 %all-gather.5.cloned.1.call-start = ((), (), s32[]{:S(2)}) async-start(), calls=%async_computation.7 | async-start | bytes 1310720 | tf_op jit(solution)/shard_map/all_gather | solution.py:654
  31.4 26.6 %collective-permute-start.3 = (bf16[256,512]{0,1:T(8,128)(2,1)S(1)}, bf16[256,512]{0,1:T(8,128)(2,1)S(1)}, u32[]{:S(2)}, u32[]{:S(2)}) collective-permute-start(bf16[256,512]{0,1:T(8,128)(2,1)S(1)} %pad_maximum_fusion.9), channel_id=1, source_target_pairs={{0,24},{8,0},{16,8},{24,16},{1,25},{9,1},{17,9},{25,17},{2,26},{10... | collective-permute-start | bytes 786440 | tf_op jit(solution)/shard_map/ppermute | solution.py:531
  35.1 27.8 %collective-permute-start.1 = (bf16[256,512]{0,1:T(8,128)(2,1)S(1)}, bf16[256,512]{0,1:T(8,128)(2,1)S(1)}, u32[]{:S(2)}, u32[]{:S(2)}) collective-permute-start(bf16[256,512]{0,1:T(8,128)(2,1)S(1)} %pad_maximum_fusion.9), channel_id=1, source_target_pairs={{0,8},{8,16},{16,24},{24,0},{1,9},{9,17},{17,25},{25,1},{2,10},{10... | collective-permute-start | bytes 786440 | tf_op jit(solution)/shard_map/ppermute | solution.py:531
  35.1 41.2 %collective-permute-start.2 = (bf16[256,512]{0,1:T(8,128)(2,1)S(1)}, bf16[256,512]{0,1:T(8,128)(2,1)}, u32[]{:S(2)}, u32[]{:S(2)}) collective-permute-start(bf16[256,512]{0,1:T(8,128)(2,1)S(1)} %pad_maximum_fusion.9), channel_id=1, source_target_pairs={{0,16},{8,24},{16,0},{24,8},{1,17},{9,25},{17,1},{25,9},{2,18},{10... | collective-permute-start | bytes 786440 | tf_op jit(solution)/shard_map/ppermute | solution.py:531
  43.7 83.9 %collective-permute-start = (bf16[1024,1024]{1,0:T(8,128)(2,1)}, bf16[1024,1024]{1,0:T(8,128)(2,1)}, u32[]{:S(2)}, u32[]{:S(2)}) collective-permute-start(bf16[1024,1024]{1,0:T(8,128)(2,1)} %fusion.3.refs_0_.mine_ref), channel_id=1, source_target_pairs={{0,1},{1,0},{2,3},{3,2},{4,5},{5,4},{6,7},{7,6},{8,9},{9,8},{10,11... | collective-permute-start | bytes 6291464 | tf_op jit(solution)/shard_map/ppermute | solution.py:504
  78.7 14.2 %collective-permute-start.6 = (bf16[512,512]{1,0:T(8,128)(2,1)}, bf16[512,512]{1,0:T(8,128)(2,1)}, u32[]{:S(2)}, u32[]{:S(2)}) collective-permute-start(bf16[512,512]{1,0:T(8,128)(2,1)} %pad_maximum_fusion.8), channel_id=1, source_target_pairs={{0,4},{1,5},{2,6},{3,7},{4,0},{5,1},{6,2},{7,3},{8,12},{9,13},{10,... | collective-permute-start | bytes 1572872 | tf_op jit(solution)/shard_map/ppermute | solution.py:504
  81.4 14.5 %collective-permute-start.4 = (bf16[512,512]{1,0:T(8,128)(2,1)}, bf16[512,512]{1,0:T(8,128)(2,1)}, u32[]{:S(2)}, u32[]{:S(2)}) collective-permute-start(bf16[512,512]{1,0:T(8,128)(2,1)} %pad_maximum_fusion.7), channel_id=1, source_target_pairs={{0,2},{1,3},{2,0},{3,1},{4,6},{5,7},{6,4},{7,5},{8,10},{9,11},{10,... | collective-permute-start | bytes 1572872 | tf_op jit(solution)/shard_map/ppermute | solution.py:504
  84.7 361.1 %reduce-scatter.3.cloned.1.call-start = ((), (), s32[]{:S(2)}) async-start(), calls=%async_computation.8 | async-start | bytes 1310720 | tf_op jit(solution)/shard_map/reduce_scatter | solution.py:720
  94.3 29.0 %copy-start.37 = (bf16[512,1024]{1,0:T(8,128)(2,1)}, bf16[512,1024]{1,0:T(8,128)(2,1)S(1)}, u32[]{:S(2)}) copy-start(bf16[512,1024]{1,0:T(8,128)(2,1)S(1)} %pad_maximum_fusion.2.c_ref) | copy-start | bytes 3145732
  94.3 24.5 %collective-permute-start.7 = (bf16[512,1024]{1,0:T(8,128)(2,1)S(1)}, bf16[512,1024]{1,0:T(8,128)(2,1)}, u32[]{:S(2)}, u32[]{:S(2)}) collective-permute-start(bf16[512,1024]{1,0:T(8,128)(2,1)S(1)} %pad_maximum_fusion.2.c_ref), channel_id=1, source_target_pairs={{0,2},{1,3},{2,0},{3,1},{4,6},{5,7},{6,4},{7,5},{8,10},{9,11},{10,... | collective-permute-start | bytes 3145736 | tf_op jit(solution)/shard_map/ppermute | solution.py:504
  98.0 24.4 %collective-permute-start.5 = (bf16[512,1024]{1,0:T(8,128)(2,1)}, bf16[512,1024]{1,0:T(8,128)(2,1)}, u32[]{:S(2)}, u32[]{:S(2)}) collective-permute-start(bf16[512,1024]{1,0:T(8,128)(2,1)} %pad_maximum_fusion.1.a_ref), channel_id=1, source_target_pairs={{0,4},{1,5},{2,6},{3,7},{4,0},{5,1},{6,2},{7,3},{8,12},{9,13},{10,... | collective-permute-start | bytes 3145736 | tf_op jit(solution)/shard_map/ppermute | solution.py:504
  122.3 23.4 %collective-permute-start.8 = (bf16[1024,512]{1,0:T(8,128)(2,1)}, bf16[1024,512]{1,0:T(8,128)(2,1)}, u32[]{:S(2)}, u32[]{:S(2)}) collective-permute-start(bf16[1024,512]{1,0:T(8,128)(2,1)} %all-gather.3.cloned.1.call-done), channel_id=1, source_target_pairs={{0,2},{1,3},{2,0},{3,1},{4,6},{5,7},{6,4},{7,5},{8,10},{9,11},{10,... | collective-permute-start | bytes 3145736 | tf_op jit(solution)/shard_map/ppermute | solution.py:504
  140.7 44.5 %collective-permute-start.9 = (bf16[1024,512]{1,0:T(8,128)(2,1)}, bf16[1024,512]{1,0:T(8,128)(2,1)S(1)}, u32[]{:S(2)}, u32[]{:S(2)}) collective-permute-start(bf16[1024,512]{1,0:T(8,128)(2,1)} %all-gather.5.cloned.1.call-done), channel_id=1, source_target_pairs={{0,4},{1,5},{2,6},{3,7},{4,0},{5,1},{6,2},{7,3},{8,12},{9,13},{10,... | collective-permute-start | bytes 3145736 | tf_op jit(solution)/shard_map/ppermute | solution.py:504
  147.1 61.5 %collective-permute-start.10 = (bf16[1024,1024]{1,0:T(8,128)(2,1)S(1)}, bf16[1024,1024]{1,0:T(8,128)(2,1)S(1)}, u32[]{:S(2)}, u32[]{:S(2)}) collective-permute-start(bf16[1024,1024]{1,0:T(8,128)(2,1)S(1)} %constant_dynamic-update-slice_fusion.1.refs_2_.refs_3_.refs_1_), channel_id=1, source_target_pairs={{0,4},{1,5},{2,6},{3,7},{4,0},{5,1},{6,2},{7,3},{8,12},{9,13},{10,... | collective-permute-start | bytes 6291464 | tf_op jit(solution)/shard_map/ppermute | solution.py:504
  185.2 147.1 %copy-start.9 = (bf16[2048,512]{1,0:T(8,128)(2,1)}, bf16[2048,512]{1,0:T(8,128)(2,1)S(1)}, u32[]{:S(2)}) copy-start(bf16[2048,512]{1,0:T(8,128)(2,1)S(1)} %get-tuple-element.105.refs_0_.mixed_ref) | copy-start | bytes 6291460
  185.3 81.0 %copy-start.5 = (bf16[1024,1024]{1,0:T(8,128)(2,1)}, bf16[1024,1024]{1,0:T(8,128)(2,1)S(1)}, u32[]{:S(2)}) copy-start(bf16[1024,1024]{1,0:T(8,128)(2,1)S(1)} %constant_dynamic-update-slice_fusion.3.refs_2_.refs_4_.refs_1_.refs_3_) | copy-start | bytes 6291460
  190.7 18.0 %collective-permute-start.11 = (bf16[1024,1024]{1,0:T(8,128)(2,1)S(1)}, bf16[1024,1024]{1,0:T(8,128)(2,1)S(1)}, u32[]{:S(2)}, u32[]{:S(2)}) collective-permute-start(bf16[1024,1024]{1,0:T(8,128)(2,1)S(1)} %get-tuple-element.89), channel_id=1, source_target_pairs={{0,1},{1,0},{2,3},{3,2},{4,5},{5,4},{6,7},{7,6},{8,9},{9,8},{10,11... | collective-permute-start | bytes 6291464 | tf_op jit(solution)/shard_map/ppermute | solution.py:504
  216.7 4.4 collective-permute-start.12
  217.3 23.5 %collective-permute-start.13 = (bf16[1024,1024]{1,0:T(8,128)(2,1)S(1)}, bf16[1024,1024]{1,0:T(8,128)(2,1)S(1)}, u32[]{:S(2)}, u32[]{:S(2)}) collective-permute-start(bf16[1024,1024]{1,0:T(8,128)(2,1)S(1)} %multiply_convert_fusion.mine_ref.refs_0_), channel_id=1, source_target_pairs={{0,1},{1,0},{2,3},{3,2},{4,5},{5,4},{6,7},{7,6},{8,9},{9,8},{10,11... | collective-permute-start | bytes 6291464 | tf_op jit(solution)/shard_map/ppermute | solution.py:504
  217.8 48.5 %collective-permute-start.14 = (bf16[1024,1024]{1,0:T(8,128)(2,1)S(1)}, bf16[1024,1024]{1,0:T(8,128)(2,1)S(1)}, u32[]{:S(2)}, u32[]{:S(2)}) collective-permute-start(bf16[1024,1024]{1,0:T(8,128)(2,1)S(1)} %constant_dynamic-update-slice_fusion.3.refs_2_.refs_4_.refs_1_.refs_3_), channel_id=1, source_target_pairs={{0,2},{1,3},{2,0},{3,1},{4,6},{5,7},{6,4},{7,5},{8,10},{9,11},{10,... | collective-permute-start | bytes 6291464 | tf_op jit(solution)/shard_map/ppermute | solution.py:504
  221.0 19.8 %copy-start.19 = (bf16[1024,1024]{1,0:T(8,128)(2,1)}, bf16[1024,1024]{1,0:T(8,128)(2,1)S(1)}, u32[]{:S(2)}) copy-start(bf16[1024,1024]{1,0:T(8,128)(2,1)S(1)} %collective-permute-done.12.refs_1_.theirs_ref) | copy-start | bytes 6291460
  240.8 25.5 %copy-start.17 = (bf16[1024,1024]{1,0:T(8,128)(2,1)}, bf16[1024,1024]{1,0:T(8,128)(2,1)S(1)}, u32[]{:S(2)}) copy-start(bf16[1024,1024]{1,0:T(8,128)(2,1)S(1)} %collective-permute-done.13.theirs_ref.refs_1_) | copy-start | bytes 6291460
  249.9 39.1 %collective-permute-start.15 = (bf16[1024,512]{1,0:T(8,128)(2,1)}, bf16[1024,512]{1,0:T(8,128)(2,1)S(1)}, u32[]{:S(2)}, u32[]{:S(2)}) collective-permute-start(bf16[1024,512]{1,0:T(8,128)(2,1)} %get-tuple-element.92), channel_id=1, source_target_pairs={{0,4},{1,5},{2,6},{3,7},{4,0},{5,1},{6,2},{7,3},{8,12},{9,13},{10,... | collective-permute-start | bytes 3145736 | tf_op jit(solution)/shard_map/ppermute | solution.py:504
  251.1 38.9 %collective-permute-start.16 = (bf16[1024,512]{1,0:T(8,128)(2,1)}, bf16[1024,512]{1,0:T(8,128)(2,1)}, u32[]{:S(2)}, u32[]{:S(2)}) collective-permute-start(bf16[1024,512]{1,0:T(8,128)(2,1)} %get-tuple-element.96), channel_id=1, source_target_pairs={{0,2},{1,3},{2,0},{3,1},{4,6},{5,7},{6,4},{7,5},{8,10},{9,11},{10,... | collective-permute-start | bytes 3145736 | tf_op jit(solution)/shard_map/ppermute | solution.py:504
  303.7 9.3 %collective-permute-start.17 = (bf16[1024,1024]{1,0:T(8,128)(2,1)S(1)}, bf16[1024,1024]{1,0:T(8,128)(2,1)S(1)}, u32[]{:S(2)}, u32[]{:S(2)}) collective-permute-start(bf16[1024,1024]{1,0:T(8,128)(2,1)S(1)} %get-tuple-element.102), channel_id=1, source_target_pairs={{0,1},{1,0},{2,3},{3,2},{4,5},{5,4},{6,7},{7,6},{8,9},{9,8},{10,11... | collective-permute-start | bytes 6291464 | tf_op jit(solution)/shard_map/ppermute | solution.py:504
  321.5 4.3 collective-permute-start.18
  322.0 50.0 %collective-permute-start.19 = (bf16[1024,256]{1,0:T(8,128)(2,1)S(1)}, bf16[1024,256]{1,0:T(8,128)(2,1)S(1)}, u32[]{:S(2)}, u32[]{:S(2)}) collective-permute-start(bf16[1024,256]{1,0:T(8,128)(2,1)S(1)} %get-tuple-element.109), channel_id=1, source_target_pairs={{0,2},{1,3},{2,0},{3,1},{4,6},{5,7},{6,4},{7,5},{8,10},{9,11},{10,... | collective-permute-start | bytes 1572872 | tf_op jit(solution)/shard_map/ppermute | solution.py:504
  323.1 49.0 %collective-permute-start.20 = (bf16[1024,256]{1,0:T(8,128)(2,1)S(1)}, bf16[1024,256]{1,0:T(8,128)(2,1)S(1)}, u32[]{:S(2)}, u32[]{:S(2)}) collective-permute-start(bf16[1024,256]{1,0:T(8,128)(2,1)S(1)} %get-tuple-element.112), channel_id=1, source_target_pairs={{0,4},{1,5},{2,6},{3,7},{4,0},{5,1},{6,2},{7,3},{8,12},{9,13},{10,... | collective-permute-start | bytes 1572872 | tf_op jit(solution)/shard_map/ppermute | solution.py:504
  324.6 63.6 %collective-permute-start.21 = (bf16[1024,1024]{1,0:T(8,128)(2,1)}, bf16[1024,1024]{1,0:T(8,128)(2,1)}, u32[]{:S(2)}, u32[]{:S(2)}) collective-permute-start(bf16[1024,1024]{1,0:T(8,128)(2,1)} %columns_product.8), channel_id=1, source_target_pairs={{0,4},{1,5},{2,6},{3,7},{4,0},{5,1},{6,2},{7,3},{8,12},{9,13},{10,... | collective-permute-start | bytes 6291464 | tf_op jit(solution)/shard_map/ppermute | solution.py:504
  373.4 107.1 %reduce-scatter.5.cloned.1.call-start = ((), (), s32[]{:S(2)}) async-start(), calls=%async_computation.9 | async-start | bytes 1310720 | tf_op jit(solution)/shard_map/reduce_scatter | solution.py:720
  385.2 30.8 %collective-permute-start.23 = (bf16[512,1024]{1,0:T(8,128)(2,1)S(1)}, bf16[512,1024]{1,0:T(8,128)(2,1)}, u32[]{:S(2)}, u32[]{:S(2)}) collective-permute-start(bf16[512,1024]{1,0:T(8,128)(2,1)S(1)} %pad_maximum_fusion.5), channel_id=1, source_target_pairs={{0,2},{1,3},{2,0},{3,1},{4,6},{5,7},{6,4},{7,5},{8,10},{9,11},{10,... | collective-permute-start | bytes 3145736 | tf_op jit(solution)/shard_map/ppermute | solution.py:504
  386.7 31.7 %collective-permute-start.22 = (bf16[512,1024]{1,0:T(8,128)(2,1)S(1)}, bf16[512,1024]{1,0:T(8,128)(2,1)}, u32[]{:S(2)}, u32[]{:S(2)}) collective-permute-start(bf16[512,1024]{1,0:T(8,128)(2,1)S(1)} %pad_maximum_fusion.4), channel_id=1, source_target_pairs={{0,4},{1,5},{2,6},{3,7},{4,0},{5,1},{6,2},{7,3},{8,12},{9,13},{10,... | collective-permute-start | bytes 3145736 | tf_op jit(solution)/shard_map/ppermute | solution.py:504
  397.7 38.9 %collective-permute-start.26 = (bf16[1024,512]{1,0:T(8,128)(2,1)}, bf16[1024,512]{1,0:T(8,128)(2,1)S(1)}, u32[]{:S(2)}, u32[]{:S(2)}) collective-permute-start(bf16[1024,512]{1,0:T(8,128)(2,1)} %get-tuple-element.125), channel_id=1, source_target_pairs={{0,2},{1,3},{2,0},{3,1},{4,6},{5,7},{6,4},{7,5},{8,10},{9,11},{10,... | collective-permute-start | bytes 3145736 | tf_op jit(solution)/shard_map/ppermute | solution.py:504
  417.6 20.3 %collective-permute-start.25 = (bf16[512,512]{1,0:T(8,128)(2,1)S(1)}, bf16[512,512]{1,0:T(8,128)(2,1)}, u32[]{:S(2)}, u32[]{:S(2)}) collective-permute-start(bf16[512,512]{1,0:T(8,128)(2,1)S(1)} %slice.243), channel_id=1, source_target_pairs={{0,4},{1,5},{2,6},{3,7},{4,0},{5,1},{6,2},{7,3},{8,12},{9,13},{10,... | collective-permute-start | bytes 1572872 | tf_op jit(solution)/shard_map/ppermute | solution.py:504
  421.9 22.7 %collective-permute-start.24 = (bf16[512,512]{1,0:T(8,128)(2,1)S(1)}, bf16[512,512]{1,0:T(8,128)(2,1)}, u32[]{:S(2)}, u32[]{:S(2)}) collective-permute-start(bf16[512,512]{1,0:T(8,128)(2,1)S(1)} %slice.244), channel_id=1, source_target_pairs={{0,2},{1,3},{2,0},{3,1},{4,6},{5,7},{6,4},{7,5},{8,10},{9,11},{10,... | collective-permute-start | bytes 1572872 | tf_op jit(solution)/shard_map/ppermute | solution.py:504
  436.6 33.6 %collective-permute-start.28 = (bf16[1024,1024]{1,0:T(8,128)(2,1)}, bf16[1024,1024]{1,0:T(8,128)(2,1)}, u32[]{:S(2)}, u32[]{:S(2)}) collective-permute-start(bf16[1024,1024]{1,0:T(8,128)(2,1)} %get-tuple-element.130), channel_id=1, source_target_pairs={{0,1},{1,0},{2,3},{3,2},{4,5},{5,4},{6,7},{7,6},{8,9},{9,8},{10,11... | collective-permute-start | bytes 6291464 | tf_op jit(solution)/shard_map/ppermute | solution.py:504
  449.0 15.6 %copy-start.63 = (s32[4]{0:T(128)S(1)}, s32[4]{0:T(128)}, u32[]{:S(2)}) copy-start(s32[4]{0:T(128)} %copy-done.61) | copy-start | bytes 52
  463.6 17.0 %collective-permute-start.27 = (bf16[1024,1024]{1,0:T(8,128)(2,1)}, bf16[1024,1024]{1,0:T(8,128)(2,1)}, u32[]{:S(2)}, u32[]{:S(2)}) collective-permute-start(bf16[1024,1024]{1,0:T(8,128)(2,1)} %get-tuple-element.128), channel_id=1, source_target_pairs={{0,1},{1,0},{2,3},{3,2},{4,5},{5,4},{6,7},{7,6},{8,9},{9,8},{10,11... | collective-permute-start | bytes 6291464 | tf_op jit(solution)/shard_map/ppermute | solution.py:504
  465.8 29.3 %collective-permute-start.29 = (bf16[256,512]{0,1:T(8,128)(2,1)S(1)}, bf16[256,512]{0,1:T(8,128)(2,1)}, u32[]{:S(2)}, u32[]{:S(2)}) collective-permute-start(bf16[256,512]{0,1:T(8,128)(2,1)S(1)} %bitcast.145), channel_id=1, source_target_pairs={{0,8},{8,16},{16,24},{24,0},{1,9},{9,17},{17,25},{25,1},{2,10},{10... | collective-permute-start | bytes 786440 | tf_op jit(solution)/shard_map/ppermute | solution.py:546
  466.0 29.1 %collective-permute-start.30 = (bf16[256,512]{0,1:T(8,128)(2,1)S(1)}, bf16[256,512]{0,1:T(8,128)(2,1)}, u32[]{:S(2)}, u32[]{:S(2)}) collective-permute-start(bf16[256,512]{0,1:T(8,128)(2,1)S(1)} %bitcast.146), channel_id=1, source_target_pairs={{0,16},{8,24},{16,0},{24,8},{1,17},{9,25},{17,1},{25,9},{2,18},{10... | collective-permute-start | bytes 786440 | tf_op jit(solution)/shard_map/ppermute | solution.py:546
  467.7 27.4 %collective-permute-start.31 = (bf16[256,512]{0,1:T(8,128)(2,1)S(1)}, bf16[256,512]{0,1:T(8,128)(2,1)}, u32[]{:S(2)}, u32[]{:S(2)}) collective-permute-start(bf16[256,512]{0,1:T(8,128)(2,1)S(1)} %bitcast.147), channel_id=1, source_target_pairs={{0,24},{8,0},{16,8},{24,16},{1,25},{9,1},{17,9},{25,17},{2,26},{10... | collective-permute-start | bytes 786440 | tf_op jit(solution)/shard_map/ppermute | solution.py:546
  491.1 14.5 %all-to-all-start.2 = ((f32[32,14,128]{2,1,0:T(8,128)}), f32[32,14,128]{2,1,0:T(8,128)S(1)}, u32[]{:S(2)}, u32[]{:S(2)}) async-start(f32[32,14,128]{2,1,0:T(8,128)} %bitcast.42), calls=%async_computation.4 | async-start | bytes 524288 | tf_op jit(solution)/shard_map/all_to_all | solution.py:588
  497.8 21.0 %copy-start.60 = (bf16[8,128]{1,0:T(8,128)(2,1)S(1)}, bf16[8,128]{1,0:T(8,128)(2,1)}, u32[]{:S(2)}) copy-start(bf16[8,128]{1,0:T(8,128)(2,1)} %param.14) | copy-start | bytes 6148
  508.0 10.8 %all-to-all-start.3 = ((f32[32,8,128]{2,1,0:T(8,128)}), f32[32,8,128]{2,1,0:T(8,128)S(1)}, u32[]{:S(2)}, u32[]{:S(2)}) async-start(f32[32,8,128]{2,1,0:T(8,128)} %bitcast.46), calls=%async_computation.5 | async-start | bytes 262144 | tf_op jit(solution)/shard_map/all_to_all | solution.py:588
  (58 other events, 285.9 us)
Sparse Core Ops, SparseCore 0:
  21.6 50.4 all-gather.2
  84.8 24.9 all-gather.4
  373.6 25.5 reduce-scatter.2
  438.0 24.4 reduce-scatter.4

commit v4 on v3

--- a/solution.py
+++ b/solution.py
@@ -233,9 +233,10 @@
 
         start = 0
         for ref, span in zip(weight_refs, widths):
-            for low in range(0, span, 256):
-                cols = slice(start + low, start + low + 256)
-                product = dot(left, ref[:, low : low + 256])
+            step_width = min(256, span)
+            for low in range(0, span, step_width):
+                cols = slice(start + low, start + low + step_width)
+                product = dot(left, ref[:, low : low + step_width])
                 if kind == "bias":
                     out_refs[0][:, cols] = (product + extra_ref[:, cols]).astype(BF16)
                 elif kind == "gelu":
@@ -246,7 +247,7 @@
                     grad = (product * extra_ref[:, cols].astype(F32)).astype(BF16)
                     out_refs[0][:, cols] = grad
                     out_refs[1][:, cols] += jnp.sum(
-                        grad.astype(F32).reshape(tile // 8, 8, 256), 0
+                        grad.astype(F32).reshape(tile // 8, 8, step_width), 0
                     )
             start += span
 
@@ -649,13 +650,14 @@
         jnp.broadcast_to(small.reshape(1, -1, 128), (devices, small.size // 128, 128))
     )
 
-    attn_rows, mark = grid.gather_rows(after(attn_local, small_all))
-    fc1_rows = lax.all_gather(fc1_local, "row", axis=0, tiled=True)
-    fc2_rows = lax.all_gather(after(fc2_local, mark), "row", axis=0, tiled=True)
+    attn_rows, mark = grid.gather_rows(attn_local)
+    fc1_rows = lax.all_gather(after(fc1_local, mark), "row", axis=0, tiled=True)
+    fc2_rows = lax.all_gather(after(fc2_local, fc1_rows), "row", axis=0, tiled=True)
+    attn_rows = after(attn_rows, small_all)
     half = D // 2
     top = grid.gather_early(attn_rows[:half], grid.orders[0])
     low = grid.gather_early(attn_rows[half:], grid.orders[1])
-    small_all = small_all.reshape(rows, cols, -1)
+    small_all = after(small_all, top[0], low[0]).reshape(rows, cols, -1)
     cut = seq_rows * col_width
     cond_all = (
         small_all[:, :, :cut]
@@ -725,27 +727,48 @@
     grad_feed_low = both((cotangent.astype(F32) * gate_feed).astype(BF16))
 
     (projected,) = rows_product(hidden_attn, [(qkv_w, 0, qkv_w.shape[1])], qkv_bias_rel, "bias")
-    order1, order2 = grid.orders
-    fc1_a, ids1_a = grid.gather_early(after(fc1_rows, top[2], low[2]), order1, (projected,))
-    fc1_b, ids1_b = grid.gather_last(fc1_a, ids1_a, order1)
-    unit_ids = range(chips)
-    fc1_pieces = {
-        **pieces_of(fc1_a, ids1_a, local_units), **pieces_of(fc1_b, ids1_b, local_units)
-    }
-    fc1_all = [fc1_pieces[i] for i in unit_ids]
-    mixed, log_totals = attend(after(projected, fc1_a), latents, pairs, 0, pairs)
-    fc2_a, ids2_a = grid.gather_early(after(fc2_rows, projected), order2, (mixed,))
-    fc2_b, ids2_b = grid.gather_last(fc2_a, ids2_a, order2)
-    fc2_pieces = {
-        **pieces_of(fc2_a, ids2_a, local_units), **pieces_of(fc2_b, ids2_b, local_units)
-    }
-    fc2_all = [fc2_pieces[i] for i in unit_ids]
-    mixed = after(mixed, fc2_a)
+    unit_half = local_units // 2
+
+    def units_early(held, earlier, late):
+        held = after(held, *earlier)
+        parts = (held[:, :unit_half], held[:, unit_half:])
+        return [grid.gather_early(part, order, late) for part, order in zip(parts, grid.orders)]
+
+    def units_last(early, *earlier):
+        return [
+            grid.gather_last(after(held, *earlier), ids, order)
+            for (held, ids), order in zip(early, grid.orders)
+        ]
+
+    def unit_pieces(early, last):
+        found = [{**pieces_of(*e, unit_half), **pieces_of(*l, unit_half)} for e, l in zip(early, last)]
+        return [found[part][i] for i in range(chips) for part in range(2)]
+
+    fc1_early = units_early(fc1_rows, (top[2], low[2]), (projected,))
+    fc1_last = units_last(fc1_early)
+    fc1_got_last = [got for got, _ in fc1_last]
+    projected = after(projected, *[held for held, _ in fc1_early])
+    middle_pair = pairs // 2
+    first_half = attend(projected, latents, pairs, 0, middle_pair)
+    fc2_early = units_early(fc2_rows, (first_half[0], *fc1_got_last), ())
+    mixed, log_totals = attend(
+        after(projected, first_half[0], *fc1_got_last),
+        latents,
+        pairs,
+        middle_pair,
+        pairs - middle_pair,
+        first_half,
+    )
+    fc2_last = units_last(fc2_early, mixed)
+    mixed = after(mixed, *[held for held, _ in fc2_early])
+    fc1_all = unit_pieces(fc1_early, fc1_last)
+    fc2_all = unit_pieces(fc2_early, fc2_last)
+    order1 = grid.orders[0]
     out_all = [(out_w, 0, out_w.shape[1])]
     totals = own_total([mixed], out_all)
     attention_out, hidden_feed = token_kernel(
         middle_body,
-        [after(totals[0], fc1_b), totals[1], tokens],
+        [*totals, tokens],
         token_rows,
         [F32, BF16],
         0,
@@ -753,6 +776,7 @@
     )
     hidden_feed = both(hidden_feed)
     acts, slopes = rows_product(hidden_feed, fc1_all, fc1_bias_rel, "gelu")
+    acts = after(acts, *[got for got, _ in fc2_last])
 
     def send_units(left, right, orders):
         count = len(orders)

time: 532 us -> 503 us (0.945)
  waiting for transfers between devices: 122 us -> 76.8 us
  local copies, waits for them, and re-layouts: 61.6 us -> 74.2 us
    ppermute x26 -> x30, waiting for transfers between devices: 71.6 us -> 44.9 us  [swap(): return lax.ppermute(array, 'col', pairs)]
    ppermute x3, waiting for transfers between devices: 31.6 us -> 13.5 us  [gather_rows(): lax.ppermute(block, 'row', [(i, (i + step) % count) for i in range(count)])]
    ppermute x26 -> x30, starting transfers between devices: 24.2 us -> 22.5 us  [swap(): return lax.ppermute(array, 'col', pairs)]
    pallas_call x1 -> x2, Pallas kernels: 33.7 us -> 33.7 us  [attend(): pl.pallas_call(attend_kernel, grid=(latents, count), in_specs=parts + [pl...]
  transfers between devices with their start and end apart: 40 -> 44, of which waited for: 16 -> 14; matrix products, arithmetic and copies ran while one was open for 8% -> 10% of each run, Pallas kernels for 43% -> 43%
where the time goes in v4:
time: 503 us; the launch traced here: 497 us
  Pallas kernels  248 us (49%)
  waiting for transfers between devices  76.8 us (15%)
  local copies, waits for them, and re-layouts  74.2 us (15%)
  starting transfers between devices  48.3 us (10%)
  other arithmetic  30.4 us (6%)
  between operations  15.2 us (3%)
    unnamed x143, local copies, waits for them, and re-layouts  52.1 us
    pallas_call x7, Pallas kernels, columns_product(): kernel_call(body, (depth // tile,), [token_spec, token_spec] + [pl.BlockS...  51.3 us
    pallas_call x2, Pallas kernels, attend_back(): pl.pallas_call(attend_back_kernel, grid=(latents, count), in_specs=[*part...  50.2 us
    pallas_call x4, Pallas kernels, rows_product(): kernel_call(body, (2 * count,), [mine, theirs, *[piece_spec(w) for w in w...  46.4 us
    ppermute x30, waiting for transfers between devices, swap(): return lax.ppermute(array, 'col', pairs)  44.9 us
    pallas_call x4, Pallas kernels, rows_total(): kernel_call(body, (2 * count,), [pl.BlockSpec((tile, a.shape[1]), lambda...  40.1 us
    pallas_call x2, Pallas kernels, attend(): pl.pallas_call(attend_kernel, grid=(latents, count), in_specs=parts + [pl...  33.7 us
    pallas_call x4, Pallas kernels, token_kernel(): kernel_call(kernel, (tokens // tile,), [tokens_spec] * len(arrays) + [who...  23.1 us
  transfers between devices with their start and end apart: 44, of which 14 were waited for; matrix products, arithmetic and copies ran while one was open for 10% of the time, Pallas kernels for 43%

profile of v4, /device:TPU:0, one launch (start us, length us, event | category | flops | bytes accessed | tf_op | source)
XLA Modules:
  0.0 496.7 jit_solution(15343135305650285216)
XLA Ops:
  9.0 5.1 %collective-permute-start.2 = (bf16[256,512]{0,1:T(8,128)(2,1)S(1)}, bf16[256,512]{0,1:T(8,128)(2,1)S(1)}, u32[]{:S(2)}, u32[]{:S(2)}) collective-permute-start(bf16[256,512]{0,1:T(8,128)(2,1)S(1)} %get-tuple-element.253), channel_id=1, source_target_pairs={{0,24},{8,0},{16,8},{24,16},{1,25},{9,1},{17,9},{25,17},{2,26},{10... | collective-permute-start | bytes 786440 | tf_op jit(solution)/shard_map/ppermute | solution.py:532
  19.8 5.2 %all-to-all-start = ((bf16[32,16,128]{2,1,0:T(8,128)(2,1)}), bf16[32,16,128]{2,1,0:T(8,128)(2,1)}, u32[]{:S(2)}, u32[]{:S(2)}) async-start(bf16[32,16,128]{2,1,0:T(8,128)(2,1)} %broadcast_in_dim.32), calls=%async_computation | async-start | bytes 262144 | tf_op jit(solution)/shard_map/all_to_all | solution.py:589
  25.1 13.5 %collective-permute-done.1 = bf16[256,512]{0,1:T(8,128)(2,1)S(1)} collective-permute-done((bf16[256,512]{0,1:T(8,128)(2,1)S(1)}, bf16[256,512]{0,1:T(8,128)(2,1)S(1)}, u32[]{:S(2)}, u32[]{:S(2)}) %collective-permute-start.1) | collective-permute-done | bytes 262176 | tf_op jit(solution)/shard_map/ppermute | solution.py:532
  49.3 7.8 %collective-permute-done.4 = bf16[512,512]{1,0:T(8,128)(2,1)} collective-permute-done((bf16[512,512]{1,0:T(8,128)(2,1)}, bf16[512,512]{1,0:T(8,128)(2,1)}, u32[]{:S(2)}, u32[]{:S(2)}) %collective-permute-start.4) | collective-permute-done | bytes 524320 | tf_op jit(solution)/shard_map/ppermute | solution.py:505
  64.2 4.6 all-to-all-start.1
  69.6 7.4 %all-to-all-done.1 = f32[32,6,128]{2,1,0:T(8,128)S(1)} async-done(((f32[32,6,128]{2,1,0:T(8,128)}), f32[32,6,128]{2,1,0:T(8,128)S(1)}, u32[]{:S(2)}, u32[]{:S(2)}) %all-to-all-start.1) | async-done | bytes 98336 | tf_op jit(solution)/shard_map/all_to_all | solution.py:589
  82.3 22.6 %collective-permute-done.7.d_ref = bf16[512,1024]{1,0:T(8,128)(2,1)} collective-permute-done((bf16[512,1024]{1,0:T(8,128)(2,1)S(1)}, bf16[512,1024]{1,0:T(8,128)(2,1)}, u32[]{:S(2)}, u32[]{:S(2)}) %collective-permute-start.7) | collective-permute-done | bytes 1048608 | tf_op jit(solution)/shard_map/ppermute | solution.py:505
  105.3 2.2 fusion.34
  110.4 2.9 assemble.1
  113.4 10.3 %rows_bias.2.q_ref.k_ref.v_ref = bf16[2048,1536]{1,0:T(8,128)(2,1)S(1)} custom-call(bf16[1024,1024]{1,0:T(8,128)(2,1)} %fusion.3.refs_0_.mine_ref, bf16[1024,1024]{1,0:T(8,128)(2,1)} %collective-permute-done.5.refs_1_.theirs_ref, bf16[1024,1536]{1,0:T(8,128)(2,1)S(1)} %bitcast.123, f32[1,1536]{1,0:T(1,128)S(1)} %reshape.212.refs_3_), custom_call_target="tpu_custom_call" | custom-call | flops 1000 | bytes 1000 | tf_op jit(solution)/shard_map/rows_bias/pallas_call | solution.py:264
  125.9 2.3 pad_maximum_fusion.4.refs_2_.refs_4_.refs_1_.refs_3_
  129.2 16.8 %attend.2 = (bf16[2048,512]{1,0:T(8,128)(2,1)S(1)}, f32[2,4,2,1024]{3,2,1,0:T(2,128)S(1)}) custom-call(bf16[2048,1536]{1,0:T(8,128)(2,1)S(1)} %rows_bias.2.q_ref.k_ref.v_ref, bf16[2048,1536]{1,0:T(8,128)(2,1)S(1)} %rows_bias.2.q_ref.k_ref.v_ref, bf16[2048,1536]{1,0:T(8,128)(2,1)S(1)} %rows_bias.2.q_ref.k_ref.v_ref), custom_call_target="tpu_custom_call" | custom-call | flops 1000 | bytes 1000 | tf_op jit(solution)/shard_map/attend/pallas_call | solution.py:143
  146.1 2.6 copy-done
  155.8 2.8 copy-done.1
  158.6 16.8 %attend.3 = (bf16[2048,512]{1,0:T(8,128)(2,1)S(1)}, f32[2,4,2,1024]{3,2,1,0:T(2,128)S(1)}) custom-call(bf16[2048,1536]{1,0:T(8,128)(2,1)S(1)} %copy-done.1, bf16[2048,1536]{1,0:T(8,128)(2,1)S(1)} %copy-done.1, bf16[2048,1536]{1,0:T(8,128)(2,1)S(1)} %copy-done.1, bf16[2048,512]{1,0:T(8,128)(2,1)S(1)} %copy-done.6, ...), custom_call_target="tpu_custom_call", output_to_operand_aliasing={{0}: (3, {}), {1}: (4, {})} | custom-call | flops 1000 | bytes 1000 | tf_op jit(solution)/shard_map/attend/pallas_call | solution.py:143
  177.4 3.3 rows_total.4
  182.8 4.1 collective-permute-done.14.refs_1_
  186.9 4.3 middle.1
  201.9 19.6 %rows_gelu.1 = (bf16[2048,2048]{1,0:T(8,128)(2,1)}, bf16[2048,2048]{1,0:T(8,128)(2,1)}) custom-call(bf16[1024,1024]{1,0:T(8,128)(2,1)S(1)} %copy-done.16, bf16[1024,1024]{1,0:T(8,128)(2,1)S(1)} %copy-done.19, bf16[1024,512]{1,0:T(8,128)(2,1)} %pad_maximum_fusion.4.refs_2_.refs_4_.refs_1_.refs_3_, bf16[1024,512]{1,0:T(8,128)(2,1)S(1)} %copy-done.12, ...), custom_call_target="tpu_custom_call" | custom-call | flops 1000 | bytes 1000 | tf_op jit(solution)/shard_map/rows_gelu/pallas_call | solution.py:264
  221.6 8.0 %columns_product.7 = (bf16[1024,512]{1,0:T(8,128)(2,1)S(1)}, bf16[1024,512]{1,0:T(8,128)(2,1)S(1)}) custom-call(bf16[1024,1024]{1,0:T(8,128)(2,1)S(1)} %multiply_convert_fusion.mine_ref.refs_0_, bf16[1024,1024]{1,0:T(8,128)(2,1)S(1)} %collective-permute-done.18.theirs_ref.refs_1_, bf16[2048,2048]{1,0:T(8,128)(2,1)} %get-tuple-element.137.refs_0_.refs_1_.refs_2_.refs_3_, ...), custom_call_target="tpu_custom_call" | custom-call | flops 1000 | bytes 1000 | tf_op jit(solution)/shard_map/columns_product/pallas_call | solution.py:440
  231.4 13.6 %rows_slope.1 = (bf16[2048,2048]{1,0:T(8,128)(2,1)}, f32[8,2048]{1,0:T(8,128)S(1)}) custom-call(bf16[1024,1024]{1,0:T(8,128)(2,1)S(1)} %multiply_convert_fusion.mine_ref.refs_0_, bf16[1024,1024]{1,0:T(8,128)(2,1)S(1)} %collective-permute-done.18.theirs_ref.refs_1_, bf16[1024,512]{1,0:T(8,128)(2,1)S(1)} %pad_maximum_fusion.6.refs_2_.refs_4_.refs_1_.refs_3_, ...), custom_call_target="tpu_custom_call" | custom-call | flops 1000 | bytes 1000 | tf_op jit(solution)/shard_map/rows_slope/pallas_call | solution.py:264
  245.0 8.6 %columns_product.8 = bf16[1024,1024]{1,0:T(8,128)(2,1)} custom-call(bf16[1024,1024]{1,0:T(8,128)(2,1)S(1)} %copy-done.16, bf16[1024,1024]{1,0:T(8,128)(2,1)S(1)} %copy-done.20, bf16[2048,2048]{1,0:T(8,128)(2,1)} %get-tuple-element.128.refs_0_.refs_1_, bf16[2048,2048]{1,0:T(8,128)(2,1)} %get-tuple-element.128.refs_0_.refs_1_), custom_call_target="tpu_custom_call" | custom-call | flops 1000 | bytes 1000 | tf_op jit(solution)/shard_map/columns_product/pallas_call | solution.py:440
  255.9 12.6 %rows_total.5 = (f32[1024,1024]{1,0:T(8,128)S(1)}, bf16[1024,1024]{1,0:T(8,128)(2,1)S(1)}) custom-call(bf16[2048,2048]{1,0:T(8,128)(2,1)} %get-tuple-element.128.refs_0_.refs_1_, bf16[1024,512]{1,0:T(8,128)(2,1)} %pad_maximum_fusion.4.refs_2_.refs_4_.refs_1_.refs_3_, bf16[1024,512]{1,0:T(8,128)(2,1)S(1)} %copy-done.12, ...), custom_call_target="tpu_custom_call" | custom-call | flops 1000 | bytes 1000 | tf_op jit(solution)/shard_map/rows_total/pallas_call | solution.py:312
  270.5 8.0 %columns_product.9 = (bf16[1024,256]{1,0:T(8,128)(2,1)S(1)}, bf16[1024,256]{1,0:T(8,128)(2,1)S(1)}, bf16[1024,256]{1,0:T(8,128)(2,1)S(1)}, bf16[1024,256]{1,0:T(8,128)(2,1)S(1)}) custom-call(bf16[1024,1024]{1,0:T(8,128)(2,1)S(1)} %multiply_convert_fusion.mine_ref.refs_0_, bf16[1024,1024]{1,0:T(8,128)(2,1)S(1)} %collective-permute-done.18.theirs_ref.refs_1_, ...), custom_call_target="tpu_custom_call" | custom-call | flops 1000 | bytes 1000 | tf_op jit(solution)/shard_map/columns_product/pallas_call | solution.py:440
  281.4 7.0 %middle_back.1 = (f32[1024,1024]{1,0:T(8,128)S(1)}, bf16[1024,1024]{1,0:T(8,128)(2,1)S(1)}, f32[4,8,1024]{2,1,0:T(8,128)S(1)}) custom-call(f32[1024,1024]{1,0:T(8,128)} %copy-done.37, bf16[1024,1024]{1,0:T(8,128)(2,1)S(1)} %copy-done.45, bf16[1024,1024]{1,0:T(8,128)(2,1)S(1)} %copy-done.13, bf16[1024,1024]{1,0:T(8,128)(2,1)S(1)} %copy-done.4, ...), custom_call_target="tpu_custom_call" | custom-call | flops 1000 | bytes 1000 | tf_op jit(solution)/shard_map/middle_back/pallas_call | solution.py:360
  294.8 2.9 rows_bias.3.grad_ref
  297.6 3.6 columns_product.10
  301.3 37.9 %attend_back.2 = (bf16[2048,1152]{1,0:T(8,128)(2,1)S(1)}, f32[2,3,8,384]{3,2,1,0:T(8,128)S(1)}) custom-call(bf16[2048,1536]{1,0:T(8,128)(2,1)} %copy-done, bf16[2048,1536]{1,0:T(8,128)(2,1)} %copy-done, bf16[2048,1536]{1,0:T(8,128)(2,1)} %copy-done, bf16[2048,512]{1,0:T(8,128)(2,1)S(1)} %get-tuple-element.119.refs_0_.mixed_ref, ...), custom_call_target="tpu_custom_call" | custom-call | flops 1000 | bytes 1000 | tf_op jit(solution)/shard_map/attend_back/pallas_call | solution.py:162
  339.1 2.2 copy-done.2
  342.8 2.3 copy-done.3
  345.1 9.0 %columns_product.12 = (bf16[1024,384]{1,0:T(8,128)(2,1)S(1)}, bf16[1024,384]{1,0:T(8,128)(2,1)S(1)}, bf16[1024,384]{1,0:T(8,128)(2,1)S(1)}) custom-call(bf16[1024,1024]{1,0:T(8,128)(2,1)} %fusion.3.refs_0_.mine_ref, bf16[1024,1024]{1,0:T(8,128)(2,1)} %collective-permute-done.5.refs_1_.theirs_ref, bf16[2048,1152]{1,0:T(8,128)(2,1)S(1)} %copy-done.3, ...), custom_call_target="tpu_custom_call" | custom-call | flops 1000 | bytes 1000 | tf_op jit(solution)/shard_map/columns_product/pallas_call | solution.py:440
  359.2 8.8 %columns_product.11 = (bf16[1024,512]{1,0:T(8,128)(2,1)S(1)}, bf16[1024,512]{1,0:T(8,128)(2,1)S(1)}) custom-call(bf16[1024,1024]{1,0:T(8,128)(2,1)S(1)} %copy-done.17, bf16[1024,1024]{1,0:T(8,128)(2,1)S(1)} %copy-done.21, bf16[2048,2048]{1,0:T(8,128)(2,1)} %get-tuple-element.128.refs_0_.refs_1_, bf16[2048,2048]{1,0:T(8,128)(2,1)} %get-tuple-element.128.refs_0_.refs_1_, ...), custom_call_target="tpu_custom_call" | custom-call | flops 1000 | bytes 1000 | tf_op jit(solution)/shard_map/columns_product/pallas_call | solution.py:440
  369.3 12.3 %attend_back.3 = (bf16[2048,384]{1,0:T(8,128)(2,1)S(1)}, f32[2,1,8,384]{3,2,1,0:T(8,128)S(1)}) custom-call(bf16[2048,1536]{1,0:T(8,128)(2,1)S(1)} %bitcast.122, bf16[2048,1536]{1,0:T(8,128)(2,1)S(1)} %bitcast.122, bf16[2048,1536]{1,0:T(8,128)(2,1)S(1)} %bitcast.122, bf16[2048,512]{1,0:T(8,128)(2,1)S(1)} %copy-done.8, bf16[2048,512]{1,0:T(8,128)(2,1)S(1)} %copy-done.23, ...), custom_call_target="tpu_custom_call" | custom-call | flops 1000 | bytes 1000 | tf_op jit(solution)/shard_map/attend_back/pallas_call | solution.py:162
  381.7 5.4 %columns_product.13 = bf16[1024,384]{1,0:T(8,128)(2,1)S(1)} custom-call(bf16[1024,1024]{1,0:T(8,128)(2,1)} %fusion.3.refs_0_.mine_ref, bf16[1024,1024]{1,0:T(8,128)(2,1)} %collective-permute-done.5.refs_1_.theirs_ref, bf16[2048,384]{1,0:T(8,128)(2,1)S(1)} %get-tuple-element.135.refs_0_), custom_call_target="tpu_custom_call" | custom-call | flops 1000 | bytes 1000 | tf_op jit(solution)/shard_map/columns_product/pallas_call | solution.py:440
  394.9 11.3 %rows_total.6 = (f32[1024,1024]{1,0:T(8,128)S(1)}, bf16[1024,1024]{1,0:T(8,128)(2,1)}) custom-call(bf16[2048,384]{1,0:T(8,128)(2,1)S(1)} %copy-done.30, bf16[2048,1152]{1,0:T(8,128)(2,1)} %copy-done.2, bf16[1024,1536]{1,0:T(8,128)(2,1)S(1)} %bitcast.124), custom_call_target="tpu_custom_call" | custom-call | flops 1000 | bytes 1000 | tf_op jit(solution)/shard_map/rows_total/pallas_call | solution.py:312
  409.5 2.5 slice_add_fusion
  411.9 3.8 collective-permute-done.28
  420.2 12.9 %rows_total.7 = (f32[1024,1024]{1,0:T(8,128)S(1)}, bf16[1024,1024]{1,0:T(8,128)(2,1)}) custom-call(bf16[2048,2048]{1,0:T(8,128)(2,1)} %get-tuple-element.137.refs_0_.refs_1_.refs_2_.refs_3_, bf16[1024,512]{1,0:T(8,128)(2,1)S(1)} %copy-done.10, bf16[1024,512]{1,0:T(8,128)(2,1)S(1)} %pad_maximum_fusion.7.refs_3_.refs_7_.refs_2_.refs_6_, ...), custom_call_target="tpu_custom_call" | custom-call | flops 1000 | bytes 1000 | tf_op jit(solution)/shard_map/rows_total/pallas_call | solution.py:312
  441.7 2.2 copy-done.32
  443.9 2.2 copy-done.34
  446.1 6.0 %first_back.1 = (f32[1024,1024]{1,0:T(8,128)}, f32[2,8,1024]{2,1,0:T(8,128)S(1)}) custom-call(f32[1024,1024]{1,0:T(8,128)S(1)} %copy-done.34, bf16[1024,1024]{1,0:T(8,128)(2,1)} %collective-permute-done.32.refs_1_, bf16[1024,1024]{1,0:T(8,128)(2,1)S(1)} %copy-done.4, f32[1024,1024]{1,0:T(8,128)S(1)} %copy-done.32, ...), custom_call_target="tpu_custom_call" | custom-call | flops 1000 | bytes 1000 | tf_op jit(solution)/shard_map/first_back/pallas_call | solution.py:360
  453.7 2.2 copy-done.36
  455.9 5.8 %last.1 = (bf16[1024,1024]{1,0:T(8,128)(2,1)}, f32[2,8,1024]{2,1,0:T(8,128)S(1)}) custom-call(f32[1024,1024]{1,0:T(8,128)S(1)} %copy-done.36, bf16[1024,1024]{1,0:T(8,128)(2,1)} %collective-permute-done.31.refs_1_, bf16[1024,1024]{1,0:T(8,128)(2,1)S(1)} %copy-done.4, f32[1024,1024]{1,0:T(8,128)} %copy-done.24, bf16[1024,1024]{1,0:T(8,128)(2,1)S(1)} %copy-done.14, ...), custom_call_target="tpu_custom_call" | custom-call | flops 1000 | bytes 1000 | tf_op jit(solution)/shard_map/last/pallas_call | solution.py:360
  462.6 2.9 all-to-all-start.2
  470.2 5.9 %all-to-all-done.2 = f32[32,14,128]{2,1,0:T(8,128)S(1)} async-done(((f32[32,14,128]{2,1,0:T(8,128)}), f32[32,14,128]{2,1,0:T(8,128)S(1)}, u32[]{:S(2)}, u32[]{:S(2)}) %all-to-all-start.2) | async-done | bytes 229408 | tf_op jit(solution)/shard_map/all_to_all | solution.py:589
  478.5 2.6 all-to-all-start.3
  482.8 2.2 fusion.9
  484.9 4.4 all-to-all-done.3
  (313 shorter events, 118.5 us)
Async XLA Ops:
  9.0 16.1 %collective-permute-start.2 = (bf16[256,512]{0,1:T(8,128)(2,1)S(1)}, bf16[256,512]{0,1:T(8,128)(2,1)S(1)}, u32[]{:S(2)}, u32[]{:S(2)}) collective-permute-start(bf16[256,512]{0,1:T(8,128)(2,1)S(1)} %get-tuple-element.253), channel_id=1, source_target_pairs={{0,24},{8,0},{16,8},{24,16},{1,25},{9,1},{17,9},{25,17},{2,26},{10... | collective-permute-start | bytes 786440 | tf_op jit(solution)/shard_map/ppermute | solution.py:532
  14.1 24.5 %collective-permute-start.1 = (bf16[256,512]{0,1:T(8,128)(2,1)S(1)}, bf16[256,512]{0,1:T(8,128)(2,1)S(1)}, u32[]{:S(2)}, u32[]{:S(2)}) collective-permute-start(bf16[256,512]{0,1:T(8,128)(2,1)S(1)} %get-tuple-element.253), channel_id=1, source_target_pairs={{0,16},{8,24},{16,0},{24,8},{1,17},{9,25},{17,1},{25,9},{2,18},{10... | collective-permute-start | bytes 786440 | tf_op jit(solution)/shard_map/ppermute | solution.py:532
  14.1 24.5 %collective-permute-start = (bf16[256,512]{0,1:T(8,128)(2,1)S(1)}, bf16[256,512]{0,1:T(8,128)(2,1)S(1)}, u32[]{:S(2)}, u32[]{:S(2)}) collective-permute-start(bf16[256,512]{0,1:T(8,128)(2,1)S(1)} %get-tuple-element.253), channel_id=1, source_target_pairs={{0,8},{8,16},{16,24},{24,0},{1,9},{9,17},{17,25},{25,1},{2,10},{10... | collective-permute-start | bytes 786440 | tf_op jit(solution)/shard_map/ppermute | solution.py:532
  19.8 23.8 %all-to-all-start = ((bf16[32,16,128]{2,1,0:T(8,128)(2,1)}), bf16[32,16,128]{2,1,0:T(8,128)(2,1)}, u32[]{:S(2)}, u32[]{:S(2)}) async-start(bf16[32,16,128]{2,1,0:T(8,128)(2,1)} %broadcast_in_dim.32), calls=%async_computation | async-start | bytes 262144 | tf_op jit(solution)/shard_map/all_to_all | solution.py:589
  44.6 12.4 %collective-permute-start.4 = (bf16[512,512]{1,0:T(8,128)(2,1)}, bf16[512,512]{1,0:T(8,128)(2,1)}, u32[]{:S(2)}, u32[]{:S(2)}) collective-permute-start(bf16[512,512]{1,0:T(8,128)(2,1)} %get-tuple-element.236), channel_id=1, source_target_pairs={{0,4},{1,5},{2,6},{3,7},{4,0},{5,1},{6,2},{7,3},{8,12},{9,13},{10,... | collective-permute-start | bytes 1572872 | tf_op jit(solution)/shard_map/ppermute | solution.py:505
  47.1 12.1 %collective-permute-start.3 = (bf16[512,512]{1,0:T(8,128)(2,1)}, bf16[512,512]{1,0:T(8,128)(2,1)S(1)}, u32[]{:S(2)}, u32[]{:S(2)}) collective-permute-start(bf16[512,512]{1,0:T(8,128)(2,1)} %get-tuple-element.237), channel_id=1, source_target_pairs={{0,2},{1,3},{2,0},{3,1},{4,6},{5,7},{6,4},{7,5},{8,10},{9,11},{10,... | collective-permute-start | bytes 1572872 | tf_op jit(solution)/shard_map/ppermute | solution.py:505
  64.2 12.8 %all-to-all-start.1 = ((f32[32,6,128]{2,1,0:T(8,128)}), f32[32,6,128]{2,1,0:T(8,128)S(1)}, u32[]{:S(2)}, u32[]{:S(2)}) async-start(f32[32,6,128]{2,1,0:T(8,128)} %copy.101), calls=%async_computation.1 | async-start | bytes 262144 | tf_op jit(solution)/shard_map/all_to_all | solution.py:589
  68.8 36.5 %all-gather.3.cloned.1.call-start = ((), (), s32[]{:S(2)}) async-start(), calls=%async_computation.6 | async-start | bytes 1310720 | tf_op jit(solution)/shard_map/all_gather | solution.py:654
  69.5 80.5 %all-gather.5.cloned.1.call-start = ((), (), s32[]{:S(2)}) async-start(), calls=%async_computation.7 | async-start | bytes 1310720 | tf_op jit(solution)/shard_map/all_gather | solution.py:655
  79.2 34.2 %collective-permute-start.5 = (bf16[1024,1024]{1,0:T(8,128)(2,1)}, bf16[1024,1024]{1,0:T(8,128)(2,1)}, u32[]{:S(2)}, u32[]{:S(2)}) collective-permute-start(bf16[1024,1024]{1,0:T(8,128)(2,1)} %fusion.3.refs_0_.mine_ref), channel_id=1, source_target_pairs={{0,1},{1,0},{2,3},{3,2},{4,5},{5,4},{6,7},{7,6},{8,9},{9,8},{10,11... | collective-permute-start | bytes 6291464 | tf_op jit(solution)/shard_map/ppermute | solution.py:505
  79.4 25.5 %collective-permute-start.7 = (bf16[512,1024]{1,0:T(8,128)(2,1)S(1)}, bf16[512,1024]{1,0:T(8,128)(2,1)}, u32[]{:S(2)}, u32[]{:S(2)}) collective-permute-start(bf16[512,1024]{1,0:T(8,128)(2,1)S(1)} %pad_maximum_fusion.3.c_ref), channel_id=1, source_target_pairs={{0,2},{1,3},{2,0},{3,1},{4,6},{5,7},{6,4},{7,5},{8,10},{9,11},{10,... | collective-permute-start | bytes 3145736 | tf_op jit(solution)/shard_map/ppermute | solution.py:505
  79.8 25.5 %collective-permute-start.6 = (bf16[512,1024]{1,0:T(8,128)(2,1)}, bf16[512,1024]{1,0:T(8,128)(2,1)}, u32[]{:S(2)}, u32[]{:S(2)}) collective-permute-start(bf16[512,1024]{1,0:T(8,128)(2,1)} %pad_maximum_fusion.2.a_ref), channel_id=1, source_target_pairs={{0,4},{1,5},{2,6},{3,7},{4,0},{5,1},{6,2},{7,3},{8,12},{9,13},{10,... | collective-permute-start | bytes 3145736 | tf_op jit(solution)/shard_map/ppermute | solution.py:505
  107.5 16.3 %collective-permute-start.9 = (bf16[1024,256]{1,0:T(8,128)(2,1)}, bf16[1024,256]{1,0:T(8,128)(2,1)}, u32[]{:S(2)}, u32[]{:S(2)}) collective-permute-start(bf16[1024,256]{1,0:T(8,128)(2,1)} %get-tuple-element.234), channel_id=1, source_target_pairs={{0,4},{1,5},{2,6},{3,7},{4,0},{5,1},{6,2},{7,3},{8,12},{9,13},{10,... | collective-permute-start | bytes 1572872 | tf_op jit(solution)/shard_map/ppermute | solution.py:505
  108.5 15.3 %collective-permute-start.8 = (bf16[1024,256]{1,0:T(8,128)(2,1)}, bf16[1024,256]{1,0:T(8,128)(2,1)}, u32[]{:S(2)}, u32[]{:S(2)}) collective-permute-start(bf16[1024,256]{1,0:T(8,128)(2,1)} %get-tuple-element.235), channel_id=1, source_target_pairs={{0,2},{1,3},{2,0},{3,1},{4,6},{5,7},{6,4},{7,5},{8,10},{9,11},{10,... | collective-permute-start | bytes 1572872 | tf_op jit(solution)/shard_map/ppermute | solution.py:505
  110.0 307.7 %reduce-scatter.3.cloned.1.call-start = ((), (), s32[]{:S(2)}) async-start(), calls=%async_computation.8 | async-start | bytes 1310720 | tf_op jit(solution)/shard_map/reduce_scatter | solution.py:722
  125.1 24.9 %collective-permute-start.11 = (bf16[1024,512]{1,0:T(8,128)(2,1)S(1)}, bf16[1024,512]{1,0:T(8,128)(2,1)}, u32[]{:S(2)}, u32[]{:S(2)}) collective-permute-start(bf16[1024,512]{1,0:T(8,128)(2,1)S(1)} %pad_maximum_fusion.5.refs_3_.refs_7_.refs_2_.refs_6_), channel_id=1, source_target_pairs={{0,2},{1,3},{2,0},{3,1},{4,6},{5,7},{6,4},{7,5},{8,10},{9,11},{10,... | collective-permute-start | bytes 3145736 | tf_op jit(solution)/shard_map/ppermute | solution.py:505
  128.1 23.9 %collective-permute-start.10 = (bf16[1024,512]{1,0:T(8,128)(2,1)}, bf16[1024,512]{1,0:T(8,128)(2,1)}, u32[]{:S(2)}, u32[]{:S(2)}) collective-permute-start(bf16[1024,512]{1,0:T(8,128)(2,1)} %pad_maximum_fusion.4.refs_2_.refs_4_.refs_1_.refs_3_), channel_id=1, source_target_pairs={{0,4},{1,5},{2,6},{3,7},{4,0},{5,1},{6,2},{7,3},{8,12},{9,13},{10,... | collective-permute-start | bytes 3145736 | tf_op jit(solution)/shard_map/ppermute | solution.py:505
  153.4 22.1 %collective-permute-start.13 = (bf16[1024,256]{1,0:T(8,128)(2,1)S(1)}, bf16[1024,256]{1,0:T(8,128)(2,1)S(1)}, u32[]{:S(2)}, u32[]{:S(2)}) collective-permute-start(bf16[1024,256]{1,0:T(8,128)(2,1)S(1)} %get-tuple-element.232), channel_id=1, source_target_pairs={{0,4},{1,5},{2,6},{3,7},{4,0},{5,1},{6,2},{7,3},{8,12},{9,13},{10,... | collective-permute-start | bytes 1572872 | tf_op jit(solution)/shard_map/ppermute | solution.py:505
  154.3 21.2 %collective-permute-start.12 = (bf16[1024,256]{1,0:T(8,128)(2,1)S(1)}, bf16[1024,256]{1,0:T(8,128)(2,1)S(1)}, u32[]{:S(2)}, u32[]{:S(2)}) collective-permute-start(bf16[1024,256]{1,0:T(8,128)(2,1)S(1)} %get-tuple-element.233), channel_id=1, source_target_pairs={{0,2},{1,3},{2,0},{3,1},{4,6},{5,7},{6,4},{7,5},{8,10},{9,11},{10,... | collective-permute-start | bytes 1572872 | tf_op jit(solution)/shard_map/ppermute | solution.py:505
  175.4 125.8 %copy-start.7 = (bf16[2048,512]{1,0:T(8,128)(2,1)}, bf16[2048,512]{1,0:T(8,128)(2,1)S(1)}, u32[]{:S(2)}) copy-start(bf16[2048,512]{1,0:T(8,128)(2,1)S(1)} %get-tuple-element.119.refs_0_.mixed_ref) | copy-start | bytes 6291460
  175.6 55.7 %copy-start.9 = (bf16[1024,512]{1,0:T(8,128)(2,1)}, bf16[1024,512]{1,0:T(8,128)(2,1)S(1)}, u32[]{:S(2)}) copy-start(bf16[1024,512]{1,0:T(8,128)(2,1)S(1)} %pad_maximum_fusion.6.refs_2_.refs_4_.refs_1_.refs_3_) | copy-start | bytes 3145732
  182.7 4.2 collective-permute-start.14
  193.3 4.2 collective-permute-start.15
  194.6 26.9 %collective-permute-start.18 = (bf16[1024,1024]{1,0:T(8,128)(2,1)S(1)}, bf16[1024,1024]{1,0:T(8,128)(2,1)S(1)}, u32[]{:S(2)}, u32[]{:S(2)}) collective-permute-start(bf16[1024,1024]{1,0:T(8,128)(2,1)S(1)} %multiply_convert_fusion.mine_ref.refs_0_), channel_id=1, source_target_pairs={{0,1},{1,0},{2,3},{3,2},{4,5},{5,4},{6,7},{7,6},{8,9},{9,8},{10,11... | collective-permute-start | bytes 6291464 | tf_op jit(solution)/shard_map/ppermute | solution.py:505
  194.8 26.7 %collective-permute-start.17 = (bf16[1024,512]{1,0:T(8,128)(2,1)S(1)}, bf16[1024,512]{1,0:T(8,128)(2,1)S(1)}, u32[]{:S(2)}, u32[]{:S(2)}) collective-permute-start(bf16[1024,512]{1,0:T(8,128)(2,1)S(1)} %pad_maximum_fusion.7.refs_3_.refs_7_.refs_2_.refs_6_), channel_id=1, source_target_pairs={{0,2},{1,3},{2,0},{3,1},{4,6},{5,7},{6,4},{7,5},{8,10},{9,11},{10,... | collective-permute-start | bytes 3145736 | tf_op jit(solution)/shard_map/ppermute | solution.py:505
  195.4 26.2 %collective-permute-start.16 = (bf16[1024,512]{1,0:T(8,128)(2,1)S(1)}, bf16[1024,512]{1,0:T(8,128)(2,1)}, u32[]{:S(2)}, u32[]{:S(2)}) collective-permute-start(bf16[1024,512]{1,0:T(8,128)(2,1)S(1)} %pad_maximum_fusion.6.refs_2_.refs_4_.refs_1_.refs_3_), channel_id=1, source_target_pairs={{0,4},{1,5},{2,6},{3,7},{4,0},{5,1},{6,2},{7,3},{8,12},{9,13},{10,... | collective-permute-start | bytes 3145736 | tf_op jit(solution)/shard_map/ppermute | solution.py:505
  229.6 25.3 %collective-permute-start.19 = (bf16[1024,512]{1,0:T(8,128)(2,1)S(1)}, bf16[1024,512]{1,0:T(8,128)(2,1)S(1)}, u32[]{:S(2)}, u32[]{:S(2)}) collective-permute-start(bf16[1024,512]{1,0:T(8,128)(2,1)S(1)} %get-tuple-element.106), channel_id=1, source_target_pairs={{0,4},{1,5},{2,6},{3,7},{4,0},{5,1},{6,2},{7,3},{8,12},{9,13},{10,... | collective-permute-start | bytes 3145736 | tf_op jit(solution)/shard_map/ppermute | solution.py:505
  230.6 25.3 %collective-permute-start.20 = (bf16[1024,512]{1,0:T(8,128)(2,1)S(1)}, bf16[1024,512]{1,0:T(8,128)(2,1)}, u32[]{:S(2)}, u32[]{:S(2)}) collective-permute-start(bf16[1024,512]{1,0:T(8,128)(2,1)S(1)} %get-tuple-element.110), channel_id=1, source_target_pairs={{0,2},{1,3},{2,0},{3,1},{4,6},{5,7},{6,4},{7,5},{8,10},{9,11},{10,... | collective-permute-start | bytes 3145736 | tf_op jit(solution)/shard_map/ppermute | solution.py:505
  270.5 8.0 %collective-permute-start.21 = (bf16[1024,1024]{1,0:T(8,128)(2,1)S(1)}, bf16[1024,1024]{1,0:T(8,128)(2,1)S(1)}, u32[]{:S(2)}, u32[]{:S(2)}) collective-permute-start(bf16[1024,1024]{1,0:T(8,128)(2,1)S(1)} %get-tuple-element.116), channel_id=1, source_target_pairs={{0,1},{1,0},{2,3},{3,2},{4,5},{5,4},{6,7},{7,6},{8,9},{9,8},{10,11... | collective-permute-start | bytes 6291464 | tf_op jit(solution)/shard_map/ppermute | solution.py:505
  290.5 4.3 collective-permute-start.22
  291.0 50.3 %collective-permute-start.23 = (bf16[1024,256]{1,0:T(8,128)(2,1)S(1)}, bf16[1024,256]{1,0:T(8,128)(2,1)S(1)}, u32[]{:S(2)}, u32[]{:S(2)}) collective-permute-start(bf16[1024,256]{1,0:T(8,128)(2,1)S(1)} %get-tuple-element.123), channel_id=1, source_target_pairs={{0,2},{1,3},{2,0},{3,1},{4,6},{5,7},{6,4},{7,5},{8,10},{9,11},{10,... | collective-permute-start | bytes 1572872 | tf_op jit(solution)/shard_map/ppermute | solution.py:505
  291.5 49.9 %collective-permute-start.24 = (bf16[1024,256]{1,0:T(8,128)(2,1)S(1)}, bf16[1024,256]{1,0:T(8,128)(2,1)S(1)}, u32[]{:S(2)}, u32[]{:S(2)}) collective-permute-start(bf16[1024,256]{1,0:T(8,128)(2,1)S(1)} %get-tuple-element.126), channel_id=1, source_target_pairs={{0,4},{1,5},{2,6},{3,7},{4,0},{5,1},{6,2},{7,3},{8,12},{9,13},{10,... | collective-permute-start | bytes 1572872 | tf_op jit(solution)/shard_map/ppermute | solution.py:505
  292.7 66.5 %collective-permute-start.25 = (bf16[1024,1024]{1,0:T(8,128)(2,1)}, bf16[1024,1024]{1,0:T(8,128)(2,1)}, u32[]{:S(2)}, u32[]{:S(2)}) collective-permute-start(bf16[1024,1024]{1,0:T(8,128)(2,1)} %columns_product.8), channel_id=1, source_target_pairs={{0,4},{1,5},{2,6},{3,7},{4,0},{5,1},{6,2},{7,3},{8,12},{9,13},{10,... | collective-permute-start | bytes 6291464 | tf_op jit(solution)/shard_map/ppermute | solution.py:505
  301.2 37.9 %copy-start.38 = (bf16[1024,512]{1,0:T(8,128)(2,1)}, bf16[1024,512]{1,0:T(8,128)(2,1)S(1)}, u32[]{:S(2)}) copy-start(bf16[1024,512]{1,0:T(8,128)(2,1)S(1)} %columns_product.10) | copy-start | bytes 3145732
  342.7 109.4 %reduce-scatter.5.cloned.1.call-start = ((), (), s32[]{:S(2)}) async-start(), calls=%async_computation.9 | async-start | bytes 1310720 | tf_op jit(solution)/shard_map/reduce_scatter | solution.py:722
  356.3 30.9 %collective-permute-start.27 = (bf16[512,1024]{1,0:T(8,128)(2,1)}, bf16[512,1024]{1,0:T(8,128)(2,1)}, u32[]{:S(2)}, u32[]{:S(2)}) collective-permute-start(bf16[512,1024]{1,0:T(8,128)(2,1)} %pad_maximum_fusion.10), channel_id=1, source_target_pairs={{0,2},{1,3},{2,0},{3,1},{4,6},{5,7},{6,4},{7,5},{8,10},{9,11},{10,... | collective-permute-start | bytes 3145736 | tf_op jit(solution)/shard_map/ppermute | solution.py:505
  358.1 32.9 %collective-permute-start.26 = (bf16[512,1024]{1,0:T(8,128)(2,1)}, bf16[512,1024]{1,0:T(8,128)(2,1)}, u32[]{:S(2)}, u32[]{:S(2)}) collective-permute-start(bf16[512,1024]{1,0:T(8,128)(2,1)} %pad_maximum_fusion.9), channel_id=1, source_target_pairs={{0,4},{1,5},{2,6},{3,7},{4,0},{5,1},{6,2},{7,3},{8,12},{9,13},{10,... | collective-permute-start | bytes 3145736 | tf_op jit(solution)/shard_map/ppermute | solution.py:505
  368.0 40.2 %collective-permute-start.30 = (bf16[1024,512]{1,0:T(8,128)(2,1)S(1)}, bf16[1024,512]{1,0:T(8,128)(2,1)S(1)}, u32[]{:S(2)}, u32[]{:S(2)}) collective-permute-start(bf16[1024,512]{1,0:T(8,128)(2,1)S(1)} %get-tuple-element.139), channel_id=1, source_target_pairs={{0,2},{1,3},{2,0},{3,1},{4,6},{5,7},{6,4},{7,5},{8,10},{9,11},{10,... | collective-permute-start | bytes 3145736 | tf_op jit(solution)/shard_map/ppermute | solution.py:505
  389.8 19.7 %collective-permute-start.29 = (bf16[512,512]{1,0:T(8,128)(2,1)}, bf16[512,512]{1,0:T(8,128)(2,1)}, u32[]{:S(2)}, u32[]{:S(2)}) collective-permute-start(bf16[512,512]{1,0:T(8,128)(2,1)} %slice.263), channel_id=1, source_target_pairs={{0,4},{1,5},{2,6},{3,7},{4,0},{5,1},{6,2},{7,3},{8,12},{9,13},{10,... | collective-permute-start | bytes 1572872 | tf_op jit(solution)/shard_map/ppermute | solution.py:505
  394.4 21.4 %collective-permute-start.28 = (bf16[512,512]{1,0:T(8,128)(2,1)}, bf16[512,512]{1,0:T(8,128)(2,1)}, u32[]{:S(2)}, u32[]{:S(2)}) collective-permute-start(bf16[512,512]{1,0:T(8,128)(2,1)} %slice.264), channel_id=1, source_target_pairs={{0,2},{1,3},{2,0},{3,1},{4,6},{5,7},{6,4},{7,5},{8,10},{9,11},{10,... | collective-permute-start | bytes 1572872 | tf_op jit(solution)/shard_map/ppermute | solution.py:505
  408.2 33.6 %collective-permute-start.32 = (bf16[1024,1024]{1,0:T(8,128)(2,1)}, bf16[1024,1024]{1,0:T(8,128)(2,1)}, u32[]{:S(2)}, u32[]{:S(2)}) collective-permute-start(bf16[1024,1024]{1,0:T(8,128)(2,1)} %get-tuple-element.144), channel_id=1, source_target_pairs={{0,1},{1,0},{2,3},{3,2},{4,5},{5,4},{6,7},{7,6},{8,9},{9,8},{10,11... | collective-permute-start | bytes 6291464 | tf_op jit(solution)/shard_map/ppermute | solution.py:505
  435.1 17.1 %collective-permute-start.31 = (bf16[1024,1024]{1,0:T(8,128)(2,1)}, bf16[1024,1024]{1,0:T(8,128)(2,1)}, u32[]{:S(2)}, u32[]{:S(2)}) collective-permute-start(bf16[1024,1024]{1,0:T(8,128)(2,1)} %get-tuple-element.142), channel_id=1, source_target_pairs={{0,1},{1,0},{2,3},{3,2},{4,5},{5,4},{6,7},{7,6},{8,9},{9,8},{10,11... | collective-permute-start | bytes 6291464 | tf_op jit(solution)/shard_map/ppermute | solution.py:505
  437.2 28.3 %collective-permute-start.33 = (bf16[256,512]{0,1:T(8,128)(2,1)S(1)}, bf16[256,512]{0,1:T(8,128)(2,1)}, u32[]{:S(2)}, u32[]{:S(2)}) collective-permute-start(bf16[256,512]{0,1:T(8,128)(2,1)S(1)} %bitcast.141), channel_id=1, source_target_pairs={{0,8},{8,16},{16,24},{24,0},{1,9},{9,17},{17,25},{25,1},{2,10},{10... | collective-permute-start | bytes 786440 | tf_op jit(solution)/shard_map/ppermute | solution.py:547
  438.3 27.2 %collective-permute-start.34 = (bf16[256,512]{0,1:T(8,128)(2,1)S(1)}, bf16[256,512]{0,1:T(8,128)(2,1)}, u32[]{:S(2)}, u32[]{:S(2)}) collective-permute-start(bf16[256,512]{0,1:T(8,128)(2,1)S(1)} %bitcast.142), channel_id=1, source_target_pairs={{0,16},{8,24},{16,0},{24,8},{1,17},{9,25},{17,1},{25,9},{2,18},{10... | collective-permute-start | bytes 786440 | tf_op jit(solution)/shard_map/ppermute | solution.py:547
  439.8 25.7 %collective-permute-start.35 = (bf16[256,512]{0,1:T(8,128)(2,1)S(1)}, bf16[256,512]{0,1:T(8,128)(2,1)}, u32[]{:S(2)}, u32[]{:S(2)}) collective-permute-start(bf16[256,512]{0,1:T(8,128)(2,1)S(1)} %bitcast.143), channel_id=1, source_target_pairs={{0,24},{8,0},{16,8},{24,16},{1,25},{9,1},{17,9},{25,17},{2,26},{10... | collective-permute-start | bytes 786440 | tf_op jit(solution)/shard_map/ppermute | solution.py:547
  462.6 13.5 %all-to-all-start.2 = ((f32[32,14,128]{2,1,0:T(8,128)}), f32[32,14,128]{2,1,0:T(8,128)S(1)}, u32[]{:S(2)}, u32[]{:S(2)}) async-start(f32[32,14,128]{2,1,0:T(8,128)} %bitcast.42), calls=%async_computation.4 | async-start | bytes 524288 | tf_op jit(solution)/shard_map/all_to_all | solution.py:589
  468.3 21.0 %copy-start.63 = (bf16[8,128]{1,0:T(8,128)(2,1)S(1)}, bf16[8,128]{1,0:T(8,128)(2,1)}, u32[]{:S(2)}) copy-start(bf16[8,128]{1,0:T(8,128)(2,1)} %param.14) | copy-start | bytes 6148
  478.5 10.8 %all-to-all-start.3 = ((f32[32,8,128]{2,1,0:T(8,128)}), f32[32,8,128]{2,1,0:T(8,128)S(1)}, u32[]{:S(2)}, u32[]{:S(2)}) async-start(f32[32,8,128]{2,1,0:T(8,128)} %bitcast.46), calls=%async_computation.5 | async-start | bytes 262144 | tf_op jit(solution)/shard_map/all_to_all | solution.py:589
  (63 other events, 328.9 us)
Sparse Core Ops, SparseCore 0:
  71.2 29.1 all-gather.2
  110.2 25.8 all-gather.4
  342.8 24.8 reduce-scatter.2
  409.6 25.7 reduce-scatter.4

commit v5 on v4

--- a/solution.py
+++ b/solution.py
@@ -22,8 +22,20 @@
 BF16 = jnp.bfloat16
 QUERY_ROWS = 512
 TOKEN_ROWS = 32
-VMEM_BYTES = 40 * 1024 * 1024
+VMEM_NEEDS = {
+    "attend": 14,
+    "attend_back": 20,
+    "tokens": 14,
+    "rows": 26,
+    "rows_total": 20,
+    "columns_product": 26,
+    "assemble": 12,
+}
 SMALL_COST = pl.CostEstimate(flops=1000, bytes_accessed=1000, transcendentals=0)
+
+
+def vmem_of(need):
+    return VMEM_NEEDS[need] * 1024 * 1024
 
 
 def dot(left, right, dims=NN):
@@ -150,7 +162,7 @@
             jax.ShapeDtypeStruct((latents, pairs, 2, LEN), F32),
         ],
         input_output_aliases={3 + i: i for i in range(len(earlier))},
-        compiler_params=pltpu.CompilerParams(vmem_limit_bytes=VMEM_BYTES),
+        compiler_params=pltpu.CompilerParams(vmem_limit_bytes=vmem_of("attend")),
         cost_estimate=SMALL_COST,
         name="attend",
     )(projected, projected, projected, *earlier)
@@ -171,20 +183,20 @@
             jax.ShapeDtypeStruct((rows, count * 3 * PAIR), BF16),
             jax.ShapeDtypeStruct((latents, count, 8, 3 * PAIR), F32),
         ],
-        compiler_params=pltpu.CompilerParams(vmem_limit_bytes=VMEM_BYTES),
+        compiler_params=pltpu.CompilerParams(vmem_limit_bytes=vmem_of("attend_back")),
         cost_estimate=SMALL_COST,
         name="attend_back",
     )(projected, projected, projected, mixed, grad_mixed, log_totals)
 
 
-def kernel_call(body, grid, in_specs, out_specs, out_shape, name):
+def kernel_call(body, grid, in_specs, out_specs, out_shape, name, need):
     return pl.pallas_call(
         body,
         grid=grid,
         in_specs=in_specs,
         out_specs=out_specs,
         out_shape=out_shape,
-        compiler_params=pltpu.CompilerParams(vmem_limit_bytes=VMEM_BYTES),
+        compiler_params=pltpu.CompilerParams(vmem_limit_bytes=vmem_of(need)),
         cost_estimate=SMALL_COST,
         name=name,
     )
@@ -268,6 +280,7 @@
         out_specs,
         out_shape,
         "rows_" + kind,
+        "rows",
     )(*pair, *[w[0] for w in weights], extra)
 
 
@@ -323,6 +336,7 @@
             jax.ShapeDtypeStruct((local_rows, width), BF16),
         ],
         "rows_total",
+        "rows_total",
     )(*lefts, *[w[0] for w in weights])
 
 
@@ -364,6 +378,7 @@
         out_specs,
         out_shape,
         name,
+        "tokens",
     )(*arrays, rows_of)
 
 
@@ -446,6 +461,7 @@
         [out_spec(len(ids)) for ids in outs],
         [jax.ShapeDtypeStruct((depth, len(ids) * width), BF16) for ids in outs],
         "columns_product",
+        "columns_product",
     )(*pair, *[right] * len(blocks), *extra)
 
 
@@ -480,6 +496,7 @@
             jax.ShapeDtypeStruct((2, half, blocks * qkv_width), BF16),
             jax.ShapeDtypeStruct((2, half, blocks * out_width), BF16),
         ],
+        "assemble",
         "assemble",
     )(*parts)
     return qkv.reshape(2 * half, -1), out.reshape(2 * half, -1)
@@ -653,11 +670,10 @@
     attn_rows, mark = grid.gather_rows(attn_local)
     fc1_rows = lax.all_gather(after(fc1_local, mark), "row", axis=0, tiled=True)
     fc2_rows = lax.all_gather(after(fc2_local, fc1_rows), "row", axis=0, tiled=True)
-    attn_rows = after(attn_rows, small_all)
     half = D // 2
     top = grid.gather_early(attn_rows[:half], grid.orders[0])
     low = grid.gather_early(attn_rows[half:], grid.orders[1])
-    small_all = after(small_all, top[0], low[0]).reshape(rows, cols, -1)
+    small_all = small_all.reshape(rows, cols, -1)
     cut = seq_rows * col_width
     cond_all = (
         small_all[:, :, :cut]

time: 503 us -> 496 us (0.986)
  Pallas kernels: 248 us -> 230 us
  local copies, waits for them, and re-layouts: 74.2 us -> 89.4 us
  waiting for transfers between devices: 76.8 us -> 69.3 us
    unnamed x143 -> x187, local copies, waits for them, and re-layouts: 52.1 us -> 69 us
    ppermute x3, waiting for transfers between devices: 13.5 us -> 0.01 us  [gather_rows(): lax.ppermute(block, 'row', [(i, (i + step) % count) for i in range(count)])]
    all_to_all x4, waiting for transfers between devices: 17.7 us -> 25.5 us  [all_exchange(): return lax.all_to_all(pieces, ('row', 'col'), 0, 0, tiled=True)]
    pallas_call x7, Pallas kernels: 51.3 us -> 46.2 us  [columns_product(): kernel_call(body, (depth // tile,), [token_spec, token_spec] + [pl.BlockS...]
    pallas_call x4, Pallas kernels: 23.1 us -> 18.1 us  [token_kernel(): kernel_call(kernel, (tokens // tile,), [tokens_spec] * len(arrays) + [who...]
  transfers between devices with their start and end apart: 44 -> 44, of which waited for: 14 -> 14; matrix products, arithmetic and copies ran while one was open for 10% -> 11% of each run, Pallas kernels for 43% -> 41%
where the time goes in v5:
time: 496 us; the launch traced here: 489 us
  Pallas kernels  230 us (46%)
  local copies, waits for them, and re-layouts  89.4 us (18%)
  waiting for transfers between devices  69.3 us (14%)
  starting transfers between devices  51.6 us (10%)
  other arithmetic  28.7 us (6%)
  between operations  15.4 us (3%)
    unnamed x187, local copies, waits for them, and re-layouts  69 us
    pallas_call x2, Pallas kernels, attend_back(): pl.pallas_call(attend_back_kernel, grid=(latents, count), in_specs=[*part...  49.8 us
    pallas_call x7, Pallas kernels, columns_product(): kernel_call(body, (depth // tile,), [token_spec, token_spec] + [pl.BlockS...  46.2 us
    ppermute x30, waiting for transfers between devices, swap(): return lax.ppermute(array, 'col', pairs)  43.7 us
    pallas_call x4, Pallas kernels, rows_product(): kernel_call(body, (2 * count,), [mine, theirs, *[piece_spec(w) for w in w...  41.8 us
    pallas_call x4, Pallas kernels, rows_total(): kernel_call(body, (2 * count,), [pl.BlockSpec((tile, a.shape[1]), lambda...  38.1 us
    pallas_call x2, Pallas kernels, attend(): pl.pallas_call(attend_kernel, grid=(latents, count), in_specs=parts + [pl...  33.7 us
    ppermute x30, starting transfers between devices, swap(): return lax.ppermute(array, 'col', pairs)  26.1 us
  transfers between devices with their start and end apart: 44, of which 14 were waited for; matrix products, arithmetic and copies ran while one was open for 11% of the time, Pallas kernels for 41%

profile of v5, /device:TPU:0, one launch (start us, length us, event | category | flops | bytes accessed | tf_op | source)
XLA Modules:
  0.0 489.1 jit_solution(7103023085279695371)
XLA Ops:
  9.1 5.1 %collective-permute-start.3 = (bf16[256,512]{0,1:T(8,128)(2,1)S(1)}, bf16[256,512]{0,1:T(8,128)(2,1)S(1)}, u32[]{:S(2)}, u32[]{:S(2)}) collective-permute-start(bf16[256,512]{0,1:T(8,128)(2,1)S(1)} %get-tuple-element.247), channel_id=1, source_target_pairs={{0,24},{8,0},{16,8},{24,16},{1,25},{9,1},{17,9},{25,17},{2,26},{10... | collective-permute-start | bytes 786440 | tf_op jit(solution)/shard_map/ppermute | solution.py:549
  19.9 5.6 %all-to-all-start = ((bf16[32,16,128]{2,1,0:T(8,128)(2,1)}), bf16[32,16,128]{2,1,0:T(8,128)(2,1)S(1)}, u32[]{:S(2)}, u32[]{:S(2)}) async-start(bf16[32,16,128]{2,1,0:T(8,128)(2,1)} %broadcast_in_dim.32), calls=%async_computation | async-start | bytes 262144 | tf_op jit(solution)/shard_map/all_to_all | solution.py:606
  25.5 2.3 convert_reduce_fusion
  28.1 12.8 %all-to-all-done = bf16[32,16,128]{2,1,0:T(8,128)(2,1)S(1)} async-done(((bf16[32,16,128]{2,1,0:T(8,128)(2,1)}), bf16[32,16,128]{2,1,0:T(8,128)(2,1)S(1)}, u32[]{:S(2)}, u32[]{:S(2)}) %all-to-all-start) | async-done | bytes 131104 | tf_op jit(solution)/shard_map/all_to_all | solution.py:606
  42.1 3.4 all-to-all-start.1
  51.4 2.4 all-to-all-done.1
  57.0 5.2 %collective-permute-done.6 = bf16[512,512]{1,0:T(8,128)(2,1)} collective-permute-done((bf16[512,512]{1,0:T(8,128)(2,1)}, bf16[512,512]{1,0:T(8,128)(2,1)}, u32[]{:S(2)}, u32[]{:S(2)}) %collective-permute-start.6) | collective-permute-done | bytes 524320 | tf_op jit(solution)/shard_map/ppermute | solution.py:522
  70.9 17.4 %collective-permute-done.7.d_ref = bf16[512,1024]{1,0:T(8,128)(2,1)} collective-permute-done((bf16[512,1024]{1,0:T(8,128)(2,1)S(1)}, bf16[512,1024]{1,0:T(8,128)(2,1)}, u32[]{:S(2)}, u32[]{:S(2)}) %collective-permute-start.7) | collective-permute-done | bytes 1048608 | tf_op jit(solution)/shard_map/ppermute | solution.py:522
  88.3 3.3 collective-permute-done.5.b_ref
  96.6 2.9 assemble.1
  100.5 10.0 %rows_bias.2.q_ref.k_ref.v_ref = bf16[2048,1536]{1,0:T(8,128)(2,1)S(1)} custom-call(bf16[1024,1024]{1,0:T(8,128)(2,1)} %fusion.3.refs_0_.mine_ref, bf16[1024,1024]{1,0:T(8,128)(2,1)} %collective-permute-done.refs_1_.theirs_ref, bf16[1024,1536]{1,0:T(8,128)(2,1)S(1)} %bitcast.127, f32[1,1536]{1,0:T(1,128)S(1)} %reshape.212.refs_3_), custom_call_target="tpu_custom_call" | custom-call | flops 1000 | bytes 1000 | tf_op jit(solution)/shard_map/rows_bias/pallas_call | solution.py:276
  113.2 2.3 pad_maximum_fusion.3.refs_2_.refs_4_.refs_1_.refs_3_
  116.1 16.8 %attend.2 = (bf16[2048,512]{1,0:T(8,128)(2,1)S(1)}, f32[2,4,2,1024]{3,2,1,0:T(2,128)S(1)}) custom-call(bf16[2048,1536]{1,0:T(8,128)(2,1)S(1)} %rows_bias.2.q_ref.k_ref.v_ref, bf16[2048,1536]{1,0:T(8,128)(2,1)S(1)} %rows_bias.2.q_ref.k_ref.v_ref, bf16[2048,1536]{1,0:T(8,128)(2,1)S(1)} %rows_bias.2.q_ref.k_ref.v_ref), custom_call_target="tpu_custom_call" | custom-call | flops 1000 | bytes 1000 | tf_op jit(solution)/shard_map/attend/pallas_call | solution.py:155
  133.0 2.6 copy-done
  141.1 2.8 copy-done.1
  143.9 16.8 %attend.3 = (bf16[2048,512]{1,0:T(8,128)(2,1)S(1)}, f32[2,4,2,1024]{3,2,1,0:T(2,128)S(1)}) custom-call(bf16[2048,1536]{1,0:T(8,128)(2,1)S(1)} %copy-done.1, bf16[2048,1536]{1,0:T(8,128)(2,1)S(1)} %copy-done.1, bf16[2048,1536]{1,0:T(8,128)(2,1)S(1)} %copy-done.1, bf16[2048,512]{1,0:T(8,128)(2,1)S(1)} %copy-done.10, ...), custom_call_target="tpu_custom_call", output_to_operand_aliasing={{0}: (3, {}), {1}: (4, {})} | custom-call | flops 1000 | bytes 1000 | tf_op jit(solution)/shard_map/attend/pallas_call | solution.py:155
  162.8 3.3 rows_total.4
  166.2 4.1 collective-permute-done.14.refs_1_
  178.6 18.3 %rows_gelu.1 = (bf16[2048,2048]{1,0:T(8,128)(2,1)S(1)}, bf16[2048,2048]{1,0:T(8,128)(2,1)S(1)}) custom-call(bf16[1024,1024]{1,0:T(8,128)(2,1)S(1)} %get-tuple-element.97.refs_0_.mine_ref, bf16[1024,1024]{1,0:T(8,128)(2,1)S(1)} %collective-permute-done.15.refs_1_.theirs_ref, bf16[1024,512]{1,0:T(8,128)(2,1)} %pad_maximum_fusion.3.refs_2_.refs_4_.refs_1_.refs_3_, ...), custom_call_target="tpu_custom_call" | custom-call | flops 1000 | bytes 1000 | tf_op jit(solution)/shard_map/rows_gelu/pallas_call | solution.py:276
  196.9 3.9 collective-permute-done.17.refs_5_.refs_9_.refs_4_.refs_8_
  201.8 7.1 %columns_product.7 = (bf16[1024,512]{1,0:T(8,128)(2,1)}, bf16[1024,512]{1,0:T(8,128)(2,1)}) custom-call(bf16[1024,1024]{1,0:T(8,128)(2,1)S(1)} %multiply_convert_fusion.mine_ref.refs_0_, bf16[1024,1024]{1,0:T(8,128)(2,1)S(1)} %collective-permute-done.18.theirs_ref.refs_1_, bf16[2048,2048]{1,0:T(8,128)(2,1)S(1)} %get-tuple-element.133.refs_0_.refs_1_.refs_2_.refs_3_, ...), custom_call_target="tpu_custom_call" | custom-call | flops 1000 | bytes 1000 | tf_op jit(solution)/shard_map/columns_product/pallas_call | solution.py:455
  216.7 3.4 copy-done.47
  220.1 10.7 %rows_slope.1 = (bf16[2048,2048]{1,0:T(8,128)(2,1)S(1)}, f32[8,2048]{1,0:T(8,128)S(1)}) custom-call(bf16[1024,1024]{1,0:T(8,128)(2,1)S(1)} %copy-done.14, bf16[1024,1024]{1,0:T(8,128)(2,1)S(1)} %copy-done.25, bf16[1024,512]{1,0:T(8,128)(2,1)S(1)} %pad_maximum_fusion.5.refs_2_.refs_4_.refs_1_.refs_3_, ...), custom_call_target="tpu_custom_call" | custom-call | flops 1000 | bytes 1000 | tf_op jit(solution)/shard_map/rows_slope/pallas_call | solution.py:276
  230.8 3.1 copy-done.28
  236.0 6.9 %columns_product.8 = bf16[1024,1024]{1,0:T(8,128)(2,1)} custom-call(bf16[1024,1024]{1,0:T(8,128)(2,1)S(1)} %copy-done.28, bf16[1024,1024]{1,0:T(8,128)(2,1)S(1)} %copy-done.31, bf16[2048,2048]{1,0:T(8,128)(2,1)S(1)} %get-tuple-element.124.refs_0_.refs_1_, bf16[2048,2048]{1,0:T(8,128)(2,1)S(1)} %get-tuple-element.124.refs_0_.refs_1_), custom_call_target="tpu_custom_call" | custom-call | flops 1000 | bytes 1000 | tf_op jit(solution)/shard_map/columns_product/pallas_call | solution.py:455
  243.8 13.5 %rows_total.5 = (f32[1024,1024]{1,0:T(8,128)S(1)}, bf16[1024,1024]{1,0:T(8,128)(2,1)}) custom-call(bf16[2048,2048]{1,0:T(8,128)(2,1)S(1)} %get-tuple-element.124.refs_0_.refs_1_, bf16[1024,512]{1,0:T(8,128)(2,1)} %pad_maximum_fusion.3.refs_2_.refs_4_.refs_1_.refs_3_, bf16[1024,512]{1,0:T(8,128)(2,1)S(1)} %copy-done.20, ...), custom_call_target="tpu_custom_call" | custom-call | flops 1000 | bytes 1000 | tf_op jit(solution)/shard_map/rows_total/pallas_call | solution.py:325
  260.6 8.0 %columns_product.9 = (bf16[1024,256]{1,0:T(8,128)(2,1)S(1)}, bf16[1024,256]{1,0:T(8,128)(2,1)}, bf16[1024,256]{1,0:T(8,128)(2,1)S(1)}, bf16[1024,256]{1,0:T(8,128)(2,1)}) custom-call(bf16[1024,1024]{1,0:T(8,128)(2,1)S(1)} %copy-done.15, bf16[1024,1024]{1,0:T(8,128)(2,1)S(1)} %copy-done.26, ...), custom_call_target="tpu_custom_call" | custom-call | flops 1000 | bytes 1000 | tf_op jit(solution)/shard_map/columns_product/pallas_call | solution.py:455
  268.6 4.6 middle_back.1
  279.6 2.9 rows_bias.3.grad_ref
  282.5 3.6 columns_product.10
  286.1 37.5 %attend_back.2 = (bf16[2048,1152]{1,0:T(8,128)(2,1)S(1)}, f32[2,3,8,384]{3,2,1,0:T(8,128)S(1)}) custom-call(bf16[2048,1536]{1,0:T(8,128)(2,1)S(1)} %bitcast.122, bf16[2048,1536]{1,0:T(8,128)(2,1)S(1)} %bitcast.122, bf16[2048,1536]{1,0:T(8,128)(2,1)S(1)} %bitcast.122, bf16[2048,512]{1,0:T(8,128)(2,1)S(1)} %get-tuple-element.115.refs_0_.mixed_ref, ...), custom_call_target="tpu_custom_call" | custom-call | flops 1000 | bytes 1000 | tf_op jit(solution)/shard_map/attend_back/pallas_call | solution.py:174
  327.3 2.3 copy-done.7
  329.6 8.9 %columns_product.12 = (bf16[1024,384]{1,0:T(8,128)(2,1)S(1)}, bf16[1024,384]{1,0:T(8,128)(2,1)S(1)}, bf16[1024,384]{1,0:T(8,128)(2,1)S(1)}) custom-call(bf16[1024,1024]{1,0:T(8,128)(2,1)} %fusion.3.refs_0_.mine_ref, bf16[1024,1024]{1,0:T(8,128)(2,1)} %collective-permute-done.refs_1_.theirs_ref, bf16[2048,1152]{1,0:T(8,128)(2,1)S(1)} %copy-done.7, ...), custom_call_target="tpu_custom_call" | custom-call | flops 1000 | bytes 1000 | tf_op jit(solution)/shard_map/columns_product/pallas_call | solution.py:455
  341.5 3.9 copy-done.5
  345.4 6.8 %columns_product.11 = (bf16[1024,512]{1,0:T(8,128)(2,1)S(1)}, bf16[1024,512]{1,0:T(8,128)(2,1)S(1)}) custom-call(bf16[1024,1024]{1,0:T(8,128)(2,1)S(1)} %copy-done.29, bf16[1024,1024]{1,0:T(8,128)(2,1)S(1)} %copy-done.32, bf16[2048,2048]{1,0:T(8,128)(2,1)S(1)} %copy-done.5, bf16[2048,2048]{1,0:T(8,128)(2,1)S(1)} %copy-done.5, ...), custom_call_target="tpu_custom_call" | custom-call | flops 1000 | bytes 1000 | tf_op jit(solution)/shard_map/columns_product/pallas_call | solution.py:455
  353.3 12.4 %attend_back.3 = (bf16[2048,384]{1,0:T(8,128)(2,1)S(1)}, f32[2,1,8,384]{3,2,1,0:T(8,128)S(1)}) custom-call(bf16[2048,1536]{1,0:T(8,128)(2,1)S(1)} %bitcast.124, bf16[2048,1536]{1,0:T(8,128)(2,1)S(1)} %bitcast.124, bf16[2048,1536]{1,0:T(8,128)(2,1)S(1)} %bitcast.124, bf16[2048,512]{1,0:T(8,128)(2,1)S(1)} %copy-done.12, bf16[2048,512]{1,0:T(8,128)(2,1)S(1)} %copy-done.34, ...), custom_call_target="tpu_custom_call" | custom-call | flops 1000 | bytes 1000 | tf_op jit(solution)/shard_map/attend_back/pallas_call | solution.py:174
  365.7 5.0 %columns_product.13 = bf16[1024,384]{1,0:T(8,128)(2,1)S(1)} custom-call(bf16[1024,1024]{1,0:T(8,128)(2,1)} %fusion.3.refs_0_.mine_ref, bf16[1024,1024]{1,0:T(8,128)(2,1)} %collective-permute-done.refs_1_.theirs_ref, bf16[2048,384]{1,0:T(8,128)(2,1)S(1)} %get-tuple-element.131.refs_0_), custom_call_target="tpu_custom_call" | custom-call | flops 1000 | bytes 1000 | tf_op jit(solution)/shard_map/columns_product/pallas_call | solution.py:455
  376.0 9.9 %rows_total.6 = (f32[1024,1024]{1,0:T(8,128)S(1)}, bf16[1024,1024]{1,0:T(8,128)(2,1)}) custom-call(bf16[2048,384]{1,0:T(8,128)(2,1)S(1)} %get-tuple-element.131.refs_0_, bf16[2048,1152]{1,0:T(8,128)(2,1)S(1)} %bitcast.126, bf16[1024,1536]{1,0:T(8,128)(2,1)S(1)} %bitcast.128), custom_call_target="tpu_custom_call" | custom-call | flops 1000 | bytes 1000 | tf_op jit(solution)/shard_map/rows_total/pallas_call | solution.py:325
  389.2 2.5 slice_add_fusion
  391.7 6.7 %collective-permute-done.28 = bf16[512,512]{1,0:T(8,128)(2,1)} collective-permute-done((bf16[512,512]{1,0:T(8,128)(2,1)}, bf16[512,512]{1,0:T(8,128)(2,1)}, u32[]{:S(2)}, u32[]{:S(2)}) %collective-permute-start.28) | collective-permute-done | bytes 524320 | tf_op jit(solution)/shard_map/ppermute | solution.py:522
  400.4 3.4 copy-done.3
  407.5 11.3 %rows_total.7 = (f32[1024,1024]{1,0:T(8,128)S(1)}, bf16[1024,1024]{1,0:T(8,128)(2,1)}) custom-call(bf16[2048,2048]{1,0:T(8,128)(2,1)S(1)} %copy-done.3, bf16[1024,512]{1,0:T(8,128)(2,1)S(1)} %copy-done.17, bf16[1024,512]{1,0:T(8,128)(2,1)S(1)} %pad_maximum_fusion.6.refs_3_.refs_7_.refs_2_.refs_6_, bf16[1024,512]{1,0:T(8,128)(2,1)S(1)} %copy-done.17, ...), custom_call_target="tpu_custom_call" | custom-call | flops 1000 | bytes 1000 | tf_op jit(solution)/shard_map/rows_total/pallas_call | solution.py:325
  437.2 6.2 %first_back.1 = (f32[1024,1024]{1,0:T(8,128)}, f32[2,8,1024]{2,1,0:T(8,128)S(1)}) custom-call(f32[1024,1024]{1,0:T(8,128)S(1)} %copy-done.51, bf16[1024,1024]{1,0:T(8,128)(2,1)} %collective-permute-done.32.refs_1_, bf16[1024,1024]{1,0:T(8,128)(2,1)S(1)} %copy-done.8, f32[1024,1024]{1,0:T(8,128)S(1)} %copy-done.49, ...), custom_call_target="tpu_custom_call" | custom-call | flops 1000 | bytes 1000 | tf_op jit(solution)/shard_map/first_back/pallas_call | solution.py:374
  449.3 5.1 %last.1 = (bf16[1024,1024]{1,0:T(8,128)(2,1)}, f32[2,8,1024]{2,1,0:T(8,128)S(1)}) custom-call(f32[1024,1024]{1,0:T(8,128)S(1)} %copy-done.53, bf16[1024,1024]{1,0:T(8,128)(2,1)} %collective-permute-done.31.refs_1_, bf16[1024,1024]{1,0:T(8,128)(2,1)S(1)} %copy-done.8, f32[1024,1024]{1,0:T(8,128)S(1)} %copy-done.37, bf16[1024,1024]{1,0:T(8,128)(2,1)S(1)} %copy-done.23, ...), custom_call_target="tpu_custom_call" | custom-call | flops 1000 | bytes 1000 | tf_op jit(solution)/shard_map/last/pallas_call | solution.py:374
  455.3 2.6 all-to-all-start.2
  462.6 5.9 %all-to-all-done.2 = f32[32,14,128]{2,1,0:T(8,128)S(1)} async-done(((f32[32,14,128]{2,1,0:T(8,128)}), f32[32,14,128]{2,1,0:T(8,128)S(1)}, u32[]{:S(2)}, u32[]{:S(2)}) %all-to-all-start.2) | async-done | bytes 229408 | tf_op jit(solution)/shard_map/all_to_all | solution.py:606
  470.9 2.6 all-to-all-start.3
  477.3 4.4 all-to-all-done.3
  (359 shorter events, 131.4 us)
Async XLA Ops:
  9.1 36.4 %collective-permute-start.3 = (bf16[256,512]{0,1:T(8,128)(2,1)S(1)}, bf16[256,512]{0,1:T(8,128)(2,1)S(1)}, u32[]{:S(2)}, u32[]{:S(2)}) collective-permute-start(bf16[256,512]{0,1:T(8,128)(2,1)S(1)} %get-tuple-element.247), channel_id=1, source_target_pairs={{0,24},{8,0},{16,8},{24,16},{1,25},{9,1},{17,9},{25,17},{2,26},{10... | collective-permute-start | bytes 786440 | tf_op jit(solution)/shard_map/ppermute | solution.py:549
  14.2 31.3 %collective-permute-start.1 = (bf16[256,512]{0,1:T(8,128)(2,1)S(1)}, bf16[256,512]{0,1:T(8,128)(2,1)S(1)}, u32[]{:S(2)}, u32[]{:S(2)}) collective-permute-start(bf16[256,512]{0,1:T(8,128)(2,1)S(1)} %get-tuple-element.247), channel_id=1, source_target_pairs={{0,8},{8,16},{16,24},{24,0},{1,9},{9,17},{17,25},{25,1},{2,10},{10... | collective-permute-start | bytes 786440 | tf_op jit(solution)/shard_map/ppermute | solution.py:549
  14.2 31.3 %collective-permute-start.2 = (bf16[256,512]{0,1:T(8,128)(2,1)S(1)}, bf16[256,512]{0,1:T(8,128)(2,1)S(1)}, u32[]{:S(2)}, u32[]{:S(2)}) collective-permute-start(bf16[256,512]{0,1:T(8,128)(2,1)S(1)} %get-tuple-element.247), channel_id=1, source_target_pairs={{0,16},{8,24},{16,0},{24,8},{1,17},{9,25},{17,1},{25,9},{2,18},{10... | collective-permute-start | bytes 786440 | tf_op jit(solution)/shard_map/ppermute | solution.py:549
  19.9 21.1 %all-to-all-start = ((bf16[32,16,128]{2,1,0:T(8,128)(2,1)}), bf16[32,16,128]{2,1,0:T(8,128)(2,1)S(1)}, u32[]{:S(2)}, u32[]{:S(2)}) async-start(bf16[32,16,128]{2,1,0:T(8,128)(2,1)} %broadcast_in_dim.32), calls=%async_computation | async-start | bytes 262144 | tf_op jit(solution)/shard_map/all_to_all | solution.py:606
  42.1 11.7 %all-to-all-start.1 = ((f32[32,6,128]{2,1,0:T(8,128)}), f32[32,6,128]{2,1,0:T(8,128)}, u32[]{:S(2)}, u32[]{:S(2)}) async-start(f32[32,6,128]{2,1,0:T(8,128)} %copy.96), calls=%async_computation.1 | async-start | bytes 262144 | tf_op jit(solution)/shard_map/all_to_all | solution.py:606
  45.4 46.2 %all-gather.3.cloned.1.call-start = ((), (), s32[]{:S(2)}) async-start(), calls=%async_computation.6 | async-start | bytes 1310720 | tf_op jit(solution)/shard_map/all_gather | solution.py:671
  46.9 15.2 %collective-permute-start.6 = (bf16[512,512]{1,0:T(8,128)(2,1)}, bf16[512,512]{1,0:T(8,128)(2,1)}, u32[]{:S(2)}, u32[]{:S(2)}) collective-permute-start(bf16[512,512]{1,0:T(8,128)(2,1)} %pad_maximum_fusion.12), channel_id=1, source_target_pairs={{0,4},{1,5},{2,6},{3,7},{4,0},{5,1},{6,2},{7,3},{8,12},{9,13},{10,... | collective-permute-start | bytes 1572872 | tf_op jit(solution)/shard_map/ppermute | solution.py:522
  49.8 15.1 %collective-permute-start.4 = (bf16[512,512]{1,0:T(8,128)(2,1)}, bf16[512,512]{1,0:T(8,128)(2,1)}, u32[]{:S(2)}, u32[]{:S(2)}) collective-permute-start(bf16[512,512]{1,0:T(8,128)(2,1)} %pad_maximum_fusion.11), channel_id=1, source_target_pairs={{0,2},{1,3},{2,0},{3,1},{4,6},{5,7},{6,4},{7,5},{8,10},{9,11},{10,... | collective-permute-start | bytes 1572872 | tf_op jit(solution)/shard_map/ppermute | solution.py:522
  51.3 85.6 %all-gather.5.cloned.1.call-start = ((), (), s32[]{:S(2)}) async-start(), calls=%async_computation.7 | async-start | bytes 1310720 | tf_op jit(solution)/shard_map/all_gather | solution.py:672
  56.9 43.6 %collective-permute-start = (bf16[1024,1024]{1,0:T(8,128)(2,1)}, bf16[1024,1024]{1,0:T(8,128)(2,1)}, u32[]{:S(2)}, u32[]{:S(2)}) collective-permute-start(bf16[1024,1024]{1,0:T(8,128)(2,1)} %fusion.3.refs_0_.mine_ref), channel_id=1, source_target_pairs={{0,1},{1,0},{2,3},{3,2},{4,5},{5,4},{6,7},{7,6},{8,9},{9,8},{10,11... | collective-permute-start | bytes 6291464 | tf_op jit(solution)/shard_map/ppermute | solution.py:522
  63.4 24.8 %collective-permute-start.7 = (bf16[512,1024]{1,0:T(8,128)(2,1)S(1)}, bf16[512,1024]{1,0:T(8,128)(2,1)}, u32[]{:S(2)}, u32[]{:S(2)}) collective-permute-start(bf16[512,1024]{1,0:T(8,128)(2,1)S(1)} %pad_maximum_fusion.2.c_ref), channel_id=1, source_target_pairs={{0,2},{1,3},{2,0},{3,1},{4,6},{5,7},{6,4},{7,5},{8,10},{9,11},{10,... | collective-permute-start | bytes 3145736 | tf_op jit(solution)/shard_map/ppermute | solution.py:522
  67.0 24.6 %collective-permute-start.5 = (bf16[512,1024]{1,0:T(8,128)(2,1)}, bf16[512,1024]{1,0:T(8,128)(2,1)}, u32[]{:S(2)}, u32[]{:S(2)}) collective-permute-start(bf16[512,1024]{1,0:T(8,128)(2,1)} %pad_maximum_fusion.1.a_ref), channel_id=1, source_target_pairs={{0,4},{1,5},{2,6},{3,7},{4,0},{5,1},{6,2},{7,3},{8,12},{9,13},{10,... | collective-permute-start | bytes 3145736 | tf_op jit(solution)/shard_map/ppermute | solution.py:522
  93.8 16.7 %collective-permute-start.9 = (bf16[1024,256]{1,0:T(8,128)(2,1)}, bf16[1024,256]{1,0:T(8,128)(2,1)}, u32[]{:S(2)}, u32[]{:S(2)}) collective-permute-start(bf16[1024,256]{1,0:T(8,128)(2,1)} %get-tuple-element.230), channel_id=1, source_target_pairs={{0,4},{1,5},{2,6},{3,7},{4,0},{5,1},{6,2},{7,3},{8,12},{9,13},{10,... | collective-permute-start | bytes 1572872 | tf_op jit(solution)/shard_map/ppermute | solution.py:522
  95.2 15.3 %collective-permute-start.8 = (bf16[1024,256]{1,0:T(8,128)(2,1)}, bf16[1024,256]{1,0:T(8,128)(2,1)}, u32[]{:S(2)}, u32[]{:S(2)}) collective-permute-start(bf16[1024,256]{1,0:T(8,128)(2,1)} %get-tuple-element.231), channel_id=1, source_target_pairs={{0,2},{1,3},{2,0},{3,1},{4,6},{5,7},{6,4},{7,5},{8,10},{9,11},{10,... | collective-permute-start | bytes 1572872 | tf_op jit(solution)/shard_map/ppermute | solution.py:522
  96.2 304.2 %reduce-scatter.3.cloned.1.call-start = ((), (), s32[]{:S(2)}) async-start(), calls=%async_computation.8 | async-start | bytes 1310720 | tf_op jit(solution)/shard_map/reduce_scatter | solution.py:738
  111.8 25.1 %collective-permute-start.11 = (bf16[1024,512]{1,0:T(8,128)(2,1)S(1)}, bf16[1024,512]{1,0:T(8,128)(2,1)}, u32[]{:S(2)}, u32[]{:S(2)}) collective-permute-start(bf16[1024,512]{1,0:T(8,128)(2,1)S(1)} %pad_maximum_fusion.4.refs_3_.refs_7_.refs_2_.refs_6_), channel_id=1, source_target_pairs={{0,2},{1,3},{2,0},{3,1},{4,6},{5,7},{6,4},{7,5},{8,10},{9,11},{10,... | collective-permute-start | bytes 3145736 | tf_op jit(solution)/shard_map/ppermute | solution.py:522
  115.5 22.9 %collective-permute-start.10 = (bf16[1024,512]{1,0:T(8,128)(2,1)}, bf16[1024,512]{1,0:T(8,128)(2,1)}, u32[]{:S(2)}, u32[]{:S(2)}) collective-permute-start(bf16[1024,512]{1,0:T(8,128)(2,1)} %pad_maximum_fusion.3.refs_2_.refs_4_.refs_1_.refs_3_), channel_id=1, source_target_pairs={{0,4},{1,5},{2,6},{3,7},{4,0},{5,1},{6,2},{7,3},{8,12},{9,13},{10,... | collective-permute-start | bytes 3145736 | tf_op jit(solution)/shard_map/ppermute | solution.py:522
  139.6 21.2 %collective-permute-start.13 = (bf16[1024,256]{1,0:T(8,128)(2,1)S(1)}, bf16[1024,256]{1,0:T(8,128)(2,1)S(1)}, u32[]{:S(2)}, u32[]{:S(2)}) collective-permute-start(bf16[1024,256]{1,0:T(8,128)(2,1)S(1)} %get-tuple-element.228), channel_id=1, source_target_pairs={{0,4},{1,5},{2,6},{3,7},{4,0},{5,1},{6,2},{7,3},{8,12},{9,13},{10,... | collective-permute-start | bytes 1572872 | tf_op jit(solution)/shard_map/ppermute | solution.py:522
  140.3 20.6 %collective-permute-start.12 = (bf16[1024,256]{1,0:T(8,128)(2,1)S(1)}, bf16[1024,256]{1,0:T(8,128)(2,1)S(1)}, u32[]{:S(2)}, u32[]{:S(2)}) collective-permute-start(bf16[1024,256]{1,0:T(8,128)(2,1)S(1)} %get-tuple-element.229), channel_id=1, source_target_pairs={{0,2},{1,3},{2,0},{3,1},{4,6},{5,7},{6,4},{7,5},{8,10},{9,11},{10,... | collective-permute-start | bytes 1572872 | tf_op jit(solution)/shard_map/ppermute | solution.py:522
  160.8 125.3 %copy-start.11 = (bf16[2048,512]{1,0:T(8,128)(2,1)}, bf16[2048,512]{1,0:T(8,128)(2,1)S(1)}, u32[]{:S(2)}) copy-start(bf16[2048,512]{1,0:T(8,128)(2,1)S(1)} %get-tuple-element.115.refs_0_.mixed_ref) | copy-start | bytes 6291460
  161.0 50.1 %copy-start.16 = (bf16[1024,512]{1,0:T(8,128)(2,1)}, bf16[1024,512]{1,0:T(8,128)(2,1)S(1)}, u32[]{:S(2)}) copy-start(bf16[1024,512]{1,0:T(8,128)(2,1)S(1)} %pad_maximum_fusion.5.refs_2_.refs_4_.refs_1_.refs_3_) | copy-start | bytes 3145732
  166.1 4.2 collective-permute-start.14
  174.5 4.2 collective-permute-start.15
  175.2 26.6 %collective-permute-start.18 = (bf16[1024,1024]{1,0:T(8,128)(2,1)S(1)}, bf16[1024,1024]{1,0:T(8,128)(2,1)S(1)}, u32[]{:S(2)}, u32[]{:S(2)}) collective-permute-start(bf16[1024,1024]{1,0:T(8,128)(2,1)S(1)} %multiply_convert_fusion.mine_ref.refs_0_), channel_id=1, source_target_pairs={{0,1},{1,0},{2,3},{3,2},{4,5},{5,4},{6,7},{7,6},{8,9},{9,8},{10,11... | collective-permute-start | bytes 6291464 | tf_op jit(solution)/shard_map/ppermute | solution.py:522
  175.7 25.2 %collective-permute-start.17 = (bf16[1024,512]{1,0:T(8,128)(2,1)S(1)}, bf16[1024,512]{1,0:T(8,128)(2,1)S(1)}, u32[]{:S(2)}, u32[]{:S(2)}) collective-permute-start(bf16[1024,512]{1,0:T(8,128)(2,1)S(1)} %pad_maximum_fusion.6.refs_3_.refs_7_.refs_2_.refs_6_), channel_id=1, source_target_pairs={{0,2},{1,3},{2,0},{3,1},{4,6},{5,7},{6,4},{7,5},{8,10},{9,11},{10,... | collective-permute-start | bytes 3145736 | tf_op jit(solution)/shard_map/ppermute | solution.py:522
  176.9 24.9 %collective-permute-start.16 = (bf16[1024,512]{1,0:T(8,128)(2,1)S(1)}, bf16[1024,512]{1,0:T(8,128)(2,1)S(1)}, u32[]{:S(2)}, u32[]{:S(2)}) collective-permute-start(bf16[1024,512]{1,0:T(8,128)(2,1)S(1)} %pad_maximum_fusion.5.refs_2_.refs_4_.refs_1_.refs_3_), channel_id=1, source_target_pairs={{0,4},{1,5},{2,6},{3,7},{4,0},{5,1},{6,2},{7,3},{8,12},{9,13},{10,... | collective-permute-start | bytes 3145736 | tf_op jit(solution)/shard_map/ppermute | solution.py:522
  196.9 62.4 %copy-start.2 = (bf16[2048,2048]{1,0:T(8,128)(2,1)}, bf16[2048,2048]{1,0:T(8,128)(2,1)S(1)}, u32[]{:S(2)}) copy-start(bf16[2048,2048]{1,0:T(8,128)(2,1)S(1)} %get-tuple-element.133.refs_0_.refs_1_.refs_2_.refs_3_) | copy-start | bytes 25165828
  208.9 33.9 %collective-permute-start.19 = (bf16[1024,512]{1,0:T(8,128)(2,1)}, bf16[1024,512]{1,0:T(8,128)(2,1)S(1)}, u32[]{:S(2)}, u32[]{:S(2)}) collective-permute-start(bf16[1024,512]{1,0:T(8,128)(2,1)} %get-tuple-element.102), channel_id=1, source_target_pairs={{0,4},{1,5},{2,6},{3,7},{4,0},{5,1},{6,2},{7,3},{8,12},{9,13},{10,... | collective-permute-start | bytes 3145736 | tf_op jit(solution)/shard_map/ppermute | solution.py:522
  210.4 33.4 %collective-permute-start.20 = (bf16[1024,512]{1,0:T(8,128)(2,1)}, bf16[1024,512]{1,0:T(8,128)(2,1)}, u32[]{:S(2)}, u32[]{:S(2)}) collective-permute-start(bf16[1024,512]{1,0:T(8,128)(2,1)} %get-tuple-element.106), channel_id=1, source_target_pairs={{0,2},{1,3},{2,0},{3,1},{4,6},{5,7},{6,4},{7,5},{8,10},{9,11},{10,... | collective-permute-start | bytes 3145736 | tf_op jit(solution)/shard_map/ppermute | solution.py:522
  259.3 9.2 %collective-permute-start.21 = (bf16[1024,1024]{1,0:T(8,128)(2,1)}, bf16[1024,1024]{1,0:T(8,128)(2,1)S(1)}, u32[]{:S(2)}, u32[]{:S(2)}) collective-permute-start(bf16[1024,1024]{1,0:T(8,128)(2,1)} %get-tuple-element.112), channel_id=1, source_target_pairs={{0,1},{1,0},{2,3},{3,2},{4,5},{5,4},{6,7},{7,6},{8,9},{9,8},{10,11... | collective-permute-start | bytes 6291464 | tf_op jit(solution)/shard_map/ppermute | solution.py:522
  275.3 4.3 collective-permute-start.22
  275.8 50.0 %collective-permute-start.23 = (bf16[1024,256]{1,0:T(8,128)(2,1)}, bf16[1024,256]{1,0:T(8,128)(2,1)S(1)}, u32[]{:S(2)}, u32[]{:S(2)}) collective-permute-start(bf16[1024,256]{1,0:T(8,128)(2,1)} %get-tuple-element.119), channel_id=1, source_target_pairs={{0,2},{1,3},{2,0},{3,1},{4,6},{5,7},{6,4},{7,5},{8,10},{9,11},{10,... | collective-permute-start | bytes 1572872 | tf_op jit(solution)/shard_map/ppermute | solution.py:522
  277.1 48.9 %collective-permute-start.24 = (bf16[1024,256]{1,0:T(8,128)(2,1)}, bf16[1024,256]{1,0:T(8,128)(2,1)S(1)}, u32[]{:S(2)}, u32[]{:S(2)}) collective-permute-start(bf16[1024,256]{1,0:T(8,128)(2,1)} %get-tuple-element.122), channel_id=1, source_target_pairs={{0,4},{1,5},{2,6},{3,7},{4,0},{5,1},{6,2},{7,3},{8,12},{9,13},{10,... | collective-permute-start | bytes 1572872 | tf_op jit(solution)/shard_map/ppermute | solution.py:522
  277.8 63.7 %collective-permute-start.25 = (bf16[1024,1024]{1,0:T(8,128)(2,1)}, bf16[1024,1024]{1,0:T(8,128)(2,1)}, u32[]{:S(2)}, u32[]{:S(2)}) collective-permute-start(bf16[1024,1024]{1,0:T(8,128)(2,1)} %columns_product.8), channel_id=1, source_target_pairs={{0,4},{1,5},{2,6},{3,7},{4,0},{5,1},{6,2},{7,3},{8,12},{9,13},{10,... | collective-permute-start | bytes 6291464 | tf_op jit(solution)/shard_map/ppermute | solution.py:522
  286.1 39.9 %copy-start.64 = (bf16[1024,256]{1,0:T(8,128)(2,1)S(1)}, bf16[1024,256]{1,0:T(8,128)(2,1)}, u32[]{:S(2)}) copy-start(bf16[1024,256]{1,0:T(8,128)(2,1)} %copy-done.63) | copy-start | bytes 1572868
  327.2 116.1 %reduce-scatter.5.cloned.1.call-start = ((), (), s32[]{:S(2)}) async-start(), calls=%async_computation.9 | async-start | bytes 1310720 | tf_op jit(solution)/shard_map/reduce_scatter | solution.py:738
  339.1 31.7 %collective-permute-start.27 = (bf16[512,1024]{1,0:T(8,128)(2,1)S(1)}, bf16[512,1024]{1,0:T(8,128)(2,1)S(1)}, u32[]{:S(2)}, u32[]{:S(2)}) collective-permute-start(bf16[512,1024]{1,0:T(8,128)(2,1)S(1)} %pad_maximum_fusion.9), channel_id=1, source_target_pairs={{0,2},{1,3},{2,0},{3,1},{4,6},{5,7},{6,4},{7,5},{8,10},{9,11},{10,... | collective-permute-start | bytes 3145736 | tf_op jit(solution)/shard_map/ppermute | solution.py:522
  340.8 32.2 %collective-permute-start.26 = (bf16[512,1024]{1,0:T(8,128)(2,1)S(1)}, bf16[512,1024]{1,0:T(8,128)(2,1)S(1)}, u32[]{:S(2)}, u32[]{:S(2)}) collective-permute-start(bf16[512,1024]{1,0:T(8,128)(2,1)S(1)} %pad_maximum_fusion.8), channel_id=1, source_target_pairs={{0,4},{1,5},{2,6},{3,7},{4,0},{5,1},{6,2},{7,3},{8,12},{9,13},{10,... | collective-permute-start | bytes 3145736 | tf_op jit(solution)/shard_map/ppermute | solution.py:522
  352.2 35.7 %collective-permute-start.30 = (bf16[1024,512]{1,0:T(8,128)(2,1)S(1)}, bf16[1024,512]{1,0:T(8,128)(2,1)S(1)}, u32[]{:S(2)}, u32[]{:S(2)}) collective-permute-start(bf16[1024,512]{1,0:T(8,128)(2,1)S(1)} %get-tuple-element.135), channel_id=1, source_target_pairs={{0,2},{1,3},{2,0},{3,1},{4,6},{5,7},{6,4},{7,5},{8,10},{9,11},{10,... | collective-permute-start | bytes 3145736 | tf_op jit(solution)/shard_map/ppermute | solution.py:522
  372.1 17.2 %collective-permute-start.29 = (bf16[512,512]{1,0:T(8,128)(2,1)}, bf16[512,512]{1,0:T(8,128)(2,1)}, u32[]{:S(2)}, u32[]{:S(2)}) collective-permute-start(bf16[512,512]{1,0:T(8,128)(2,1)} %slice.259), channel_id=1, source_target_pairs={{0,4},{1,5},{2,6},{3,7},{4,0},{5,1},{6,2},{7,3},{8,12},{9,13},{10,... | collective-permute-start | bytes 1572872 | tf_op jit(solution)/shard_map/ppermute | solution.py:522
  374.7 23.7 %collective-permute-start.28 = (bf16[512,512]{1,0:T(8,128)(2,1)}, bf16[512,512]{1,0:T(8,128)(2,1)}, u32[]{:S(2)}, u32[]{:S(2)}) collective-permute-start(bf16[512,512]{1,0:T(8,128)(2,1)} %slice.260), channel_id=1, source_target_pairs={{0,2},{1,3},{2,0},{3,1},{4,6},{5,7},{6,4},{7,5},{8,10},{9,11},{10,... | collective-permute-start | bytes 1572872 | tf_op jit(solution)/shard_map/ppermute | solution.py:522
  387.9 44.9 %collective-permute-start.32 = (bf16[1024,1024]{1,0:T(8,128)(2,1)}, bf16[1024,1024]{1,0:T(8,128)(2,1)}, u32[]{:S(2)}, u32[]{:S(2)}) collective-permute-start(bf16[1024,1024]{1,0:T(8,128)(2,1)} %get-tuple-element.140), channel_id=1, source_target_pairs={{0,1},{1,0},{2,3},{3,2},{4,5},{5,4},{6,7},{7,6},{8,9},{9,8},{10,11... | collective-permute-start | bytes 6291464 | tf_op jit(solution)/shard_map/ppermute | solution.py:522
  420.9 22.5 %collective-permute-start.31 = (bf16[1024,1024]{1,0:T(8,128)(2,1)}, bf16[1024,1024]{1,0:T(8,128)(2,1)}, u32[]{:S(2)}, u32[]{:S(2)}) collective-permute-start(bf16[1024,1024]{1,0:T(8,128)(2,1)} %get-tuple-element.138), channel_id=1, source_target_pairs={{0,1},{1,0},{2,3},{3,2},{4,5},{5,4},{6,7},{7,6},{8,9},{9,8},{10,11... | collective-permute-start | bytes 6291464 | tf_op jit(solution)/shard_map/ppermute | solution.py:522
  424.8 33.1 %collective-permute-start.33 = (bf16[256,512]{0,1:T(8,128)(2,1)S(1)}, bf16[256,512]{0,1:T(8,128)(2,1)}, u32[]{:S(2)}, u32[]{:S(2)}) collective-permute-start(bf16[256,512]{0,1:T(8,128)(2,1)S(1)} %bitcast.148), channel_id=1, source_target_pairs={{0,8},{8,16},{16,24},{24,0},{1,9},{9,17},{17,25},{25,1},{2,10},{10... | collective-permute-start | bytes 786440 | tf_op jit(solution)/shard_map/ppermute | solution.py:564
  426.9 31.0 %collective-permute-start.34 = (bf16[256,512]{0,1:T(8,128)(2,1)S(1)}, bf16[256,512]{0,1:T(8,128)(2,1)}, u32[]{:S(2)}, u32[]{:S(2)}) collective-permute-start(bf16[256,512]{0,1:T(8,128)(2,1)S(1)} %bitcast.149), channel_id=1, source_target_pairs={{0,16},{8,24},{16,0},{24,8},{1,17},{9,25},{17,1},{25,9},{2,18},{10... | collective-permute-start | bytes 786440 | tf_op jit(solution)/shard_map/ppermute | solution.py:564
  430.9 27.0 %collective-permute-start.35 = (bf16[256,512]{0,1:T(8,128)(2,1)}, bf16[256,512]{0,1:T(8,128)(2,1)}, u32[]{:S(2)}, u32[]{:S(2)}) collective-permute-start(bf16[256,512]{0,1:T(8,128)(2,1)} %bitcast.52), channel_id=1, source_target_pairs={{0,24},{8,0},{16,8},{24,16},{1,25},{9,1},{17,9},{25,17},{2,26},{10... | collective-permute-start | bytes 786440 | tf_op jit(solution)/shard_map/ppermute | solution.py:564
  455.3 13.2 %all-to-all-start.2 = ((f32[32,14,128]{2,1,0:T(8,128)}), f32[32,14,128]{2,1,0:T(8,128)S(1)}, u32[]{:S(2)}, u32[]{:S(2)}) async-start(f32[32,14,128]{2,1,0:T(8,128)} %bitcast.42), calls=%async_computation.4 | async-start | bytes 524288 | tf_op jit(solution)/shard_map/all_to_all | solution.py:606
  470.9 10.8 %all-to-all-start.3 = ((f32[32,8,128]{2,1,0:T(8,128)}), f32[32,8,128]{2,1,0:T(8,128)S(1)}, u32[]{:S(2)}, u32[]{:S(2)}) async-start(f32[32,8,128]{2,1,0:T(8,128)} %bitcast.46), calls=%async_computation.5 | async-start | bytes 262144 | tf_op jit(solution)/shard_map/all_to_all | solution.py:606
  (85 other events, 603.8 us)
Sparse Core Ops, SparseCore 0:
  51.4 27.0 all-gather.2
  96.3 27.4 all-gather.4
  327.4 26.5 reduce-scatter.2
  389.4 26.7 reduce-scatter.4

commit v6 on v5

--- a/solution.py
+++ b/solution.py
@@ -22,6 +22,7 @@
 BF16 = jnp.bfloat16
 QUERY_ROWS = 512
 TOKEN_ROWS = 32
+LARGE_BYTES = 4 * 1024 * 1024
 VMEM_NEEDS = {
     "attend": 14,
     "attend_back": 20,
@@ -36,6 +37,26 @@
 
 def vmem_of(need):
     return VMEM_NEEDS[need] * 1024 * 1024
+
+
+def is_large(array):
+    return array.size * array.dtype.itemsize >= LARGE_BYTES
+
+
+def large_in_hbm(call):
+    def wrapped(*arrays):
+        return call(
+            *[
+                pltpu.with_memory_space_constraint(a, pltpu.HBM) if is_large(a) else a
+                for a in arrays
+            ]
+        )
+
+    return wrapped
+
+
+def large_out(shapes):
+    return jax.tree.map(lambda a: pltpu.HBM(a.shape, a.dtype) if is_large(a) else a, shapes)
 
 
 def dot(left, right, dims=NN):
@@ -152,7 +173,7 @@
 def attend(projected, latents, pairs, first, count, earlier=()):
     parts, plain, logs = attention_specs(first)
     rows = projected.shape[0]
-    return pl.pallas_call(
+    call = pl.pallas_call(
         attend_kernel,
         grid=(latents, count),
         in_specs=parts + [pl.BlockSpec(memory_space=pl.ANY)] * len(earlier),
@@ -165,13 +186,14 @@
         compiler_params=pltpu.CompilerParams(vmem_limit_bytes=vmem_of("attend")),
         cost_estimate=SMALL_COST,
         name="attend",
-    )(projected, projected, projected, *earlier)
+    )
+    return large_in_hbm(call)(projected, projected, projected, *earlier)
 
 
 def attend_back(projected, mixed, grad_mixed, log_totals, latents, first, count):
     parts, plain, logs = attention_specs(first)
     rows = projected.shape[0]
-    return pl.pallas_call(
+    call = pl.pallas_call(
         attend_back_kernel,
         grid=(latents, count),
         in_specs=[*parts, plain, plain, logs],
@@ -179,27 +201,29 @@
             pl.BlockSpec((LEN, 3 * PAIR), lambda s, p: (s, p)),
             pl.BlockSpec((1, 1, 8, 3 * PAIR), lambda s, p: (s, p, 0, 0)),
         ],
-        out_shape=[
+        out_shape=large_out([
             jax.ShapeDtypeStruct((rows, count * 3 * PAIR), BF16),
             jax.ShapeDtypeStruct((latents, count, 8, 3 * PAIR), F32),
-        ],
+        ]),
         compiler_params=pltpu.CompilerParams(vmem_limit_bytes=vmem_of("attend_back")),
         cost_estimate=SMALL_COST,
         name="attend_back",
-    )(projected, projected, projected, mixed, grad_mixed, log_totals)
+    )
+    return large_in_hbm(call)(projected, projected, projected, mixed, grad_mixed, log_totals)
 
 
 def kernel_call(body, grid, in_specs, out_specs, out_shape, name, need):
-    return pl.pallas_call(
+    call = pl.pallas_call(
         body,
         grid=grid,
         in_specs=in_specs,
         out_specs=out_specs,
-        out_shape=out_shape,
+        out_shape=large_out(out_shape),
         compiler_params=pltpu.CompilerParams(vmem_limit_bytes=vmem_of(need)),
         cost_estimate=SMALL_COST,
         name=name,
     )
+    return large_in_hbm(call)
 
 
 def whole(array):

time: 496 us -> 476 us (0.960)
  local copies, waits for them, and re-layouts: 89.4 us -> 37.7 us
  Pallas kernels: 230 us -> 261 us
    unnamed x187 -> x95, local copies, waits for them, and re-layouts: 69 us -> 17.3 us
    pallas_call x24, Pallas kernels: 230 us -> 261 us  [wrapped(): call(*[pltpu.with_memory_space_constraint(a, pltpu.HBM) if is_large(a) el...]
  transfers between devices with their start and end apart: 44 -> 44, of which waited for: 14 -> 16; matrix products, arithmetic and copies ran while one was open for 11% -> 11% of each run, Pallas kernels for 41% -> 47%
where the time goes in v6:
time: 476 us; the launch traced here: 470 us
  Pallas kernels  261 us (55%)
  waiting for transfers between devices  72.2 us (15%)
  starting transfers between devices  50.6 us (11%)
  local copies, waits for them, and re-layouts  37.7 us (8%)
  other arithmetic  28.7 us (6%)
  between operations  15.1 us (3%)
    pallas_call x24, Pallas kernels, wrapped(): call(*[pltpu.with_memory_space_constraint(a, pltpu.HBM) if is_large(a) el...  261 us
    ppermute x30, waiting for transfers between devices, swap(): return lax.ppermute(array, 'col', pairs)  46.6 us
    all_to_all x4, waiting for transfers between devices, all_exchange(): return lax.all_to_all(pieces, ('row', 'col'), 0, 0, tiled=True)  25.5 us
    ppermute x30, starting transfers between devices, swap(): return lax.ppermute(array, 'col', pairs)  25.4 us
    unnamed x95, local copies, waits for them, and re-layouts  17.3 us
    all_to_all x4, starting transfers between devices, all_exchange(): return lax.all_to_all(pieces, ('row', 'col'), 0, 0, tiled=True)  14.1 us
  transfers between devices with their start and end apart: 44, of which 16 were waited for; matrix products, arithmetic and copies ran while one was open for 11% of the time, Pallas kernels for 47%

profile of v6, /device:TPU:0, one launch (start us, length us, event | category | flops | bytes accessed | tf_op | source)
XLA Modules:
  0.0 469.5 jit_solution(16048991226027573006)
XLA Ops:
  9.1 5.1 %collective-permute-start.3 = (bf16[256,512]{0,1:T(8,128)(2,1)S(1)}, bf16[256,512]{0,1:T(8,128)(2,1)S(1)}, u32[]{:S(2)}, u32[]{:S(2)}) collective-permute-start(bf16[256,512]{0,1:T(8,128)(2,1)S(1)} %get-tuple-element.247), channel_id=1, source_target_pairs={{0,24},{8,0},{16,8},{24,16},{1,25},{9,1},{17,9},{25,17},{2,26},{10... | collective-permute-start | bytes 786440 | tf_op jit(solution)/shard_map/ppermute | solution.py:573
  19.9 5.6 %all-to-all-start = ((bf16[32,16,128]{2,1,0:T(8,128)(2,1)}), bf16[32,16,128]{2,1,0:T(8,128)(2,1)S(1)}, u32[]{:S(2)}, u32[]{:S(2)}) async-start(bf16[32,16,128]{2,1,0:T(8,128)(2,1)} %broadcast_in_dim.32), calls=%async_computation | async-start | bytes 262144 | tf_op jit(solution)/shard_map/all_to_all | solution.py:630
  25.5 2.3 convert_reduce_fusion
  28.1 12.8 %all-to-all-done = bf16[32,16,128]{2,1,0:T(8,128)(2,1)S(1)} async-done(((bf16[32,16,128]{2,1,0:T(8,128)(2,1)}), bf16[32,16,128]{2,1,0:T(8,128)(2,1)S(1)}, u32[]{:S(2)}, u32[]{:S(2)}) %all-to-all-start) | async-done | bytes 131104 | tf_op jit(solution)/shard_map/all_to_all | solution.py:630
  42.1 3.4 all-to-all-start.1
  51.4 2.4 all-to-all-done.1
  54.7 2.1 fusion.3.refs_0_.mine_ref
  57.0 5.2 %collective-permute-done.6 = bf16[512,512]{1,0:T(8,128)(2,1)} collective-permute-done((bf16[512,512]{1,0:T(8,128)(2,1)}, bf16[512,512]{1,0:T(8,128)(2,1)}, u32[]{:S(2)}, u32[]{:S(2)}) %collective-permute-start.6) | collective-permute-done | bytes 524320 | tf_op jit(solution)/shard_map/ppermute | solution.py:546
  64.9 2.1 pad_maximum_fusion.1.a_ref
  70.9 17.4 %collective-permute-done.7.d_ref = bf16[512,1024]{1,0:T(8,128)(2,1)} collective-permute-done((bf16[512,1024]{1,0:T(8,128)(2,1)S(1)}, bf16[512,1024]{1,0:T(8,128)(2,1)}, u32[]{:S(2)}, u32[]{:S(2)}) %collective-permute-start.7) | collective-permute-done | bytes 1048608 | tf_op jit(solution)/shard_map/ppermute | solution.py:546
  88.3 3.3 collective-permute-done.5.b_ref
  91.6 2.2 fusion.34
  96.6 2.9 assemble.1
  100.5 11.2 %rows_bias.2.q_ref.k_ref.v_ref = bf16[2048,1536]{1,0:T(8,128)(2,1)} custom-call(bf16[1024,1024]{1,0:T(8,128)(2,1)} %fusion.3.refs_0_.mine_ref, bf16[1024,1024]{1,0:T(8,128)(2,1)} %collective-permute-done.refs_1_.theirs_ref, bf16[1024,1536]{1,0:T(8,128)(2,1)S(1)} %bitcast.121, f32[1,1536]{1,0:T(1,128)S(1)} %reshape.212.refs_3_), custom_call_target="tpu_custom_call" | custom-call | flops 1000 | bytes 1000 | tf_op jit(solution)/shard_map/rows_bias/pallas_call | solution.py:48
  114.3 2.2 pad_maximum_fusion.3.refs_2_.refs_4_.refs_1_.refs_3_
  117.2 17.4 %attend.2 = (bf16[2048,512]{1,0:T(8,128)(2,1)S(1)}, f32[2,4,2,1024]{3,2,1,0:T(2,128)S(1)}) custom-call(bf16[2048,1536]{1,0:T(8,128)(2,1)} %rows_bias.2.q_ref.k_ref.v_ref, bf16[2048,1536]{1,0:T(8,128)(2,1)} %rows_bias.2.q_ref.k_ref.v_ref, bf16[2048,1536]{1,0:T(8,128)(2,1)} %rows_bias.2.q_ref.k_ref.v_ref), custom_call_target="tpu_custom_call" | custom-call | flops 1000 | bytes 1000 | tf_op jit(solution)/shard_map/attend/pallas_call | solution.py:48
  136.0 3.4 collective-permute-done.10.refs_6_.refs_8_.refs_5_.refs_7_
  142.2 17.4 %attend.3 = (bf16[2048,512]{1,0:T(8,128)(2,1)S(1)}, f32[2,4,2,1024]{3,2,1,0:T(2,128)S(1)}) custom-call(bf16[2048,1536]{1,0:T(8,128)(2,1)} %rows_bias.2.q_ref.k_ref.v_ref, bf16[2048,1536]{1,0:T(8,128)(2,1)} %rows_bias.2.q_ref.k_ref.v_ref, bf16[2048,1536]{1,0:T(8,128)(2,1)} %rows_bias.2.q_ref.k_ref.v_ref, ...), custom_call_target="tpu_custom_call", output_to_operand_aliasing={{0}: (3, {}), {1}: (4, {})} | custom-call | flops 1000 | bytes 1000 | tf_op jit(solution)/shard_map/attend/pallas_call | solution.py:48
  161.7 5.1 %rows_total.4 = (f32[1024,1024]{1,0:T(8,128)}, bf16[1024,1024]{1,0:T(8,128)(2,1)S(1)}) custom-call(bf16[2048,512]{1,0:T(8,128)(2,1)S(1)} %get-tuple-element.115.refs_0_.mixed_ref, bf16[1024,512]{1,0:T(8,128)(2,1)S(1)} %bitcast.123), custom_call_target="tpu_custom_call" | custom-call | flops 1000 | bytes 1000 | tf_op jit(solution)/shard_map/rows_total/pallas_call | solution.py:48
  166.8 4.1 collective-permute-done.14.refs_1_
  171.0 5.3 %middle.1 = (f32[1024,1024]{1,0:T(8,128)}, bf16[1024,1024]{1,0:T(8,128)(2,1)S(1)}) custom-call(f32[1024,1024]{1,0:T(8,128)} %get-tuple-element.95.refs_0_, bf16[1024,1024]{1,0:T(8,128)(2,1)S(1)} %collective-permute-done.14.refs_1_, bf16[1024,1024]{1,0:T(8,128)(2,1)S(1)} %copy-done, f32[8,1024]{1,0:T(8,128)S(1)} %pad_maximum_fusion.15.refs_3_.refs_5_.refs_4_), custom_call_target="tpu_custom_call" | custom-call | flops 1000 | bytes 1000 | tf_op jit(solution)/shard_map/middle/pallas_call | solution.py:48
  180.4 20.5 %rows_gelu.1 = (bf16[2048,2048]{1,0:T(8,128)(2,1)}, bf16[2048,2048]{1,0:T(8,128)(2,1)}) custom-call(bf16[1024,1024]{1,0:T(8,128)(2,1)S(1)} %get-tuple-element.97.refs_0_.mine_ref, bf16[1024,1024]{1,0:T(8,128)(2,1)S(1)} %collective-permute-done.15.refs_1_.theirs_ref, bf16[1024,512]{1,0:T(8,128)(2,1)} %pad_maximum_fusion.3.refs_2_.refs_4_.refs_1_.refs_3_, ...), custom_call_target="tpu_custom_call" | custom-call | flops 1000 | bytes 1000 | tf_op jit(solution)/shard_map/rows_gelu/pallas_call | solution.py:48
  203.5 8.1 %columns_product.7 = (bf16[1024,512]{1,0:T(8,128)(2,1)S(1)}, bf16[1024,512]{1,0:T(8,128)(2,1)S(1)}) custom-call(bf16[1024,1024]{1,0:T(8,128)(2,1)S(1)} %multiply_convert_fusion.mine_ref.refs_0_, bf16[1024,1024]{1,0:T(8,128)(2,1)S(1)} %collective-permute-done.18.theirs_ref.refs_1_, bf16[2048,2048]{1,0:T(8,128)(2,1)} %get-tuple-element.133.refs_0_.refs_1_.refs_2_.refs_3_, ...), custom_call_target="tpu_custom_call" | custom-call | flops 1000 | bytes 1000 | tf_op jit(solution)/shard_map/columns_product/pallas_call | solution.py:48
  213.8 13.2 %rows_slope.1 = (bf16[2048,2048]{1,0:T(8,128)(2,1)}, f32[8,2048]{1,0:T(8,128)S(1)}) custom-call(bf16[1024,1024]{1,0:T(8,128)(2,1)S(1)} %multiply_convert_fusion.mine_ref.refs_0_, bf16[1024,1024]{1,0:T(8,128)(2,1)S(1)} %collective-permute-done.18.theirs_ref.refs_1_, bf16[1024,512]{1,0:T(8,128)(2,1)S(1)} %pad_maximum_fusion.5.refs_2_.refs_4_.refs_1_.refs_3_, ...), custom_call_target="tpu_custom_call" | custom-call | flops 1000 | bytes 1000 | tf_op jit(solution)/shard_map/rows_slope/pallas_call | solution.py:48
  227.1 8.7 %columns_product.8 = bf16[1024,1024]{1,0:T(8,128)(2,1)} custom-call(bf16[1024,1024]{1,0:T(8,128)(2,1)S(1)} %get-tuple-element.97.refs_0_.mine_ref, bf16[1024,1024]{1,0:T(8,128)(2,1)S(1)} %collective-permute-done.15.refs_1_.theirs_ref, bf16[2048,2048]{1,0:T(8,128)(2,1)} %get-tuple-element.124.refs_0_.refs_1_, ...), custom_call_target="tpu_custom_call" | custom-call | flops 1000 | bytes 1000 | tf_op jit(solution)/shard_map/columns_product/pallas_call | solution.py:48
  236.9 13.9 %rows_total.5 = (f32[1024,1024]{1,0:T(8,128)}, bf16[1024,1024]{1,0:T(8,128)(2,1)S(1)}) custom-call(bf16[2048,2048]{1,0:T(8,128)(2,1)} %get-tuple-element.124.refs_0_.refs_1_, bf16[1024,512]{1,0:T(8,128)(2,1)} %pad_maximum_fusion.3.refs_2_.refs_4_.refs_1_.refs_3_, bf16[1024,512]{1,0:T(8,128)(2,1)S(1)} %copy-done.8, ...), custom_call_target="tpu_custom_call" | custom-call | flops 1000 | bytes 1000 | tf_op jit(solution)/shard_map/rows_total/pallas_call | solution.py:48
  250.7 7.9 %columns_product.9 = (bf16[1024,256]{1,0:T(8,128)(2,1)S(1)}, bf16[1024,256]{1,0:T(8,128)(2,1)S(1)}, bf16[1024,256]{1,0:T(8,128)(2,1)S(1)}, bf16[1024,256]{1,0:T(8,128)(2,1)S(1)}) custom-call(bf16[1024,1024]{1,0:T(8,128)(2,1)S(1)} %multiply_convert_fusion.mine_ref.refs_0_, bf16[1024,1024]{1,0:T(8,128)(2,1)S(1)} %collective-permute-done.18.theirs_ref.refs_1_, ...), custom_call_target="tpu_custom_call" | custom-call | flops 1000 | bytes 1000 | tf_op jit(solution)/shard_map/columns_product/pallas_call | solution.py:48
  258.7 8.4 %middle_back.1 = (f32[1024,1024]{1,0:T(8,128)}, bf16[1024,1024]{1,0:T(8,128)(2,1)S(1)}, f32[4,8,1024]{2,1,0:T(8,128)S(1)}) custom-call(f32[1024,1024]{1,0:T(8,128)} %get-tuple-element.111.refs_0_, bf16[1024,1024]{1,0:T(8,128)(2,1)S(1)} %collective-permute-done.21.refs_1_, bf16[1024,1024]{1,0:T(8,128)(2,1)S(1)} %copy-done.9, bf16[1024,1024]{1,0:T(8,128)(2,1)S(1)} %copy-done, ...), custom_call_target="tpu_custom_call" | custom-call | flops 1000 | bytes 1000 | tf_op jit(solution)/shard_map/middle_back/pallas_call | solution.py:48
  271.4 2.9 rows_bias.3.grad_ref
  274.3 3.6 columns_product.10
  277.9 38.3 %attend_back.2 = (bf16[2048,1152]{1,0:T(8,128)(2,1)}, f32[2,3,8,384]{3,2,1,0:T(8,128)S(1)}) custom-call(bf16[2048,1536]{1,0:T(8,128)(2,1)} %rows_bias.2.q_ref.k_ref.v_ref, bf16[2048,1536]{1,0:T(8,128)(2,1)} %rows_bias.2.q_ref.k_ref.v_ref, bf16[2048,1536]{1,0:T(8,128)(2,1)} %rows_bias.2.q_ref.k_ref.v_ref, ...), custom_call_target="tpu_custom_call" | custom-call | flops 1000 | bytes 1000 | tf_op jit(solution)/shard_map/attend_back/pallas_call | solution.py:48
  317.7 10.5 %columns_product.12 = (bf16[1024,384]{1,0:T(8,128)(2,1)S(1)}, bf16[1024,384]{1,0:T(8,128)(2,1)S(1)}, bf16[1024,384]{1,0:T(8,128)(2,1)S(1)}) custom-call(bf16[1024,1024]{1,0:T(8,128)(2,1)} %fusion.3.refs_0_.mine_ref, bf16[1024,1024]{1,0:T(8,128)(2,1)} %collective-permute-done.refs_1_.theirs_ref, ...), custom_call_target="tpu_custom_call" | custom-call | flops 1000 | bytes 1000 | tf_op jit(solution)/shard_map/columns_product/pallas_call | solution.py:48
  330.9 8.3 %columns_product.11 = (bf16[1024,512]{1,0:T(8,128)(2,1)S(1)}, bf16[1024,512]{1,0:T(8,128)(2,1)S(1)}) custom-call(bf16[1024,1024]{1,0:T(8,128)(2,1)S(1)} %copy-done.12, bf16[1024,1024]{1,0:T(8,128)(2,1)S(1)} %copy-done.14, bf16[2048,2048]{1,0:T(8,128)(2,1)} %get-tuple-element.124.refs_0_.refs_1_, bf16[2048,2048]{1,0:T(8,128)(2,1)} %get-tuple-element.124.refs_0_.refs_1_, ...), custom_call_target="tpu_custom_call" | custom-call | flops 1000 | bytes 1000 | tf_op jit(solution)/shard_map/columns_product/pallas_call | solution.py:48
  340.3 12.9 %attend_back.3 = (bf16[2048,384]{1,0:T(8,128)(2,1)S(1)}, f32[2,1,8,384]{3,2,1,0:T(8,128)S(1)}) custom-call(bf16[2048,1536]{1,0:T(8,128)(2,1)} %rows_bias.2.q_ref.k_ref.v_ref, bf16[2048,1536]{1,0:T(8,128)(2,1)} %rows_bias.2.q_ref.k_ref.v_ref, bf16[2048,1536]{1,0:T(8,128)(2,1)} %rows_bias.2.q_ref.k_ref.v_ref, bf16[2048,512]{1,0:T(8,128)(2,1)S(1)} %copy-done.4, ...), custom_call_target="tpu_custom_call" | custom-call | flops 1000 | bytes 1000 | tf_op jit(solution)/shard_map/attend_back/pallas_call | solution.py:48
  353.2 4.8 %columns_product.13 = bf16[1024,384]{1,0:T(8,128)(2,1)S(1)} custom-call(bf16[1024,1024]{1,0:T(8,128)(2,1)} %fusion.3.refs_0_.mine_ref, bf16[1024,1024]{1,0:T(8,128)(2,1)} %collective-permute-done.refs_1_.theirs_ref, bf16[2048,384]{1,0:T(8,128)(2,1)S(1)} %get-tuple-element.131.refs_0_), custom_call_target="tpu_custom_call" | custom-call | flops 1000 | bytes 1000 | tf_op jit(solution)/shard_map/columns_product/pallas_call | solution.py:48
  364.1 11.9 %rows_total.6 = (f32[1024,1024]{1,0:T(8,128)}, bf16[1024,1024]{1,0:T(8,128)(2,1)}) custom-call(bf16[2048,384]{1,0:T(8,128)(2,1)S(1)} %get-tuple-element.131.refs_0_, bf16[2048,1152]{1,0:T(8,128)(2,1)} %get-tuple-element.118.refs_0_.refs_1_.refs_2_, bf16[1024,1536]{1,0:T(8,128)(2,1)S(1)} %bitcast.122), custom_call_target="tpu_custom_call" | custom-call | flops 1000 | bytes 1000 | tf_op jit(solution)/shard_map/rows_total/pallas_call | solution.py:48
  378.6 2.5 slice_add_fusion
  381.1 7.0 %collective-permute-done.28 = bf16[512,512]{1,0:T(8,128)(2,1)} collective-permute-done((bf16[512,512]{1,0:T(8,128)(2,1)}, bf16[512,512]{1,0:T(8,128)(2,1)}, u32[]{:S(2)}, u32[]{:S(2)}) %collective-permute-start.28) | collective-permute-done | bytes 524320 | tf_op jit(solution)/shard_map/ppermute | solution.py:546
  388.1 2.0 slice_add_fusion.1
  393.8 13.4 %rows_total.7 = (f32[1024,1024]{1,0:T(8,128)}, bf16[1024,1024]{1,0:T(8,128)(2,1)}) custom-call(bf16[2048,2048]{1,0:T(8,128)(2,1)} %get-tuple-element.133.refs_0_.refs_1_.refs_2_.refs_3_, bf16[1024,512]{1,0:T(8,128)(2,1)S(1)} %copy-done.6, bf16[1024,512]{1,0:T(8,128)(2,1)S(1)} %pad_maximum_fusion.6.refs_3_.refs_7_.refs_2_.refs_6_, ...), custom_call_target="tpu_custom_call" | custom-call | flops 1000 | bytes 1000 | tf_op jit(solution)/shard_map/rows_total/pallas_call | solution.py:48
  413.3 2.0 collective-permute-start.34
  418.7 7.7 %first_back.1 = (f32[1024,1024]{1,0:T(8,128)}, f32[2,8,1024]{2,1,0:T(8,128)S(1)}) custom-call(f32[1024,1024]{1,0:T(8,128)} %get-tuple-element.132.refs_0_, bf16[1024,1024]{1,0:T(8,128)(2,1)} %collective-permute-done.32.refs_1_, bf16[1024,1024]{1,0:T(8,128)(2,1)S(1)} %copy-done, f32[1024,1024]{1,0:T(8,128)} %get-tuple-element.141.refs_3_, ...), custom_call_target="tpu_custom_call" | custom-call | flops 1000 | bytes 1000 | tf_op jit(solution)/shard_map/first_back/pallas_call | solution.py:48
  428.0 6.8 %last.1 = (bf16[1024,1024]{1,0:T(8,128)(2,1)}, f32[2,8,1024]{2,1,0:T(8,128)S(1)}) custom-call(f32[1024,1024]{1,0:T(8,128)} %get-tuple-element.137.refs_0_, bf16[1024,1024]{1,0:T(8,128)(2,1)} %collective-permute-done.31.refs_1_, bf16[1024,1024]{1,0:T(8,128)(2,1)S(1)} %copy-done, f32[1024,1024]{1,0:T(8,128)} %get-tuple-element.113.refs_4_.refs_3_, ...), custom_call_target="tpu_custom_call" | custom-call | flops 1000 | bytes 1000 | tf_op jit(solution)/shard_map/last/pallas_call | solution.py:48
  435.7 2.6 all-to-all-start.2
  443.0 5.9 %all-to-all-done.2 = f32[32,14,128]{2,1,0:T(8,128)S(1)} async-done(((f32[32,14,128]{2,1,0:T(8,128)}), f32[32,14,128]{2,1,0:T(8,128)S(1)}, u32[]{:S(2)}, u32[]{:S(2)}) %all-to-all-start.2) | async-done | bytes 229408 | tf_op jit(solution)/shard_map/all_to_all | solution.py:630
  451.3 2.6 all-to-all-start.3
  455.6 2.2 fusion.9
  457.7 4.4 all-to-all-done.3
  (264 shorter events, 88.4 us)
Async XLA Ops:
  9.1 36.4 %collective-permute-start.3 = (bf16[256,512]{0,1:T(8,128)(2,1)S(1)}, bf16[256,512]{0,1:T(8,128)(2,1)S(1)}, u32[]{:S(2)}, u32[]{:S(2)}) collective-permute-start(bf16[256,512]{0,1:T(8,128)(2,1)S(1)} %get-tuple-element.247), channel_id=1, source_target_pairs={{0,24},{8,0},{16,8},{24,16},{1,25},{9,1},{17,9},{25,17},{2,26},{10... | collective-permute-start | bytes 786440 | tf_op jit(solution)/shard_map/ppermute | solution.py:573
  14.2 31.3 %collective-permute-start.1 = (bf16[256,512]{0,1:T(8,128)(2,1)S(1)}, bf16[256,512]{0,1:T(8,128)(2,1)S(1)}, u32[]{:S(2)}, u32[]{:S(2)}) collective-permute-start(bf16[256,512]{0,1:T(8,128)(2,1)S(1)} %get-tuple-element.247), channel_id=1, source_target_pairs={{0,8},{8,16},{16,24},{24,0},{1,9},{9,17},{17,25},{25,1},{2,10},{10... | collective-permute-start | bytes 786440 | tf_op jit(solution)/shard_map/ppermute | solution.py:573
  14.2 31.3 %collective-permute-start.2 = (bf16[256,512]{0,1:T(8,128)(2,1)S(1)}, bf16[256,512]{0,1:T(8,128)(2,1)S(1)}, u32[]{:S(2)}, u32[]{:S(2)}) collective-permute-start(bf16[256,512]{0,1:T(8,128)(2,1)S(1)} %get-tuple-element.247), channel_id=1, source_target_pairs={{0,16},{8,24},{16,0},{24,8},{1,17},{9,25},{17,1},{25,9},{2,18},{10... | collective-permute-start | bytes 786440 | tf_op jit(solution)/shard_map/ppermute | solution.py:573
  19.9 21.1 %all-to-all-start = ((bf16[32,16,128]{2,1,0:T(8,128)(2,1)}), bf16[32,16,128]{2,1,0:T(8,128)(2,1)S(1)}, u32[]{:S(2)}, u32[]{:S(2)}) async-start(bf16[32,16,128]{2,1,0:T(8,128)(2,1)} %broadcast_in_dim.32), calls=%async_computation | async-start | bytes 262144 | tf_op jit(solution)/shard_map/all_to_all | solution.py:630
  42.1 11.7 %all-to-all-start.1 = ((f32[32,6,128]{2,1,0:T(8,128)}), f32[32,6,128]{2,1,0:T(8,128)}, u32[]{:S(2)}, u32[]{:S(2)}) async-start(f32[32,6,128]{2,1,0:T(8,128)} %copy.96), calls=%async_computation.1 | async-start | bytes 262144 | tf_op jit(solution)/shard_map/all_to_all | solution.py:630
  45.4 46.2 %all-gather.3.cloned.1.call-start = ((), (), s32[]{:S(2)}) async-start(), calls=%async_computation.6 | async-start | bytes 1310720 | tf_op jit(solution)/shard_map/all_gather | solution.py:695
  46.9 15.2 %collective-permute-start.6 = (bf16[512,512]{1,0:T(8,128)(2,1)}, bf16[512,512]{1,0:T(8,128)(2,1)}, u32[]{:S(2)}, u32[]{:S(2)}) collective-permute-start(bf16[512,512]{1,0:T(8,128)(2,1)} %pad_maximum_fusion.12), channel_id=1, source_target_pairs={{0,4},{1,5},{2,6},{3,7},{4,0},{5,1},{6,2},{7,3},{8,12},{9,13},{10,... | collective-permute-start | bytes 1572872 | tf_op jit(solution)/shard_map/ppermute | solution.py:546
  49.8 15.1 %collective-permute-start.4 = (bf16[512,512]{1,0:T(8,128)(2,1)}, bf16[512,512]{1,0:T(8,128)(2,1)}, u32[]{:S(2)}, u32[]{:S(2)}) collective-permute-start(bf16[512,512]{1,0:T(8,128)(2,1)} %pad_maximum_fusion.11), channel_id=1, source_target_pairs={{0,2},{1,3},{2,0},{3,1},{4,6},{5,7},{6,4},{7,5},{8,10},{9,11},{10,... | collective-permute-start | bytes 1572872 | tf_op jit(solution)/shard_map/ppermute | solution.py:546
  51.3 84.7 %all-gather.5.cloned.1.call-start = ((), (), s32[]{:S(2)}) async-start(), calls=%async_computation.7 | async-start | bytes 1310720 | tf_op jit(solution)/shard_map/all_gather | solution.py:696
  56.9 43.6 %collective-permute-start = (bf16[1024,1024]{1,0:T(8,128)(2,1)}, bf16[1024,1024]{1,0:T(8,128)(2,1)}, u32[]{:S(2)}, u32[]{:S(2)}) collective-permute-start(bf16[1024,1024]{1,0:T(8,128)(2,1)} %fusion.3.refs_0_.mine_ref), channel_id=1, source_target_pairs={{0,1},{1,0},{2,3},{3,2},{4,5},{5,4},{6,7},{7,6},{8,9},{9,8},{10,11... | collective-permute-start | bytes 6291464 | tf_op jit(solution)/shard_map/ppermute | solution.py:546
  63.4 24.8 %collective-permute-start.7 = (bf16[512,1024]{1,0:T(8,128)(2,1)S(1)}, bf16[512,1024]{1,0:T(8,128)(2,1)}, u32[]{:S(2)}, u32[]{:S(2)}) collective-permute-start(bf16[512,1024]{1,0:T(8,128)(2,1)S(1)} %pad_maximum_fusion.2.c_ref), channel_id=1, source_target_pairs={{0,2},{1,3},{2,0},{3,1},{4,6},{5,7},{6,4},{7,5},{8,10},{9,11},{10,... | collective-permute-start | bytes 3145736 | tf_op jit(solution)/shard_map/ppermute | solution.py:546
  67.0 24.6 %collective-permute-start.5 = (bf16[512,1024]{1,0:T(8,128)(2,1)}, bf16[512,1024]{1,0:T(8,128)(2,1)}, u32[]{:S(2)}, u32[]{:S(2)}) collective-permute-start(bf16[512,1024]{1,0:T(8,128)(2,1)} %pad_maximum_fusion.1.a_ref), channel_id=1, source_target_pairs={{0,4},{1,5},{2,6},{3,7},{4,0},{5,1},{6,2},{7,3},{8,12},{9,13},{10,... | collective-permute-start | bytes 3145736 | tf_op jit(solution)/shard_map/ppermute | solution.py:546
  93.8 17.8 %collective-permute-start.9 = (bf16[1024,256]{1,0:T(8,128)(2,1)}, bf16[1024,256]{1,0:T(8,128)(2,1)}, u32[]{:S(2)}, u32[]{:S(2)}) collective-permute-start(bf16[1024,256]{1,0:T(8,128)(2,1)} %get-tuple-element.230), channel_id=1, source_target_pairs={{0,4},{1,5},{2,6},{3,7},{4,0},{5,1},{6,2},{7,3},{8,12},{9,13},{10,... | collective-permute-start | bytes 1572872 | tf_op jit(solution)/shard_map/ppermute | solution.py:546
  95.2 16.5 %collective-permute-start.8 = (bf16[1024,256]{1,0:T(8,128)(2,1)}, bf16[1024,256]{1,0:T(8,128)(2,1)}, u32[]{:S(2)}, u32[]{:S(2)}) collective-permute-start(bf16[1024,256]{1,0:T(8,128)(2,1)} %get-tuple-element.231), channel_id=1, source_target_pairs={{0,2},{1,3},{2,0},{3,1},{4,6},{5,7},{6,4},{7,5},{8,10},{9,11},{10,... | collective-permute-start | bytes 1572872 | tf_op jit(solution)/shard_map/ppermute | solution.py:546
  96.2 293.9 %reduce-scatter.3.cloned.1.call-start = ((), (), s32[]{:S(2)}) async-start(), calls=%async_computation.8 | async-start | bytes 1310720 | tf_op jit(solution)/shard_map/reduce_scatter | solution.py:762
  113.0 23.0 %collective-permute-start.11 = (bf16[1024,512]{1,0:T(8,128)(2,1)S(1)}, bf16[1024,512]{1,0:T(8,128)(2,1)}, u32[]{:S(2)}, u32[]{:S(2)}) collective-permute-start(bf16[1024,512]{1,0:T(8,128)(2,1)S(1)} %pad_maximum_fusion.4.refs_3_.refs_7_.refs_2_.refs_6_), channel_id=1, source_target_pairs={{0,2},{1,3},{2,0},{3,1},{4,6},{5,7},{6,4},{7,5},{8,10},{9,11},{10,... | collective-permute-start | bytes 3145736 | tf_op jit(solution)/shard_map/ppermute | solution.py:546
  116.6 22.9 %collective-permute-start.10 = (bf16[1024,512]{1,0:T(8,128)(2,1)}, bf16[1024,512]{1,0:T(8,128)(2,1)}, u32[]{:S(2)}, u32[]{:S(2)}) collective-permute-start(bf16[1024,512]{1,0:T(8,128)(2,1)} %pad_maximum_fusion.3.refs_2_.refs_4_.refs_1_.refs_3_), channel_id=1, source_target_pairs={{0,4},{1,5},{2,6},{3,7},{4,0},{5,1},{6,2},{7,3},{8,12},{9,13},{10,... | collective-permute-start | bytes 3145736 | tf_op jit(solution)/shard_map/ppermute | solution.py:546
  140.7 19.0 %collective-permute-start.13 = (bf16[1024,256]{1,0:T(8,128)(2,1)S(1)}, bf16[1024,256]{1,0:T(8,128)(2,1)S(1)}, u32[]{:S(2)}, u32[]{:S(2)}) collective-permute-start(bf16[1024,256]{1,0:T(8,128)(2,1)S(1)} %get-tuple-element.228), channel_id=1, source_target_pairs={{0,4},{1,5},{2,6},{3,7},{4,0},{5,1},{6,2},{7,3},{8,12},{9,13},{10,... | collective-permute-start | bytes 1572872 | tf_op jit(solution)/shard_map/ppermute | solution.py:546
  141.4 18.4 %collective-permute-start.12 = (bf16[1024,256]{1,0:T(8,128)(2,1)S(1)}, bf16[1024,256]{1,0:T(8,128)(2,1)S(1)}, u32[]{:S(2)}, u32[]{:S(2)}) collective-permute-start(bf16[1024,256]{1,0:T(8,128)(2,1)S(1)} %get-tuple-element.229), channel_id=1, source_target_pairs={{0,2},{1,3},{2,0},{3,1},{4,6},{5,7},{6,4},{7,5},{8,10},{9,11},{10,... | collective-permute-start | bytes 1572872 | tf_op jit(solution)/shard_map/ppermute | solution.py:546
  159.7 118.2 %copy-start.3 = (bf16[2048,512]{1,0:T(8,128)(2,1)}, bf16[2048,512]{1,0:T(8,128)(2,1)S(1)}, u32[]{:S(2)}) copy-start(bf16[2048,512]{1,0:T(8,128)(2,1)S(1)} %get-tuple-element.115.refs_0_.mixed_ref) | copy-start | bytes 6291460
  159.9 53.9 %copy-start.5 = (bf16[1024,512]{1,0:T(8,128)(2,1)}, bf16[1024,512]{1,0:T(8,128)(2,1)S(1)}, u32[]{:S(2)}) copy-start(bf16[1024,512]{1,0:T(8,128)(2,1)S(1)} %pad_maximum_fusion.5.refs_2_.refs_4_.refs_1_.refs_3_) | copy-start | bytes 3145732
  166.8 4.2 collective-permute-start.14
  176.3 50.8 %copy-start.11 = (bf16[1024,1024]{1,0:T(8,128)(2,1)}, bf16[1024,1024]{1,0:T(8,128)(2,1)S(1)}, u32[]{:S(2)}) copy-start(bf16[1024,1024]{1,0:T(8,128)(2,1)S(1)} %get-tuple-element.97.refs_0_.mine_ref) | copy-start | bytes 6291460
  176.3 4.2 collective-permute-start.15
  177.0 26.5 %collective-permute-start.18 = (bf16[1024,1024]{1,0:T(8,128)(2,1)S(1)}, bf16[1024,1024]{1,0:T(8,128)(2,1)S(1)}, u32[]{:S(2)}, u32[]{:S(2)}) collective-permute-start(bf16[1024,1024]{1,0:T(8,128)(2,1)S(1)} %multiply_convert_fusion.mine_ref.refs_0_), channel_id=1, source_target_pairs={{0,1},{1,0},{2,3},{3,2},{4,5},{5,4},{6,7},{7,6},{8,9},{9,8},{10,11... | collective-permute-start | bytes 6291464 | tf_op jit(solution)/shard_map/ppermute | solution.py:546
  177.5 25.2 %collective-permute-start.17 = (bf16[1024,512]{1,0:T(8,128)(2,1)S(1)}, bf16[1024,512]{1,0:T(8,128)(2,1)S(1)}, u32[]{:S(2)}, u32[]{:S(2)}) collective-permute-start(bf16[1024,512]{1,0:T(8,128)(2,1)S(1)} %pad_maximum_fusion.6.refs_3_.refs_7_.refs_2_.refs_6_), channel_id=1, source_target_pairs={{0,2},{1,3},{2,0},{3,1},{4,6},{5,7},{6,4},{7,5},{8,10},{9,11},{10,... | collective-permute-start | bytes 3145736 | tf_op jit(solution)/shard_map/ppermute | solution.py:546
  178.6 24.9 %collective-permute-start.16 = (bf16[1024,512]{1,0:T(8,128)(2,1)S(1)}, bf16[1024,512]{1,0:T(8,128)(2,1)S(1)}, u32[]{:S(2)}, u32[]{:S(2)}) collective-permute-start(bf16[1024,512]{1,0:T(8,128)(2,1)S(1)} %pad_maximum_fusion.5.refs_2_.refs_4_.refs_1_.refs_3_), channel_id=1, source_target_pairs={{0,4},{1,5},{2,6},{3,7},{4,0},{5,1},{6,2},{7,3},{8,12},{9,13},{10,... | collective-permute-start | bytes 3145736 | tf_op jit(solution)/shard_map/ppermute | solution.py:546
  180.4 46.6 %copy-start.13 = (bf16[1024,1024]{1,0:T(8,128)(2,1)}, bf16[1024,1024]{1,0:T(8,128)(2,1)S(1)}, u32[]{:S(2)}) copy-start(bf16[1024,1024]{1,0:T(8,128)(2,1)S(1)} %collective-permute-done.15.refs_1_.theirs_ref) | copy-start | bytes 6291460
  211.6 24.1 %collective-permute-start.19 = (bf16[1024,512]{1,0:T(8,128)(2,1)S(1)}, bf16[1024,512]{1,0:T(8,128)(2,1)S(1)}, u32[]{:S(2)}, u32[]{:S(2)}) collective-permute-start(bf16[1024,512]{1,0:T(8,128)(2,1)S(1)} %get-tuple-element.102), channel_id=1, source_target_pairs={{0,4},{1,5},{2,6},{3,7},{4,0},{5,1},{6,2},{7,3},{8,12},{9,13},{10,... | collective-permute-start | bytes 3145736 | tf_op jit(solution)/shard_map/ppermute | solution.py:546
  213.1 23.8 %collective-permute-start.20 = (bf16[1024,512]{1,0:T(8,128)(2,1)S(1)}, bf16[1024,512]{1,0:T(8,128)(2,1)S(1)}, u32[]{:S(2)}, u32[]{:S(2)}) collective-permute-start(bf16[1024,512]{1,0:T(8,128)(2,1)S(1)} %get-tuple-element.106), channel_id=1, source_target_pairs={{0,2},{1,3},{2,0},{3,1},{4,6},{5,7},{6,4},{7,5},{8,10},{9,11},{10,... | collective-permute-start | bytes 3145736 | tf_op jit(solution)/shard_map/ppermute | solution.py:546
  250.7 7.9 %collective-permute-start.21 = (bf16[1024,1024]{1,0:T(8,128)(2,1)S(1)}, bf16[1024,1024]{1,0:T(8,128)(2,1)S(1)}, u32[]{:S(2)}, u32[]{:S(2)}) collective-permute-start(bf16[1024,1024]{1,0:T(8,128)(2,1)S(1)} %get-tuple-element.112), channel_id=1, source_target_pairs={{0,1},{1,0},{2,3},{3,2},{4,5},{5,4},{6,7},{7,6},{8,9},{9,8},{10,11... | collective-permute-start | bytes 6291464 | tf_op jit(solution)/shard_map/ppermute | solution.py:546
  267.0 4.3 collective-permute-start.22
  267.6 48.6 %collective-permute-start.23 = (bf16[1024,256]{1,0:T(8,128)(2,1)S(1)}, bf16[1024,256]{1,0:T(8,128)(2,1)S(1)}, u32[]{:S(2)}, u32[]{:S(2)}) collective-permute-start(bf16[1024,256]{1,0:T(8,128)(2,1)S(1)} %get-tuple-element.119), channel_id=1, source_target_pairs={{0,2},{1,3},{2,0},{3,1},{4,6},{5,7},{6,4},{7,5},{8,10},{9,11},{10,... | collective-permute-start | bytes 1572872 | tf_op jit(solution)/shard_map/ppermute | solution.py:546
  268.6 47.8 %collective-permute-start.24 = (bf16[1024,256]{1,0:T(8,128)(2,1)S(1)}, bf16[1024,256]{1,0:T(8,128)(2,1)S(1)}, u32[]{:S(2)}, u32[]{:S(2)}) collective-permute-start(bf16[1024,256]{1,0:T(8,128)(2,1)S(1)} %get-tuple-element.122), channel_id=1, source_target_pairs={{0,4},{1,5},{2,6},{3,7},{4,0},{5,1},{6,2},{7,3},{8,12},{9,13},{10,... | collective-permute-start | bytes 1572872 | tf_op jit(solution)/shard_map/ppermute | solution.py:546
  269.1 61.6 %collective-permute-start.25 = (bf16[1024,1024]{1,0:T(8,128)(2,1)}, bf16[1024,1024]{1,0:T(8,128)(2,1)}, u32[]{:S(2)}, u32[]{:S(2)}) collective-permute-start(bf16[1024,1024]{1,0:T(8,128)(2,1)} %columns_product.8), channel_id=1, source_target_pairs={{0,4},{1,5},{2,6},{3,7},{4,0},{5,1},{6,2},{7,3},{8,12},{9,13},{10,... | collective-permute-start | bytes 6291464 | tf_op jit(solution)/shard_map/ppermute | solution.py:546
  317.7 108.7 %reduce-scatter.5.cloned.1.call-start = ((), (), s32[]{:S(2)}) async-start(), calls=%async_computation.9 | async-start | bytes 1310720 | tf_op jit(solution)/shard_map/reduce_scatter | solution.py:762
  328.8 29.4 %collective-permute-start.27 = (bf16[512,1024]{1,0:T(8,128)(2,1)S(1)}, bf16[512,1024]{1,0:T(8,128)(2,1)S(1)}, u32[]{:S(2)}, u32[]{:S(2)}) collective-permute-start(bf16[512,1024]{1,0:T(8,128)(2,1)S(1)} %pad_maximum_fusion.9), channel_id=1, source_target_pairs={{0,2},{1,3},{2,0},{3,1},{4,6},{5,7},{6,4},{7,5},{8,10},{9,11},{10,... | collective-permute-start | bytes 3145736 | tf_op jit(solution)/shard_map/ppermute | solution.py:546
  330.1 30.4 %collective-permute-start.26 = (bf16[512,1024]{1,0:T(8,128)(2,1)S(1)}, bf16[512,1024]{1,0:T(8,128)(2,1)S(1)}, u32[]{:S(2)}, u32[]{:S(2)}) collective-permute-start(bf16[512,1024]{1,0:T(8,128)(2,1)S(1)} %pad_maximum_fusion.8), channel_id=1, source_target_pairs={{0,4},{1,5},{2,6},{3,7},{4,0},{5,1},{6,2},{7,3},{8,12},{9,13},{10,... | collective-permute-start | bytes 3145736 | tf_op jit(solution)/shard_map/ppermute | solution.py:546
  339.2 38.1 %collective-permute-start.30 = (bf16[1024,512]{1,0:T(8,128)(2,1)S(1)}, bf16[1024,512]{1,0:T(8,128)(2,1)S(1)}, u32[]{:S(2)}, u32[]{:S(2)}) collective-permute-start(bf16[1024,512]{1,0:T(8,128)(2,1)S(1)} %get-tuple-element.135), channel_id=1, source_target_pairs={{0,2},{1,3},{2,0},{3,1},{4,6},{5,7},{6,4},{7,5},{8,10},{9,11},{10,... | collective-permute-start | bytes 3145736 | tf_op jit(solution)/shard_map/ppermute | solution.py:546
  359.5 19.2 %collective-permute-start.29 = (bf16[512,512]{1,0:T(8,128)(2,1)}, bf16[512,512]{1,0:T(8,128)(2,1)}, u32[]{:S(2)}, u32[]{:S(2)}) collective-permute-start(bf16[512,512]{1,0:T(8,128)(2,1)} %slice.259), channel_id=1, source_target_pairs={{0,4},{1,5},{2,6},{3,7},{4,0},{5,1},{6,2},{7,3},{8,12},{9,13},{10,... | collective-permute-start | bytes 1572872 | tf_op jit(solution)/shard_map/ppermute | solution.py:546
  363.1 25.0 %collective-permute-start.28 = (bf16[512,512]{1,0:T(8,128)(2,1)}, bf16[512,512]{1,0:T(8,128)(2,1)}, u32[]{:S(2)}, u32[]{:S(2)}) collective-permute-start(bf16[512,512]{1,0:T(8,128)(2,1)} %slice.260), channel_id=1, source_target_pairs={{0,2},{1,3},{2,0},{3,1},{4,6},{5,7},{6,4},{7,5},{8,10},{9,11},{10,... | collective-permute-start | bytes 1572872 | tf_op jit(solution)/shard_map/ppermute | solution.py:546
  377.3 41.4 %collective-permute-start.32 = (bf16[1024,1024]{1,0:T(8,128)(2,1)}, bf16[1024,1024]{1,0:T(8,128)(2,1)}, u32[]{:S(2)}, u32[]{:S(2)}) collective-permute-start(bf16[1024,1024]{1,0:T(8,128)(2,1)} %get-tuple-element.140), channel_id=1, source_target_pairs={{0,1},{1,0},{2,3},{3,2},{4,5},{5,4},{6,7},{7,6},{8,9},{9,8},{10,11... | collective-permute-start | bytes 6291464 | tf_op jit(solution)/shard_map/ppermute | solution.py:546
  407.2 19.2 %collective-permute-start.31 = (bf16[1024,1024]{1,0:T(8,128)(2,1)}, bf16[1024,1024]{1,0:T(8,128)(2,1)}, u32[]{:S(2)}, u32[]{:S(2)}) collective-permute-start(bf16[1024,1024]{1,0:T(8,128)(2,1)} %get-tuple-element.138), channel_id=1, source_target_pairs={{0,1},{1,0},{2,3},{3,2},{4,5},{5,4},{6,7},{7,6},{8,9},{9,8},{10,11... | collective-permute-start | bytes 6291464 | tf_op jit(solution)/shard_map/ppermute | solution.py:546
  411.1 27.2 %collective-permute-start.33 = (bf16[256,512]{0,1:T(8,128)(2,1)S(1)}, bf16[256,512]{0,1:T(8,128)(2,1)}, u32[]{:S(2)}, u32[]{:S(2)}) collective-permute-start(bf16[256,512]{0,1:T(8,128)(2,1)S(1)} %bitcast.142), channel_id=1, source_target_pairs={{0,8},{8,16},{16,24},{24,0},{1,9},{9,17},{17,25},{25,1},{2,10},{10... | collective-permute-start | bytes 786440 | tf_op jit(solution)/shard_map/ppermute | solution.py:588
  413.3 25.0 %collective-permute-start.34 = (bf16[256,512]{0,1:T(8,128)(2,1)S(1)}, bf16[256,512]{0,1:T(8,128)(2,1)}, u32[]{:S(2)}, u32[]{:S(2)}) collective-permute-start(bf16[256,512]{0,1:T(8,128)(2,1)S(1)} %bitcast.143), channel_id=1, source_target_pairs={{0,16},{8,24},{16,0},{24,8},{1,17},{9,25},{17,1},{25,9},{2,18},{10... | collective-permute-start | bytes 786440 | tf_op jit(solution)/shard_map/ppermute | solution.py:588
  417.1 21.2 %collective-permute-start.35 = (bf16[256,512]{0,1:T(8,128)(2,1)}, bf16[256,512]{0,1:T(8,128)(2,1)}, u32[]{:S(2)}, u32[]{:S(2)}) collective-permute-start(bf16[256,512]{0,1:T(8,128)(2,1)} %bitcast.52), channel_id=1, source_target_pairs={{0,24},{8,0},{16,8},{24,16},{1,25},{9,1},{17,9},{25,17},{2,26},{10... | collective-permute-start | bytes 786440 | tf_op jit(solution)/shard_map/ppermute | solution.py:588
  435.7 13.2 %all-to-all-start.2 = ((f32[32,14,128]{2,1,0:T(8,128)}), f32[32,14,128]{2,1,0:T(8,128)S(1)}, u32[]{:S(2)}, u32[]{:S(2)}) async-start(f32[32,14,128]{2,1,0:T(8,128)} %bitcast.42), calls=%async_computation.4 | async-start | bytes 524288 | tf_op jit(solution)/shard_map/all_to_all | solution.py:630
  451.3 10.8 %all-to-all-start.3 = ((f32[32,8,128]{2,1,0:T(8,128)}), f32[32,8,128]{2,1,0:T(8,128)S(1)}, u32[]{:S(2)}, u32[]{:S(2)}) async-start(f32[32,8,128]{2,1,0:T(8,128)} %bitcast.46), calls=%async_computation.5 | async-start | bytes 262144 | tf_op jit(solution)/shard_map/all_to_all | solution.py:630
  (39 other events, 309.3 us)
Sparse Core Ops, SparseCore 0:
  51.4 27.0 all-gather.2
  96.3 27.3 all-gather.4
  317.8 26.2 reduce-scatter.2
  378.7 26.3 reduce-scatter.4

commit v7 on v6

--- a/solution.py
+++ b/solution.py
@@ -803,7 +803,6 @@
     mixed = after(mixed, *[held for held, _ in fc2_early])
     fc1_all = unit_pieces(fc1_early, fc1_last)
     fc2_all = unit_pieces(fc2_early, fc2_last)
-    order1 = grid.orders[0]
     out_all = [(out_w, 0, out_w.shape[1])]
     totals = own_total([mixed], out_all)
     attention_out, hidden_feed = token_kernel(
@@ -846,7 +845,7 @@
     grad_pre, bias_fc1 = rows_product(
         (after(grad_feed_low[0], fc2_sent), grad_feed_low[1]), fc2_all, slopes, "slope"
     )
-    fc1_got, sent = send_units(hidden_feed, grad_pre, [order1])
+    fc1_got, sent = send_units(hidden_feed, grad_pre, grid.orders)
     totals = own_total([after(grad_pre, sent, *fc2_got)], fc1_all)
     fc2_kept = keep_units(grad_feed_low, after(acts, totals[0]), fc2_got, grid.orders)
     grad_resid_mid, grad_attention_low, middle_sums = token_kernel(
@@ -870,7 +869,7 @@
         projected, mixed, grad_mixed, log_totals, latents, 1, pairs - 1
     )
     fc2_sums = sum_chips(fc2_kept, grid.orders, (grad_late,))
-    fc1_kept = keep_units(hidden_feed, after(grad_pre, grad_late), fc1_got, [order1])
+    fc1_kept = keep_units(hidden_feed, after(grad_pre, grad_late), fc1_got, grid.orders)
     late_chips = chips * (pairs - 1) // pairs
     qkv_late = columns_product(
         hidden_attn, grad_late, [], [[i] for i in range(late_chips)], qkv_width
@@ -881,7 +880,7 @@
     grad_early, bias_early = attend_back(
         projected, mixed, early_input, log_totals, latents, 0, 1
     )
-    fc1_sums = sum_chips(fc1_kept, [order1], (grad_early,))
+    fc1_sums = sum_chips(fc1_kept, grid.orders, (grad_early,))
     fc2_part = sum_rows(fc2_sums)
     fc1_part = sum_rows(fc1_sums)
     bias_qkv = jnp.concatenate([bias_early, bias_late], 1).sum((0, 2))

time: 476 us -> 489 us (1.027)
  local copies, waits for them, and re-layouts: 37.7 us -> 45.1 us
  other arithmetic: 28.7 us -> 34 us
    unnamed x95 -> x109, local copies, waits for them, and re-layouts: 17.3 us -> 20.8 us
    ppermute x30 -> x32, starting transfers between devices: 25.4 us -> 27.6 us  [swap(): return lax.ppermute(array, 'col', pairs)]
    ppermute x30 -> x32, waiting for transfers between devices: 46.6 us -> 45.4 us  [swap(): return lax.ppermute(array, 'col', pairs)]
  transfers between devices with their start and end apart: 44 -> 46, of which waited for: 16 -> 15; matrix products, arithmetic and copies ran while one was open for 11% -> 13% of each run, Pallas kernels for 47% -> 45%
where the time goes in v7:
time: 489 us; the launch traced here: 483 us
  Pallas kernels  260 us (53%)
  waiting for transfers between devices  71.1 us (15%)
  starting transfers between devices  53.3 us (11%)
  local copies, waits for them, and re-layouts  45.1 us (9%)
  other arithmetic  34 us (7%)
  between operations  15.2 us (3%)
    pallas_call x24, Pallas kernels, wrapped(): call(*[pltpu.with_memory_space_constraint(a, pltpu.HBM) if is_large(a) el...  260 us
    ppermute x32, waiting for transfers between devices, swap(): return lax.ppermute(array, 'col', pairs)  45.4 us
    ppermute x32, starting transfers between devices, swap(): return lax.ppermute(array, 'col', pairs)  27.6 us
    all_to_all x4, waiting for transfers between devices, all_exchange(): return lax.all_to_all(pieces, ('row', 'col'), 0, 0, tiled=True)  25.5 us
    unnamed x109, local copies, waits for them, and re-layouts  20.8 us
    all_to_all x4, starting transfers between devices, all_exchange(): return lax.all_to_all(pieces, ('row', 'col'), 0, 0, tiled=True)  14.1 us
  transfers between devices with their start and end apart: 46, of which 15 were waited for; matrix products, arithmetic and copies ran while one was open for 13% of the time, Pallas kernels for 45%

profile of v7, /device:TPU:0, one launch (start us, length us, event | category | flops | bytes accessed | tf_op | source)
XLA Modules:
  0.0 482.9 jit_solution(17004731383443862289)
XLA Ops:
  9.1 5.1 %collective-permute-start.3 = (bf16[256,512]{0,1:T(8,128)(2,1)S(1)}, bf16[256,512]{0,1:T(8,128)(2,1)S(1)}, u32[]{:S(2)}, u32[]{:S(2)}) collective-permute-start(bf16[256,512]{0,1:T(8,128)(2,1)S(1)} %get-tuple-element.257), channel_id=1, source_target_pairs={{0,24},{8,0},{16,8},{24,16},{1,25},{9,1},{17,9},{25,17},{2,26},{10... | collective-permute-start | bytes 786440 | tf_op jit(solution)/shard_map/ppermute | solution.py:573
  19.9 5.6 %all-to-all-start = ((bf16[32,16,128]{2,1,0:T(8,128)(2,1)}), bf16[32,16,128]{2,1,0:T(8,128)(2,1)S(1)}, u32[]{:S(2)}, u32[]{:S(2)}) async-start(bf16[32,16,128]{2,1,0:T(8,128)(2,1)} %broadcast_in_dim.32), calls=%async_computation | async-start | bytes 262144 | tf_op jit(solution)/shard_map/all_to_all | solution.py:630
  25.5 2.3 convert_reduce_fusion
  28.1 12.8 %all-to-all-done = bf16[32,16,128]{2,1,0:T(8,128)(2,1)S(1)} async-done(((bf16[32,16,128]{2,1,0:T(8,128)(2,1)}), bf16[32,16,128]{2,1,0:T(8,128)(2,1)S(1)}, u32[]{:S(2)}, u32[]{:S(2)}) %all-to-all-start) | async-done | bytes 131104 | tf_op jit(solution)/shard_map/all_to_all | solution.py:630
  42.1 3.4 all-to-all-start.1
  51.4 2.4 all-to-all-done.1
  54.7 2.1 fusion.3.refs_0_.mine_ref
  57.0 5.2 %collective-permute-done.6 = bf16[512,512]{1,0:T(8,128)(2,1)} collective-permute-done((bf16[512,512]{1,0:T(8,128)(2,1)}, bf16[512,512]{1,0:T(8,128)(2,1)}, u32[]{:S(2)}, u32[]{:S(2)}) %collective-permute-start.6) | collective-permute-done | bytes 524320 | tf_op jit(solution)/shard_map/ppermute | solution.py:546
  64.9 2.1 pad_maximum_fusion.1.a_ref
  70.9 17.4 %collective-permute-done.7.d_ref = bf16[512,1024]{1,0:T(8,128)(2,1)} collective-permute-done((bf16[512,1024]{1,0:T(8,128)(2,1)S(1)}, bf16[512,1024]{1,0:T(8,128)(2,1)}, u32[]{:S(2)}, u32[]{:S(2)}) %collective-permute-start.7) | collective-permute-done | bytes 1048608 | tf_op jit(solution)/shard_map/ppermute | solution.py:546
  88.3 3.3 collective-permute-done.5.b_ref
  91.6 2.2 fusion.34
  96.9 2.9 assemble.1
  100.9 11.2 %rows_bias.2.q_ref.k_ref.v_ref = bf16[2048,1536]{1,0:T(8,128)(2,1)} custom-call(bf16[1024,1024]{1,0:T(8,128)(2,1)} %fusion.3.refs_0_.mine_ref, bf16[1024,1024]{1,0:T(8,128)(2,1)} %collective-permute-done.refs_1_.theirs_ref, bf16[1024,1536]{1,0:T(8,128)(2,1)S(1)} %bitcast.121, f32[1,1536]{1,0:T(1,128)S(1)} %reshape.212.refs_3_), custom_call_target="tpu_custom_call" | custom-call | flops 1000 | bytes 1000 | tf_op jit(solution)/shard_map/rows_bias/pallas_call | solution.py:48
  114.7 2.3 pad_maximum_fusion.3.refs_2_.refs_4_.refs_1_.refs_3_
  117.6 17.4 %attend.2 = (bf16[2048,512]{1,0:T(8,128)(2,1)S(1)}, f32[2,4,2,1024]{3,2,1,0:T(2,128)S(1)}) custom-call(bf16[2048,1536]{1,0:T(8,128)(2,1)} %rows_bias.2.q_ref.k_ref.v_ref, bf16[2048,1536]{1,0:T(8,128)(2,1)} %rows_bias.2.q_ref.k_ref.v_ref, bf16[2048,1536]{1,0:T(8,128)(2,1)} %rows_bias.2.q_ref.k_ref.v_ref), custom_call_target="tpu_custom_call" | custom-call | flops 1000 | bytes 1000 | tf_op jit(solution)/shard_map/attend/pallas_call | solution.py:48
  136.4 3.5 collective-permute-done.10.refs_6_.refs_8_.refs_5_.refs_7_
  142.7 17.4 %attend.3 = (bf16[2048,512]{1,0:T(8,128)(2,1)S(1)}, f32[2,4,2,1024]{3,2,1,0:T(2,128)S(1)}) custom-call(bf16[2048,1536]{1,0:T(8,128)(2,1)} %rows_bias.2.q_ref.k_ref.v_ref, bf16[2048,1536]{1,0:T(8,128)(2,1)} %rows_bias.2.q_ref.k_ref.v_ref, bf16[2048,1536]{1,0:T(8,128)(2,1)} %rows_bias.2.q_ref.k_ref.v_ref, ...), custom_call_target="tpu_custom_call", output_to_operand_aliasing={{0}: (3, {}), {1}: (4, {})} | custom-call | flops 1000 | bytes 1000 | tf_op jit(solution)/shard_map/attend/pallas_call | solution.py:48
  162.1 5.1 %rows_total.4 = (f32[1024,1024]{1,0:T(8,128)}, bf16[1024,1024]{1,0:T(8,128)(2,1)S(1)}) custom-call(bf16[2048,512]{1,0:T(8,128)(2,1)S(1)} %get-tuple-element.121.refs_0_.mixed_ref, bf16[1024,512]{1,0:T(8,128)(2,1)S(1)} %bitcast.123), custom_call_target="tpu_custom_call" | custom-call | flops 1000 | bytes 1000 | tf_op jit(solution)/shard_map/rows_total/pallas_call | solution.py:48
  167.3 4.1 collective-permute-done.14.refs_1_
  171.4 5.3 %middle.1 = (f32[1024,1024]{1,0:T(8,128)}, bf16[1024,1024]{1,0:T(8,128)(2,1)S(1)}) custom-call(f32[1024,1024]{1,0:T(8,128)} %get-tuple-element.100.refs_0_, bf16[1024,1024]{1,0:T(8,128)(2,1)S(1)} %collective-permute-done.14.refs_1_, bf16[1024,1024]{1,0:T(8,128)(2,1)S(1)} %copy-done, f32[8,1024]{1,0:T(8,128)S(1)} %pad_maximum_fusion.16.refs_3_.refs_5_.refs_4_), custom_call_target="tpu_custom_call" | custom-call | flops 1000 | bytes 1000 | tf_op jit(solution)/shard_map/middle/pallas_call | solution.py:48
  180.9 19.9 %rows_gelu.1 = (bf16[2048,2048]{1,0:T(8,128)(2,1)}, bf16[2048,2048]{1,0:T(8,128)(2,1)}) custom-call(bf16[1024,1024]{1,0:T(8,128)(2,1)S(1)} %get-tuple-element.102.refs_0_.mine_ref, bf16[1024,1024]{1,0:T(8,128)(2,1)S(1)} %collective-permute-done.15.refs_1_.theirs_ref, bf16[1024,512]{1,0:T(8,128)(2,1)} %pad_maximum_fusion.3.refs_2_.refs_4_.refs_1_.refs_3_, ...), custom_call_target="tpu_custom_call" | custom-call | flops 1000 | bytes 1000 | tf_op jit(solution)/shard_map/rows_gelu/pallas_call | solution.py:48
  200.8 2.3 collective-permute-done.17.refs_5_.refs_9_.refs_4_.refs_8_
  204.0 8.1 %columns_product.7 = (bf16[1024,512]{1,0:T(8,128)(2,1)S(1)}, bf16[1024,512]{1,0:T(8,128)(2,1)S(1)}) custom-call(bf16[1024,1024]{1,0:T(8,128)(2,1)S(1)} %multiply_convert_fusion.mine_ref.refs_0_, bf16[1024,1024]{1,0:T(8,128)(2,1)S(1)} %collective-permute-done.18.theirs_ref.refs_1_, bf16[2048,2048]{1,0:T(8,128)(2,1)} %get-tuple-element.140.refs_0_.refs_1_.refs_2_.refs_3_, ...), custom_call_target="tpu_custom_call" | custom-call | flops 1000 | bytes 1000 | tf_op jit(solution)/shard_map/columns_product/pallas_call | solution.py:48
  214.3 13.2 %rows_slope.1 = (bf16[2048,2048]{1,0:T(8,128)(2,1)}, f32[8,2048]{1,0:T(8,128)S(1)}) custom-call(bf16[1024,1024]{1,0:T(8,128)(2,1)S(1)} %multiply_convert_fusion.mine_ref.refs_0_, bf16[1024,1024]{1,0:T(8,128)(2,1)S(1)} %collective-permute-done.18.theirs_ref.refs_1_, bf16[1024,512]{1,0:T(8,128)(2,1)S(1)} %pad_maximum_fusion.5.refs_2_.refs_4_.refs_1_.refs_3_, ...), custom_call_target="tpu_custom_call" | custom-call | flops 1000 | bytes 1000 | tf_op jit(solution)/shard_map/rows_slope/pallas_call | solution.py:48
  227.5 7.8 %columns_product.8 = (bf16[1024,512]{1,0:T(8,128)(2,1)S(1)}, bf16[1024,512]{1,0:T(8,128)(2,1)S(1)}) custom-call(bf16[1024,1024]{1,0:T(8,128)(2,1)S(1)} %get-tuple-element.102.refs_0_.mine_ref, bf16[1024,1024]{1,0:T(8,128)(2,1)S(1)} %collective-permute-done.15.refs_1_.theirs_ref, bf16[2048,2048]{1,0:T(8,128)(2,1)} %get-tuple-element.130.refs_0_.refs_1_.refs_2_.refs_3_, ...), custom_call_target="tpu_custom_call" | custom-call | flops 1000 | bytes 1000 | tf_op jit(solution)/shard_map/columns_product/pallas_call | solution.py:48
  237.3 13.9 %rows_total.5 = (f32[1024,1024]{1,0:T(8,128)}, bf16[1024,1024]{1,0:T(8,128)(2,1)S(1)}) custom-call(bf16[2048,2048]{1,0:T(8,128)(2,1)} %get-tuple-element.130.refs_0_.refs_1_.refs_2_.refs_3_, bf16[1024,512]{1,0:T(8,128)(2,1)} %pad_maximum_fusion.3.refs_2_.refs_4_.refs_1_.refs_3_, bf16[1024,512]{1,0:T(8,128)(2,1)S(1)} %copy-done.8, ...), custom_call_target="tpu_custom_call" | custom-call | flops 1000 | bytes 1000 | tf_op jit(solution)/shard_map/rows_total/pallas_call | solution.py:48
  251.2 7.9 %columns_product.9 = (bf16[1024,256]{1,0:T(8,128)(2,1)S(1)}, bf16[1024,256]{1,0:T(8,128)(2,1)S(1)}, bf16[1024,256]{1,0:T(8,128)(2,1)S(1)}, bf16[1024,256]{1,0:T(8,128)(2,1)S(1)}) custom-call(bf16[1024,1024]{1,0:T(8,128)(2,1)S(1)} %multiply_convert_fusion.mine_ref.refs_0_, bf16[1024,1024]{1,0:T(8,128)(2,1)S(1)} %collective-permute-done.18.theirs_ref.refs_1_, ...), custom_call_target="tpu_custom_call" | custom-call | flops 1000 | bytes 1000 | tf_op jit(solution)/shard_map/columns_product/pallas_call | solution.py:48
  259.1 8.2 %middle_back.1 = (f32[1024,1024]{1,0:T(8,128)}, bf16[1024,1024]{1,0:T(8,128)(2,1)S(1)}, f32[4,8,1024]{2,1,0:T(8,128)S(1)}) custom-call(f32[1024,1024]{1,0:T(8,128)} %get-tuple-element.117.refs_0_, bf16[1024,1024]{1,0:T(8,128)(2,1)S(1)} %collective-permute-done.21.refs_1_, bf16[1024,1024]{1,0:T(8,128)(2,1)S(1)} %copy-done.9, bf16[1024,1024]{1,0:T(8,128)(2,1)S(1)} %copy-done, ...), custom_call_target="tpu_custom_call" | custom-call | flops 1000 | bytes 1000 | tf_op jit(solution)/shard_map/middle_back/pallas_call | solution.py:48
  271.9 2.9 rows_bias.3.grad_ref
  274.8 3.6 columns_product.10
  278.4 38.0 %attend_back.2 = (bf16[2048,1152]{1,0:T(8,128)(2,1)}, f32[2,3,8,384]{3,2,1,0:T(8,128)S(1)}) custom-call(bf16[2048,1536]{1,0:T(8,128)(2,1)} %rows_bias.2.q_ref.k_ref.v_ref, bf16[2048,1536]{1,0:T(8,128)(2,1)} %rows_bias.2.q_ref.k_ref.v_ref, bf16[2048,1536]{1,0:T(8,128)(2,1)} %rows_bias.2.q_ref.k_ref.v_ref, ...), custom_call_target="tpu_custom_call" | custom-call | flops 1000 | bytes 1000 | tf_op jit(solution)/shard_map/attend_back/pallas_call | solution.py:48
  316.4 10.2 %columns_product.12 = (bf16[1024,384]{1,0:T(8,128)(2,1)S(1)}, bf16[1024,384]{1,0:T(8,128)(2,1)S(1)}, bf16[1024,384]{1,0:T(8,128)(2,1)S(1)}) custom-call(bf16[1024,1024]{1,0:T(8,128)(2,1)} %fusion.3.refs_0_.mine_ref, bf16[1024,1024]{1,0:T(8,128)(2,1)} %collective-permute-done.refs_1_.theirs_ref, ...), custom_call_target="tpu_custom_call" | custom-call | flops 1000 | bytes 1000 | tf_op jit(solution)/shard_map/columns_product/pallas_call | solution.py:48
  331.7 8.6 %columns_product.11 = (bf16[1024,256]{1,0:T(8,128)(2,1)S(1)}, bf16[1024,256]{1,0:T(8,128)(2,1)}, bf16[1024,256]{1,0:T(8,128)(2,1)S(1)}, bf16[1024,256]{1,0:T(8,128)(2,1)}) custom-call(bf16[1024,1024]{1,0:T(8,128)(2,1)S(1)} %get-tuple-element.102.refs_0_.mine_ref, bf16[1024,1024]{1,0:T(8,128)(2,1)S(1)} %collective-permute-done.15.refs_1_.theirs_ref, ...), custom_call_target="tpu_custom_call" | custom-call | flops 1000 | bytes 1000 | tf_op jit(solution)/shard_map/columns_product/pallas_call | solution.py:48
  349.0 13.3 %attend_back.3 = (bf16[2048,384]{1,0:T(8,128)(2,1)S(1)}, f32[2,1,8,384]{3,2,1,0:T(8,128)S(1)}) custom-call(bf16[2048,1536]{1,0:T(8,128)(2,1)} %rows_bias.2.q_ref.k_ref.v_ref, bf16[2048,1536]{1,0:T(8,128)(2,1)} %rows_bias.2.q_ref.k_ref.v_ref, bf16[2048,1536]{1,0:T(8,128)(2,1)} %rows_bias.2.q_ref.k_ref.v_ref, bf16[2048,512]{1,0:T(8,128)(2,1)S(1)} %copy-done.4, ...), custom_call_target="tpu_custom_call" | custom-call | flops 1000 | bytes 1000 | tf_op jit(solution)/shard_map/attend_back/pallas_call | solution.py:48
  362.4 5.4 %columns_product.13 = bf16[1024,384]{1,0:T(8,128)(2,1)S(1)} custom-call(bf16[1024,1024]{1,0:T(8,128)(2,1)} %fusion.3.refs_0_.mine_ref, bf16[1024,1024]{1,0:T(8,128)(2,1)} %collective-permute-done.refs_1_.theirs_ref, bf16[2048,384]{1,0:T(8,128)(2,1)S(1)} %get-tuple-element.138.refs_0_), custom_call_target="tpu_custom_call" | custom-call | flops 1000 | bytes 1000 | tf_op jit(solution)/shard_map/columns_product/pallas_call | solution.py:48
  372.4 6.5 %collective-permute-done.27 = bf16[512,1024]{1,0:T(8,128)(2,1)S(1)} collective-permute-done((bf16[512,1024]{1,0:T(8,128)(2,1)S(1)}, bf16[512,1024]{1,0:T(8,128)(2,1)S(1)}, u32[]{:S(2)}, u32[]{:S(2)}) %collective-permute-start.27) | collective-permute-done | bytes 1048608 | tf_op jit(solution)/shard_map/ppermute | solution.py:546
  386.8 11.9 %rows_total.6 = (f32[1024,1024]{1,0:T(8,128)}, bf16[1024,1024]{1,0:T(8,128)(2,1)}) custom-call(bf16[2048,384]{1,0:T(8,128)(2,1)S(1)} %copy-done.20, bf16[2048,1152]{1,0:T(8,128)(2,1)} %get-tuple-element.124.refs_0_.refs_1_.refs_2_, bf16[1024,1536]{1,0:T(8,128)(2,1)S(1)} %bitcast.122), custom_call_target="tpu_custom_call" | custom-call | flops 1000 | bytes 1000 | tf_op jit(solution)/shard_map/rows_total/pallas_call | solution.py:48
  398.7 2.2 slice_add_fusion
  400.9 2.0 slice_add_fusion.1
  406.6 13.4 %rows_total.7 = (f32[1024,1024]{1,0:T(8,128)}, bf16[1024,1024]{1,0:T(8,128)(2,1)}) custom-call(bf16[2048,2048]{1,0:T(8,128)(2,1)} %get-tuple-element.140.refs_0_.refs_1_.refs_2_.refs_3_, bf16[1024,512]{1,0:T(8,128)(2,1)S(1)} %copy-done.6, bf16[1024,512]{1,0:T(8,128)(2,1)S(1)} %pad_maximum_fusion.6.refs_3_.refs_7_.refs_2_.refs_6_, ...), custom_call_target="tpu_custom_call" | custom-call | flops 1000 | bytes 1000 | tf_op jit(solution)/shard_map/rows_total/pallas_call | solution.py:48
  432.1 7.7 %first_back.1 = (f32[1024,1024]{1,0:T(8,128)}, f32[2,8,1024]{2,1,0:T(8,128)S(1)}) custom-call(f32[1024,1024]{1,0:T(8,128)} %get-tuple-element.139.refs_0_, bf16[1024,1024]{1,0:T(8,128)(2,1)} %collective-permute-done.34.refs_1_, bf16[1024,1024]{1,0:T(8,128)(2,1)S(1)} %copy-done, f32[1024,1024]{1,0:T(8,128)} %get-tuple-element.151.refs_3_, ...), custom_call_target="tpu_custom_call" | custom-call | flops 1000 | bytes 1000 | tf_op jit(solution)/shard_map/first_back/pallas_call | solution.py:48
  441.5 6.8 %last.1 = (bf16[1024,1024]{1,0:T(8,128)(2,1)}, f32[2,8,1024]{2,1,0:T(8,128)S(1)}) custom-call(f32[1024,1024]{1,0:T(8,128)} %get-tuple-element.147.refs_0_, bf16[1024,1024]{1,0:T(8,128)(2,1)} %collective-permute-done.33.refs_1_, bf16[1024,1024]{1,0:T(8,128)(2,1)S(1)} %copy-done, f32[1024,1024]{1,0:T(8,128)} %get-tuple-element.119.refs_4_.refs_3_, ...), custom_call_target="tpu_custom_call" | custom-call | flops 1000 | bytes 1000 | tf_op jit(solution)/shard_map/last/pallas_call | solution.py:48
  449.1 2.6 all-to-all-start.2
  456.4 5.9 %all-to-all-done.2 = f32[32,14,128]{2,1,0:T(8,128)S(1)} async-done(((f32[32,14,128]{2,1,0:T(8,128)}), f32[32,14,128]{2,1,0:T(8,128)S(1)}, u32[]{:S(2)}, u32[]{:S(2)}) %all-to-all-start.2) | async-done | bytes 229408 | tf_op jit(solution)/shard_map/all_to_all | solution.py:630
  464.7 2.6 all-to-all-start.3
  469.0 2.2 fusion.9
  471.1 4.4 all-to-all-done.3
  (284 shorter events, 103.2 us)
Async XLA Ops:
  9.1 36.4 %collective-permute-start.3 = (bf16[256,512]{0,1:T(8,128)(2,1)S(1)}, bf16[256,512]{0,1:T(8,128)(2,1)S(1)}, u32[]{:S(2)}, u32[]{:S(2)}) collective-permute-start(bf16[256,512]{0,1:T(8,128)(2,1)S(1)} %get-tuple-element.257), channel_id=1, source_target_pairs={{0,24},{8,0},{16,8},{24,16},{1,25},{9,1},{17,9},{25,17},{2,26},{10... | collective-permute-start | bytes 786440 | tf_op jit(solution)/shard_map/ppermute | solution.py:573
  14.2 31.3 %collective-permute-start.1 = (bf16[256,512]{0,1:T(8,128)(2,1)S(1)}, bf16[256,512]{0,1:T(8,128)(2,1)S(1)}, u32[]{:S(2)}, u32[]{:S(2)}) collective-permute-start(bf16[256,512]{0,1:T(8,128)(2,1)S(1)} %get-tuple-element.257), channel_id=1, source_target_pairs={{0,8},{8,16},{16,24},{24,0},{1,9},{9,17},{17,25},{25,1},{2,10},{10... | collective-permute-start | bytes 786440 | tf_op jit(solution)/shard_map/ppermute | solution.py:573
  14.2 31.3 %collective-permute-start.2 = (bf16[256,512]{0,1:T(8,128)(2,1)S(1)}, bf16[256,512]{0,1:T(8,128)(2,1)S(1)}, u32[]{:S(2)}, u32[]{:S(2)}) collective-permute-start(bf16[256,512]{0,1:T(8,128)(2,1)S(1)} %get-tuple-element.257), channel_id=1, source_target_pairs={{0,16},{8,24},{16,0},{24,8},{1,17},{9,25},{17,1},{25,9},{2,18},{10... | collective-permute-start | bytes 786440 | tf_op jit(solution)/shard_map/ppermute | solution.py:573
  19.9 21.1 %all-to-all-start = ((bf16[32,16,128]{2,1,0:T(8,128)(2,1)}), bf16[32,16,128]{2,1,0:T(8,128)(2,1)S(1)}, u32[]{:S(2)}, u32[]{:S(2)}) async-start(bf16[32,16,128]{2,1,0:T(8,128)(2,1)} %broadcast_in_dim.32), calls=%async_computation | async-start | bytes 262144 | tf_op jit(solution)/shard_map/all_to_all | solution.py:630
  42.1 11.7 %all-to-all-start.1 = ((f32[32,6,128]{2,1,0:T(8,128)}), f32[32,6,128]{2,1,0:T(8,128)}, u32[]{:S(2)}, u32[]{:S(2)}) async-start(f32[32,6,128]{2,1,0:T(8,128)} %copy.96), calls=%async_computation.1 | async-start | bytes 262144 | tf_op jit(solution)/shard_map/all_to_all | solution.py:630
  45.4 46.2 %all-gather.3.cloned.1.call-start = ((), (), s32[]{:S(2)}) async-start(), calls=%async_computation.6 | async-start | bytes 1310720 | tf_op jit(solution)/shard_map/all_gather | solution.py:695
  46.9 15.2 %collective-permute-start.6 = (bf16[512,512]{1,0:T(8,128)(2,1)}, bf16[512,512]{1,0:T(8,128)(2,1)}, u32[]{:S(2)}, u32[]{:S(2)}) collective-permute-start(bf16[512,512]{1,0:T(8,128)(2,1)} %pad_maximum_fusion.13), channel_id=1, source_target_pairs={{0,4},{1,5},{2,6},{3,7},{4,0},{5,1},{6,2},{7,3},{8,12},{9,13},{10,... | collective-permute-start | bytes 1572872 | tf_op jit(solution)/shard_map/ppermute | solution.py:546
  49.8 15.1 %collective-permute-start.4 = (bf16[512,512]{1,0:T(8,128)(2,1)}, bf16[512,512]{1,0:T(8,128)(2,1)}, u32[]{:S(2)}, u32[]{:S(2)}) collective-permute-start(bf16[512,512]{1,0:T(8,128)(2,1)} %pad_maximum_fusion.12), channel_id=1, source_target_pairs={{0,2},{1,3},{2,0},{3,1},{4,6},{5,7},{6,4},{7,5},{8,10},{9,11},{10,... | collective-permute-start | bytes 1572872 | tf_op jit(solution)/shard_map/ppermute | solution.py:546
  51.3 85.1 %all-gather.5.cloned.1.call-start = ((), (), s32[]{:S(2)}) async-start(), calls=%async_computation.7 | async-start | bytes 1310720 | tf_op jit(solution)/shard_map/all_gather | solution.py:696
  56.9 44.0 %collective-permute-start = (bf16[1024,1024]{1,0:T(8,128)(2,1)}, bf16[1024,1024]{1,0:T(8,128)(2,1)}, u32[]{:S(2)}, u32[]{:S(2)}) collective-permute-start(bf16[1024,1024]{1,0:T(8,128)(2,1)} %fusion.3.refs_0_.mine_ref), channel_id=1, source_target_pairs={{0,1},{1,0},{2,3},{3,2},{4,5},{5,4},{6,7},{7,6},{8,9},{9,8},{10,11... | collective-permute-start | bytes 6291464 | tf_op jit(solution)/shard_map/ppermute | solution.py:546
  63.4 24.8 %collective-permute-start.7 = (bf16[512,1024]{1,0:T(8,128)(2,1)S(1)}, bf16[512,1024]{1,0:T(8,128)(2,1)}, u32[]{:S(2)}, u32[]{:S(2)}) collective-permute-start(bf16[512,1024]{1,0:T(8,128)(2,1)S(1)} %pad_maximum_fusion.2.c_ref), channel_id=1, source_target_pairs={{0,2},{1,3},{2,0},{3,1},{4,6},{5,7},{6,4},{7,5},{8,10},{9,11},{10,... | collective-permute-start | bytes 3145736 | tf_op jit(solution)/shard_map/ppermute | solution.py:546
  67.0 24.6 %collective-permute-start.5 = (bf16[512,1024]{1,0:T(8,128)(2,1)}, bf16[512,1024]{1,0:T(8,128)(2,1)}, u32[]{:S(2)}, u32[]{:S(2)}) collective-permute-start(bf16[512,1024]{1,0:T(8,128)(2,1)} %pad_maximum_fusion.1.a_ref), channel_id=1, source_target_pairs={{0,4},{1,5},{2,6},{3,7},{4,0},{5,1},{6,2},{7,3},{8,12},{9,13},{10,... | collective-permute-start | bytes 3145736 | tf_op jit(solution)/shard_map/ppermute | solution.py:546
  93.8 18.2 %collective-permute-start.9 = (bf16[1024,256]{1,0:T(8,128)(2,1)}, bf16[1024,256]{1,0:T(8,128)(2,1)}, u32[]{:S(2)}, u32[]{:S(2)}) collective-permute-start(bf16[1024,256]{1,0:T(8,128)(2,1)} %get-tuple-element.240), channel_id=1, source_target_pairs={{0,4},{1,5},{2,6},{3,7},{4,0},{5,1},{6,2},{7,3},{8,12},{9,13},{10,... | collective-permute-start | bytes 1572872 | tf_op jit(solution)/shard_map/ppermute | solution.py:546
  95.2 16.9 %collective-permute-start.8 = (bf16[1024,256]{1,0:T(8,128)(2,1)}, bf16[1024,256]{1,0:T(8,128)(2,1)}, u32[]{:S(2)}, u32[]{:S(2)}) collective-permute-start(bf16[1024,256]{1,0:T(8,128)(2,1)} %get-tuple-element.241), channel_id=1, source_target_pairs={{0,2},{1,3},{2,0},{3,1},{4,6},{5,7},{6,4},{7,5},{8,10},{9,11},{10,... | collective-permute-start | bytes 1572872 | tf_op jit(solution)/shard_map/ppermute | solution.py:546
  96.2 306.7 %reduce-scatter.3.cloned.1.call-start = ((), (), s32[]{:S(2)}) async-start(), calls=%async_computation.8 | async-start | bytes 1310720 | tf_op jit(solution)/shard_map/reduce_scatter | solution.py:762
  113.4 23.1 %collective-permute-start.11 = (bf16[1024,512]{1,0:T(8,128)(2,1)S(1)}, bf16[1024,512]{1,0:T(8,128)(2,1)}, u32[]{:S(2)}, u32[]{:S(2)}) collective-permute-start(bf16[1024,512]{1,0:T(8,128)(2,1)S(1)} %pad_maximum_fusion.4.refs_3_.refs_7_.refs_2_.refs_6_), channel_id=1, source_target_pairs={{0,2},{1,3},{2,0},{3,1},{4,6},{5,7},{6,4},{7,5},{8,10},{9,11},{10,... | collective-permute-start | bytes 3145736 | tf_op jit(solution)/shard_map/ppermute | solution.py:546
  117.0 22.9 %collective-permute-start.10 = (bf16[1024,512]{1,0:T(8,128)(2,1)}, bf16[1024,512]{1,0:T(8,128)(2,1)}, u32[]{:S(2)}, u32[]{:S(2)}) collective-permute-start(bf16[1024,512]{1,0:T(8,128)(2,1)} %pad_maximum_fusion.3.refs_2_.refs_4_.refs_1_.refs_3_), channel_id=1, source_target_pairs={{0,4},{1,5},{2,6},{3,7},{4,0},{5,1},{6,2},{7,3},{8,12},{9,13},{10,... | collective-permute-start | bytes 3145736 | tf_op jit(solution)/shard_map/ppermute | solution.py:546
  141.2 18.9 %collective-permute-start.13 = (bf16[1024,256]{1,0:T(8,128)(2,1)S(1)}, bf16[1024,256]{1,0:T(8,128)(2,1)S(1)}, u32[]{:S(2)}, u32[]{:S(2)}) collective-permute-start(bf16[1024,256]{1,0:T(8,128)(2,1)S(1)} %get-tuple-element.238), channel_id=1, source_target_pairs={{0,4},{1,5},{2,6},{3,7},{4,0},{5,1},{6,2},{7,3},{8,12},{9,13},{10,... | collective-permute-start | bytes 1572872 | tf_op jit(solution)/shard_map/ppermute | solution.py:546
  141.8 18.4 %collective-permute-start.12 = (bf16[1024,256]{1,0:T(8,128)(2,1)S(1)}, bf16[1024,256]{1,0:T(8,128)(2,1)S(1)}, u32[]{:S(2)}, u32[]{:S(2)}) collective-permute-start(bf16[1024,256]{1,0:T(8,128)(2,1)S(1)} %get-tuple-element.239), channel_id=1, source_target_pairs={{0,2},{1,3},{2,0},{3,1},{4,6},{5,7},{6,4},{7,5},{8,10},{9,11},{10,... | collective-permute-start | bytes 1572872 | tf_op jit(solution)/shard_map/ppermute | solution.py:546
  160.1 118.3 %copy-start.3 = (bf16[2048,512]{1,0:T(8,128)(2,1)}, bf16[2048,512]{1,0:T(8,128)(2,1)S(1)}, u32[]{:S(2)}) copy-start(bf16[2048,512]{1,0:T(8,128)(2,1)S(1)} %get-tuple-element.121.refs_0_.mixed_ref) | copy-start | bytes 6291460
  160.3 54.0 %copy-start.5 = (bf16[1024,512]{1,0:T(8,128)(2,1)}, bf16[1024,512]{1,0:T(8,128)(2,1)S(1)}, u32[]{:S(2)}) copy-start(bf16[1024,512]{1,0:T(8,128)(2,1)S(1)} %pad_maximum_fusion.5.refs_2_.refs_4_.refs_1_.refs_3_) | copy-start | bytes 3145732
  167.2 4.2 collective-permute-start.14
  176.7 4.2 collective-permute-start.15
  177.5 26.5 %collective-permute-start.18 = (bf16[1024,1024]{1,0:T(8,128)(2,1)S(1)}, bf16[1024,1024]{1,0:T(8,128)(2,1)S(1)}, u32[]{:S(2)}, u32[]{:S(2)}) collective-permute-start(bf16[1024,1024]{1,0:T(8,128)(2,1)S(1)} %multiply_convert_fusion.mine_ref.refs_0_), channel_id=1, source_target_pairs={{0,1},{1,0},{2,3},{3,2},{4,5},{5,4},{6,7},{7,6},{8,9},{9,8},{10,11... | collective-permute-start | bytes 6291464 | tf_op jit(solution)/shard_map/ppermute | solution.py:546
  177.9 25.2 %collective-permute-start.17 = (bf16[1024,512]{1,0:T(8,128)(2,1)S(1)}, bf16[1024,512]{1,0:T(8,128)(2,1)S(1)}, u32[]{:S(2)}, u32[]{:S(2)}) collective-permute-start(bf16[1024,512]{1,0:T(8,128)(2,1)S(1)} %pad_maximum_fusion.6.refs_3_.refs_7_.refs_2_.refs_6_), channel_id=1, source_target_pairs={{0,2},{1,3},{2,0},{3,1},{4,6},{5,7},{6,4},{7,5},{8,10},{9,11},{10,... | collective-permute-start | bytes 3145736 | tf_op jit(solution)/shard_map/ppermute | solution.py:546
  179.1 24.9 %collective-permute-start.16 = (bf16[1024,512]{1,0:T(8,128)(2,1)S(1)}, bf16[1024,512]{1,0:T(8,128)(2,1)S(1)}, u32[]{:S(2)}, u32[]{:S(2)}) collective-permute-start(bf16[1024,512]{1,0:T(8,128)(2,1)S(1)} %pad_maximum_fusion.5.refs_2_.refs_4_.refs_1_.refs_3_), channel_id=1, source_target_pairs={{0,4},{1,5},{2,6},{3,7},{4,0},{5,1},{6,2},{7,3},{8,12},{9,13},{10,... | collective-permute-start | bytes 3145736 | tf_op jit(solution)/shard_map/ppermute | solution.py:546
  212.1 24.1 %collective-permute-start.19 = (bf16[1024,512]{1,0:T(8,128)(2,1)S(1)}, bf16[1024,512]{1,0:T(8,128)(2,1)S(1)}, u32[]{:S(2)}, u32[]{:S(2)}) collective-permute-start(bf16[1024,512]{1,0:T(8,128)(2,1)S(1)} %get-tuple-element.107), channel_id=1, source_target_pairs={{0,4},{1,5},{2,6},{3,7},{4,0},{5,1},{6,2},{7,3},{8,12},{9,13},{10,... | collective-permute-start | bytes 3145736 | tf_op jit(solution)/shard_map/ppermute | solution.py:546
  213.6 23.8 %collective-permute-start.20 = (bf16[1024,512]{1,0:T(8,128)(2,1)S(1)}, bf16[1024,512]{1,0:T(8,128)(2,1)S(1)}, u32[]{:S(2)}, u32[]{:S(2)}) collective-permute-start(bf16[1024,512]{1,0:T(8,128)(2,1)S(1)} %get-tuple-element.112), channel_id=1, source_target_pairs={{0,2},{1,3},{2,0},{3,1},{4,6},{5,7},{6,4},{7,5},{8,10},{9,11},{10,... | collective-permute-start | bytes 3145736 | tf_op jit(solution)/shard_map/ppermute | solution.py:546
  251.2 7.9 %collective-permute-start.21 = (bf16[1024,1024]{1,0:T(8,128)(2,1)S(1)}, bf16[1024,1024]{1,0:T(8,128)(2,1)S(1)}, u32[]{:S(2)}, u32[]{:S(2)}) collective-permute-start(bf16[1024,1024]{1,0:T(8,128)(2,1)S(1)} %get-tuple-element.118), channel_id=1, source_target_pairs={{0,1},{1,0},{2,3},{3,2},{4,5},{5,4},{6,7},{7,6},{8,9},{9,8},{10,11... | collective-permute-start | bytes 6291464 | tf_op jit(solution)/shard_map/ppermute | solution.py:546
  267.3 4.6 collective-permute-start.22
  267.9 48.5 %collective-permute-start.23 = (bf16[1024,256]{1,0:T(8,128)(2,1)S(1)}, bf16[1024,256]{1,0:T(8,128)(2,1)S(1)}, u32[]{:S(2)}, u32[]{:S(2)}) collective-permute-start(bf16[1024,256]{1,0:T(8,128)(2,1)S(1)} %get-tuple-element.125), channel_id=1, source_target_pairs={{0,2},{1,3},{2,0},{3,1},{4,6},{5,7},{6,4},{7,5},{8,10},{9,11},{10,... | collective-permute-start | bytes 1572872 | tf_op jit(solution)/shard_map/ppermute | solution.py:546
  268.9 47.6 %collective-permute-start.24 = (bf16[1024,256]{1,0:T(8,128)(2,1)S(1)}, bf16[1024,256]{1,0:T(8,128)(2,1)S(1)}, u32[]{:S(2)}, u32[]{:S(2)}) collective-permute-start(bf16[1024,256]{1,0:T(8,128)(2,1)S(1)} %get-tuple-element.128), channel_id=1, source_target_pairs={{0,4},{1,5},{2,6},{3,7},{4,0},{5,1},{6,2},{7,3},{8,12},{9,13},{10,... | collective-permute-start | bytes 1572872 | tf_op jit(solution)/shard_map/ppermute | solution.py:546
  269.4 62.3 %collective-permute-start.25 = (bf16[1024,512]{1,0:T(8,128)(2,1)S(1)}, bf16[1024,512]{1,0:T(8,128)(2,1)S(1)}, u32[]{:S(2)}, u32[]{:S(2)}) collective-permute-start(bf16[1024,512]{1,0:T(8,128)(2,1)S(1)} %get-tuple-element.111), channel_id=1, source_target_pairs={{0,4},{1,5},{2,6},{3,7},{4,0},{5,1},{6,2},{7,3},{8,12},{9,13},{10,... | collective-permute-start | bytes 3145736 | tf_op jit(solution)/shard_map/ppermute | solution.py:546
  270.9 60.8 %collective-permute-start.26 = (bf16[1024,512]{1,0:T(8,128)(2,1)S(1)}, bf16[1024,512]{1,0:T(8,128)(2,1)S(1)}, u32[]{:S(2)}, u32[]{:S(2)}) collective-permute-start(bf16[1024,512]{1,0:T(8,128)(2,1)S(1)} %get-tuple-element.131), channel_id=1, source_target_pairs={{0,2},{1,3},{2,0},{3,1},{4,6},{5,7},{6,4},{7,5},{8,10},{9,11},{10,... | collective-permute-start | bytes 3145736 | tf_op jit(solution)/shard_map/ppermute | solution.py:546
  330.6 38.6 %collective-permute-start.28 = (bf16[512,1024]{1,0:T(8,128)(2,1)}, bf16[512,1024]{1,0:T(8,128)(2,1)}, u32[]{:S(2)}, u32[]{:S(2)}) collective-permute-start(bf16[512,1024]{1,0:T(8,128)(2,1)} %pad_maximum_fusion.9), channel_id=1, source_target_pairs={{0,2},{1,3},{2,0},{3,1},{4,6},{5,7},{6,4},{7,5},{8,10},{9,11},{10,... | collective-permute-start | bytes 3145736 | tf_op jit(solution)/shard_map/ppermute | solution.py:546
  340.3 27.6 %collective-permute-start.31 = (bf16[1024,256]{1,0:T(8,128)(2,1)}, bf16[1024,256]{1,0:T(8,128)(2,1)}, u32[]{:S(2)}, u32[]{:S(2)}) collective-permute-start(bf16[1024,256]{1,0:T(8,128)(2,1)} %get-tuple-element.142), channel_id=1, source_target_pairs={{0,2},{1,3},{2,0},{3,1},{4,6},{5,7},{6,4},{7,5},{8,10},{9,11},{10,... | collective-permute-start | bytes 1572872 | tf_op jit(solution)/shard_map/ppermute | solution.py:546
  341.3 26.6 %collective-permute-start.32 = (bf16[1024,256]{1,0:T(8,128)(2,1)}, bf16[1024,256]{1,0:T(8,128)(2,1)}, u32[]{:S(2)}, u32[]{:S(2)}) collective-permute-start(bf16[1024,256]{1,0:T(8,128)(2,1)} %get-tuple-element.145), channel_id=1, source_target_pairs={{0,4},{1,5},{2,6},{3,7},{4,0},{5,1},{6,2},{7,3},{8,12},{9,13},{10,... | collective-permute-start | bytes 1572872 | tf_op jit(solution)/shard_map/ppermute | solution.py:546
  343.2 88.9 %reduce-scatter.5.cloned.1.call-start = ((), (), s32[]{:S(2)}) async-start(), calls=%async_computation.9 | async-start | bytes 1310720 | tf_op jit(solution)/shard_map/reduce_scatter | solution.py:762
  345.8 33.0 %collective-permute-start.27 = (bf16[512,1024]{1,0:T(8,128)(2,1)S(1)}, bf16[512,1024]{1,0:T(8,128)(2,1)S(1)}, u32[]{:S(2)}, u32[]{:S(2)}) collective-permute-start(bf16[512,1024]{1,0:T(8,128)(2,1)S(1)} %pad_maximum_fusion.8), channel_id=1, source_target_pairs={{0,4},{1,5},{2,6},{3,7},{4,0},{5,1},{6,2},{7,3},{8,12},{9,13},{10,... | collective-permute-start | bytes 3145736 | tf_op jit(solution)/shard_map/ppermute | solution.py:546
  371.8 26.9 %collective-permute-start.30 = (bf16[512,512]{1,0:T(8,128)(2,1)}, bf16[512,512]{1,0:T(8,128)(2,1)}, u32[]{:S(2)}, u32[]{:S(2)}) collective-permute-start(bf16[512,512]{1,0:T(8,128)(2,1)} %slice.259), channel_id=1, source_target_pairs={{0,4},{1,5},{2,6},{3,7},{4,0},{5,1},{6,2},{7,3},{8,12},{9,13},{10,... | collective-permute-start | bytes 1572872 | tf_op jit(solution)/shard_map/ppermute | solution.py:546
  380.2 20.6 %collective-permute-start.29 = (bf16[512,512]{1,0:T(8,128)(2,1)}, bf16[512,512]{1,0:T(8,128)(2,1)}, u32[]{:S(2)}, u32[]{:S(2)}) collective-permute-start(bf16[512,512]{1,0:T(8,128)(2,1)} %slice.260), channel_id=1, source_target_pairs={{0,2},{1,3},{2,0},{3,1},{4,6},{5,7},{6,4},{7,5},{8,10},{9,11},{10,... | collective-permute-start | bytes 1572872 | tf_op jit(solution)/shard_map/ppermute | solution.py:546
  398.7 33.4 %collective-permute-start.34 = (bf16[1024,1024]{1,0:T(8,128)(2,1)}, bf16[1024,1024]{1,0:T(8,128)(2,1)}, u32[]{:S(2)}, u32[]{:S(2)}) collective-permute-start(bf16[1024,1024]{1,0:T(8,128)(2,1)} %get-tuple-element.150), channel_id=1, source_target_pairs={{0,1},{1,0},{2,3},{3,2},{4,5},{5,4},{6,7},{7,6},{8,9},{9,8},{10,11... | collective-permute-start | bytes 6291464 | tf_op jit(solution)/shard_map/ppermute | solution.py:546
  420.0 19.9 %collective-permute-start.33 = (bf16[1024,1024]{1,0:T(8,128)(2,1)}, bf16[1024,1024]{1,0:T(8,128)(2,1)}, u32[]{:S(2)}, u32[]{:S(2)}) collective-permute-start(bf16[1024,1024]{1,0:T(8,128)(2,1)} %get-tuple-element.148), channel_id=1, source_target_pairs={{0,1},{1,0},{2,3},{3,2},{4,5},{5,4},{6,7},{7,6},{8,9},{9,8},{10,11... | collective-permute-start | bytes 6291464 | tf_op jit(solution)/shard_map/ppermute | solution.py:546
  424.2 27.5 %collective-permute-start.35 = (bf16[256,512]{0,1:T(8,128)(2,1)S(1)}, bf16[256,512]{0,1:T(8,128)(2,1)}, u32[]{:S(2)}, u32[]{:S(2)}) collective-permute-start(bf16[256,512]{0,1:T(8,128)(2,1)S(1)} %bitcast.142), channel_id=1, source_target_pairs={{0,8},{8,16},{16,24},{24,0},{1,9},{9,17},{17,25},{25,1},{2,10},{10... | collective-permute-start | bytes 786440 | tf_op jit(solution)/shard_map/ppermute | solution.py:588
  426.4 25.3 %collective-permute-start.36 = (bf16[256,512]{0,1:T(8,128)(2,1)S(1)}, bf16[256,512]{0,1:T(8,128)(2,1)}, u32[]{:S(2)}, u32[]{:S(2)}) collective-permute-start(bf16[256,512]{0,1:T(8,128)(2,1)S(1)} %bitcast.143), channel_id=1, source_target_pairs={{0,16},{8,24},{16,0},{24,8},{1,17},{9,25},{17,1},{25,9},{2,18},{10... | collective-permute-start | bytes 786440 | tf_op jit(solution)/shard_map/ppermute | solution.py:588
  430.2 21.5 %collective-permute-start.37 = (bf16[256,512]{0,1:T(8,128)(2,1)}, bf16[256,512]{0,1:T(8,128)(2,1)}, u32[]{:S(2)}, u32[]{:S(2)}) collective-permute-start(bf16[256,512]{0,1:T(8,128)(2,1)} %bitcast.52), channel_id=1, source_target_pairs={{0,24},{8,0},{16,8},{24,16},{1,25},{9,1},{17,9},{25,17},{2,26},{10... | collective-permute-start | bytes 786440 | tf_op jit(solution)/shard_map/ppermute | solution.py:588
  449.1 13.2 %all-to-all-start.2 = ((f32[32,14,128]{2,1,0:T(8,128)}), f32[32,14,128]{2,1,0:T(8,128)S(1)}, u32[]{:S(2)}, u32[]{:S(2)}) async-start(f32[32,14,128]{2,1,0:T(8,128)} %bitcast.42), calls=%async_computation.4 | async-start | bytes 524288 | tf_op jit(solution)/shard_map/all_to_all | solution.py:630
  464.7 10.8 %all-to-all-start.3 = ((f32[32,8,128]{2,1,0:T(8,128)}), f32[32,8,128]{2,1,0:T(8,128)S(1)}, u32[]{:S(2)}, u32[]{:S(2)}) async-start(f32[32,8,128]{2,1,0:T(8,128)} %bitcast.46), calls=%async_computation.5 | async-start | bytes 262144 | tf_op jit(solution)/shard_map/all_to_all | solution.py:630
  (48 other events, 305.4 us)
Sparse Core Ops, SparseCore 0:
  51.4 27.0 all-gather.2
  96.3 27.4 all-gather.4
  343.3 26.6 reduce-scatter.2
  383.6 26.2 reduce-scatter.4
